TPU v7x, 256 devices: a whole 4x4x8 slice. The times are simulated.
256 devices in a mesh: member: 4 (over y_lo, core), grid: 64 (over y_hi, z, x).
Axes of the slice: x: 4, y: 4 (y_hi: 2, y_lo: 2; y = y_hi * 2 + y_lo), z: 8, core: 2. Of those that a mesh axis runs over, the one named last changes fastest.
Arguments:
- mesh_features: float32 [8, 2048, 512], P('member', 'grid'), may hold values from -6 to 6
- grid_features: float32 [8, 32768, 512], P('member', 'grid'), may hold values from -6 to 6
- targets: float32 [100, 32768], P(None, 'grid'), may hold values from -12 to 12
- edges: int32 [4, 32768], P(None, 'grid'), may hold values from 0 to 2047, as said below
- src_weight: float32 [512, 512], replicated, may hold values from -0.25 to 0.25
- dst_weight: float32 [512, 512], replicated, may hold values from -0.25 to 0.25
- output_weight: float32 [512, 100], replicated, may hold values from -0.25 to 0.25
Outputs:
- loss: float32 [], replicated
- grid_grad: float32 [8, 32768, 512], P('member', 'grid')
- mesh_grad: float32 [8, 2048, 512], P('member', 'grid')
- src_grad: float32 [512, 512], replicated
- dst_grad: float32 [512, 512], replicated
- out_grad: float32 [512, 100], replicated
Inputs may be any that keep to these rules, and one draw needn't show every extreme that they name: `edges`: the mesh nodes of grid point p lie among the nodes (s - 1) * 32 to (s + 2) * 32 - 1, with s = p // 512.
All inputs are finite; a program needn't handle non-finite values.
Results may differ from a plain program's by a relative error of at most 0.0003.
Values sent between devices are 32-bit elements; how exact they have to be, the bound alone decides.
No kernel may reach another device: no remote copies, remote signals or barrier semaphores. Data moves between devices by JAX's collectives and lax.ppermute only.
A program may use at most 64 MiB of HBM per device.

v0:
```python
import jax
import jax.numpy as jnp
from jax import lax
from jax.sharding import PartitionSpec as P

alpha_fair = 0.95
smoothing = 0.1


def with_halo(shard, sides, width):
    for axis, dim in sides:
        peers, length = (lax.axis_size(axis), shard.shape[dim])
        up = [(i, (i + 1) % peers) for i in range(peers - 1)]
        down = [(j, i) for i, j in up]
        last = lax.slice_in_dim(shard, length - width, length, axis=dim)
        initial = lax.slice_in_dim(shard, 0, width, axis=dim)
        before = lax.ppermute(last, axis, up)
        after = lax.ppermute(initial, axis, down)
        shard = jnp.concatenate([before, shard, after], axis=dim)
    return shard


def passed_along(value, axis, steps):
    count = lax.axis_size(axis)
    initial, last = (max(0, -steps), min(count, count - steps))
    return lax.ppermute(value, axis, [(source, source + steps) for source in range(initial, last)])


def smooth_abs(value):
    return jnp.sqrt(value * value + smoothing * smoothing)


def silu_slope(value):
    sigma = jax.nn.sigmoid(value)
    return sigma * (1.0 + value * (1.0 - sigma))


def score_terms_list(own_members, all_members, truth):
    count = all_members.shape[0]
    spread = (1.0 - alpha_fair) / count
    factor = (1.0 - spread) / (count * (count - 1))
    error = own_members - truth[None]
    dist_truth = smooth_abs(error)
    pair_sum = jnp.zeros_like(own_members)
    pair_slope = jnp.zeros_like(own_members)
    for other in range(count):
        differ = own_members - all_members[other][None]
        distance = smooth_abs(differ)
        pair_sum = pair_sum + (distance - smoothing)
        pair_slope = pair_slope + differ / distance
    summed_loss = jnp.sum(dist_truth) / count - 0.5 * factor * jnp.sum(pair_sum)
    gradient_result = error / dist_truth / count - factor * pair_slope
    return (gradient_result, summed_loss)


def body(mesh_features, grid_features, targets, edges, src_weight, dst_weight, output_weight):
    highest_precision = lax.Precision.HIGHEST
    mesh_dev = mesh_features.shape[1]
    points_dev = grid_features.shape[1]
    slab_index = lax.axis_index("grid")
    projected = jnp.einsum("nrw,wu->nru", mesh_features, src_weight, precision=highest_precision)
    extended = with_halo(projected, (("grid", 1),), mesh_dev)
    local_index = edges - (slab_index - 1) * mesh_dev
    columns = jnp.arange(3 * mesh_dev, dtype=jnp.int32)
    one_hot = (local_index[:, :, None] == columns[None, None, :]).astype(jnp.float32)
    gathered = jnp.einsum("kpr,nru->nkpu", one_hot, extended, precision=highest_precision)
    query = jnp.einsum("npw,wu->npu", grid_features, dst_weight, precision=highest_precision)
    preact = gathered + query[:, None]
    summed_values = jnp.sum(jax.nn.silu(preact), axis=1)
    predicted_fields = jnp.einsum(
        "oyi,iz->ozy", summed_values, output_weight, precision=highest_precision
    )
    each_member_list = lax.all_gather(predicted_fields, "member", axis=0, tiled=True)
    activation_slope, partial_loss = score_terms_list(predicted_fields, each_member_list, targets)
    grad_summed = jnp.einsum(
        "nvp,wv->npw", activation_slope, output_weight, precision=highest_precision
    )
    grad_pre = grad_summed[:, None] * silu_slope(preact)
    grad_query = jnp.sum(grad_pre, axis=1)
    grad_ext = jnp.einsum("kpr,nkpu->nru", one_hot, grad_pre, precision=highest_precision)
    lower_rows = grad_ext[:, :mesh_dev]
    middle_rows = grad_ext[:, mesh_dev : 2 * mesh_dev]
    upper_rows = grad_ext[:, 2 * mesh_dev :]
    from_prev = passed_along(upper_rows, "grid", 1)
    from_next = passed_along(lower_rows, "grid", -1)
    grad_proj = middle_rows + from_prev + from_next
    grid_grad = jnp.einsum("npu,wu->npw", grad_query, dst_weight, precision=highest_precision)
    mesh_grad = jnp.einsum("nru,wu->nrw", grad_proj, src_weight, precision=highest_precision)
    src_part = jnp.einsum("nrw,nru->wu", mesh_features, grad_proj, precision=highest_precision)
    dst_part = jnp.einsum("npw,npu->wu", grid_features, grad_query, precision=highest_precision)
    out_part = jnp.einsum(
        "npw,nvp->wv", summed_values, activation_slope, precision=highest_precision
    )
    src_sum, dst_sum, out_sum, loss_total = lax.psum(
        (src_part, dst_part, out_part, partial_loss), ("member", "grid")
    )
    members_total = lax.axis_size("member") * mesh_features.shape[0]
    points_total = lax.axis_size("grid") * points_dev
    scale = 1.0 / jnp.sqrt(jnp.float32(members_total * points_total))
    loss = loss_total / (points_total * targets.shape[0])
    return (loss, grid_grad, mesh_grad, src_sum * scale, dst_sum * scale, out_sum * scale)


def solution(mesh):
    placed = (
        P("member", "grid", None),
        P("member", "grid", None),
        P(None, "grid"),
        P(None, "grid"),
        P(),
        P(),
        P(),
    )
    return jax.shard_map(
        body,
        mesh=mesh,
        in_specs=placed,
        out_specs=(P(), P("member", "grid", None), P("member", "grid", None), P(), P(), P()),
        check_vma=False,
    )
```

profile of v0, /device:TPU:1, one launch (start us, length us, event | category | flops | bytes accessed | tf_op | source)
XLA Modules:
  0.0 378.9 jit_solution(15874068050225851697)
XLA Ops:
  7.2 0.0 copy-start
  7.2 0.0 all-gather.2.cloned.1.call-start
  7.2 2.2 fusion.6
  9.4 1.3 collective-permute-start.1
  10.7 4.6 %collective-permute-start = (f32[2,32,512]{2,1,0:T(8,128)S(1)}, f32[2,32,512]{2,1,0:T(8,128)S(1)}, u32[]{:S(2)}, u32[]{:S(2)}) collective-permute-start(f32[2,32,512]{2,1,0:T(8,128)S(1)} %fusion.6), channel_id=1, source_target_pairs={{0,1},{1,2},{2,3},{3,4},{4,5},{5,6},{6,7},{7,8},{8,9},{9,10},{10,1... | collective-permute-start | bytes 393224 | tf_op jit(solution)/shard_map/ppermute | solution.py:17
  15.3 0.0 copy-done
  15.3 0.0 copy-start.17
  15.3 4.7 %fusion.2 = f32[2,512,512]{1,2,0:T(8,128)S(1)} fusion(f32[2,512,512]{2,1,0:T(8,128)S(1)} %copy-done, f32[512,512]{1,0:T(8,128)} %param.12), kind=kOutput, calls=%fused_computation.11 | convolution fusion | flops 3221225472 | bytes 5242880 | tf_op jit(solution)/shard_map/npw,wu->npu/dot_general | solution.py:67
  20.1 0.0 copy-start.5
  20.1 0.0 copy-start.9
  20.1 0.0 collective-permute-done.1
  20.1 0.0 collective-permute-done
  20.1 7.7 %multiply_reduce_fusion = (f32[2,512,512]{1,2,0:T(8,128)S(1)}, f32[2,512,4,512]{3,1,2,0:T(8,128)}) fusion(f32[2,512,512]{1,2,0:T(8,128)S(1)} %fusion.2, s32[4,512]{1,0:T(4,128)S(1)} %broadcast_subtract_fusion, f32[2,32,512]{2,1,0:T(8,128)S(1)} %collective-permute-done.1, f32[2,32,512]{2,1,0:T(8,128)S(1)} %fusion.6, f32[2,32,512]{2,1,0:T(8,128)S(1)} %collective-permute-done), kind=kOutput, calls=%fused_computation.2 | convolution fusion | flops 2428370944 | bytes 12984320 | tf_op jit(solution)/shard_map/kpr,nru->nkpu/dot_general | solution.py:66
  27.9 1.4 copy-done.2
  29.3 0.0 copy-done.9
  29.3 2.1 convolution_bitcast_fusion.2
  31.3 0.0 all-gather.2.cloned.1.call-update
  31.4 0.2 all-reduce.3.cloned.1.call-start
  31.6 35.8 %all-gather.2.cloned.1.call-done = f32[8,100,512]{2,1,0:T(8,128)} async-done(((f32[2,100,512]{2,1,0:T(8,128)}), f32[8,100,512]{2,1,0:T(8,128)}) %all-gather.2.cloned.1.call-update) | async-done | bytes 1638416 | tf_op jit(solution)/shard_map/all_gather | solution.py:73
  67.4 1.8 slice_bitcast_fusion.7
  69.2 3.2 add_reduce_fusion
  72.4 1.8 fusion.19
  74.3 0.0 copy-done.4
  74.3 4.8 %fusion.26 = (f32[2,512,512]{1,2,0:T(8,128)S(1)}, f32[2,4,512,512]{2,3,1,0:T(8,128)S(1)}) fusion(f32[2,512,512]{1,2,0:T(8,128)} %copy-done.5, f32[2,512,4,512]{3,1,2,0:T(8,128)S(1)} %copy-done.4, f32[2,512,512]{1,2,0:T(8,128)S(1)} %fusion.19), kind=kLoop, calls=%fused_computation.57 | loop fusion | flops 20447232 | bytes 23068672 | tf_op jit(solution)/shard_map/reduce_sum | solution.py:79
  79.1 4.5 %convolution_bitcast_fusion.3 = f32[2,96,512]{2,1,0:T(8,128)S(1)} fusion(f32[2,4,512,512]{2,3,1,0:T(8,128)S(1)} %get-tuple-element.24, s32[4,512]{1,0:T(4,128)S(1)} %broadcast_subtract_fusion), kind=kOutput, calls=%fused_computation.7 | convolution fusion | flops 2416115712 | bytes 8790016 | tf_op jit(solution)/shard_map/kpr,nkpu->nru/dot_general | solution.py:80
  83.7 3.1 collective-permute-start.2
  86.8 1.5 collective-permute-start.3
  88.3 4.5 %convolution_bitcast_fusion = f32[512,512]{0,1:T(8,128)} fusion(f32[2,512,512]{1,2,0:T(8,128)S(1)} %get-tuple-element.23, f32[2,512,512]{2,1,0:T(8,128)S(1)} %copy-done), kind=kOutput, calls=%fused_computation.4 | convolution fusion | flops 3221225472 | bytes 5242880 | tf_op jit(solution)/shard_map/npw,npu->wu/dot_general | solution.py:90
  92.8 0.0 copy-done.3
  92.8 2.9 convolution_bitcast_fusion.4
  95.7 0.0 collective-permute-done.2
  95.7 0.0 collective-permute-done.3
  95.7 0.6 copy-done.11
  96.3 0.7 copy-done.13
  97.0 0.0 copy-done.10
  97.0 2.0 convolution_bitcast_fusion.1
  99.0 0.0 all-reduce.3.cloned.1.call-update
  100.3 80.4 %psum.28 = f32[]{:T(128)} all-reduce(f32[]{:T(128)S(6)} %sub.167), channel_id=1, replica_groups=mesh['member'=4,'grid'=64] {'member','grid'}, use_global_device_ids=true, to_apply=%region_3.4 | all-reduce | flops 1 | bytes 8 | tf_op jit(solution)/shard_map/psum | solution.py:94
  181.4 0.0 copy-start.7
  181.4 0.0 copy-start.14
  181.4 9.7 %fusion = f32[2,512,512]{2,1,0:T(8,128)} fusion(f32[2,512,512]{1,2,0:T(8,128)} %copy-done.1, f32[512,512]{1,0:T(8,128)S(1)} %copy-done.6), kind=kOutput, calls=%fused_computation.9 | convolution fusion | flops 3221225472 | bytes 5242880 | tf_op jit(solution)/shard_map/npu,wu->npw/dot_general | solution.py:87
  191.1 1.8 fusion.4
  192.9 170.6 %all-reduce.3.cloned.1.call-done = (f32[512,512]{0,1:T(8,128)}, f32[512,512]{0,1:T(8,128)}, f32[512,100]{0,1:T(8,128)}) async-done(((f32[512,512]{0,1:T(8,128)}, f32[512,512]{0,1:T(8,128)}, f32[512,100]{0,1:T(8,128)}), (f32[512,512]{0,1:T(8,128)}, f32[512,512]{0,1:T(8,128)}, f32[512,100]{0,1:T(8,128)})) %all-reduce.3.cloned.1.call-update) | async-done | bytes 2301968 | tf_op jit(solution)/shard_map/psum | solution.py:94
  363.5 2.8 broadcast_multiply_fusion
  366.3 2.6 copy.26
  368.9 0.0 copy-done.16
  368.9 0.7 broadcast_multiply_fusion.2
  369.6 1.3 copy.25
  (23 shorter events, 0.1 us)
Async XLA Ops:
  7.2 8.1 %copy-start = (f32[2,512,512]{2,1,0:T(8,128)S(1)}, f32[2,512,512]{2,1,0:T(8,128)}, u32[]{:S(2)}) copy-start(f32[2,512,512]{2,1,0:T(8,128)} %param.8) | copy-start | bytes 6291460
  7.2 60.2 %all-gather.2.cloned.1.call-start = ((), (), s32[]{:S(2)}) async-start(), calls=%async_computation | async-start | bytes 2129920 | tf_op jit(solution)/shard_map/all_gather | solution.py:73
  9.4 10.7 %collective-permute-start.1 = (f32[2,32,512]{2,1,0:T(8,128)S(1)}, f32[2,32,512]{2,1,0:T(8,128)S(1)}, u32[]{:S(2)}, u32[]{:S(2)}) collective-permute-start(f32[2,32,512]{2,1,0:T(8,128)S(1)} %fusion.6), channel_id=1, source_target_pairs={{1,0},{2,1},{3,2},{4,3},{5,4},{6,5},{7,6},{8,7},{9,8},{10,9},{11,1... | collective-permute-start | bytes 393224 | tf_op jit(solution)/shard_map/ppermute | solution.py:18
  10.7 9.4 %collective-permute-start = (f32[2,32,512]{2,1,0:T(8,128)S(1)}, f32[2,32,512]{2,1,0:T(8,128)S(1)}, u32[]{:S(2)}, u32[]{:S(2)}) collective-permute-start(f32[2,32,512]{2,1,0:T(8,128)S(1)} %fusion.6), channel_id=1, source_target_pairs={{0,1},{1,2},{2,3},{3,4},{4,5},{5,6},{6,7},{7,8},{8,9},{9,10},{10,1... | collective-permute-start | bytes 393224 | tf_op jit(solution)/shard_map/ppermute | solution.py:17
  15.3 4.8 %copy-start.17 = (s32[4,512]{1,0:T(4,128)S(1)}, s32[4,512]{1,0:T(4,128)}, u32[]{:S(2)}) copy-start(s32[4,512]{1,0:T(4,128)} %param.10) | copy-start | bytes 24580
  20.1 7.8 %copy-start.5 = (f32[2,512,512]{1,2,0:T(8,128)}, f32[2,512,512]{1,2,0:T(8,128)S(1)}, u32[]{:S(2)}) copy-start(f32[2,512,512]{1,2,0:T(8,128)S(1)} %fusion.2) | copy-start | bytes 6291460
  20.1 9.2 %copy-start.9 = (f32[512,100]{0,1:T(8,128)S(1)}, f32[512,100]{0,1:T(8,128)}, u32[]{:S(2)}) copy-start(f32[512,100]{0,1:T(8,128)} %param.13) | copy-start | bytes 614404
  27.9 1.4 copy-start.2
  31.3 37.9 %copy-start.8 = (f32[2,100,512]{2,1,0:T(8,128)S(1)}, f32[2,100,512]{2,1,0:T(8,128)}, u32[]{:S(2)}) copy-start(f32[2,100,512]{2,1,0:T(8,128)} %convolution_bitcast_fusion.2) | copy-start | bytes 1228804
  31.3 37.9 %copy-start.15 = (f32[100,512]{1,0:T(8,128)S(1)}, f32[100,512]{1,0:T(8,128)}, u32[]{:S(2)}) copy-start(f32[100,512]{1,0:T(8,128)} %param.9) | copy-start | bytes 614404
  31.4 332.1 %all-reduce.3.cloned.1.call-start = ((), (), s32[]{:S(2)}) async-start(), calls=%async_computation.1 | async-start | bytes 4620288 | tf_op jit(solution)/shard_map/psum | solution.py:94
  67.4 6.9 %copy-start.4 = (f32[2,512,4,512]{3,1,2,0:T(8,128)S(1)}, f32[2,512,4,512]{3,1,2,0:T(8,128)}, u32[]{:S(2)}) copy-start(f32[2,512,4,512]{3,1,2,0:T(8,128)} %get-tuple-element.37) | copy-start | bytes 25165828
  79.1 9.2 %copy-start.1 = (f32[2,512,512]{1,2,0:T(8,128)}, f32[2,512,512]{1,2,0:T(8,128)S(1)}, u32[]{:S(2)}) copy-start(f32[2,512,512]{1,2,0:T(8,128)S(1)} %get-tuple-element.23) | copy-start | bytes 6291460
  83.7 12.0 %collective-permute-start.2 = (f32[2,32,512]{2,1,0:T(8,128)S(1)}, f32[2,32,512]{2,1,0:T(8,128)S(1)}, u32[]{:S(2)}, u32[]{:S(2)}) collective-permute-start(f32[2,32,512]{2,1,0:T(8,128)S(1)} %get-tuple-element.34), channel_id=1, source_target_pairs={{0,1},{1,2},{2,3},{3,4},{4,5},{5,6},{6,7},{7,8},{8,9},{9,10},{10,1... | collective-permute-start | bytes 393224 | tf_op jit(solution)/shard_map/ppermute | solution.py:26
  86.8 8.9 %collective-permute-start.3 = (f32[2,32,512]{2,1,0:T(8,128)S(1)}, f32[2,32,512]{2,1,0:T(8,128)S(1)}, u32[]{:S(2)}, u32[]{:S(2)}) collective-permute-start(f32[2,32,512]{2,1,0:T(8,128)S(1)} %get-tuple-element.35), channel_id=1, source_target_pairs={{1,0},{2,1},{3,2},{4,3},{5,4},{6,5},{7,6},{8,7},{9,8},{10,9},{11,1... | collective-permute-start | bytes 393224 | tf_op jit(solution)/shard_map/ppermute | solution.py:26
  88.3 4.5 %copy-start.3 = (f32[2,512,512]{1,2,0:T(8,128)S(1)}, f32[2,512,512]{1,2,0:T(8,128)}, u32[]{:S(2)}) copy-start(f32[2,512,512]{1,2,0:T(8,128)} %copy-done.2) | copy-start | bytes 6291460
  92.8 4.2 %copy-start.10 = (f32[2,32,512]{2,1,0:T(8,128)S(1)}, f32[2,32,512]{2,1,0:T(8,128)}, u32[]{:S(2)}) copy-start(f32[2,32,512]{2,1,0:T(8,128)} %param.7) | copy-start | bytes 393220
  95.7 85.7 %copy-start.6 = (f32[512,512]{1,0:T(8,128)S(1)}, f32[512,512]{1,0:T(8,128)}, u32[]{:S(2)}) copy-start(f32[512,512]{1,0:T(8,128)} %param.12) | copy-start | bytes 3145732
  95.7 0.7 copy-start.11
  96.3 0.7 copy-start.13
  181.4 9.7 %copy-start.7 = (f32[512,512]{1,0:T(8,128)S(1)}, f32[512,512]{1,0:T(8,128)}, u32[]{:S(2)}) copy-start(f32[512,512]{1,0:T(8,128)} %param.11) | copy-start | bytes 3145732
  181.4 9.7 %copy-start.12 = (f32[2,32,512]{2,1,0:T(8,128)S(1)}, f32[2,32,512]{2,1,0:T(8,128)}, u32[]{:S(2)}) copy-start(f32[2,32,512]{2,1,0:T(8,128)} %copy-done.11) | copy-start | bytes 393220
  181.4 9.7 %copy-start.14 = (f32[2,32,512]{2,1,0:T(8,128)S(1)}, f32[2,32,512]{2,1,0:T(8,128)}, u32[]{:S(2)}) copy-start(f32[2,32,512]{2,1,0:T(8,128)} %copy-done.13) | copy-start | bytes 393220
  366.3 2.6 copy-start.16
Sparse Core Ops, SparseCore 0:
  31.5 35.8 all-gather.1
  99.1 264.3 all-reduce.2
where the time goes:
time: 380 us; the launch traced here: 379 us
  waiting for transfers between devices  206 us (54%)
  blocking collectives  80.4 us (21%)
  matrix products  43.9 us (12%)
  between operations  17.3 us (5%)
  other arithmetic  11.6 us (3%)
  starting transfers between devices  10.7 us (3%)
  local copies, waits for them, and re-layouts  8.45 us (2%)
    psum x1, waiting for transfers between devices, body(): lax.psum((src_part, dst_part, out_part, partial_loss), ('member', 'grid'))  171 us
    psum x1, blocking collectives, body(): lax.psum((src_part, dst_part, out_part, partial_loss), ('member', 'grid'))  80.4 us
    all_gather x1, waiting for transfers between devices, body(): lax.all_gather(predicted_fields, 'member', axis=0, tiled=True)  35.8 us
    dot_general x1, matrix products, body(): jnp.einsum('npu,wu->npw', grad_query, dst_weight, precision=highest_preci...  9.67 us
    dot_general x1, matrix products, body(): jnp.einsum('kpr,nru->nkpu', one_hot, extended, precision=highest_precision)  7.75 us
  transfers between devices with their start and end apart: 6, of which 2 were waited for; matrix products, arithmetic and copies ran while one was open for 6% of the time, Pallas kernels for 0%

commit v1 on v0

v1 whole, which is shorter than its diff:
```python
import functools

import jax
import jax.numpy as jnp
from jax import lax
from jax.experimental import pallas as pl
from jax.experimental.pallas import tpu as pltpu
from jax.sharding import PartitionSpec as P

alpha_fair = 0.95
smoothing = 0.1
axes = ("member", "grid")
vmem_limit = 56 * 1024 * 1024
f32 = jnp.float32
bf16 = jnp.bfloat16
interpret = False


def place_of(member, grid):
    return {
        "core": member & 1,
        "y": ((grid >> 5) << 1) | (member >> 1),
        "z": (grid >> 2) & 7,
        "x": grid & 3,
    }


def exchange(change):
    pairs = []
    for member in range(4):
        for grid in range(64):
            place = place_of(member, grid)
            place = {**place, **change(place)}
            member_to = ((place["y"] & 1) << 1) | place["core"]
            grid_to = ((place["y"] >> 1) << 5) | (place["z"] << 2) | place["x"]
            pairs.append((member * 64 + grid, member_to * 64 + grid_to))
    return pairs


swap_core = exchange(lambda c: {"core": c["core"] ^ 1})
first_axis = [
    exchange(lambda c, k=k: {"x": c["x"] ^ k} if c["core"] == 0 else {"y": c["y"] ^ k}) for k in range(4)
]
second_axis = [
    exchange(lambda c, k=k: {"y": c["y"] ^ k} if c["core"] == 0 else {"x": c["x"] ^ k}) for k in range(4)
]
along_z = [exchange(lambda c, k=k: {"z": c["z"] ^ k}) for k in range(8)]


def send(value, pairs):
    return lax.ppermute(value, axes, pairs)


def split(value):
    high = value.astype(bf16)
    return high, (value - high.astype(f32)).astype(bf16)


def dot3(left, right, dims):
    def one(a, b):
        return lax.dot_general(a, b, (dims, ((), ())), preferred_element_type=f32)

    return one(left[0], right[0]) + (one(left[0], right[1]) + one(left[1], right[0]))


NN = ((1,), (0,))
NT = ((1,), (1,))
TN = ((0,), (0,))


def forward_kernel(points, me, query, edges, before, own, after, src_weight, out_weight,
                   slope, summed, part0, part1, part2, part3, nodes, fields):
    member, tile = pl.program_id(0), pl.program_id(1)
    tiles = pl.num_programs(1)
    rows = own.shape[1]

    @pl.when((member == 0) & (tile == 0))
    def _():
        nodes[...] = jnp.zeros_like(nodes)
        weight = split(src_weight[...])
        for n in range(own.shape[0]):
            ext = jnp.concatenate([before[n], own[n], after[n]], axis=0)
            high, low = split(dot3(split(ext), weight, NN))
            nodes[n, 0 : 3 * rows] = high
            nodes[n, 128 : 128 + 3 * rows] = low

    local = edges[...] - (me[1] - 1) * rows
    columns = lax.broadcasted_iota(jnp.int32, (points, 256), 1) & 127
    total = None
    for k in range(4):
        hot = jnp.where(local[:, k : k + 1] == columns, 1.0, 0.0).astype(bf16)
        value = query[0] + jnp.dot(hot, nodes[member], preferred_element_type=f32)
        sigma = 0.5 * jnp.tanh(0.5 * value) + 0.5
        active = value * sigma
        slope[0, k] = sigma + active * (1.0 - sigma)
        total = active if total is None else total + active
    summed[0] = total
    weight = split(out_weight[...])
    fields[:, pl.ds(pl.multiple_of(tile * points, 128), points)] = dot3(weight, split(total), NT)

    @pl.when(tile == tiles - 1)
    def _():
        for k, part in enumerate((part0, part1, part2, part3)):
            part[member] = fields[:, pl.ds(pl.multiple_of((me[0] ^ k) * 128, 128), 128)]


def score_kernel(count_vars, me, part0, part1, part2, part3, targets, out0, out1, out2, out3, loss):
    parts, outs = (part0, part1, part2, part3), (out0, out1, out2, out3)
    count = 8
    spread = (1.0 - alpha_fair) / count
    factor = (1.0 - spread) / (count * (count - 1))
    rows = targets.shape[0]
    near = jnp.zeros((8, 128), f32)
    far = jnp.zeros((8, 128), f32)
    for block in range(rows // 8):
        at = pl.ds(block * 8, 8)
        real = block * 8 + lax.broadcasted_iota(jnp.int32, (8, 128), 0) < count_vars
        truth = targets[at]
        fields = [parts[j // 2][j % 2, at] for j in range(count)]
        slopes, dist_sum = [], None
        for field in fields:
            error = field - truth
            square = error * error + smoothing * smoothing
            inverse = lax.rsqrt(square)
            dist = square * inverse
            dist_sum = dist if dist_sum is None else dist_sum + dist
            slopes.append(error * inverse * (1.0 / count))
        pair_sum = None
        pairs = [None] * count
        for j in range(count):
            for k in range(j + 1, count):
                differ = fields[j] - fields[k]
                square = differ * differ + smoothing * smoothing
                inverse = lax.rsqrt(square)
                dist = square * inverse - smoothing
                pair_sum = dist if pair_sum is None else pair_sum + dist
                term = differ * inverse
                pairs[j] = term if pairs[j] is None else pairs[j] + term
                pairs[k] = -term if pairs[k] is None else pairs[k] - term
        near += jnp.where(real, dist_sum, 0.0)
        far += jnp.where(real, pair_sum, 0.0)
        for j in range(count):
            outs[j // 2][j % 2, at] = slopes[j] - factor * pairs[j]
    loss[...] = near * (1.0 / count) - factor * far


def backward_kernel(points, scale, loss_scale, me, part0, part1, part2, part3, loss, slope, summed, features,
                    edges, before, own, after, out_weight,
                    grad_query, grad_ext, keep, away, slopes, sums):
    member, tile = pl.program_id(0), pl.program_id(1)
    members, tiles = pl.num_programs(0), pl.num_programs(1)
    rows = own.shape[1]
    width = features.shape[2]
    vars_rows = out_weight.shape[0]

    @pl.when((member == 0) & (tile == 0))
    def _():
        sums[...] = jnp.zeros_like(sums)
        grad_ext[...] = jnp.zeros_like(grad_ext)
        for k, part in enumerate((part0, part1, part2, part3)):
            for n in range(2):
                slopes[n, :, pl.ds(pl.multiple_of((me[0] ^ k) * 128, 128), 128)] = part[n]

    here = split(slopes[member, :, pl.ds(pl.multiple_of(tile * points, 128), points)])
    back = dot3(here, split(out_weight[...]), TN)
    sums[2 * width : 2 * width + vars_rows] += dot3(here, split(summed[0]), NN)
    local = edges[...] - (me[1] - 1) * rows
    nodes = lax.broadcasted_iota(jnp.int32, (3 * rows, points), 0)
    scattered = None
    slope_sum = None
    for k in range(4):
        hot = jnp.where(local[k : k + 1] == nodes, 1.0, 0.0).astype(bf16)
        slope_k = slope[0, k]
        slope_sum = slope_k if slope_sum is None else slope_sum + slope_k
        high, low = split(back * slope_k)
        term = jnp.dot(hot, high, preferred_element_type=f32) + jnp.dot(
            hot, low, preferred_element_type=f32
        )
        scattered = term if scattered is None else scattered + term
    grad_ext[member] += scattered
    into_query = back * slope_sum
    grad_query[0] = into_query
    sums[width : 2 * width] += dot3(split(features[0]), split(into_query), TN)

    @pl.when((member == members - 1) & (tile == tiles - 1))
    def _():
        ext = jnp.concatenate([side[n] for n in range(2) for side in (before, own, after)], axis=0)
        grads = jnp.concatenate([grad_ext[0], grad_ext[1]], axis=0)
        sums[0:width] = dot3(split(ext), split(grads), TN)
        end = 2 * width + vars_rows
        sums[end : end + 8] = jnp.concatenate(
            [loss[...] * (loss_scale / scale), jnp.zeros((8, width - 128), f32)], axis=1
        )
        for j in range(16):
            for out, core, order in ((keep, me[2], me[3]), (away, 1 - me[2], me[4])):
                chunk = core * 16 + (j ^ order)
                at = pl.ds(pl.multiple_of((chunk >> 1) * 72, 8), 72)
                lanes = pl.ds(pl.multiple_of((chunk & 1) * 256, 128), 256)
                out[j] = sums[at, lanes] * scale


def finish_kernel(me, mine, other, src_grad, dst_grad, out_grad, loss, sums):
    width = src_grad.shape[0]
    for j in range(16):
        for part, core, order in ((mine, me[2], me[3]), (other, 1 - me[2], me[4])):
            chunk = core * 16 + (j ^ order)
            at = pl.ds(pl.multiple_of((chunk >> 1) * 72, 8), 72)
            lanes = pl.ds(pl.multiple_of((chunk & 1) * 256, 128), 256)
            sums[at, lanes] = part[j]
    src_grad[...] = sums[0:width]
    dst_grad[...] = sums[width : 2 * width]
    rows = 128
    out_grad[...] = sums[2 * width : 2 * width + rows].T[:, : out_grad.shape[1]]
    end = 2 * width + 104
    loss[...] = sums[end : end + 8, 0:128]


def whole(shape=None):
    return pl.BlockSpec(memory_space=pltpu.VMEM)


def params(dims):
    return pltpu.CompilerParams(dimension_semantics=("arbitrary",) * dims, vmem_limit_bytes=vmem_limit)


def all_reduce(keep, away):
    total = keep + send(away, swap_core)
    for group, size in ((first_axis, 4), (second_axis, 1)):
        parts = [send(total[k * size : (k + 1) * size], group[k]) for k in (1, 2, 3)]
        total = total[:size] + parts[0] + parts[1] + parts[2]
    parts = [send(total, along_z[k]) for k in (1, 2, 3)]
    total = total + parts[0] + parts[1] + parts[2]
    total = total + send(total, along_z[4])
    for group in (second_axis, first_axis):
        total = jnp.concatenate([total] + [send(total, group[k]) for k in (1, 2, 3)], axis=0)
    return total, send(total, swap_core)


def body(mesh_features, grid_features, targets, edges, src_weight, dst_weight, output_weight):
    members, rows, width = mesh_features.shape
    points = grid_features.shape[1]
    count_vars = targets.shape[0]
    var_rows = -(-count_vars // 8) * 8
    slabs = lax.axis_size("grid")
    member, grid = lax.axis_index("member"), lax.axis_index("grid")
    place = place_of(member, grid)
    x_then_y = place["x"] * 4 + place["y"]
    y_then_x = place["y"] * 4 + place["x"]
    straight = place["core"] == 0
    me = jnp.stack([
        member,
        grid,
        place["core"],
        jnp.where(straight, x_then_y, y_then_x),
        jnp.where(straight, y_then_x, x_then_y),
    ]).astype(jnp.int32)

    up = [(i, i + 1) for i in range(slabs - 1)]
    down = [(j, i) for i, j in up]
    before = lax.ppermute(mesh_features, "grid", up)
    after = lax.ppermute(mesh_features, "grid", down)
    query = jnp.einsum("npw,wu->npu", grid_features, dst_weight, precision=lax.Precision.HIGH)
    edges_t = edges.T
    out_weight = jnp.pad(output_weight.T, ((0, var_rows - count_vars), (0, 0)))
    targets = jnp.pad(targets, ((0, var_rows - count_vars), (0, 0)))

    tile = 256
    tiles = points // tile
    part_shape = jax.ShapeDtypeStruct((members, var_rows, 128), f32)
    slope, summed, *parts = pl.pallas_call(
        functools.partial(forward_kernel, tile),
        grid_spec=pltpu.PrefetchScalarGridSpec(
            num_scalar_prefetch=1,
            grid=(members, tiles),
            in_specs=[
                pl.BlockSpec((1, tile, width), lambda n, t, me: (n, t, 0)),
                pl.BlockSpec((tile, 4), lambda n, t, me: (t, 0)),
                whole(), whole(), whole(), whole(), whole(),
            ],
            out_specs=[
                pl.BlockSpec((1, 4, tile, width), lambda n, t, me: (n, 0, t, 0)),
                pl.BlockSpec((1, tile, width), lambda n, t, me: (n, t, 0)),
            ] + [whole()] * 4,
            scratch_shapes=[
                pltpu.VMEM((members, 256, width), bf16),
                pltpu.VMEM((var_rows, points), f32),
            ],
        ),
        out_shape=[
            jax.ShapeDtypeStruct((members, 4, points, width), f32),
            jax.ShapeDtypeStruct((members, points, width), f32),
        ] + [part_shape] * 4,
        compiler_params=params(2),
        name="forward",
        interpret=interpret,
    )(me, query, edges_t, before, mesh_features, after, src_weight, out_weight)

    to_peer = [[(i, i ^ k) for i in range(4)] for k in range(4)]
    parts = [parts[0]] + [lax.ppermute(parts[k], "member", to_peer[k]) for k in (1, 2, 3)]
    *slopes, loss = pl.pallas_call(
        functools.partial(score_kernel, count_vars),
        grid_spec=pltpu.PrefetchScalarGridSpec(
            num_scalar_prefetch=1,
            grid=(1,),
            in_specs=[whole()] * 4 + [pl.BlockSpec((var_rows, 128), lambda i, me: (0, me[0]))],
            out_specs=[whole()] * 5,
        ),
        out_shape=[part_shape] * 4 + [jax.ShapeDtypeStruct((8, 128), f32)],
        compiler_params=params(1),
        name="score",
        interpret=interpret,
    )(me, *parts, targets)
    slopes = [slopes[0]] + [lax.ppermute(slopes[k], "member", to_peer[k]) for k in (1, 2, 3)]

    total_members = lax.axis_size("member") * members
    scale = 1.0 / (total_members * points * slabs) ** 0.5
    loss_scale = 1.0 / (points * slabs * count_vars)
    chunks = jax.ShapeDtypeStruct((16, 72, 256), f32)
    grad_query, grad_ext, keep, away = pl.pallas_call(
        functools.partial(backward_kernel, tile, scale, loss_scale),
        grid_spec=pltpu.PrefetchScalarGridSpec(
            num_scalar_prefetch=1,
            grid=(members, tiles),
            in_specs=[whole()] * 5 + [
                pl.BlockSpec((1, 4, tile, width), lambda n, t, me: (n, 0, t, 0)),
                pl.BlockSpec((1, tile, width), lambda n, t, me: (n, t, 0)),
                pl.BlockSpec((1, tile, width), lambda n, t, me: (n, t, 0)),
                pl.BlockSpec((4, tile), lambda n, t, me: (0, t)),
                whole(), whole(), whole(), whole(),
            ],
            out_specs=[
                pl.BlockSpec((1, tile, width), lambda n, t, me: (n, t, 0)),
                whole(), whole(), whole(),
            ],
            scratch_shapes=[
                pltpu.VMEM((members, var_rows, points), f32),
                pltpu.VMEM((1152, width), f32),
            ],
        ),
        out_shape=[
            jax.ShapeDtypeStruct((members, points, width), f32),
            jax.ShapeDtypeStruct((members, 3 * rows, width), f32),
            chunks,
            chunks,
        ],
        compiler_params=params(2),
        name="backward",
        interpret=interpret,
    )(me, *slopes, loss, slope, summed, grid_features, edges, before, mesh_features, after, out_weight)

    mine, other = all_reduce(keep, away)
    from_prev = lax.ppermute(grad_ext[:, 2 * rows :], "grid", up)
    from_next = lax.ppermute(grad_ext[:, :rows], "grid", down)
    grid_grad = jnp.einsum("npu,wu->npw", grad_query, dst_weight, precision=lax.Precision.HIGH)
    grad_proj = grad_ext[:, rows : 2 * rows] + from_prev + from_next
    mesh_grad = jnp.einsum("nru,wu->nrw", grad_proj, src_weight, precision=lax.Precision.HIGH)

    square = jax.ShapeDtypeStruct((width, width), f32)
    src_grad, dst_grad, out_grad, loss = pl.pallas_call(
        finish_kernel,
        grid_spec=pltpu.PrefetchScalarGridSpec(
            num_scalar_prefetch=1,
            grid=(1,),
            in_specs=[whole()] * 2,
            out_specs=[whole()] * 4,
            scratch_shapes=[pltpu.VMEM((1152, width), f32)],
        ),
        out_shape=[
            square,
            square,
            jax.ShapeDtypeStruct((width, count_vars), f32),
            jax.ShapeDtypeStruct((8, 128), f32),
        ],
        compiler_params=params(1),
        name="finish",
        interpret=interpret,
    )(me, mine, other)
    return (jnp.sum(loss), grid_grad, mesh_grad, src_grad, dst_grad, out_grad)


def solution(mesh):
    placed = (
        P("member", "grid", None),
        P("member", "grid", None),
        P(None, "grid"),
        P(None, "grid"),
        P(),
        P(),
        P(),
    )
    return jax.shard_map(
        body,
        mesh=mesh,
        in_specs=placed,
        out_specs=(P(), P("member", "grid", None), P("member", "grid", None), P(), P(), P()),
        check_vma=False,
    )
```

time: 380 us -> 154 us (0.41)
  the two profiles are of different devices: /device:TPU:1 before, /device:TPU:14 now
where the time goes in v1:
time: 154 us; the launch traced here: 153 us
  waiting for transfers between devices  53.6 us (35%)
  starting transfers between devices  48.6 us (32%)
  Pallas kernels  30.1 us (20%)
  matrix products  9.19 us (6%)
  local copies, waits for them, and re-layouts  7.89 us (5%)
  other arithmetic  2.89 us (2%)
    ppermute x18, waiting for transfers between devices, send(): return lax.ppermute(value, axes, pairs)  39.1 us
    ppermute x18, starting transfers between devices, send(): return lax.ppermute(value, axes, pairs)  28.6 us
    pallas_call x1, Pallas kernels, body(): pl.pallas_call(functools.partial(backward_kernel, tile, scale, loss_scale...  12.5 us
    pallas_call x1, Pallas kernels, body(): pl.pallas_call(functools.partial(forward_kernel, tile), grid_spec=pltpu.P...  10.6 us
    ppermute x1, starting transfers between devices, body(): from_prev = lax.ppermute(grad_ext[:, 2 * rows:], 'grid', up)  6.2 us
    unnamed x41, local copies, waits for them, and re-layouts  5.75 us
    ppermute x3, waiting for transfers between devices, body(): lax.ppermute(slopes[k], 'member', to_peer[k])  5.26 us
    ppermute x1, starting transfers between devices, body(): before = lax.ppermute(mesh_features, 'grid', up)  5.22 us
  transfers between devices with their start and end apart: 28, of which 17 were waited for; matrix products, arithmetic and copies ran while one was open for 8% of the time, Pallas kernels for 0%

profile of v1, /device:TPU:14, one launch (start us, length us, event | category | flops | bytes accessed | tf_op | source)
XLA Modules:
  0.0 153.2 jit_solution(7569771548261662320)
XLA Ops:
  0.7 2.9 %collective-permute-start.1 = (f32[2,32,512]{2,1,0:T(8,128)}, f32[2,32,512]{2,1,0:T(8,128)S(1)}, u32[]{:S(2)}, u32[]{:S(2)}) collective-permute-start(f32[2,32,512]{2,1,0:T(8,128)} %own.3), channel_id=1, source_target_pairs={{1,0},{2,1},{3,2},{4,3},{5,4},{6,5},{7,6},{8,7},{9,8},{10,9},{11,1... | collective-permute-start | bytes 393224 | tf_op jit(solution)/shard_map/ppermute | solution.py:261
  3.5 5.2 %collective-permute-start = (f32[2,32,512]{2,1,0:T(8,128)}, f32[2,32,512]{2,1,0:T(8,128)S(1)}, u32[]{:S(2)}, u32[]{:S(2)}) collective-permute-start(f32[2,32,512]{2,1,0:T(8,128)} %own.3), channel_id=1, source_target_pairs={{0,1},{1,2},{2,3},{3,4},{4,5},{5,6},{6,7},{7,8},{8,9},{9,10},{10,1... | collective-permute-start | bytes 393224 | tf_op jit(solution)/shard_map/ppermute | solution.py:260
  8.8 4.7 %fusion.4.query = f32[2,512,512]{2,1,0:T(8,128)} fusion(f32[2,512,512]{2,1,0:T(8,128)} %features.1, f32[512,512]{1,0:T(8,128)S(1)} %copy-done), kind=kOutput, calls=%fused_computation.4 | convolution fusion | flops 1610612736 | bytes 5242880 | tf_op jit(solution)/shard_map/npw,wu->npu/dot_general | solution.py:262
  13.5 0.9 copy.13
  14.4 0.7 pad.7.out_weight
  15.7 0.6 copy-done.5
  16.4 10.6 %forward.1 = (f32[2,4,512,512]{3,2,1,0:T(8,128)}, f32[2,512,512]{2,1,0:T(8,128)}, f32[2,104,128]{2,1,0:T(8,128)}, f32[2,104,128]{2,1,0:T(8,128)}, f32[2,104,128]{2,1,0:T(8,128)}, /*index=5*/f32[2,104,128]{2,1,0:T(8,128)}) custom-call(s32[5]{0:T(128)} %stack.23.me, f32[2,512,512]{2,1,0:T(8,128)} %fusion.4.query, s32[512,4]{1,0:T(8,128)} %bitcast.17, ...), custom_call_target="tpu_custom_call" | custom-call | tf_op jit(solution)/shard_map/forward/pallas_call | solution.py:270
  27.7 1.3 collective-permute-start.4
  29.0 0.7 pad.8.targets
  29.7 3.5 %collective-permute-done.3.part2 = f32[2,104,128]{2,1,0:T(8,128)S(1)} collective-permute-done((f32[2,104,128]{2,1,0:T(8,128)}, f32[2,104,128]{2,1,0:T(8,128)S(1)}, u32[]{:S(2)}, u32[]{:S(2)}) %collective-permute-start.3) | collective-permute-done | bytes 106528 | tf_op jit(solution)/shard_map/ppermute | solution.py:299
  33.2 1.3 collective-permute-done.4.part3
  35.2 3.1 %score.1 = (f32[2,104,128]{2,1,0:T(8,128)}, f32[2,104,128]{2,1,0:T(8,128)}, f32[2,104,128]{2,1,0:T(8,128)}, f32[2,104,128]{2,1,0:T(8,128)}, f32[8,128]{1,0:T(8,128)}) custom-call(s32[5]{0:T(128)} %stack.23.me, f32[2,104,128]{2,1,0:T(8,128)} %get-tuple-element.25.part0, f32[2,104,128]{2,1,0:T(8,128)} %copy-done.10, f32[2,104,128]{2,1,0:T(8,128)} %copy-done.11, ...), custom_call_target="tpu_custom_call" | custom-call | tf_op jit(solution)/shard_map/score/pallas_call | solution.py:300
  39.0 1.1 collective-permute-start.7
  40.1 4.5 %collective-permute-done.6.part2 = f32[2,104,128]{2,1,0:T(8,128)S(1)} collective-permute-done((f32[2,104,128]{2,1,0:T(8,128)}, f32[2,104,128]{2,1,0:T(8,128)S(1)}, u32[]{:S(2)}, u32[]{:S(2)}) %collective-permute-start.6) | collective-permute-done | bytes 106528 | tf_op jit(solution)/shard_map/ppermute | solution.py:313
  44.6 0.8 collective-permute-done.7.part3
  45.3 0.6 copy-done.15
  46.0 12.5 %backward.1 = (f32[2,512,512]{2,1,0:T(8,128)}, f32[2,96,512]{2,1,0:T(8,128)}, f32[16,72,256]{2,1,0:T(8,128)}, f32[16,72,256]{2,1,0:T(8,128)}) custom-call(s32[5]{0:T(128)} %stack.23.me, f32[2,104,128]{2,1,0:T(8,128)} %get-tuple-element.29.part0, f32[2,104,128]{2,1,0:T(8,128)} %copy-done.13, f32[2,104,128]{2,1,0:T(8,128)} %copy-done.14, ...), custom_call_target="tpu_custom_call" | custom-call | tf_op jit(solution)/shard_map/backward/pallas_call | solution.py:319
  58.5 0.7 collective-permute-start.8
  59.1 2.7 %collective-permute-done.8 = f32[16,72,256]{2,1,0:T(8,128)S(1)} collective-permute-done((f32[16,72,256]{2,1,0:T(8,128)}, f32[16,72,256]{2,1,0:T(8,128)S(1)}, u32[]{:S(2)}, u32[]{:S(2)}) %collective-permute-start.8) | collective-permute-done | bytes 1179680 | tf_op jit(solution)/shard_map/ppermute | solution.py:51
  61.8 1.4 add.51
  63.5 4.0 %collective-permute-start.10 = (f32[4,72,256]{2,1,0:T(8,128)S(1)}, f32[4,72,256]{2,1,0:T(8,128)S(1)}, u32[]{:S(2)}, u32[]{:S(2)}) collective-permute-start(f32[4,72,256]{2,1,0:T(8,128)S(1)} %get-tuple-element.54), channel_id=1, source_target_pairs={{0,2},{1,3},{2,0},{3,1},{4,6},{5,7},{6,4},{7,5},{8,10},{9,11},{10,... | collective-permute-start | bytes 884744 | tf_op jit(solution)/shard_map/ppermute | solution.py:51
  67.5 2.6 %collective-permute-done.9 = f32[4,72,256]{2,1,0:T(8,128)S(1)} collective-permute-done((f32[4,72,256]{2,1,0:T(8,128)S(1)}, f32[4,72,256]{2,1,0:T(8,128)S(1)}, u32[]{:S(2)}, u32[]{:S(2)}) %collective-permute-start.9) | collective-permute-done | bytes 294944 | tf_op jit(solution)/shard_map/ppermute | solution.py:51
  70.1 4.5 %collective-permute-done.11 = f32[4,72,256]{2,1,0:T(8,128)S(1)} collective-permute-done((f32[4,72,256]{2,1,0:T(8,128)S(1)}, f32[4,72,256]{2,1,0:T(8,128)S(1)}, u32[]{:S(2)}, u32[]{:S(2)}) %collective-permute-start.11) | collective-permute-done | bytes 294944 | tf_op jit(solution)/shard_map/ppermute | solution.py:51
  75.3 9.5 %collective-permute-start.14 = (f32[1,72,256]{2,1,0:T(8,128)S(1)}, f32[1,72,256]{2,1,0:T(8,128)S(1)}, u32[]{:S(2)}, u32[]{:S(2)}) collective-permute-start(f32[1,72,256]{2,1,0:T(8,128)S(1)} %get-tuple-element.58), channel_id=1, source_target_pairs={{0,160},{1,161},{2,162},{3,163},{4,164},{5,165},{6,166},{7,167},{8... | collective-permute-start | bytes 221192 | tf_op jit(solution)/shard_map/ppermute | solution.py:51
  84.8 2.3 %collective-permute-done.14 = f32[1,72,256]{2,1,0:T(8,128)S(1)} collective-permute-done((f32[1,72,256]{2,1,0:T(8,128)S(1)}, f32[1,72,256]{2,1,0:T(8,128)S(1)}, u32[]{:S(2)}, u32[]{:S(2)}) %collective-permute-start.14) | collective-permute-done | bytes 73760 | tf_op jit(solution)/shard_map/ppermute | solution.py:51
  87.1 3.5 %collective-permute-done.13 = f32[1,72,256]{2,1,0:T(8,128)S(1)} collective-permute-done((f32[1,72,256]{2,1,0:T(8,128)S(1)}, f32[1,72,256]{2,1,0:T(8,128)S(1)}, u32[]{:S(2)}, u32[]{:S(2)}) %collective-permute-start.13) | collective-permute-done | bytes 73760 | tf_op jit(solution)/shard_map/ppermute | solution.py:51
  90.8 4.3 %collective-permute-start.15 = (f32[1,72,256]{2,1,0:T(8,128)S(1)}, f32[1,72,256]{2,1,0:T(8,128)S(1)}, u32[]{:S(2)}, u32[]{:S(2)}) collective-permute-start(f32[1,72,256]{2,1,0:T(8,128)S(1)} %fusion.12), channel_id=1, source_target_pairs={{0,4},{1,5},{2,6},{3,7},{4,0},{5,1},{6,2},{7,3},{8,12},{9,13},{10,... | collective-permute-start | bytes 221192 | tf_op jit(solution)/shard_map/ppermute | solution.py:51
  95.1 1.8 %collective-permute-done.17 = f32[1,72,256]{2,1,0:T(8,128)S(1)} collective-permute-done((f32[1,72,256]{2,1,0:T(8,128)S(1)}, f32[1,72,256]{2,1,0:T(8,128)S(1)}, u32[]{:S(2)}, u32[]{:S(2)}) %collective-permute-start.17) | collective-permute-done | bytes 73760 | tf_op jit(solution)/shard_map/ppermute | solution.py:51
  96.9 1.7 %collective-permute-done.15 = f32[1,72,256]{2,1,0:T(8,128)S(1)} collective-permute-done((f32[1,72,256]{2,1,0:T(8,128)S(1)}, f32[1,72,256]{2,1,0:T(8,128)S(1)}, u32[]{:S(2)}, u32[]{:S(2)}) %collective-permute-start.15) | collective-permute-done | bytes 73760 | tf_op jit(solution)/shard_map/ppermute | solution.py:51
  98.7 0.8 collective-permute-start.18
  99.4 7.8 %collective-permute-done.18 = f32[1,72,256]{2,1,0:T(8,128)S(1)} collective-permute-done((f32[1,72,256]{2,1,0:T(8,128)S(1)}, f32[1,72,256]{2,1,0:T(8,128)S(1)}, u32[]{:S(2)}, u32[]{:S(2)}) %collective-permute-start.18) | collective-permute-done | bytes 73760 | tf_op jit(solution)/shard_map/ppermute | solution.py:51
  107.4 2.0 %collective-permute-start.20 = (f32[1,72,256]{2,1,0:T(8,128)S(1)}, f32[1,72,256]{2,1,0:T(8,128)S(1)}, u32[]{:S(2)}, u32[]{:S(2)}) collective-permute-start(f32[1,72,256]{2,1,0:T(8,128)S(1)} %get-tuple-element.51), channel_id=1, source_target_pairs={{0,32},{1,33},{2,34},{3,35},{4,36},{5,37},{6,38},{7,39},{8,40},{9,... | collective-permute-start | bytes 221192 | tf_op jit(solution)/shard_map/ppermute | solution.py:51
  109.3 2.1 %collective-permute-start.19 = (f32[1,72,256]{2,1,0:T(8,128)S(1)}, f32[1,72,256]{2,1,0:T(8,128)S(1)}, u32[]{:S(2)}, u32[]{:S(2)}) collective-permute-start(f32[1,72,256]{2,1,0:T(8,128)S(1)} %get-tuple-element.51), channel_id=1, source_target_pairs={{0,128},{1,129},{2,130},{3,131},{4,132},{5,133},{6,134},{7,135},{8... | collective-permute-start | bytes 221192 | tf_op jit(solution)/shard_map/ppermute | solution.py:51
  111.4 1.0 collective-permute-done.21
  112.5 1.4 collective-permute-done.20
  113.9 1.8 %collective-permute-done.19 = f32[1,72,256]{2,1,0:T(8,128)S(1)} collective-permute-done((f32[1,72,256]{2,1,0:T(8,128)S(1)}, f32[1,72,256]{2,1,0:T(8,128)S(1)}, u32[]{:S(2)}, u32[]{:S(2)}) %collective-permute-start.19) | collective-permute-done | bytes 73760 | tf_op jit(solution)/shard_map/ppermute | solution.py:51
  115.7 1.8 %collective-permute-start.24 = (f32[4,72,256]{2,1,0:T(8,128)S(1)}, f32[4,72,256]{2,1,0:T(8,128)S(1)}, u32[]{:S(2)}, u32[]{:S(2)}) collective-permute-start(f32[4,72,256]{2,1,0:T(8,128)S(1)} %pad_maximum_fusion), channel_id=1, source_target_pairs={{0,3},{1,2},{2,1},{3,0},{4,7},{5,6},{6,5},{7,4},{8,11},{9,10},{10,... | collective-permute-start | bytes 884744 | tf_op jit(solution)/shard_map/ppermute | solution.py:51
  117.5 2.4 %collective-permute-start.22 = (f32[4,72,256]{2,1,0:T(8,128)S(1)}, f32[4,72,256]{2,1,0:T(8,128)S(1)}, u32[]{:S(2)}, u32[]{:S(2)}) collective-permute-start(f32[4,72,256]{2,1,0:T(8,128)S(1)} %pad_maximum_fusion), channel_id=1, source_target_pairs={{0,1},{1,0},{2,3},{3,2},{4,5},{5,4},{6,7},{7,6},{8,9},{9,8},{10,11... | collective-permute-start | bytes 884744 | tf_op jit(solution)/shard_map/ppermute | solution.py:51
  119.9 7.9 %collective-permute-done.22 = f32[4,72,256]{2,1,0:T(8,128)S(1)} collective-permute-done((f32[4,72,256]{2,1,0:T(8,128)S(1)}, f32[4,72,256]{2,1,0:T(8,128)S(1)}, u32[]{:S(2)}, u32[]{:S(2)}) %collective-permute-start.22) | collective-permute-done | bytes 294944 | tf_op jit(solution)/shard_map/ppermute | solution.py:51
  128.1 6.2 %collective-permute-start.26 = (f32[2,32,512]{2,1,0:T(8,128)S(1)}, f32[2,32,512]{2,1,0:T(8,128)S(1)}, u32[]{:S(2)}, u32[]{:S(2)}) collective-permute-start(f32[2,32,512]{2,1,0:T(8,128)S(1)} %get-tuple-element.55), channel_id=1, source_target_pairs={{0,1},{1,2},{2,3},{3,4},{4,5},{5,6},{6,7},{7,8},{8,9},{9,10},{10,1... | collective-permute-start | bytes 393224 | tf_op jit(solution)/shard_map/ppermute | solution.py:352
  134.3 1.9 %collective-permute-start.27 = (f32[2,32,512]{2,1,0:T(8,128)S(1)}, f32[2,32,512]{2,1,0:T(8,128)S(1)}, u32[]{:S(2)}, u32[]{:S(2)}) collective-permute-start(f32[2,32,512]{2,1,0:T(8,128)S(1)} %get-tuple-element.56), channel_id=1, source_target_pairs={{1,0},{2,1},{3,2},{4,3},{5,4},{6,5},{7,6},{8,7},{9,8},{10,9},{11,1... | collective-permute-start | bytes 393224 | tf_op jit(solution)/shard_map/ppermute | solution.py:353
  136.2 3.2 %fusion.2 = f32[2,512,512]{2,1,0:T(8,128)} fusion(f32[2,512,512]{2,1,0:T(8,128)S(1)} %copy-done.2, f32[512,512]{1,0:T(8,128)S(1)} %copy-done), kind=kOutput, calls=%fused_computation.2 | convolution fusion | flops 1610612736 | bytes 5242880 | tf_op jit(solution)/shard_map/npu,wu->npw/dot_general | solution.py:354
  139.4 4.5 %collective-permute-done.27 = f32[2,32,512]{2,1,0:T(8,128)S(1)} collective-permute-done((f32[2,32,512]{2,1,0:T(8,128)S(1)}, f32[2,32,512]{2,1,0:T(8,128)S(1)}, u32[]{:S(2)}, u32[]{:S(2)}) %collective-permute-start.27) | collective-permute-done | bytes 131104 | tf_op jit(solution)/shard_map/ppermute | solution.py:353
  143.9 1.3 fusion
  145.2 1.0 copy-done.4
  146.2 4.0 %finish.1 = (f32[512,512]{1,0:T(8,128)}, f32[512,512]{1,0:T(8,128)}, f32[512,100]{1,0:T(8,128)}, f32[8,128]{1,0:T(8,128)}) custom-call(s32[5]{0:T(128)} %stack.23.me, f32[16,72,256]{2,1,0:T(8,128)} %copy-done.3, f32[16,72,256]{2,1,0:T(8,128)} %copy-done.4), custom_call_target="tpu_custom_call" | custom-call | tf_op jit(solution)/shard_map/finish/pallas_call | solution.py:359
  150.2 1.3 reduce_sum.9
  151.5 1.8 %copy.14 = f32[512,100]{0,1:T(8,128)} copy(f32[512,100]{1,0:T(8,128)} %get-tuple-element.49) | data formatting | bytes 409600
  (70 shorter events, 4.3 us)
Async XLA Ops:
  0.6 8.1 %copy-start = (f32[512,512]{1,0:T(8,128)S(1)}, f32[512,512]{1,0:T(8,128)}, u32[]{:S(2)}) copy-start(f32[512,512]{1,0:T(8,128)} %param.12) | copy-start | bytes 3145732
  0.6 12.9 %copy-start.16 = (s32[4,512]{1,0:T(4,128)S(1)}, s32[4,512]{1,0:T(4,128)}, u32[]{:S(2)}) copy-start(s32[4,512]{1,0:T(4,128)} %edges.1) | copy-start | bytes 24580
  0.7 13.7 %copy-start.8 = (f32[512,100]{0,1:T(8,128)S(1)}, f32[512,100]{0,1:T(8,128)}, u32[]{:S(2)}) copy-start(f32[512,100]{0,1:T(8,128)} %param.13) | copy-start | bytes 614404
  0.7 15.0 %collective-permute-start.1 = (f32[2,32,512]{2,1,0:T(8,128)}, f32[2,32,512]{2,1,0:T(8,128)S(1)}, u32[]{:S(2)}, u32[]{:S(2)}) collective-permute-start(f32[2,32,512]{2,1,0:T(8,128)} %own.3), channel_id=1, source_target_pairs={{1,0},{2,1},{3,2},{4,3},{5,4},{6,5},{7,6},{8,7},{9,8},{10,9},{11,1... | collective-permute-start | bytes 393224 | tf_op jit(solution)/shard_map/ppermute | solution.py:261
  3.5 12.2 %collective-permute-start = (f32[2,32,512]{2,1,0:T(8,128)}, f32[2,32,512]{2,1,0:T(8,128)S(1)}, u32[]{:S(2)}, u32[]{:S(2)}) collective-permute-start(f32[2,32,512]{2,1,0:T(8,128)} %own.3), channel_id=1, source_target_pairs={{0,1},{1,2},{2,3},{3,4},{4,5},{5,6},{6,7},{7,8},{8,9},{9,10},{10,1... | collective-permute-start | bytes 393224 | tf_op jit(solution)/shard_map/ppermute | solution.py:260
  15.7 0.7 copy-start.5
  15.7 0.7 copy-start.6
  16.4 12.6 %copy-start.9 = (f32[100,512]{1,0:T(8,128)S(1)}, f32[100,512]{1,0:T(8,128)}, u32[]{:S(2)}) copy-start(f32[100,512]{1,0:T(8,128)} %param.9) | copy-start | bytes 614404
  27.0 2.7 %collective-permute-start.2 = (f32[2,104,128]{2,1,0:T(8,128)}, f32[2,104,128]{2,1,0:T(8,128)S(1)}, u32[]{:S(2)}, u32[]{:S(2)}) collective-permute-start(f32[2,104,128]{2,1,0:T(8,128)} %get-tuple-element.26), channel_id=1, source_target_pairs={{0,64},{64,0},{128,192},{192,128},{1,65},{65,1},{129,193},{193,129... | collective-permute-start | bytes 319496 | tf_op jit(solution)/shard_map/ppermute | solution.py:299
  27.1 6.1 %collective-permute-start.3 = (f32[2,104,128]{2,1,0:T(8,128)}, f32[2,104,128]{2,1,0:T(8,128)S(1)}, u32[]{:S(2)}, u32[]{:S(2)}) collective-permute-start(f32[2,104,128]{2,1,0:T(8,128)} %get-tuple-element.27), channel_id=1, source_target_pairs={{0,128},{64,192},{128,0},{192,64},{1,129},{65,193},{129,1},{193,65... | collective-permute-start | bytes 319496 | tf_op jit(solution)/shard_map/ppermute | solution.py:299
  27.7 6.9 %collective-permute-start.4 = (f32[2,104,128]{2,1,0:T(8,128)}, f32[2,104,128]{2,1,0:T(8,128)S(1)}, u32[]{:S(2)}, u32[]{:S(2)}) collective-permute-start(f32[2,104,128]{2,1,0:T(8,128)} %get-tuple-element.28), channel_id=1, source_target_pairs={{0,192},{64,128},{128,64},{192,0},{1,193},{65,129},{129,65},{193,1... | collective-permute-start | bytes 319496 | tf_op jit(solution)/shard_map/ppermute | solution.py:299
  29.7 4.8 %copy-start.10 = (f32[2,104,128]{2,1,0:T(8,128)}, f32[2,104,128]{2,1,0:T(8,128)S(1)}, u32[]{:S(2)}) copy-start(f32[2,104,128]{2,1,0:T(8,128)S(1)} %collective-permute-done.2.part1) | copy-start | bytes 319492
  33.2 1.3 copy-start.11
  34.5 0.6 copy-start.12
  38.2 1.9 %collective-permute-start.5 = (f32[2,104,128]{2,1,0:T(8,128)}, f32[2,104,128]{2,1,0:T(8,128)S(1)}, u32[]{:S(2)}, u32[]{:S(2)}) collective-permute-start(f32[2,104,128]{2,1,0:T(8,128)} %get-tuple-element.30), channel_id=1, source_target_pairs={{0,64},{64,0},{128,192},{192,128},{1,65},{65,1},{129,193},{193,129... | collective-permute-start | bytes 319496 | tf_op jit(solution)/shard_map/ppermute | solution.py:313
  38.5 6.0 %collective-permute-start.6 = (f32[2,104,128]{2,1,0:T(8,128)}, f32[2,104,128]{2,1,0:T(8,128)S(1)}, u32[]{:S(2)}, u32[]{:S(2)}) collective-permute-start(f32[2,104,128]{2,1,0:T(8,128)} %get-tuple-element.31), channel_id=1, source_target_pairs={{0,128},{64,192},{128,0},{192,64},{1,129},{65,193},{129,1},{193,65... | collective-permute-start | bytes 319496 | tf_op jit(solution)/shard_map/ppermute | solution.py:313
  39.0 6.4 %collective-permute-start.7 = (f32[2,104,128]{2,1,0:T(8,128)}, f32[2,104,128]{2,1,0:T(8,128)S(1)}, u32[]{:S(2)}, u32[]{:S(2)}) collective-permute-start(f32[2,104,128]{2,1,0:T(8,128)} %get-tuple-element.32), channel_id=1, source_target_pairs={{0,192},{64,128},{128,64},{192,0},{1,193},{65,129},{129,65},{193,1... | collective-permute-start | bytes 319496 | tf_op jit(solution)/shard_map/ppermute | solution.py:313
  40.1 5.3 %copy-start.13 = (f32[2,104,128]{2,1,0:T(8,128)}, f32[2,104,128]{2,1,0:T(8,128)S(1)}, u32[]{:S(2)}) copy-start(f32[2,104,128]{2,1,0:T(8,128)S(1)} %collective-permute-done.5.part1) | copy-start | bytes 319492
  44.5 0.8 copy-start.14
  45.3 0.6 copy-start.15
  58.5 3.3 %collective-permute-start.8 = (f32[16,72,256]{2,1,0:T(8,128)}, f32[16,72,256]{2,1,0:T(8,128)S(1)}, u32[]{:S(2)}, u32[]{:S(2)}) collective-permute-start(f32[16,72,256]{2,1,0:T(8,128)} %get-tuple-element.37), channel_id=1, source_target_pairs={{0,64},{1,65},{2,66},{3,67},{4,68},{5,69},{6,70},{7,71},{8,72},{9,... | collective-permute-start | bytes 3538952 | tf_op jit(solution)/shard_map/ppermute | solution.py:51
  63.3 6.8 %collective-permute-start.9 = (f32[4,72,256]{2,1,0:T(8,128)S(1)}, f32[4,72,256]{2,1,0:T(8,128)S(1)}, u32[]{:S(2)}, u32[]{:S(2)}) collective-permute-start(f32[4,72,256]{2,1,0:T(8,128)S(1)} %get-tuple-element.52), channel_id=1, source_target_pairs={{0,1},{1,0},{2,3},{3,2},{4,5},{5,4},{6,7},{7,6},{8,9},{9,8},{10,11... | collective-permute-start | bytes 884744 | tf_op jit(solution)/shard_map/ppermute | solution.py:51
  63.4 11.2 %collective-permute-start.11 = (f32[4,72,256]{2,1,0:T(8,128)S(1)}, f32[4,72,256]{2,1,0:T(8,128)S(1)}, u32[]{:S(2)}, u32[]{:S(2)}) collective-permute-start(f32[4,72,256]{2,1,0:T(8,128)S(1)} %get-tuple-element.53), channel_id=1, source_target_pairs={{0,3},{1,2},{2,1},{3,0},{4,7},{5,6},{6,5},{7,4},{8,11},{9,10},{10,... | collective-permute-start | bytes 884744 | tf_op jit(solution)/shard_map/ppermute | solution.py:51
  63.5 11.1 %collective-permute-start.10 = (f32[4,72,256]{2,1,0:T(8,128)S(1)}, f32[4,72,256]{2,1,0:T(8,128)S(1)}, u32[]{:S(2)}, u32[]{:S(2)}) collective-permute-start(f32[4,72,256]{2,1,0:T(8,128)S(1)} %get-tuple-element.54), channel_id=1, source_target_pairs={{0,2},{1,3},{2,0},{3,1},{4,6},{5,7},{6,4},{7,5},{8,10},{9,11},{10,... | collective-permute-start | bytes 884744 | tf_op jit(solution)/shard_map/ppermute | solution.py:51
  74.7 10.0 %collective-permute-start.12 = (f32[1,72,256]{2,1,0:T(8,128)S(1)}, f32[1,72,256]{2,1,0:T(8,128)S(1)}, u32[]{:S(2)}, u32[]{:S(2)}) collective-permute-start(f32[1,72,256]{2,1,0:T(8,128)S(1)} %get-tuple-element.57), channel_id=1, source_target_pairs={{0,128},{1,129},{2,130},{3,131},{4,132},{5,133},{6,134},{7,135},{8... | collective-permute-start | bytes 221192 | tf_op jit(solution)/shard_map/ppermute | solution.py:51
  75.3 11.8 %collective-permute-start.14 = (f32[1,72,256]{2,1,0:T(8,128)S(1)}, f32[1,72,256]{2,1,0:T(8,128)S(1)}, u32[]{:S(2)}, u32[]{:S(2)}) collective-permute-start(f32[1,72,256]{2,1,0:T(8,128)S(1)} %get-tuple-element.58), channel_id=1, source_target_pairs={{0,160},{1,161},{2,162},{3,163},{4,164},{5,165},{6,166},{7,167},{8... | collective-permute-start | bytes 221192 | tf_op jit(solution)/shard_map/ppermute | solution.py:51
  84.8 5.9 %collective-permute-start.13 = (f32[1,72,256]{2,1,0:T(8,128)S(1)}, f32[1,72,256]{2,1,0:T(8,128)S(1)}, u32[]{:S(2)}, u32[]{:S(2)}) collective-permute-start(f32[1,72,256]{2,1,0:T(8,128)S(1)} %get-tuple-element.59), channel_id=1, source_target_pairs={{0,32},{1,33},{2,34},{3,35},{4,36},{5,37},{6,38},{7,39},{8,40},{9,... | collective-permute-start | bytes 221192 | tf_op jit(solution)/shard_map/ppermute | solution.py:51
  90.6 6.3 %collective-permute-start.17 = (f32[1,72,256]{2,1,0:T(8,128)S(1)}, f32[1,72,256]{2,1,0:T(8,128)S(1)}, u32[]{:S(2)}, u32[]{:S(2)}) collective-permute-start(f32[1,72,256]{2,1,0:T(8,128)S(1)} %fusion.12), channel_id=1, source_target_pairs={{0,12},{1,13},{2,14},{3,15},{4,8},{5,9},{6,10},{7,11},{8,4},{9,5},... | collective-permute-start | bytes 221192 | tf_op jit(solution)/shard_map/ppermute | solution.py:51
  90.7 6.2 %collective-permute-start.16 = (f32[1,72,256]{2,1,0:T(8,128)S(1)}, f32[1,72,256]{2,1,0:T(8,128)S(1)}, u32[]{:S(2)}, u32[]{:S(2)}) collective-permute-start(f32[1,72,256]{2,1,0:T(8,128)S(1)} %fusion.12), channel_id=1, source_target_pairs={{0,8},{1,9},{2,10},{3,11},{4,12},{5,13},{6,14},{7,15},{8,0},{9,1},... | collective-permute-start | bytes 221192 | tf_op jit(solution)/shard_map/ppermute | solution.py:51
  90.8 7.8 %collective-permute-start.15 = (f32[1,72,256]{2,1,0:T(8,128)S(1)}, f32[1,72,256]{2,1,0:T(8,128)S(1)}, u32[]{:S(2)}, u32[]{:S(2)}) collective-permute-start(f32[1,72,256]{2,1,0:T(8,128)S(1)} %fusion.12), channel_id=1, source_target_pairs={{0,4},{1,5},{2,6},{3,7},{4,0},{5,1},{6,2},{7,3},{8,12},{9,13},{10,... | collective-permute-start | bytes 221192 | tf_op jit(solution)/shard_map/ppermute | solution.py:51
  98.7 8.6 %collective-permute-start.18 = (f32[1,72,256]{2,1,0:T(8,128)S(1)}, f32[1,72,256]{2,1,0:T(8,128)S(1)}, u32[]{:S(2)}, u32[]{:S(2)}) collective-permute-start(f32[1,72,256]{2,1,0:T(8,128)S(1)} %add_add_fusion), channel_id=1, source_target_pairs={{0,16},{1,17},{2,18},{3,19},{4,20},{5,21},{6,22},{7,23},{8,24},{9,... | collective-permute-start | bytes 221192 | tf_op jit(solution)/shard_map/ppermute | solution.py:51
  107.3 5.2 %collective-permute-start.21 = (f32[1,72,256]{2,1,0:T(8,128)S(1)}, f32[1,72,256]{2,1,0:T(8,128)S(1)}, u32[]{:S(2)}, u32[]{:S(2)}) collective-permute-start(f32[1,72,256]{2,1,0:T(8,128)S(1)} %get-tuple-element.51), channel_id=1, source_target_pairs={{0,160},{1,161},{2,162},{3,163},{4,164},{5,165},{6,166},{7,167},{8... | collective-permute-start | bytes 221192 | tf_op jit(solution)/shard_map/ppermute | solution.py:51
  107.4 6.5 %collective-permute-start.20 = (f32[1,72,256]{2,1,0:T(8,128)S(1)}, f32[1,72,256]{2,1,0:T(8,128)S(1)}, u32[]{:S(2)}, u32[]{:S(2)}) collective-permute-start(f32[1,72,256]{2,1,0:T(8,128)S(1)} %get-tuple-element.51), channel_id=1, source_target_pairs={{0,32},{1,33},{2,34},{3,35},{4,36},{5,37},{6,38},{7,39},{8,40},{9,... | collective-permute-start | bytes 221192 | tf_op jit(solution)/shard_map/ppermute | solution.py:51
  109.3 6.3 %collective-permute-start.19 = (f32[1,72,256]{2,1,0:T(8,128)S(1)}, f32[1,72,256]{2,1,0:T(8,128)S(1)}, u32[]{:S(2)}, u32[]{:S(2)}) collective-permute-start(f32[1,72,256]{2,1,0:T(8,128)S(1)} %get-tuple-element.51), channel_id=1, source_target_pairs={{0,128},{1,129},{2,130},{3,131},{4,132},{5,133},{6,134},{7,135},{8... | collective-permute-start | bytes 221192 | tf_op jit(solution)/shard_map/ppermute | solution.py:51
  115.7 12.3 %copy-start.7 = (f32[2,96,512]{2,1,0:T(8,128)S(1)}, f32[2,96,512]{2,1,0:T(8,128)}, u32[]{:S(2)}) copy-start(f32[2,96,512]{2,1,0:T(8,128)} %get-tuple-element.40) | copy-start | bytes 1179652
  115.7 12.2 %collective-permute-start.24 = (f32[4,72,256]{2,1,0:T(8,128)S(1)}, f32[4,72,256]{2,1,0:T(8,128)S(1)}, u32[]{:S(2)}, u32[]{:S(2)}) collective-permute-start(f32[4,72,256]{2,1,0:T(8,128)S(1)} %pad_maximum_fusion), channel_id=1, source_target_pairs={{0,3},{1,2},{2,1},{3,0},{4,7},{5,6},{6,5},{7,4},{8,11},{9,10},{10,... | collective-permute-start | bytes 884744 | tf_op jit(solution)/shard_map/ppermute | solution.py:51
  117.5 10.3 %collective-permute-start.23 = (f32[4,72,256]{2,1,0:T(8,128)S(1)}, f32[4,72,256]{2,1,0:T(8,128)S(1)}, u32[]{:S(2)}, u32[]{:S(2)}) collective-permute-start(f32[4,72,256]{2,1,0:T(8,128)S(1)} %pad_maximum_fusion), channel_id=1, source_target_pairs={{0,2},{1,3},{2,0},{3,1},{4,6},{5,7},{6,4},{7,5},{8,10},{9,11},{10,... | collective-permute-start | bytes 884744 | tf_op jit(solution)/shard_map/ppermute | solution.py:51
  117.5 10.3 %collective-permute-start.22 = (f32[4,72,256]{2,1,0:T(8,128)S(1)}, f32[4,72,256]{2,1,0:T(8,128)S(1)}, u32[]{:S(2)}, u32[]{:S(2)}) collective-permute-start(f32[4,72,256]{2,1,0:T(8,128)S(1)} %pad_maximum_fusion), channel_id=1, source_target_pairs={{0,1},{1,0},{2,3},{3,2},{4,5},{5,4},{6,7},{7,6},{8,9},{9,8},{10,11... | collective-permute-start | bytes 884744 | tf_op jit(solution)/shard_map/ppermute | solution.py:51
  119.9 16.3 %copy-start.2 = (f32[2,512,512]{2,1,0:T(8,128)S(1)}, f32[2,512,512]{2,1,0:T(8,128)}, u32[]{:S(2)}) copy-start(f32[2,512,512]{2,1,0:T(8,128)} %get-tuple-element.39) | copy-start | bytes 6291460
  127.9 11.5 %copy-start.3 = (f32[16,72,256]{2,1,0:T(8,128)}, f32[16,72,256]{2,1,0:T(8,128)S(1)}, u32[]{:S(2)}) copy-start(f32[16,72,256]{2,1,0:T(8,128)S(1)} %constant_dynamic-update-slice_fusion.mine) | copy-start | bytes 3538948
  127.9 17.3 %collective-permute-start.25 = (f32[16,72,256]{2,1,0:T(8,128)S(1)}, f32[16,72,256]{2,1,0:T(8,128)S(1)}, u32[]{:S(2)}, u32[]{:S(2)}) collective-permute-start(f32[16,72,256]{2,1,0:T(8,128)S(1)} %constant_dynamic-update-slice_fusion.mine), channel_id=1, source_target_pairs={{0,64},{1,65},{2,66},{3,67},{4,68},{5,69},{6,70},{7,71},{8,72},{9,... | collective-permute-start | bytes 3538952 | tf_op jit(solution)/shard_map/ppermute | solution.py:51
  128.1 11.3 %collective-permute-start.26 = (f32[2,32,512]{2,1,0:T(8,128)S(1)}, f32[2,32,512]{2,1,0:T(8,128)S(1)}, u32[]{:S(2)}, u32[]{:S(2)}) collective-permute-start(f32[2,32,512]{2,1,0:T(8,128)S(1)} %get-tuple-element.55), channel_id=1, source_target_pairs={{0,1},{1,2},{2,3},{3,4},{4,5},{5,6},{6,7},{7,8},{8,9},{9,10},{10,1... | collective-permute-start | bytes 393224 | tf_op jit(solution)/shard_map/ppermute | solution.py:352
  134.3 9.6 %collective-permute-start.27 = (f32[2,32,512]{2,1,0:T(8,128)S(1)}, f32[2,32,512]{2,1,0:T(8,128)S(1)}, u32[]{:S(2)}, u32[]{:S(2)}) collective-permute-start(f32[2,32,512]{2,1,0:T(8,128)S(1)} %get-tuple-element.56), channel_id=1, source_target_pairs={{1,0},{2,1},{3,2},{4,3},{5,4},{6,5},{7,6},{8,7},{9,8},{10,9},{11,1... | collective-permute-start | bytes 393224 | tf_op jit(solution)/shard_map/ppermute | solution.py:353
  136.2 7.7 %copy-start.1 = (f32[512,512]{1,0:T(8,128)S(1)}, f32[512,512]{1,0:T(8,128)}, u32[]{:S(2)}) copy-start(f32[512,512]{1,0:T(8,128)} %src_weight.1) | copy-start | bytes 3145732
  145.2 1.0 copy-start.4

commit v2 on v1

--- a/solution.py
+++ b/solution.py
@@ -10,7 +10,7 @@
 alpha_fair = 0.95
 smoothing = 0.1
 axes = ("member", "grid")
-vmem_limit = 56 * 1024 * 1024
+vmem_limit = 24 * 1024 * 1024
 f32 = jnp.float32
 bf16 = jnp.bfloat16
 interpret = False
@@ -68,6 +68,14 @@
 TN = ((0,), (0,))
 
 
+def query_kernel(features, weight, query, high, low):
+    @pl.when(pl.program_id(0) == 0)
+    def _():
+        high[...], low[...] = split(0.5 * weight[...])
+
+    query[0] = dot3(split(features[0]), (high[...], low[...]), NN)
+
+
 def forward_kernel(points, me, query, edges, before, own, after, src_weight, out_weight,
                    slope, summed, part0, part1, part2, part3, nodes, fields):
     member, tile = pl.program_id(0), pl.program_id(1)
@@ -77,7 +85,7 @@
     @pl.when((member == 0) & (tile == 0))
     def _():
         nodes[...] = jnp.zeros_like(nodes)
-        weight = split(src_weight[...])
+        weight = split(0.5 * src_weight[...])
         for n in range(own.shape[0]):
             ext = jnp.concatenate([before[n], own[n], after[n]], axis=0)
             high, low = split(dot3(split(ext), weight, NN))
@@ -89,10 +97,11 @@
     total = None
     for k in range(4):
         hot = jnp.where(local[:, k : k + 1] == columns, 1.0, 0.0).astype(bf16)
-        value = query[0] + jnp.dot(hot, nodes[member], preferred_element_type=f32)
-        sigma = 0.5 * jnp.tanh(0.5 * value) + 0.5
-        active = value * sigma
-        slope[0, k] = sigma + active * (1.0 - sigma)
+        half = query[0] + jnp.dot(hot, nodes[member], preferred_element_type=f32)
+        curve = jnp.tanh(half)
+        active = half * curve + half
+        curve = 0.5 * curve
+        slope[0, k] = (curve + 0.5) + active * (0.5 - curve)
         total = active if total is None else total + active
     summed[0] = total
     weight = split(out_weight[...])
@@ -146,7 +155,7 @@
 
 def backward_kernel(points, scale, loss_scale, me, part0, part1, part2, part3, loss, slope, summed, features,
                     edges, before, own, after, out_weight,
-                    grad_query, grad_ext, keep, away, slopes, sums):
+                    grad_query, lower, middle, upper, keep, away, grad_ext, slopes, sums):
     member, tile = pl.program_id(0), pl.program_id(1)
     members, tiles = pl.num_programs(0), pl.num_programs(1)
     rows = own.shape[1]
@@ -187,32 +196,16 @@
         ext = jnp.concatenate([side[n] for n in range(2) for side in (before, own, after)], axis=0)
         grads = jnp.concatenate([grad_ext[0], grad_ext[1]], axis=0)
         sums[0:width] = dot3(split(ext), split(grads), TN)
+        for n in range(2):
+            for i, side in enumerate((lower, middle, upper)):
+                side[n] = grad_ext[n, i * rows : (i + 1) * rows]
         end = 2 * width + vars_rows
-        sums[end : end + 8] = jnp.concatenate(
-            [loss[...] * (loss_scale / scale), jnp.zeros((8, width - 128), f32)], axis=1
-        )
+        sums[end : end + 8] = jnp.full((8, width), jnp.sum(loss[...]) * (loss_scale / scale), f32)
         for j in range(16):
             for out, core, order in ((keep, me[2], me[3]), (away, 1 - me[2], me[4])):
-                chunk = core * 16 + (j ^ order)
-                at = pl.ds(pl.multiple_of((chunk >> 1) * 72, 8), 72)
-                lanes = pl.ds(pl.multiple_of((chunk & 1) * 256, 128), 256)
+                at = pl.ds(pl.multiple_of((j ^ order) * 72, 8), 72)
+                lanes = pl.ds(pl.multiple_of(core * 256, 128), 256)
                 out[j] = sums[at, lanes] * scale
-
-
-def finish_kernel(me, mine, other, src_grad, dst_grad, out_grad, loss, sums):
-    width = src_grad.shape[0]
-    for j in range(16):
-        for part, core, order in ((mine, me[2], me[3]), (other, 1 - me[2], me[4])):
-            chunk = core * 16 + (j ^ order)
-            at = pl.ds(pl.multiple_of((chunk >> 1) * 72, 8), 72)
-            lanes = pl.ds(pl.multiple_of((chunk & 1) * 256, 128), 256)
-            sums[at, lanes] = part[j]
-    src_grad[...] = sums[0:width]
-    dst_grad[...] = sums[width : 2 * width]
-    rows = 128
-    out_grad[...] = sums[2 * width : 2 * width + rows].T[:, : out_grad.shape[1]]
-    end = 2 * width + 104
-    loss[...] = sums[end : end + 8, 0:128]
 
 
 def whole(shape=None):
@@ -223,17 +216,16 @@
     return pltpu.CompilerParams(dimension_semantics=("arbitrary",) * dims, vmem_limit_bytes=vmem_limit)
 
 
-def all_reduce(keep, away):
-    total = keep + send(away, swap_core)
-    for group, size in ((first_axis, 4), (second_axis, 1)):
-        parts = [send(total[k * size : (k + 1) * size], group[k]) for k in (1, 2, 3)]
-        total = total[:size] + parts[0] + parts[1] + parts[2]
-    parts = [send(total, along_z[k]) for k in (1, 2, 3)]
-    total = total + parts[0] + parts[1] + parts[2]
-    total = total + send(total, along_z[4])
-    for group in (second_axis, first_axis):
-        total = jnp.concatenate([total] + [send(total, group[k]) for k in (1, 2, 3)], axis=0)
-    return total, send(total, swap_core)
+def tree(total, parts):
+    return (total + parts[0]) + (parts[1] + parts[2])
+
+
+def placed_at(place, total, parts):
+    size = total.shape[0]
+    whole_value = jnp.zeros((4 * size,) + total.shape[1:], f32)
+    for k, part in enumerate([total] + parts):
+        whole_value = lax.dynamic_update_slice(whole_value, part, ((place ^ k) * size, 0, 0))
+    return whole_value
 
 
 def body(mesh_features, grid_features, targets, edges, src_weight, dst_weight, output_weight):
@@ -259,19 +251,28 @@
     down = [(j, i) for i, j in up]
     before = lax.ppermute(mesh_features, "grid", up)
     after = lax.ppermute(mesh_features, "grid", down)
-    query = jnp.einsum("npw,wu->npu", grid_features, dst_weight, precision=lax.Precision.HIGH)
+    query = pl.pallas_call(
+        query_kernel,
+        grid=(members,),
+        in_specs=[pl.BlockSpec((1, points, width), lambda n: (n, 0, 0)), whole()],
+        out_specs=pl.BlockSpec((1, points, width), lambda n: (n, 0, 0)),
+        out_shape=jax.ShapeDtypeStruct((members, points, width), f32),
+        scratch_shapes=[pltpu.VMEM((width, width), bf16)] * 2,
+        compiler_params=params(1),
+        name="query",
+        interpret=interpret,
+    )(grid_features, dst_weight)
     edges_t = edges.T
     out_weight = jnp.pad(output_weight.T, ((0, var_rows - count_vars), (0, 0)))
     targets = jnp.pad(targets, ((0, var_rows - count_vars), (0, 0)))
 
-    tile = 256
-    tiles = points // tile
+    tile = 512
     part_shape = jax.ShapeDtypeStruct((members, var_rows, 128), f32)
     slope, summed, *parts = pl.pallas_call(
         functools.partial(forward_kernel, tile),
         grid_spec=pltpu.PrefetchScalarGridSpec(
             num_scalar_prefetch=1,
-            grid=(members, tiles),
+            grid=(members, points // tile),
             in_specs=[
                 pl.BlockSpec((1, tile, width), lambda n, t, me: (n, t, 0)),
                 pl.BlockSpec((tile, 4), lambda n, t, me: (t, 0)),
@@ -316,11 +317,13 @@
     scale = 1.0 / (total_members * points * slabs) ** 0.5
     loss_scale = 1.0 / (points * slabs * count_vars)
     chunks = jax.ShapeDtypeStruct((16, 72, 256), f32)
-    grad_query, grad_ext, keep, away = pl.pallas_call(
+    side = jax.ShapeDtypeStruct((members, rows, width), f32)
+    tile = 256
+    grad_query, lower, middle, upper, keep, away = pl.pallas_call(
         functools.partial(backward_kernel, tile, scale, loss_scale),
         grid_spec=pltpu.PrefetchScalarGridSpec(
             num_scalar_prefetch=1,
-            grid=(members, tiles),
+            grid=(members, points // tile),
             in_specs=[whole()] * 5 + [
                 pl.BlockSpec((1, 4, tile, width), lambda n, t, me: (n, 0, t, 0)),
                 pl.BlockSpec((1, tile, width), lambda n, t, me: (n, t, 0)),
@@ -330,16 +333,19 @@
             ],
             out_specs=[
                 pl.BlockSpec((1, tile, width), lambda n, t, me: (n, t, 0)),
-                whole(), whole(), whole(),
+                whole(), whole(), whole(), whole(), whole(),
             ],
             scratch_shapes=[
+                pltpu.VMEM((members, 3 * rows, width), f32),
                 pltpu.VMEM((members, var_rows, points), f32),
                 pltpu.VMEM((1152, width), f32),
             ],
         ),
         out_shape=[
             jax.ShapeDtypeStruct((members, points, width), f32),
-            jax.ShapeDtypeStruct((members, 3 * rows, width), f32),
+            side,
+            side,
+            side,
             chunks,
             chunks,
         ],
@@ -348,34 +354,38 @@
         interpret=interpret,
     )(me, *slopes, loss, slope, summed, grid_features, edges, before, mesh_features, after, out_weight)
 
-    mine, other = all_reduce(keep, away)
-    from_prev = lax.ppermute(grad_ext[:, 2 * rows :], "grid", up)
-    from_next = lax.ppermute(grad_ext[:, :rows], "grid", down)
+    core = place["core"]
+    first = jnp.where(straight, place["x"], place["y"])
+    second = jnp.where(straight, place["y"], place["x"])
+    total = keep + send(away, swap_core)
+    parts = [send(total[4 * k : 4 * k + 4], first_axis[k]) for k in (1, 2, 3)]
+    from_prev = lax.ppermute(upper, "grid", up)
+    from_next = lax.ppermute(lower, "grid", down)
     grid_grad = jnp.einsum("npu,wu->npw", grad_query, dst_weight, precision=lax.Precision.HIGH)
-    grad_proj = grad_ext[:, rows : 2 * rows] + from_prev + from_next
-    mesh_grad = jnp.einsum("nru,wu->nrw", grad_proj, src_weight, precision=lax.Precision.HIGH)
-
-    square = jax.ShapeDtypeStruct((width, width), f32)
-    src_grad, dst_grad, out_grad, loss = pl.pallas_call(
-        finish_kernel,
-        grid_spec=pltpu.PrefetchScalarGridSpec(
-            num_scalar_prefetch=1,
-            grid=(1,),
-            in_specs=[whole()] * 2,
-            out_specs=[whole()] * 4,
-            scratch_shapes=[pltpu.VMEM((1152, width), f32)],
-        ),
-        out_shape=[
-            square,
-            square,
-            jax.ShapeDtypeStruct((width, count_vars), f32),
-            jax.ShapeDtypeStruct((8, 128), f32),
-        ],
-        compiler_params=params(1),
-        name="finish",
-        interpret=interpret,
-    )(me, mine, other)
-    return (jnp.sum(loss), grid_grad, mesh_grad, src_grad, dst_grad, out_grad)
+    *parts, from_prev, from_next, grid_grad = lax.optimization_barrier(
+        (*parts, from_prev, from_next, grid_grad)
+    )
+    total = tree(total[:4], parts)
+    parts = [send(total[k : k + 1], second_axis[k]) for k in (1, 2, 3)]
+    mesh_grad = jnp.einsum(
+        "nru,wu->nrw", middle + from_prev + from_next, src_weight, precision=lax.Precision.HIGH
+    )
+    *parts, mesh_grad = lax.optimization_barrier((*parts, mesh_grad))
+    total = tree(total[:1], parts)
+    total = tree(total, [send(total, along_z[k]) for k in (1, 2, 3)])
+    total = total + send(total, along_z[4])
+    total = placed_at(second, total, [send(total, second_axis[k]) for k in (1, 2, 3)])
+    total = placed_at(first, total, [send(total, first_axis[k]) for k in (1, 2, 3)])
+    other = send(total, swap_core).reshape(1152, 256)
+    total = total.reshape(1152, 256)
+    whole_sum = jnp.where(
+        core == 0, jnp.concatenate([total, other], axis=1), jnp.concatenate([other, total], axis=1)
+    )
+    loss = whole_sum[2 * width + var_rows, 0]
+    src_grad = whole_sum[:width]
+    dst_grad = whole_sum[width : 2 * width]
+    out_grad = whole_sum[2 * width : 2 * width + count_vars].T
+    return loss, grid_grad, mesh_grad, src_grad, dst_grad, out_grad
 
 
 def solution(mesh):

time: 154 us -> 135 us (0.88)
  the two profiles are of different devices: /device:TPU:14 before, /device:TPU:1 now
where the time goes in v2:
time: 135 us; the launch traced here: 133 us
  starting transfers between devices  61.1 us (45%)
  waiting for transfers between devices  36.6 us (27%)
  Pallas kernels  19.9 us (15%)
  local copies, waits for them, and re-layouts  9.38 us (7%)
  matrix products  4.45 us (3%)
    ppermute x18, starting transfers between devices, send(): return lax.ppermute(value, axes, pairs)  44.7 us
    ppermute x18, waiting for transfers between devices, send(): return lax.ppermute(value, axes, pairs)  26.3 us
    pallas_call x1, Pallas kernels, body(): pl.pallas_call(functools.partial(backward_kernel, tile, scale, loss_scale...  9.39 us
    pallas_call x1, Pallas kernels, body(): pl.pallas_call(functools.partial(forward_kernel, tile), grid_spec=pltpu.P...  7.09 us
    unnamed x19, local copies, waits for them, and re-layouts  5.33 us
    ppermute x3, waiting for transfers between devices, body(): lax.ppermute(parts[k], 'member', to_peer[k])  5.23 us
    ppermute x3, waiting for transfers between devices, body(): lax.ppermute(slopes[k], 'member', to_peer[k])  5.05 us
    ppermute x1, starting transfers between devices, body(): before = lax.ppermute(mesh_features, 'grid', up)  4.6 us
  transfers between devices with their start and end apart: 28, of which 17 were waited for; matrix products, arithmetic and copies ran while one was open for 6% of the time, Pallas kernels for 2%

profile of v2, /device:TPU:1, one launch (start us, length us, event | category | flops | bytes accessed | tf_op | source)
XLA Modules:
  0.0 133.0 jit_solution(14833754813985634745)
XLA Ops:
  0.6 4.6 %collective-permute-start = (f32[2,32,512]{2,1,0:T(8,128)}, f32[2,32,512]{2,1,0:T(8,128)}, u32[]{:S(2)}, u32[]{:S(2)}) collective-permute-start(f32[2,32,512]{2,1,0:T(8,128)} %own.3), channel_id=1, source_target_pairs={{0,1},{1,2},{2,3},{3,4},{4,5},{5,6},{6,7},{7,8},{8,9},{9,10},{10,1... | collective-permute-start | bytes 393224 | tf_op jit(solution)/shard_map/ppermute | solution.py:252
  5.2 1.3 collective-permute-start.1
  6.5 1.6 %copy.13 = s32[4,512]{0,1:T(8,128)} copy(s32[4,512]{1,0:T(4,128)} %edges.1) | data formatting | bytes 16384 | tf_op args[3]
  8.1 0.9 pad.7.out_weight
  9.1 1.6 %copy-done = f32[2,512,512]{2,1,0:T(8,128)S(1)} copy-done((f32[2,512,512]{2,1,0:T(8,128)S(1)}, f32[2,512,512]{2,1,0:T(8,128)}, u32[]{:S(2)}) %copy-start) | copy-done | bytes 2097176
  10.6 1.2 copy-done.2
  11.9 2.2 %query.1 = f32[2,512,512]{2,1,0:T(8,128)S(1)} custom-call(f32[2,512,512]{2,1,0:T(8,128)S(1)} %copy-done, f32[512,512]{1,0:T(8,128)S(1)} %copy-done.2), custom_call_target="tpu_custom_call" | custom-call | tf_op jit(solution)/shard_map/query/pallas_call | solution.py:254
  14.2 0.9 copy-done.5
  15.2 7.1 %forward.1 = (f32[2,4,512,512]{3,2,1,0:T(8,128)S(1)}, f32[2,512,512]{2,1,0:T(8,128)S(1)}, f32[2,104,128]{2,1,0:T(8,128)S(1)}, f32[2,104,128]{2,1,0:T(8,128)S(1)}...) custom-call(s32[5]{0:T(128)S(1)} %stack.23.me, f32[2,512,512]{2,1,0:T(8,128)S(1)} %query.1, ...), custom_call_target="tpu_custom_call" | custom-call | tf_op jit(solution)/shard_map/forward/pallas_call | solution.py:271
  22.3 1.0 collective-permute-start.2
  23.3 1.3 collective-permute-start.3
  25.1 2.8 %collective-permute-done.3.part2 = f32[2,104,128]{2,1,0:T(8,128)S(1)} collective-permute-done((f32[2,104,128]{2,1,0:T(8,128)S(1)}, f32[2,104,128]{2,1,0:T(8,128)S(1)}, u32[]{:S(2)}, u32[]{:S(2)}) %collective-permute-start.3) | collective-permute-done | bytes 106528 | tf_op jit(solution)/shard_map/ppermute | solution.py:300
  27.9 2.5 %collective-permute-done.4.part3 = f32[2,104,128]{2,1,0:T(8,128)S(1)} collective-permute-done((f32[2,104,128]{2,1,0:T(8,128)S(1)}, f32[2,104,128]{2,1,0:T(8,128)S(1)}, u32[]{:S(2)}, u32[]{:S(2)}) %collective-permute-start.4) | collective-permute-done | bytes 106528 | tf_op jit(solution)/shard_map/ppermute | solution.py:300
  30.3 1.2 score.1
  31.8 1.3 collective-permute-start.6
  33.1 0.6 collective-permute-start.7
  33.7 2.3 %collective-permute-done.6.part2 = f32[2,104,128]{2,1,0:T(8,128)S(1)} collective-permute-done((f32[2,104,128]{2,1,0:T(8,128)S(1)}, f32[2,104,128]{2,1,0:T(8,128)S(1)}, u32[]{:S(2)}, u32[]{:S(2)}) %collective-permute-start.6) | collective-permute-done | bytes 106528 | tf_op jit(solution)/shard_map/ppermute | solution.py:314
  36.1 2.7 %collective-permute-done.7.part3 = f32[2,104,128]{2,1,0:T(8,128)S(1)} collective-permute-done((f32[2,104,128]{2,1,0:T(8,128)S(1)}, f32[2,104,128]{2,1,0:T(8,128)S(1)}, u32[]{:S(2)}, u32[]{:S(2)}) %collective-permute-start.7) | collective-permute-done | bytes 106528 | tf_op jit(solution)/shard_map/ppermute | solution.py:314
  38.8 9.4 %backward.1 = (f32[2,512,512]{2,1,0:T(8,128)S(1)}, f32[2,32,512]{2,1,0:T(8,128)S(1)}, f32[2,32,512]{2,1,0:T(8,128)S(1)}, f32[2,32,512]{2,1,0:T(8,128)S(1)}, f32[...) custom-call(s32[5]{0:T(128)S(1)} %stack.23.me, f32[2,104,128]{2,1,0:T(8,128)S(1)} %get-tuple-element.37.part0, ...), custom_call_target="tpu_custom_call" | custom-call | tf_op jit(solution)/shard_map/backward/pallas_call | solution.py:322
  48.5 4.3 %collective-permute-start.12 = (f32[2,32,512]{2,1,0:T(8,128)S(1)}, f32[2,32,512]{2,1,0:T(8,128)S(1)}, u32[]{:S(2)}, u32[]{:S(2)}) collective-permute-start(f32[2,32,512]{2,1,0:T(8,128)S(1)} %get-tuple-element.46), channel_id=1, source_target_pairs={{0,1},{1,2},{2,3},{3,4},{4,5},{5,6},{6,7},{7,8},{8,9},{9,10},{10,1... | collective-permute-start | bytes 393224 | tf_op jit(solution)/shard_map/ppermute | solution.py:362
  52.7 1.3 collective-permute-start.13
  54.3 15.4 %collective-permute-start.10 = (f32[4,72,256]{2,1,0:T(8,128)S(1)}, f32[4,72,256]{2,1,0:T(8,128)S(1)}, u32[]{:S(2)}, u32[]{:S(2)}) collective-permute-start(f32[4,72,256]{2,1,0:T(8,128)S(1)} %get-tuple-element.65), channel_id=1, source_target_pairs={{0,2},{1,3},{2,0},{3,1},{4,6},{5,7},{6,4},{7,5},{8,10},{9,11},{10,... | collective-permute-start | bytes 884744 | tf_op jit(solution)/shard_map/ppermute | solution.py:51
  70.2 3.2 %fusion.2 = f32[2,512,512]{2,1,0:T(8,128)} fusion(f32[2,512,512]{2,1,0:T(8,128)S(1)} %get-tuple-element.48, f32[512,512]{1,0:T(8,128)S(1)} %copy-done.3), kind=kOutput, calls=%fused_computation.3 | convolution fusion | flops 1610612736 | bytes 5242880 | tf_op jit(solution)/shard_map/npu,wu->npw/dot_general | solution.py:364
  73.4 0.5 collective-permute-done.10
  73.9 3.1 %collective-permute-done.11 = f32[4,72,256]{2,1,0:T(8,128)S(1)} collective-permute-done((f32[4,72,256]{2,1,0:T(8,128)S(1)}, f32[4,72,256]{2,1,0:T(8,128)S(1)}, u32[]{:S(2)}, u32[]{:S(2)}) %collective-permute-start.11) | collective-permute-done | bytes 294944 | tf_op jit(solution)/shard_map/ppermute | solution.py:51
  77.0 1.3 collective-permute-done.9
  78.6 3.7 %collective-permute-start.16 = (f32[1,72,256]{2,1,0:T(8,128)S(1)}, f32[1,72,256]{2,1,0:T(8,128)S(1)}, u32[]{:S(2)}, u32[]{:S(2)}) collective-permute-start(f32[1,72,256]{2,1,0:T(8,128)S(1)} %get-tuple-element.67), channel_id=1, source_target_pairs={{0,160},{1,161},{2,162},{3,163},{4,164},{5,165},{6,166},{7,167},{8... | collective-permute-start | bytes 221192 | tf_op jit(solution)/shard_map/ppermute | solution.py:51
  82.4 1.3 fusion
  84.3 3.4 %collective-permute-start.19 = (f32[1,72,256]{2,1,0:T(8,128)S(1)}, f32[1,72,256]{2,1,0:T(8,128)S(1)}, u32[]{:S(2)}, u32[]{:S(2)}) collective-permute-start(f32[1,72,256]{2,1,0:T(8,128)S(1)} %fusion.7), channel_id=1, source_target_pairs={{0,12},{1,13},{2,14},{3,15},{4,8},{5,9},{6,10},{7,11},{8,4},{9,5},... | collective-permute-start | bytes 221192 | tf_op jit(solution)/shard_map/ppermute | solution.py:51
  87.8 0.9 collective-permute-done.18
  88.7 1.7 %collective-permute-done.19 = f32[1,72,256]{2,1,0:T(8,128)S(1)} collective-permute-done((f32[1,72,256]{2,1,0:T(8,128)S(1)}, f32[1,72,256]{2,1,0:T(8,128)S(1)}, u32[]{:S(2)}, u32[]{:S(2)}) %collective-permute-start.19) | collective-permute-done | bytes 73760 | tf_op jit(solution)/shard_map/ppermute | solution.py:51
  90.4 4.6 %collective-permute-start.20 = (f32[1,72,256]{2,1,0:T(8,128)S(1)}, f32[1,72,256]{2,1,0:T(8,128)S(1)}, u32[]{:S(2)}, u32[]{:S(2)}) collective-permute-start(f32[1,72,256]{2,1,0:T(8,128)S(1)} %add_add_fusion), channel_id=1, source_target_pairs={{0,16},{1,17},{2,18},{3,19},{4,20},{5,21},{6,22},{7,23},{8,24},{9,... | collective-permute-start | bytes 221192 | tf_op jit(solution)/shard_map/ppermute | solution.py:51
  95.0 2.9 %collective-permute-done.20 = f32[1,72,256]{2,1,0:T(8,128)S(1)} collective-permute-done((f32[1,72,256]{2,1,0:T(8,128)S(1)}, f32[1,72,256]{2,1,0:T(8,128)S(1)}, u32[]{:S(2)}, u32[]{:S(2)}) %collective-permute-start.20) | collective-permute-done | bytes 73760 | tf_op jit(solution)/shard_map/ppermute | solution.py:51
  97.9 1.5 %collective-permute-start.21 = (f32[1,72,256]{2,1,0:T(8,128)S(1)}, f32[1,72,256]{2,1,0:T(8,128)S(1)}, u32[]{:S(2)}, u32[]{:S(2)}) collective-permute-start(f32[1,72,256]{2,1,0:T(8,128)S(1)} %get-tuple-element.61), channel_id=1, source_target_pairs={{0,128},{1,129},{2,130},{3,131},{4,132},{5,133},{6,134},{7,135},{8... | collective-permute-start | bytes 221192 | tf_op jit(solution)/shard_map/ppermute | solution.py:51
  99.4 3.3 %collective-permute-start.22 = (f32[1,72,256]{2,1,0:T(8,128)S(1)}, f32[1,72,256]{2,1,0:T(8,128)S(1)}, u32[]{:S(2)}, u32[]{:S(2)}) collective-permute-start(f32[1,72,256]{2,1,0:T(8,128)S(1)} %get-tuple-element.61), channel_id=1, source_target_pairs={{0,32},{1,33},{2,34},{3,35},{4,36},{5,37},{6,38},{7,39},{8,40},{9,... | collective-permute-start | bytes 221192 | tf_op jit(solution)/shard_map/ppermute | solution.py:51
  102.7 2.5 %collective-permute-done.22 = f32[1,72,256]{2,1,0:T(8,128)S(1)} collective-permute-done((f32[1,72,256]{2,1,0:T(8,128)S(1)}, f32[1,72,256]{2,1,0:T(8,128)S(1)}, u32[]{:S(2)}, u32[]{:S(2)}) %collective-permute-start.22) | collective-permute-done | bytes 73760 | tf_op jit(solution)/shard_map/ppermute | solution.py:51
  105.3 1.8 %collective-permute-done.23 = f32[1,72,256]{2,1,0:T(8,128)S(1)} collective-permute-done((f32[1,72,256]{2,1,0:T(8,128)S(1)}, f32[1,72,256]{2,1,0:T(8,128)S(1)}, u32[]{:S(2)}, u32[]{:S(2)}) %collective-permute-start.23) | collective-permute-done | bytes 73760 | tf_op jit(solution)/shard_map/ppermute | solution.py:51
  107.1 0.6 collective-permute-start.24
  107.7 2.1 %collective-permute-start.25 = (f32[4,72,256]{2,1,0:T(8,128)S(1)}, f32[4,72,256]{2,1,0:T(8,128)S(1)}, u32[]{:S(2)}, u32[]{:S(2)}) collective-permute-start(f32[4,72,256]{2,1,0:T(8,128)S(1)} %constant_dynamic-update-slice_fusion.4), channel_id=1, source_target_pairs={{0,2},{1,3},{2,0},{3,1},{4,6},{5,7},{6,4},{7,5},{8,10},{9,11},{10,... | collective-permute-start | bytes 884744 | tf_op jit(solution)/shard_map/ppermute | solution.py:51
  109.9 1.2 collective-permute-start.26
  111.2 2.2 %collective-permute-done.24 = f32[4,72,256]{2,1,0:T(8,128)S(1)} collective-permute-done((f32[4,72,256]{2,1,0:T(8,128)S(1)}, f32[4,72,256]{2,1,0:T(8,128)S(1)}, u32[]{:S(2)}, u32[]{:S(2)}) %collective-permute-start.24) | collective-permute-done | bytes 294944 | tf_op jit(solution)/shard_map/ppermute | solution.py:51
  113.4 4.1 %collective-permute-done.25 = f32[4,72,256]{2,1,0:T(8,128)S(1)} collective-permute-done((f32[4,72,256]{2,1,0:T(8,128)S(1)}, f32[4,72,256]{2,1,0:T(8,128)S(1)}, u32[]{:S(2)}, u32[]{:S(2)}) %collective-permute-start.25) | collective-permute-done | bytes 294944 | tf_op jit(solution)/shard_map/ppermute | solution.py:51
  117.5 2.3 %collective-permute-done.26 = f32[4,72,256]{2,1,0:T(8,128)S(1)} collective-permute-done((f32[4,72,256]{2,1,0:T(8,128)S(1)}, f32[4,72,256]{2,1,0:T(8,128)S(1)}, u32[]{:S(2)}, u32[]{:S(2)}) %collective-permute-start.26) | collective-permute-done | bytes 294944 | tf_op jit(solution)/shard_map/ppermute | solution.py:51
  119.8 7.6 %collective-permute-start.27 = (f32[16,72,256]{2,1,0:T(8,128)S(1)}, f32[16,72,256]{2,1,0:T(8,128)S(1)}, u32[]{:S(2)}, u32[]{:S(2)}) collective-permute-start(f32[16,72,256]{2,1,0:T(8,128)S(1)} %constant_dynamic-update-slice_fusion), channel_id=1, source_target_pairs={{0,64},{1,65},{2,66},{3,67},{4,68},{5,69},{6,70},{7,71},{8,72},{9,... | collective-permute-start | bytes 3538952 | tf_op jit(solution)/shard_map/ppermute | solution.py:51
  127.4 2.5 %collective-permute-done.27 = f32[16,72,256]{2,1,0:T(8,128)S(1)} collective-permute-done((f32[16,72,256]{2,1,0:T(8,128)S(1)}, f32[16,72,256]{2,1,0:T(8,128)S(1)}, u32[]{:S(2)}, u32[]{:S(2)}) %collective-permute-start.27) | collective-permute-done | bytes 1179680 | tf_op jit(solution)/shard_map/ppermute | solution.py:51
  130.3 1.5 %fusion.8 = (f32[512,512]{1,0:T(8,128)}, f32[512,512]{1,0:T(8,128)}) fusion(f32[1152,512]{1,0:T(8,128)S(1)} %maximum_select_fusion), kind=kLoop, calls=%fused_computation.21 | loop fusion | bytes 4194304 | tf_op jit(solution)/shard_map/slice | solution.py:386
  131.8 0.7 slice_bitcast_fusion
  132.5 0.5 slice.56
  (56 shorter events, 3.4 us)
Async XLA Ops:
  0.6 13.6 %collective-permute-start = (f32[2,32,512]{2,1,0:T(8,128)}, f32[2,32,512]{2,1,0:T(8,128)}, u32[]{:S(2)}, u32[]{:S(2)}) collective-permute-start(f32[2,32,512]{2,1,0:T(8,128)} %own.3), channel_id=1, source_target_pairs={{0,1},{1,2},{2,3},{3,4},{4,5},{5,6},{6,7},{7,8},{8,9},{9,10},{10,1... | collective-permute-start | bytes 393224 | tf_op jit(solution)/shard_map/ppermute | solution.py:252
  5.2 9.0 %collective-permute-start.1 = (f32[2,32,512]{2,1,0:T(8,128)}, f32[2,32,512]{2,1,0:T(8,128)}, u32[]{:S(2)}, u32[]{:S(2)}) collective-permute-start(f32[2,32,512]{2,1,0:T(8,128)} %own.3), channel_id=1, source_target_pairs={{1,0},{2,1},{3,2},{4,3},{5,4},{6,5},{7,6},{8,7},{9,8},{10,9},{11,1... | collective-permute-start | bytes 393224 | tf_op jit(solution)/shard_map/ppermute | solution.py:253
  9.0 1.6 %copy-start = (f32[2,512,512]{2,1,0:T(8,128)S(1)}, f32[2,512,512]{2,1,0:T(8,128)}, u32[]{:S(2)}) copy-start(f32[2,512,512]{2,1,0:T(8,128)} %features.3) | copy-start | bytes 6291460
  10.6 1.2 copy-start.2
  11.9 2.3 %copy-start.4 = (f32[512,512]{1,0:T(8,128)S(1)}, f32[512,512]{1,0:T(8,128)}, u32[]{:S(2)}) copy-start(f32[512,512]{1,0:T(8,128)} %src_weight.1) | copy-start | bytes 3145732
  11.9 2.4 %copy-start.6 = (f32[2,32,512]{2,1,0:T(8,128)S(1)}, f32[2,32,512]{2,1,0:T(8,128)}, u32[]{:S(2)}) copy-start(f32[2,32,512]{2,1,0:T(8,128)} %own.3) | copy-start | bytes 393220
  14.2 1.0 copy-start.5
  15.2 9.9 %copy-start.8 = (f32[100,512]{1,0:T(8,128)S(1)}, f32[100,512]{1,0:T(8,128)}, u32[]{:S(2)}) copy-start(f32[100,512]{1,0:T(8,128)} %param.9) | copy-start | bytes 614404
  15.2 23.6 %copy-start.1 = (f32[2,512,512]{2,1,0:T(8,128)S(1)}, f32[2,512,512]{2,1,0:T(8,128)}, u32[]{:S(2)}) copy-start(f32[2,512,512]{2,1,0:T(8,128)} %features.3) | copy-start | bytes 6291460
  15.2 23.6 %copy-start.7 = (s32[4,512]{1,0:T(4,128)S(1)}, s32[4,512]{1,0:T(4,128)}, u32[]{:S(2)}) copy-start(s32[4,512]{1,0:T(4,128)} %edges.1) | copy-start | bytes 24580
  22.3 2.8 %collective-permute-start.2 = (f32[2,104,128]{2,1,0:T(8,128)S(1)}, f32[2,104,128]{2,1,0:T(8,128)S(1)}, u32[]{:S(2)}, u32[]{:S(2)}) collective-permute-start(f32[2,104,128]{2,1,0:T(8,128)S(1)} %get-tuple-element.34), channel_id=1, source_target_pairs={{0,64},{64,0},{128,192},{192,128},{1,65},{65,1},{129,193},{193,129... | collective-permute-start | bytes 319496 | tf_op jit(solution)/shard_map/ppermute | solution.py:300
  23.3 4.5 %collective-permute-start.3 = (f32[2,104,128]{2,1,0:T(8,128)S(1)}, f32[2,104,128]{2,1,0:T(8,128)S(1)}, u32[]{:S(2)}, u32[]{:S(2)}) collective-permute-start(f32[2,104,128]{2,1,0:T(8,128)S(1)} %get-tuple-element.35), channel_id=1, source_target_pairs={{0,128},{64,192},{128,0},{192,64},{1,129},{65,193},{129,1},{193,65... | collective-permute-start | bytes 319496 | tf_op jit(solution)/shard_map/ppermute | solution.py:300
  24.7 5.7 %collective-permute-start.4 = (f32[2,104,128]{2,1,0:T(8,128)S(1)}, f32[2,104,128]{2,1,0:T(8,128)S(1)}, u32[]{:S(2)}, u32[]{:S(2)}) collective-permute-start(f32[2,104,128]{2,1,0:T(8,128)S(1)} %get-tuple-element.36), channel_id=1, source_target_pairs={{0,192},{64,128},{128,64},{192,0},{1,193},{65,129},{129,65},{193,1... | collective-permute-start | bytes 319496 | tf_op jit(solution)/shard_map/ppermute | solution.py:300
  31.5 2.2 %collective-permute-start.5 = (f32[2,104,128]{2,1,0:T(8,128)S(1)}, f32[2,104,128]{2,1,0:T(8,128)S(1)}, u32[]{:S(2)}, u32[]{:S(2)}) collective-permute-start(f32[2,104,128]{2,1,0:T(8,128)S(1)} %get-tuple-element.38), channel_id=1, source_target_pairs={{0,64},{64,0},{128,192},{192,128},{1,65},{65,1},{129,193},{193,129... | collective-permute-start | bytes 319496 | tf_op jit(solution)/shard_map/ppermute | solution.py:314
  31.8 4.3 %collective-permute-start.6 = (f32[2,104,128]{2,1,0:T(8,128)S(1)}, f32[2,104,128]{2,1,0:T(8,128)S(1)}, u32[]{:S(2)}, u32[]{:S(2)}) collective-permute-start(f32[2,104,128]{2,1,0:T(8,128)S(1)} %get-tuple-element.39), channel_id=1, source_target_pairs={{0,128},{64,192},{128,0},{192,64},{1,129},{65,193},{129,1},{193,65... | collective-permute-start | bytes 319496 | tf_op jit(solution)/shard_map/ppermute | solution.py:314
  33.1 5.7 %collective-permute-start.7 = (f32[2,104,128]{2,1,0:T(8,128)S(1)}, f32[2,104,128]{2,1,0:T(8,128)S(1)}, u32[]{:S(2)}, u32[]{:S(2)}) collective-permute-start(f32[2,104,128]{2,1,0:T(8,128)S(1)} %get-tuple-element.40), channel_id=1, source_target_pairs={{0,192},{64,128},{128,64},{192,0},{1,193},{65,129},{129,65},{193,1... | collective-permute-start | bytes 319496 | tf_op jit(solution)/shard_map/ppermute | solution.py:314
  48.2 5.8 %collective-permute-start.8 = (f32[16,72,256]{2,1,0:T(8,128)S(1)}, f32[16,72,256]{2,1,0:T(8,128)S(1)}, u32[]{:S(2)}, u32[]{:S(2)}) collective-permute-start(f32[16,72,256]{2,1,0:T(8,128)S(1)} %get-tuple-element.45), channel_id=1, source_target_pairs={{0,64},{1,65},{2,66},{3,67},{4,68},{5,69},{6,70},{7,71},{8,72},{9,... | collective-permute-start | bytes 3538952 | tf_op jit(solution)/shard_map/ppermute | solution.py:51
  48.5 24.9 %collective-permute-start.12 = (f32[2,32,512]{2,1,0:T(8,128)S(1)}, f32[2,32,512]{2,1,0:T(8,128)S(1)}, u32[]{:S(2)}, u32[]{:S(2)}) collective-permute-start(f32[2,32,512]{2,1,0:T(8,128)S(1)} %get-tuple-element.46), channel_id=1, source_target_pairs={{0,1},{1,2},{2,3},{3,4},{4,5},{5,6},{6,7},{7,8},{8,9},{9,10},{10,1... | collective-permute-start | bytes 393224 | tf_op jit(solution)/shard_map/ppermute | solution.py:362
  52.7 20.6 %collective-permute-start.13 = (f32[2,32,512]{2,1,0:T(8,128)S(1)}, f32[2,32,512]{2,1,0:T(8,128)S(1)}, u32[]{:S(2)}, u32[]{:S(2)}) collective-permute-start(f32[2,32,512]{2,1,0:T(8,128)S(1)} %get-tuple-element.47), channel_id=1, source_target_pairs={{1,0},{2,1},{3,2},{4,3},{5,4},{6,5},{7,6},{8,7},{9,8},{10,9},{11,1... | collective-permute-start | bytes 393224 | tf_op jit(solution)/shard_map/ppermute | solution.py:363
  54.2 16.0 %copy-start.3 = (f32[512,512]{1,0:T(8,128)S(1)}, f32[512,512]{1,0:T(8,128)}, u32[]{:S(2)}) copy-start(f32[512,512]{1,0:T(8,128)} %weight.1) | copy-start | bytes 3145732
  54.3 19.6 %collective-permute-start.10 = (f32[4,72,256]{2,1,0:T(8,128)S(1)}, f32[4,72,256]{2,1,0:T(8,128)S(1)}, u32[]{:S(2)}, u32[]{:S(2)}) collective-permute-start(f32[4,72,256]{2,1,0:T(8,128)S(1)} %get-tuple-element.65), channel_id=1, source_target_pairs={{0,2},{1,3},{2,0},{3,1},{4,6},{5,7},{6,4},{7,5},{8,10},{9,11},{10,... | collective-permute-start | bytes 884744 | tf_op jit(solution)/shard_map/ppermute | solution.py:51
  69.7 7.3 %collective-permute-start.11 = (f32[4,72,256]{2,1,0:T(8,128)S(1)}, f32[4,72,256]{2,1,0:T(8,128)S(1)}, u32[]{:S(2)}, u32[]{:S(2)}) collective-permute-start(f32[4,72,256]{2,1,0:T(8,128)S(1)} %get-tuple-element.64), channel_id=1, source_target_pairs={{0,3},{1,2},{2,1},{3,0},{4,7},{5,6},{6,5},{7,4},{8,11},{9,10},{10,... | collective-permute-start | bytes 884744 | tf_op jit(solution)/shard_map/ppermute | solution.py:51
  69.9 8.4 %collective-permute-start.9 = (f32[4,72,256]{2,1,0:T(8,128)S(1)}, f32[4,72,256]{2,1,0:T(8,128)S(1)}, u32[]{:S(2)}, u32[]{:S(2)}) collective-permute-start(f32[4,72,256]{2,1,0:T(8,128)S(1)} %get-tuple-element.66), channel_id=1, source_target_pairs={{0,1},{1,0},{2,3},{3,2},{4,5},{5,4},{6,7},{7,6},{8,9},{9,8},{10,11... | collective-permute-start | bytes 884744 | tf_op jit(solution)/shard_map/ppermute | solution.py:51
  78.4 5.2 %collective-permute-start.14 = (f32[1,72,256]{2,1,0:T(8,128)S(1)}, f32[1,72,256]{2,1,0:T(8,128)S(1)}, u32[]{:S(2)}, u32[]{:S(2)}) collective-permute-start(f32[1,72,256]{2,1,0:T(8,128)S(1)} %get-tuple-element.69), channel_id=1, source_target_pairs={{0,128},{1,129},{2,130},{3,131},{4,132},{5,133},{6,134},{7,135},{8... | collective-permute-start | bytes 221192 | tf_op jit(solution)/shard_map/ppermute | solution.py:51
  78.5 5.1 %collective-permute-start.15 = (f32[1,72,256]{2,1,0:T(8,128)S(1)}, f32[1,72,256]{2,1,0:T(8,128)S(1)}, u32[]{:S(2)}, u32[]{:S(2)}) collective-permute-start(f32[1,72,256]{2,1,0:T(8,128)S(1)} %get-tuple-element.68), channel_id=1, source_target_pairs={{0,32},{1,33},{2,34},{3,35},{4,36},{5,37},{6,38},{7,39},{8,40},{9,... | collective-permute-start | bytes 221192 | tf_op jit(solution)/shard_map/ppermute | solution.py:51
  78.6 5.5 %collective-permute-start.16 = (f32[1,72,256]{2,1,0:T(8,128)S(1)}, f32[1,72,256]{2,1,0:T(8,128)S(1)}, u32[]{:S(2)}, u32[]{:S(2)}) collective-permute-start(f32[1,72,256]{2,1,0:T(8,128)S(1)} %get-tuple-element.67), channel_id=1, source_target_pairs={{0,160},{1,161},{2,162},{3,163},{4,164},{5,165},{6,166},{7,167},{8... | collective-permute-start | bytes 221192 | tf_op jit(solution)/shard_map/ppermute | solution.py:51
  84.1 3.6 %collective-permute-start.17 = (f32[1,72,256]{2,1,0:T(8,128)S(1)}, f32[1,72,256]{2,1,0:T(8,128)S(1)}, u32[]{:S(2)}, u32[]{:S(2)}) collective-permute-start(f32[1,72,256]{2,1,0:T(8,128)S(1)} %fusion.7), channel_id=1, source_target_pairs={{0,4},{1,5},{2,6},{3,7},{4,0},{5,1},{6,2},{7,3},{8,12},{9,13},{10,... | collective-permute-start | bytes 221192 | tf_op jit(solution)/shard_map/ppermute | solution.py:51
  84.2 4.5 %collective-permute-start.18 = (f32[1,72,256]{2,1,0:T(8,128)S(1)}, f32[1,72,256]{2,1,0:T(8,128)S(1)}, u32[]{:S(2)}, u32[]{:S(2)}) collective-permute-start(f32[1,72,256]{2,1,0:T(8,128)S(1)} %fusion.7), channel_id=1, source_target_pairs={{0,8},{1,9},{2,10},{3,11},{4,12},{5,13},{6,14},{7,15},{8,0},{9,1},... | collective-permute-start | bytes 221192 | tf_op jit(solution)/shard_map/ppermute | solution.py:51
  84.3 6.1 %collective-permute-start.19 = (f32[1,72,256]{2,1,0:T(8,128)S(1)}, f32[1,72,256]{2,1,0:T(8,128)S(1)}, u32[]{:S(2)}, u32[]{:S(2)}) collective-permute-start(f32[1,72,256]{2,1,0:T(8,128)S(1)} %fusion.7), channel_id=1, source_target_pairs={{0,12},{1,13},{2,14},{3,15},{4,8},{5,9},{6,10},{7,11},{8,4},{9,5},... | collective-permute-start | bytes 221192 | tf_op jit(solution)/shard_map/ppermute | solution.py:51
  90.4 7.5 %collective-permute-start.20 = (f32[1,72,256]{2,1,0:T(8,128)S(1)}, f32[1,72,256]{2,1,0:T(8,128)S(1)}, u32[]{:S(2)}, u32[]{:S(2)}) collective-permute-start(f32[1,72,256]{2,1,0:T(8,128)S(1)} %add_add_fusion), channel_id=1, source_target_pairs={{0,16},{1,17},{2,18},{3,19},{4,20},{5,21},{6,22},{7,23},{8,24},{9,... | collective-permute-start | bytes 221192 | tf_op jit(solution)/shard_map/ppermute | solution.py:51
  97.9 4.8 %collective-permute-start.21 = (f32[1,72,256]{2,1,0:T(8,128)S(1)}, f32[1,72,256]{2,1,0:T(8,128)S(1)}, u32[]{:S(2)}, u32[]{:S(2)}) collective-permute-start(f32[1,72,256]{2,1,0:T(8,128)S(1)} %get-tuple-element.61), channel_id=1, source_target_pairs={{0,128},{1,129},{2,130},{3,131},{4,132},{5,133},{6,134},{7,135},{8... | collective-permute-start | bytes 221192 | tf_op jit(solution)/shard_map/ppermute | solution.py:51
  99.4 5.8 %collective-permute-start.22 = (f32[1,72,256]{2,1,0:T(8,128)S(1)}, f32[1,72,256]{2,1,0:T(8,128)S(1)}, u32[]{:S(2)}, u32[]{:S(2)}) collective-permute-start(f32[1,72,256]{2,1,0:T(8,128)S(1)} %get-tuple-element.61), channel_id=1, source_target_pairs={{0,32},{1,33},{2,34},{3,35},{4,36},{5,37},{6,38},{7,39},{8,40},{9,... | collective-permute-start | bytes 221192 | tf_op jit(solution)/shard_map/ppermute | solution.py:51
  102.7 4.4 %collective-permute-start.23 = (f32[1,72,256]{2,1,0:T(8,128)S(1)}, f32[1,72,256]{2,1,0:T(8,128)S(1)}, u32[]{:S(2)}, u32[]{:S(2)}) collective-permute-start(f32[1,72,256]{2,1,0:T(8,128)S(1)} %get-tuple-element.61), channel_id=1, source_target_pairs={{0,160},{1,161},{2,162},{3,163},{4,164},{5,165},{6,166},{7,167},{8... | collective-permute-start | bytes 221192 | tf_op jit(solution)/shard_map/ppermute | solution.py:51
  107.1 6.3 %collective-permute-start.24 = (f32[4,72,256]{2,1,0:T(8,128)S(1)}, f32[4,72,256]{2,1,0:T(8,128)S(1)}, u32[]{:S(2)}, u32[]{:S(2)}) collective-permute-start(f32[4,72,256]{2,1,0:T(8,128)S(1)} %constant_dynamic-update-slice_fusion.4), channel_id=1, source_target_pairs={{0,1},{1,0},{2,3},{3,2},{4,5},{5,4},{6,7},{7,6},{8,9},{9,8},{10,11... | collective-permute-start | bytes 884744 | tf_op jit(solution)/shard_map/ppermute | solution.py:51
  107.7 9.8 %collective-permute-start.25 = (f32[4,72,256]{2,1,0:T(8,128)S(1)}, f32[4,72,256]{2,1,0:T(8,128)S(1)}, u32[]{:S(2)}, u32[]{:S(2)}) collective-permute-start(f32[4,72,256]{2,1,0:T(8,128)S(1)} %constant_dynamic-update-slice_fusion.4), channel_id=1, source_target_pairs={{0,2},{1,3},{2,0},{3,1},{4,6},{5,7},{6,4},{7,5},{8,10},{9,11},{10,... | collective-permute-start | bytes 884744 | tf_op jit(solution)/shard_map/ppermute | solution.py:51
  109.9 9.9 %collective-permute-start.26 = (f32[4,72,256]{2,1,0:T(8,128)S(1)}, f32[4,72,256]{2,1,0:T(8,128)S(1)}, u32[]{:S(2)}, u32[]{:S(2)}) collective-permute-start(f32[4,72,256]{2,1,0:T(8,128)S(1)} %constant_dynamic-update-slice_fusion.4), channel_id=1, source_target_pairs={{0,3},{1,2},{2,1},{3,0},{4,7},{5,6},{6,5},{7,4},{8,11},{9,10},{10,... | collective-permute-start | bytes 884744 | tf_op jit(solution)/shard_map/ppermute | solution.py:51
  119.8 10.1 %collective-permute-start.27 = (f32[16,72,256]{2,1,0:T(8,128)S(1)}, f32[16,72,256]{2,1,0:T(8,128)S(1)}, u32[]{:S(2)}, u32[]{:S(2)}) collective-permute-start(f32[16,72,256]{2,1,0:T(8,128)S(1)} %constant_dynamic-update-slice_fusion), channel_id=1, source_target_pairs={{0,64},{1,65},{2,66},{3,67},{4,68},{5,69},{6,70},{7,71},{8,72},{9,... | collective-permute-start | bytes 3538952 | tf_op jit(solution)/shard_map/ppermute | solution.py:51

commit v3 on v2

--- a/solution.py
+++ b/solution.py
@@ -14,6 +14,8 @@
 f32 = jnp.float32
 bf16 = jnp.bfloat16
 interpret = False
+node_rows = 32
+loss_row = 104
 
 
 def place_of(member, grid):
@@ -68,15 +70,30 @@
 TN = ((0,), (0,))
 
 
-def query_kernel(features, weight, query, high, low):
-    @pl.when(pl.program_id(0) == 0)
-    def _():
-        high[...], low[...] = split(0.5 * weight[...])
-
-    query[0] = dot3(split(features[0]), (high[...], low[...]), NN)
-
-
-def forward_kernel(points, me, query, edges, before, own, after, src_weight, out_weight,
+def query_kernel(me, edges, features, weight, src_weight, query, edges_t, src_high, src_low,
+                 held, held_weight, held_src, sems):
+    members, points = features.shape[0], features.shape[1]
+    half = points // 2
+    loads = [pltpu.make_async_copy(weight, held_weight, sems.at[0])]
+    for i in range(2 * members):
+        piece = (i // 2, pl.ds((i % 2) * half, half))
+        loads.append(pltpu.make_async_copy(features.at[piece], held.at[piece], sems.at[1 + i]))
+    loads.append(pltpu.make_async_copy(src_weight, held_src, sems.at[1 + 2 * members]))
+    for load in loads:
+        load.start()
+    local = edges[...] - (me[1] - 1) * node_rows
+    edges_t[...] = jnp.concatenate([local, local], axis=0).T
+    loads[0].wait()
+    high, low = split(0.5 * held_weight[...])
+    for i in range(2 * members):
+        loads[1 + i].wait()
+        piece = (i // 2, pl.ds((i % 2) * half, half))
+        query[piece] = dot3(split(held[piece]), (high, low), NN)
+    loads[-1].wait()
+    src_high[...], src_low[...] = split(0.5 * held_src[...])
+
+
+def forward_kernel(points, me, query, edges, before, own, after, src_high, src_low, out_weight,
                    slope, summed, part0, part1, part2, part3, nodes, fields):
     member, tile = pl.program_id(0), pl.program_id(1)
     tiles = pl.num_programs(1)
@@ -85,14 +102,14 @@
     @pl.when((member == 0) & (tile == 0))
     def _():
         nodes[...] = jnp.zeros_like(nodes)
-        weight = split(0.5 * src_weight[...])
-        for n in range(own.shape[0]):
-            ext = jnp.concatenate([before[n], own[n], after[n]], axis=0)
-            high, low = split(dot3(split(ext), weight, NN))
-            nodes[n, 0 : 3 * rows] = high
-            nodes[n, 128 : 128 + 3 * rows] = low
-
-    local = edges[...] - (me[1] - 1) * rows
+        ext = jnp.concatenate([side[n] for n in range(2) for side in (before, own, after)], axis=0)
+        high, low = split(dot3(split(ext), (src_high[...], src_low[...]), NN))
+        for n in range(2):
+            at = slice(n * 3 * rows, (n + 1) * 3 * rows)
+            nodes[n, 0 : 3 * rows] = high[at]
+            nodes[n, 128 : 128 + 3 * rows] = low[at]
+
+    local = edges[...]
     columns = lax.broadcasted_iota(jnp.int32, (points, 256), 1) & 127
     total = None
     for k in range(4):
@@ -113,17 +130,17 @@
             part[member] = fields[:, pl.ds(pl.multiple_of((me[0] ^ k) * 128, 128), 128)]
 
 
-def score_kernel(count_vars, me, part0, part1, part2, part3, targets, out0, out1, out2, out3, loss):
+def score_kernel(me, part0, part1, part2, part3, targets, out0, out1, out2, out3, loss):
     parts, outs = (part0, part1, part2, part3), (out0, out1, out2, out3)
     count = 8
     spread = (1.0 - alpha_fair) / count
     factor = (1.0 - spread) / (count * (count - 1))
     rows = targets.shape[0]
-    near = jnp.zeros((8, 128), f32)
-    far = jnp.zeros((8, 128), f32)
-    for block in range(rows // 8):
-        at = pl.ds(block * 8, 8)
-        real = block * 8 + lax.broadcasted_iota(jnp.int32, (8, 128), 0) < count_vars
+    near = jnp.zeros((1, 128), f32)
+    far = jnp.zeros((1, 128), f32)
+    for start in range(0, rows, 8):
+        height = min(8, rows - start)
+        at = pl.ds(start, height)
         truth = targets[at]
         fields = [parts[j // 2][j % 2, at] for j in range(count)]
         slopes, dist_sum = [], None
@@ -146,16 +163,17 @@
                 term = differ * inverse
                 pairs[j] = term if pairs[j] is None else pairs[j] + term
                 pairs[k] = -term if pairs[k] is None else pairs[k] - term
-        near += jnp.where(real, dist_sum, 0.0)
-        far += jnp.where(real, pair_sum, 0.0)
+        near += jnp.sum(dist_sum, axis=0, keepdims=True)
+        far += jnp.sum(pair_sum, axis=0, keepdims=True)
         for j in range(count):
             outs[j // 2][j % 2, at] = slopes[j] - factor * pairs[j]
-    loss[...] = near * (1.0 / count) - factor * far
+    loss[...] = jnp.broadcast_to(near * (1.0 / count) - factor * far, loss.shape)
 
 
 def backward_kernel(points, scale, loss_scale, me, part0, part1, part2, part3, loss, slope, summed, features,
                     edges, before, own, after, out_weight,
-                    grad_query, lower, middle, upper, keep, away, grad_ext, slopes, sums):
+                    grad_query, lower, middle, upper, *rest):
+    keep, away, (grad_ext, slopes, sums) = rest[:4], rest[4:8], rest[8:]
     member, tile = pl.program_id(0), pl.program_id(1)
     members, tiles = pl.num_programs(0), pl.num_programs(1)
     rows = own.shape[1]
@@ -199,13 +217,13 @@
         for n in range(2):
             for i, side in enumerate((lower, middle, upper)):
                 side[n] = grad_ext[n, i * rows : (i + 1) * rows]
-        end = 2 * width + vars_rows
-        sums[end : end + 8] = jnp.full((8, width), jnp.sum(loss[...]) * (loss_scale / scale), f32)
+        end = 2 * width + loss_row
+        sums[end : end + 8] = jnp.full((8, width), jnp.sum(loss[0:1]) * (loss_scale / scale), f32)
         for j in range(16):
             for out, core, order in ((keep, me[2], me[3]), (away, 1 - me[2], me[4])):
                 at = pl.ds(pl.multiple_of((j ^ order) * 72, 8), 72)
                 lanes = pl.ds(pl.multiple_of(core * 256, 128), 256)
-                out[j] = sums[at, lanes] * scale
+                out[j // 4][j % 4] = sums[at, lanes] * scale
 
 
 def whole(shape=None):
@@ -232,7 +250,6 @@
     members, rows, width = mesh_features.shape
     points = grid_features.shape[1]
     count_vars = targets.shape[0]
-    var_rows = -(-count_vars // 8) * 8
     slabs = lax.axis_size("grid")
     member, grid = lax.axis_index("member"), lax.axis_index("grid")
     place = place_of(member, grid)
@@ -251,23 +268,38 @@
     down = [(j, i) for i, j in up]
     before = lax.ppermute(mesh_features, "grid", up)
     after = lax.ppermute(mesh_features, "grid", down)
-    query = pl.pallas_call(
+    out_weight = output_weight.T
+    me_spec = pl.BlockSpec(memory_space=pltpu.SMEM)
+    in_hbm = pl.BlockSpec(memory_space=pltpu.HBM)
+    query, edges_t, src_high, src_low = pl.pallas_call(
         query_kernel,
-        grid=(members,),
-        in_specs=[pl.BlockSpec((1, points, width), lambda n: (n, 0, 0)), whole()],
-        out_specs=pl.BlockSpec((1, points, width), lambda n: (n, 0, 0)),
-        out_shape=jax.ShapeDtypeStruct((members, points, width), f32),
-        scratch_shapes=[pltpu.VMEM((width, width), bf16)] * 2,
-        compiler_params=params(1),
+        in_specs=[me_spec, whole(), in_hbm, in_hbm, in_hbm],
+        out_specs=[whole()] * 4,
+        out_shape=[
+            jax.ShapeDtypeStruct((members, points, width), f32),
+            jax.ShapeDtypeStruct((points, 8), jnp.int32),
+            jax.ShapeDtypeStruct((width, width), bf16),
+            jax.ShapeDtypeStruct((width, width), bf16),
+        ],
+        scratch_shapes=[
+            pltpu.VMEM((members, points, width), f32),
+            pltpu.VMEM((width, width), f32),
+            pltpu.VMEM((width, width), f32),
+            pltpu.SemaphoreType.DMA((2 + 2 * members,)),
+        ],
+        compiler_params=pltpu.CompilerParams(vmem_limit_bytes=vmem_limit),
         name="query",
         interpret=interpret,
-    )(grid_features, dst_weight)
-    edges_t = edges.T
-    out_weight = jnp.pad(output_weight.T, ((0, var_rows - count_vars), (0, 0)))
-    targets = jnp.pad(targets, ((0, var_rows - count_vars), (0, 0)))
+    )(
+        me,
+        pltpu.with_memory_space_constraint(edges, pltpu.HBM),
+        pltpu.with_memory_space_constraint(grid_features, pltpu.HBM),
+        pltpu.with_memory_space_constraint(dst_weight, pltpu.HBM),
+        pltpu.with_memory_space_constraint(src_weight, pltpu.HBM),
+    )
 
     tile = 512
-    part_shape = jax.ShapeDtypeStruct((members, var_rows, 128), f32)
+    part_shape = jax.ShapeDtypeStruct((members, count_vars, 128), f32)
     slope, summed, *parts = pl.pallas_call(
         functools.partial(forward_kernel, tile),
         grid_spec=pltpu.PrefetchScalarGridSpec(
@@ -275,8 +307,8 @@
             grid=(members, points // tile),
             in_specs=[
                 pl.BlockSpec((1, tile, width), lambda n, t, me: (n, t, 0)),
-                pl.BlockSpec((tile, 4), lambda n, t, me: (t, 0)),
-                whole(), whole(), whole(), whole(), whole(),
+                pl.BlockSpec((tile, 8), lambda n, t, me: (t, 0)),
+                whole(), whole(), whole(), whole(), whole(), whole(),
             ],
             out_specs=[
                 pl.BlockSpec((1, 4, tile, width), lambda n, t, me: (n, 0, t, 0)),
@@ -284,7 +316,7 @@
             ] + [whole()] * 4,
             scratch_shapes=[
                 pltpu.VMEM((members, 256, width), bf16),
-                pltpu.VMEM((var_rows, points), f32),
+                pltpu.VMEM((count_vars, points), f32),
             ],
         ),
         out_shape=[
@@ -294,16 +326,16 @@
         compiler_params=params(2),
         name="forward",
         interpret=interpret,
-    )(me, query, edges_t, before, mesh_features, after, src_weight, out_weight)
+    )(me, query, edges_t, before, mesh_features, after, src_high, src_low, out_weight)
 
     to_peer = [[(i, i ^ k) for i in range(4)] for k in range(4)]
     parts = [parts[0]] + [lax.ppermute(parts[k], "member", to_peer[k]) for k in (1, 2, 3)]
     *slopes, loss = pl.pallas_call(
-        functools.partial(score_kernel, count_vars),
+        score_kernel,
         grid_spec=pltpu.PrefetchScalarGridSpec(
             num_scalar_prefetch=1,
             grid=(1,),
-            in_specs=[whole()] * 4 + [pl.BlockSpec((var_rows, 128), lambda i, me: (0, me[0]))],
+            in_specs=[whole()] * 4 + [pl.BlockSpec((count_vars, 128), lambda i, me: (0, me[0]))],
             out_specs=[whole()] * 5,
         ),
         out_shape=[part_shape] * 4 + [jax.ShapeDtypeStruct((8, 128), f32)],
@@ -316,10 +348,10 @@
     total_members = lax.axis_size("member") * members
     scale = 1.0 / (total_members * points * slabs) ** 0.5
     loss_scale = 1.0 / (points * slabs * count_vars)
-    chunks = jax.ShapeDtypeStruct((16, 72, 256), f32)
+    chunks = jax.ShapeDtypeStruct((4, 72, 256), f32)
     side = jax.ShapeDtypeStruct((members, rows, width), f32)
     tile = 256
-    grad_query, lower, middle, upper, keep, away = pl.pallas_call(
+    grad_query, lower, middle, upper, *parts = pl.pallas_call(
         functools.partial(backward_kernel, tile, scale, loss_scale),
         grid_spec=pltpu.PrefetchScalarGridSpec(
             num_scalar_prefetch=1,
@@ -333,11 +365,11 @@
             ],
             out_specs=[
                 pl.BlockSpec((1, tile, width), lambda n, t, me: (n, t, 0)),
-                whole(), whole(), whole(), whole(), whole(),
-            ],
+                whole(), whole(), whole(),
+            ] + [whole()] * 8,
             scratch_shapes=[
                 pltpu.VMEM((members, 3 * rows, width), f32),
-                pltpu.VMEM((members, var_rows, points), f32),
+                pltpu.VMEM((members, count_vars, points), f32),
                 pltpu.VMEM((1152, width), f32),
             ],
         ),
@@ -346,42 +378,43 @@
             side,
             side,
             side,
-            chunks,
-            chunks,
-        ],
+        ] + [chunks] * 8,
         compiler_params=params(2),
         name="backward",
         interpret=interpret,
     )(me, *slopes, loss, slope, summed, grid_features, edges, before, mesh_features, after, out_weight)
 
+    keep, away = parts[:4], parts[4:]
     core = place["core"]
     first = jnp.where(straight, place["x"], place["y"])
     second = jnp.where(straight, place["y"], place["x"])
-    total = keep + send(away, swap_core)
-    parts = [send(total[4 * k : 4 * k + 4], first_axis[k]) for k in (1, 2, 3)]
+    halves = [keep[k] + send(away[k], swap_core) for k in (1, 2, 3, 0)]
+    parts = [send(half, first_axis[k]) for k, half in zip((1, 2, 3), halves)]
+    grid_grad = jnp.einsum("npu,wu->npw", grad_query, dst_weight, precision=lax.Precision.HIGH)
+    upper, lower, grid_grad = lax.optimization_barrier((upper, lower, grid_grad))
     from_prev = lax.ppermute(upper, "grid", up)
     from_next = lax.ppermute(lower, "grid", down)
-    grid_grad = jnp.einsum("npu,wu->npw", grad_query, dst_weight, precision=lax.Precision.HIGH)
-    *parts, from_prev, from_next, grid_grad = lax.optimization_barrier(
-        (*parts, from_prev, from_next, grid_grad)
-    )
-    total = tree(total[:4], parts)
+    *parts, grid_grad = lax.optimization_barrier((*parts, grid_grad))
+    total = tree(halves[3], parts)
     parts = [send(total[k : k + 1], second_axis[k]) for k in (1, 2, 3)]
+    *parts, from_prev, from_next = lax.optimization_barrier((*parts, from_prev, from_next))
+    total = tree(total[:1], parts)
+    parts = [send(total, along_z[k]) for k in (1, 2, 3)]
     mesh_grad = jnp.einsum(
         "nru,wu->nrw", middle + from_prev + from_next, src_weight, precision=lax.Precision.HIGH
     )
     *parts, mesh_grad = lax.optimization_barrier((*parts, mesh_grad))
-    total = tree(total[:1], parts)
-    total = tree(total, [send(total, along_z[k]) for k in (1, 2, 3)])
+    total = tree(total, parts)
     total = total + send(total, along_z[4])
     total = placed_at(second, total, [send(total, second_axis[k]) for k in (1, 2, 3)])
-    total = placed_at(first, total, [send(total, first_axis[k]) for k in (1, 2, 3)])
-    other = send(total, swap_core).reshape(1152, 256)
-    total = total.reshape(1152, 256)
+    parts = [total] + [send(total, first_axis[k]) for k in (1, 2, 3)]
+    others = [send(part, swap_core) for part in parts]
+    total = placed_at(first, parts[0], parts[1:]).reshape(1152, 256)
+    other = placed_at(second, others[0], others[1:]).reshape(1152, 256)
     whole_sum = jnp.where(
         core == 0, jnp.concatenate([total, other], axis=1), jnp.concatenate([other, total], axis=1)
     )
-    loss = whole_sum[2 * width + var_rows, 0]
+    loss = whole_sum[2 * width + loss_row, 0]
     src_grad = whole_sum[:width]
     dst_grad = whole_sum[width : 2 * width]
     out_grad = whole_sum[2 * width : 2 * width + count_vars].T

time: 135 us -> 126 us (0.933)
  waiting for transfers between devices: 36.6 us -> 29.4 us
  local copies, waits for them, and re-layouts: 9.38 us -> 3.24 us
  starting transfers between devices: 61.1 us -> 65.8 us
    ppermute x18 -> x24, starting transfers between devices: 44.7 us -> 52.2 us  [send(): return lax.ppermute(value, axes, pairs)]
    ppermute x18 -> x24, waiting for transfers between devices: 26.3 us -> 19.1 us  [send(): return lax.ppermute(value, axes, pairs)]
    unnamed x19 -> x14, local copies, waits for them, and re-layouts: 5.33 us -> 0.03 us
    ppermute x1, starting transfers between devices: 4.26 us -> 1.29 us  [body(): from_prev = lax.ppermute(upper, 'grid', up)]
    pallas_call x2, Pallas kernels: 3.41 us -> 6.06 us  [the longest x1 4.86 us: body(): pl.pallas_call(query_kernel, in_specs=[me_spec, whole(), in_hbm, in_hbm,...]
  transfers between devices with their start and end apart: 28 -> 34, of which waited for: 17 -> 15; matrix products, arithmetic and copies ran while one was open for 6% -> 4% of each run, Pallas kernels for 2% -> 4%
where the time goes in v3:
time: 126 us; the launch traced here: 125 us
  starting transfers between devices  65.8 us (52%)
  waiting for transfers between devices  29.4 us (23%)
  Pallas kernels  20.6 us (16%)
  matrix products  4.48 us (4%)
  local copies, waits for them, and re-layouts  3.24 us (3%)
    ppermute x24, starting transfers between devices, send(): return lax.ppermute(value, axes, pairs)  52.2 us
    ppermute x24, waiting for transfers between devices, send(): return lax.ppermute(value, axes, pairs)  19.1 us
    pallas_call x1, Pallas kernels, body(): pl.pallas_call(functools.partial(backward_kernel, tile, scale, loss_scale...  8.61 us
    pallas_call x1, Pallas kernels, body(): pl.pallas_call(functools.partial(forward_kernel, tile), grid_spec=pltpu.P...  5.91 us
    ppermute x3, waiting for transfers between devices, body(): lax.ppermute(parts[k], 'member', to_peer[k])  5.26 us
    ppermute x3, waiting for transfers between devices, body(): lax.ppermute(slopes[k], 'member', to_peer[k])  5.05 us
    pallas_call x1, Pallas kernels, body(): pl.pallas_call(query_kernel, in_specs=[me_spec, whole(), in_hbm, in_hbm,...  4.86 us
    ppermute x1, starting transfers between devices, body(): before = lax.ppermute(mesh_features, 'grid', up)  3.95 us
  transfers between devices with their start and end apart: 34, of which 15 were waited for; matrix products, arithmetic and copies ran while one was open for 4% of the time, Pallas kernels for 4%

profile of v3, /device:TPU:1, one launch (start us, length us, event | category | flops | bytes accessed | tf_op | source)
XLA Modules:
  0.0 125.2 jit_solution(8774049434877133539)
XLA Ops:
  0.6 4.0 %collective-permute-start = (f32[2,32,512]{2,1,0:T(8,128)}, f32[2,32,512]{2,1,0:T(8,128)S(1)}, u32[]{:S(2)}, u32[]{:S(2)}) collective-permute-start(f32[2,32,512]{2,1,0:T(8,128)} %own.3), channel_id=1, source_target_pairs={{0,1},{1,2},{2,3},{3,4},{4,5},{5,6},{6,7},{7,8},{8,9},{9,10},{10,1... | collective-permute-start | bytes 393224 | tf_op jit(solution)/shard_map/ppermute | solution.py:269
  4.6 1.3 %collective-permute-start.1 = (f32[2,32,512]{2,1,0:T(8,128)}, f32[2,32,512]{2,1,0:T(8,128)S(1)}, u32[]{:S(2)}, u32[]{:S(2)}) collective-permute-start(f32[2,32,512]{2,1,0:T(8,128)} %own.3), channel_id=1, source_target_pairs={{1,0},{2,1},{3,2},{4,3},{5,4},{6,5},{7,6},{8,7},{9,8},{10,9},{11,1... | collective-permute-start | bytes 393224 | tf_op jit(solution)/shard_map/ppermute | solution.py:270
  6.0 4.9 %query.1 = (f32[2,512,512]{2,1,0:T(8,128)S(1)}, s32[512,8]{1,0:T(8,128)S(1)}, bf16[512,512]{1,0:T(8,128)(2,1)S(1)}, bf16[512,512]{1,0:T(8,128)(2,1)S(1)}) custom-call(s32[5]{0:T(128)S(1)} %stack.23.me, s32[4,512]{1,0:T(4,128)} %edges.3, f32[2,512,512]{2,1,0:T(8,128)} %features.3, f32[512,512]{1,0:T(8,128)} %weight.1, f32[512,512]{1,0:T(8,128)} %src_weight.1), custom_call_target="tpu_custom_call" | custom-call | tf_op jit(solution)/shard_map/query/pallas_call | solution.py:274
  10.9 5.9 %forward.1 = (f32[2,4,512,512]{3,2,1,0:T(8,128)S(1)}, f32[2,512,512]{2,1,0:T(8,128)S(1)}, f32[2,100,128]{2,1,0:T(8,128)S(1)}, f32[2,100,128]{2,1,0:T(8,128)S(1)}...) custom-call(s32[5]{0:T(128)S(1)} %stack.23.me, f32[2,512,512]{2,1,0:T(8,128)S(1)} %get-tuple-element.49.query, ...), custom_call_target="tpu_custom_call" | custom-call | tf_op jit(solution)/shard_map/forward/pallas_call | solution.py:303
  16.9 1.8 %collective-permute-start.2 = (f32[2,100,128]{2,1,0:T(8,128)S(1)}, f32[2,100,128]{2,1,0:T(8,128)S(1)}, u32[]{:S(2)}, u32[]{:S(2)}) collective-permute-start(f32[2,100,128]{2,1,0:T(8,128)S(1)} %get-tuple-element.54), channel_id=1, source_target_pairs={{0,64},{64,0},{128,192},{192,128},{1,65},{65,1},{129,193},{193,129... | collective-permute-start | bytes 307208 | tf_op jit(solution)/shard_map/ppermute | solution.py:332
  18.6 1.3 %collective-permute-start.3 = (f32[2,100,128]{2,1,0:T(8,128)S(1)}, f32[2,100,128]{2,1,0:T(8,128)S(1)}, u32[]{:S(2)}, u32[]{:S(2)}) collective-permute-start(f32[2,100,128]{2,1,0:T(8,128)S(1)} %get-tuple-element.55), channel_id=1, source_target_pairs={{0,128},{64,192},{128,0},{192,64},{1,129},{65,193},{129,1},{193,65... | collective-permute-start | bytes 307208 | tf_op jit(solution)/shard_map/ppermute | solution.py:332
  20.0 0.4 collective-permute-start.4
  20.4 2.8 %collective-permute-done.3.part2 = f32[2,100,128]{2,1,0:T(8,128)S(1)} collective-permute-done((f32[2,100,128]{2,1,0:T(8,128)S(1)}, f32[2,100,128]{2,1,0:T(8,128)S(1)}, u32[]{:S(2)}, u32[]{:S(2)}) %collective-permute-start.3) | collective-permute-done | bytes 102432 | tf_op jit(solution)/shard_map/ppermute | solution.py:332
  23.2 2.5 %collective-permute-done.4.part3 = f32[2,100,128]{2,1,0:T(8,128)S(1)} collective-permute-done((f32[2,100,128]{2,1,0:T(8,128)S(1)}, f32[2,100,128]{2,1,0:T(8,128)S(1)}, u32[]{:S(2)}, u32[]{:S(2)}) %collective-permute-start.4) | collective-permute-done | bytes 102432 | tf_op jit(solution)/shard_map/ppermute | solution.py:332
  25.7 1.2 score.1
  27.2 1.3 %collective-permute-start.6 = (f32[2,100,128]{2,1,0:T(8,128)S(1)}, f32[2,100,128]{2,1,0:T(8,128)S(1)}, u32[]{:S(2)}, u32[]{:S(2)}) collective-permute-start(f32[2,100,128]{2,1,0:T(8,128)S(1)} %get-tuple-element.59), channel_id=1, source_target_pairs={{0,128},{64,192},{128,0},{192,64},{1,129},{65,193},{129,1},{193,65... | collective-permute-start | bytes 307208 | tf_op jit(solution)/shard_map/ppermute | solution.py:346
  28.5 0.6 collective-permute-start.7
  29.1 2.3 %collective-permute-done.6.part2 = f32[2,100,128]{2,1,0:T(8,128)S(1)} collective-permute-done((f32[2,100,128]{2,1,0:T(8,128)S(1)}, f32[2,100,128]{2,1,0:T(8,128)S(1)}, u32[]{:S(2)}, u32[]{:S(2)}) %collective-permute-start.6) | collective-permute-done | bytes 102432 | tf_op jit(solution)/shard_map/ppermute | solution.py:346
  31.4 2.7 %collective-permute-done.7.part3 = f32[2,100,128]{2,1,0:T(8,128)S(1)} collective-permute-done((f32[2,100,128]{2,1,0:T(8,128)S(1)}, f32[2,100,128]{2,1,0:T(8,128)S(1)}, u32[]{:S(2)}, u32[]{:S(2)}) %collective-permute-start.7) | collective-permute-done | bytes 102432 | tf_op jit(solution)/shard_map/ppermute | solution.py:346
  34.1 8.6 %backward.1 = (f32[2,512,512]{2,1,0:T(8,128)S(1)}, f32[2,32,512]{2,1,0:T(8,128)S(1)}, f32[2,32,512]{2,1,0:T(8,128)S(1)}, f32[2,32,512]{2,1,0:T(8,128)S(1)}, f32[...) custom-call(s32[5]{0:T(128)S(1)} %stack.23.me, ...), custom_call_target="tpu_custom_call" | custom-call | tf_op jit(solution)/shard_map/backward/pallas_call | solution.py:354
  43.0 0.3 collective-permute-start.11
  43.9 0.6 collective-permute-done.13
  44.5 9.9 %collective-permute-start.14 = (f32[4,72,256]{2,1,0:T(8,128)S(1)}, f32[4,72,256]{2,1,0:T(8,128)S(1)}, u32[]{:S(2)}, u32[]{:S(2)}) collective-permute-start(f32[4,72,256]{2,1,0:T(8,128)S(1)} %add.95), channel_id=1, source_target_pairs={{0,3},{1,2},{2,1},{3,0},{4,7},{5,6},{6,5},{7,4},{8,11},{9,10},{10,... | collective-permute-start | bytes 884744 | tf_op jit(solution)/shard_map/ppermute | solution.py:53
  54.8 0.8 collective-permute-start.10
  55.5 3.2 %fusion.2 = f32[2,512,512]{2,1,0:T(8,128)} fusion(f32[2,512,512]{2,1,0:T(8,128)S(1)} %get-tuple-element.74, f32[512,512]{1,0:T(8,128)S(1)} %copy-done.5), kind=kOutput, calls=%fused_computation.3 | convolution fusion | flops 1610612736 | bytes 5242880 | tf_op jit(solution)/shard_map/npu,wu->npw/dot_general | solution.py:393
  58.7 1.3 %collective-permute-start.18 = (f32[2,32,512]{2,1,0:T(8,128)S(1)}, f32[2,32,512]{2,1,0:T(8,128)S(1)}, u32[]{:S(2)}, u32[]{:S(2)}) collective-permute-start(f32[2,32,512]{2,1,0:T(8,128)S(1)} %get-tuple-element.79), channel_id=1, source_target_pairs={{0,1},{1,2},{2,3},{3,4},{4,5},{5,6},{6,7},{7,8},{8,9},{9,10},{10,1... | collective-permute-start | bytes 393224 | tf_op jit(solution)/shard_map/ppermute | solution.py:395
  60.0 1.2 collective-permute-done.14
  61.2 1.3 %collective-permute-start.19 = (f32[2,32,512]{2,1,0:T(8,128)S(1)}, f32[2,32,512]{2,1,0:T(8,128)S(1)}, u32[]{:S(2)}, u32[]{:S(2)}) collective-permute-start(f32[2,32,512]{2,1,0:T(8,128)S(1)} %get-tuple-element.80), channel_id=1, source_target_pairs={{1,0},{2,1},{3,2},{4,3},{5,4},{6,5},{7,6},{8,7},{9,8},{10,9},{11,1... | collective-permute-start | bytes 393224 | tf_op jit(solution)/shard_map/ppermute | solution.py:396
  62.5 0.9 collective-permute-done.10
  63.6 1.3 %collective-permute-start.15 = (f32[1,72,256]{2,1,0:T(8,128)S(1)}, f32[1,72,256]{2,1,0:T(8,128)S(1)}, u32[]{:S(2)}, u32[]{:S(2)}) collective-permute-start(f32[1,72,256]{2,1,0:T(8,128)S(1)} %get-tuple-element.98), channel_id=1, source_target_pairs={{0,128},{1,129},{2,130},{3,131},{4,132},{5,133},{6,134},{7,135},{8... | collective-permute-start | bytes 221192 | tf_op jit(solution)/shard_map/ppermute | solution.py:53
  64.9 2.7 %collective-permute-start.17 = (f32[1,72,256]{2,1,0:T(8,128)S(1)}, f32[1,72,256]{2,1,0:T(8,128)S(1)}, u32[]{:S(2)}, u32[]{:S(2)}) collective-permute-start(f32[1,72,256]{2,1,0:T(8,128)S(1)} %get-tuple-element.96), channel_id=1, source_target_pairs={{0,160},{1,161},{2,162},{3,163},{4,164},{5,165},{6,166},{7,167},{8... | collective-permute-start | bytes 221192 | tf_op jit(solution)/shard_map/ppermute | solution.py:53
  67.7 2.7 %collective-permute-done.16 = f32[1,72,256]{2,1,0:T(8,128)S(1)} collective-permute-done((f32[1,72,256]{2,1,0:T(8,128)S(1)}, f32[1,72,256]{2,1,0:T(8,128)S(1)}, u32[]{:S(2)}, u32[]{:S(2)}) %collective-permute-start.16) | collective-permute-done | bytes 73760 | tf_op jit(solution)/shard_map/ppermute | solution.py:53
  70.5 2.3 %collective-permute-done.17 = f32[1,72,256]{2,1,0:T(8,128)S(1)} collective-permute-done((f32[1,72,256]{2,1,0:T(8,128)S(1)}, f32[1,72,256]{2,1,0:T(8,128)S(1)}, u32[]{:S(2)}, u32[]{:S(2)}) %collective-permute-start.17) | collective-permute-done | bytes 73760 | tf_op jit(solution)/shard_map/ppermute | solution.py:53
  72.9 2.2 %collective-permute-start.21 = (f32[1,72,256]{2,1,0:T(8,128)S(1)}, f32[1,72,256]{2,1,0:T(8,128)S(1)}, u32[]{:S(2)}, u32[]{:S(2)}) collective-permute-start(f32[1,72,256]{2,1,0:T(8,128)S(1)} %fusion.6), channel_id=1, source_target_pairs={{0,8},{1,9},{2,10},{3,11},{4,12},{5,13},{6,14},{7,15},{8,0},{9,1},... | collective-permute-start | bytes 221192 | tf_op jit(solution)/shard_map/ppermute | solution.py:53
  75.0 1.4 %collective-permute-start.22 = (f32[1,72,256]{2,1,0:T(8,128)S(1)}, f32[1,72,256]{2,1,0:T(8,128)S(1)}, u32[]{:S(2)}, u32[]{:S(2)}) collective-permute-start(f32[1,72,256]{2,1,0:T(8,128)S(1)} %fusion.6), channel_id=1, source_target_pairs={{0,12},{1,13},{2,14},{3,15},{4,8},{5,9},{6,10},{7,11},{8,4},{9,5},... | collective-permute-start | bytes 221192 | tf_op jit(solution)/shard_map/ppermute | solution.py:53
  76.4 1.3 %fusion = f32[2,32,512]{2,1,0:T(8,128)} fusion(f32[512,512]{1,0:T(8,128)S(1)} %copy-done.6, f32[2,32,512]{2,1,0:T(8,128)S(1)} %collective-permute-done.19, f32[2,32,512]{2,1,0:T(8,128)S(1)} %get-tuple-element.84, f32[2,32,512]{2,1,0:T(8,128)S(1)} %collective-permute-done.18), kind=kOutput, calls=%fused_computation.1 | convolution fusion | flops 100728832 | bytes 1572864 | tf_op jit(solution)/shard_map/nru,wu->nrw/dot_general | solution.py:403
  77.7 2.3 %collective-permute-done.22 = f32[1,72,256]{2,1,0:T(8,128)S(1)} collective-permute-done((f32[1,72,256]{2,1,0:T(8,128)S(1)}, f32[1,72,256]{2,1,0:T(8,128)S(1)}, u32[]{:S(2)}, u32[]{:S(2)}) %collective-permute-start.22) | collective-permute-done | bytes 73760 | tf_op jit(solution)/shard_map/ppermute | solution.py:53
  80.1 4.0 %collective-permute-start.23 = (f32[1,72,256]{2,1,0:T(8,128)S(1)}, f32[1,72,256]{2,1,0:T(8,128)S(1)}, u32[]{:S(2)}, u32[]{:S(2)}) collective-permute-start(f32[1,72,256]{2,1,0:T(8,128)S(1)} %add_add_fusion.1), channel_id=1, source_target_pairs={{0,16},{1,17},{2,18},{3,19},{4,20},{5,21},{6,22},{7,23},{8,24},{9,... | collective-permute-start | bytes 221192 | tf_op jit(solution)/shard_map/ppermute | solution.py:53
  84.0 3.3 %collective-permute-done.23 = f32[1,72,256]{2,1,0:T(8,128)S(1)} collective-permute-done((f32[1,72,256]{2,1,0:T(8,128)S(1)}, f32[1,72,256]{2,1,0:T(8,128)S(1)}, u32[]{:S(2)}, u32[]{:S(2)}) %collective-permute-start.23) | collective-permute-done | bytes 73760 | tf_op jit(solution)/shard_map/ppermute | solution.py:53
  87.4 1.0 collective-permute-start.24
  88.4 4.0 %collective-permute-start.25 = (f32[1,72,256]{2,1,0:T(8,128)S(1)}, f32[1,72,256]{2,1,0:T(8,128)S(1)}, u32[]{:S(2)}, u32[]{:S(2)}) collective-permute-start(f32[1,72,256]{2,1,0:T(8,128)S(1)} %get-tuple-element.93), channel_id=1, source_target_pairs={{0,32},{1,33},{2,34},{3,35},{4,36},{5,37},{6,38},{7,39},{8,40},{9,... | collective-permute-start | bytes 221192 | tf_op jit(solution)/shard_map/ppermute | solution.py:53
  92.4 2.5 %collective-permute-done.25 = f32[1,72,256]{2,1,0:T(8,128)S(1)} collective-permute-done((f32[1,72,256]{2,1,0:T(8,128)S(1)}, f32[1,72,256]{2,1,0:T(8,128)S(1)}, u32[]{:S(2)}, u32[]{:S(2)}) %collective-permute-start.25) | collective-permute-done | bytes 73760 | tf_op jit(solution)/shard_map/ppermute | solution.py:53
  94.9 2.2 %collective-permute-done.26 = f32[1,72,256]{2,1,0:T(8,128)S(1)} collective-permute-done((f32[1,72,256]{2,1,0:T(8,128)S(1)}, f32[1,72,256]{2,1,0:T(8,128)S(1)}, u32[]{:S(2)}, u32[]{:S(2)}) %collective-permute-start.26) | collective-permute-done | bytes 73760 | tf_op jit(solution)/shard_map/ppermute | solution.py:53
  97.2 6.3 %collective-permute-start.28 = (f32[4,72,256]{2,1,0:T(8,128)S(1)}, f32[4,72,256]{2,1,0:T(8,128)S(1)}, u32[]{:S(2)}, u32[]{:S(2)}) collective-permute-start(f32[4,72,256]{2,1,0:T(8,128)S(1)} %constant_dynamic-update-slice_fusion.8), channel_id=1, source_target_pairs={{0,2},{1,3},{2,0},{3,1},{4,6},{5,7},{6,4},{7,5},{8,10},{9,11},{10,... | collective-permute-start | bytes 884744 | tf_op jit(solution)/shard_map/ppermute | solution.py:53
  103.5 10.0 %collective-permute-start.30 = (f32[4,72,256]{2,1,0:T(8,128)S(1)}, f32[4,72,256]{2,1,0:T(8,128)S(1)}, u32[]{:S(2)}, u32[]{:S(2)}) collective-permute-start(f32[4,72,256]{2,1,0:T(8,128)S(1)} %constant_dynamic-update-slice_fusion.8), channel_id=1, source_target_pairs={{0,64},{1,65},{2,66},{3,67},{4,68},{5,69},{6,70},{7,71},{8,72},{9,... | collective-permute-start | bytes 884744 | tf_op jit(solution)/shard_map/ppermute | solution.py:53
  113.7 1.9 %collective-permute-start.31 = (f32[4,72,256]{2,1,0:T(8,128)S(1)}, f32[4,72,256]{2,1,0:T(8,128)S(1)}, u32[]{:S(2)}, u32[]{:S(2)}) collective-permute-start(f32[4,72,256]{2,1,0:T(8,128)S(1)} %collective-permute-done.27), channel_id=1, source_target_pairs={{0,64},{1,65},{2,66},{3,67},{4,68},{5,69},{6,70},{7,71},{8,72},{9,... | collective-permute-start | bytes 884744 | tf_op jit(solution)/shard_map/ppermute | solution.py:53
  115.6 1.9 %collective-permute-start.32 = (f32[4,72,256]{2,1,0:T(8,128)S(1)}, f32[4,72,256]{2,1,0:T(8,128)S(1)}, u32[]{:S(2)}, u32[]{:S(2)}) collective-permute-start(f32[4,72,256]{2,1,0:T(8,128)S(1)} %collective-permute-done.28), channel_id=1, source_target_pairs={{0,64},{1,65},{2,66},{3,67},{4,68},{5,69},{6,70},{7,71},{8,72},{9,... | collective-permute-start | bytes 884744 | tf_op jit(solution)/shard_map/ppermute | solution.py:53
  117.5 3.4 %collective-permute-start.33 = (f32[4,72,256]{2,1,0:T(8,128)S(1)}, f32[4,72,256]{2,1,0:T(8,128)S(1)}, u32[]{:S(2)}, u32[]{:S(2)}) collective-permute-start(f32[4,72,256]{2,1,0:T(8,128)S(1)} %collective-permute-done.29), channel_id=1, source_target_pairs={{0,64},{1,65},{2,66},{3,67},{4,68},{5,69},{6,70},{7,71},{8,72},{9,... | collective-permute-start | bytes 884744 | tf_op jit(solution)/shard_map/ppermute | solution.py:53
  121.2 0.9 collective-permute-done.33
  122.1 0.4 maximum_select_fusion
  122.5 1.5 %fusion.7 = (f32[512,512]{1,0:T(8,128)}, f32[512,512]{1,0:T(8,128)}) fusion(f32[1152,512]{1,0:T(8,128)S(1)} %maximum_select_fusion), kind=kLoop, calls=%fused_computation.24 | loop fusion | bytes 4194304 | tf_op jit(solution)/shard_map/slice | solution.py:419
  123.9 0.7 slice_bitcast_fusion
  124.6 0.5 slice.36
  (67 shorter events, 2.6 us)
Async XLA Ops:
  0.6 10.2 %collective-permute-start = (f32[2,32,512]{2,1,0:T(8,128)}, f32[2,32,512]{2,1,0:T(8,128)S(1)}, u32[]{:S(2)}, u32[]{:S(2)}) collective-permute-start(f32[2,32,512]{2,1,0:T(8,128)} %own.3), channel_id=1, source_target_pairs={{0,1},{1,2},{2,3},{3,4},{4,5},{5,6},{6,7},{7,8},{8,9},{9,10},{10,1... | collective-permute-start | bytes 393224 | tf_op jit(solution)/shard_map/ppermute | solution.py:269
  4.6 6.3 %collective-permute-start.1 = (f32[2,32,512]{2,1,0:T(8,128)}, f32[2,32,512]{2,1,0:T(8,128)S(1)}, u32[]{:S(2)}, u32[]{:S(2)}) collective-permute-start(f32[2,32,512]{2,1,0:T(8,128)} %own.3), channel_id=1, source_target_pairs={{1,0},{2,1},{3,2},{4,3},{5,4},{6,5},{7,6},{8,7},{9,8},{10,9},{11,1... | collective-permute-start | bytes 393224 | tf_op jit(solution)/shard_map/ppermute | solution.py:270
  6.0 4.9 %copy-start.1 = (f32[512,100]{0,1:T(8,128)S(1)}, f32[512,100]{0,1:T(8,128)}, u32[]{:S(2)}) copy-start(f32[512,100]{0,1:T(8,128)} %param.13) | copy-start | bytes 614404
  6.0 4.9 %copy-start.2 = (f32[2,32,512]{2,1,0:T(8,128)S(1)}, f32[2,32,512]{2,1,0:T(8,128)}, u32[]{:S(2)}) copy-start(f32[2,32,512]{2,1,0:T(8,128)} %own.3) | copy-start | bytes 393220
  10.9 14.7 %copy-start.3 = (f32[100,512]{1,0:T(8,128)S(1)}, f32[100,512]{1,0:T(8,128)}, u32[]{:S(2)}) copy-start(f32[100,512]{1,0:T(8,128)} %targets.1) | copy-start | bytes 614404
  10.9 23.2 %copy-start = (f32[2,512,512]{2,1,0:T(8,128)S(1)}, f32[2,512,512]{2,1,0:T(8,128)}, u32[]{:S(2)}) copy-start(f32[2,512,512]{2,1,0:T(8,128)} %features.3) | copy-start | bytes 6291460
  10.9 23.2 %copy-start.4 = (s32[4,512]{1,0:T(4,128)S(1)}, s32[4,512]{1,0:T(4,128)}, u32[]{:S(2)}) copy-start(s32[4,512]{1,0:T(4,128)} %edges.3) | copy-start | bytes 24580
  16.9 3.5 %collective-permute-start.2 = (f32[2,100,128]{2,1,0:T(8,128)S(1)}, f32[2,100,128]{2,1,0:T(8,128)S(1)}, u32[]{:S(2)}, u32[]{:S(2)}) collective-permute-start(f32[2,100,128]{2,1,0:T(8,128)S(1)} %get-tuple-element.54), channel_id=1, source_target_pairs={{0,64},{64,0},{128,192},{192,128},{1,65},{65,1},{129,193},{193,129... | collective-permute-start | bytes 307208 | tf_op jit(solution)/shard_map/ppermute | solution.py:332
  18.6 4.5 %collective-permute-start.3 = (f32[2,100,128]{2,1,0:T(8,128)S(1)}, f32[2,100,128]{2,1,0:T(8,128)S(1)}, u32[]{:S(2)}, u32[]{:S(2)}) collective-permute-start(f32[2,100,128]{2,1,0:T(8,128)S(1)} %get-tuple-element.55), channel_id=1, source_target_pairs={{0,128},{64,192},{128,0},{192,64},{1,129},{65,193},{129,1},{193,65... | collective-permute-start | bytes 307208 | tf_op jit(solution)/shard_map/ppermute | solution.py:332
  20.0 5.7 %collective-permute-start.4 = (f32[2,100,128]{2,1,0:T(8,128)S(1)}, f32[2,100,128]{2,1,0:T(8,128)S(1)}, u32[]{:S(2)}, u32[]{:S(2)}) collective-permute-start(f32[2,100,128]{2,1,0:T(8,128)S(1)} %get-tuple-element.56), channel_id=1, source_target_pairs={{0,192},{64,128},{128,64},{192,0},{1,193},{65,129},{129,65},{193,1... | collective-permute-start | bytes 307208 | tf_op jit(solution)/shard_map/ppermute | solution.py:332
  26.9 2.2 %collective-permute-start.5 = (f32[2,100,128]{2,1,0:T(8,128)S(1)}, f32[2,100,128]{2,1,0:T(8,128)S(1)}, u32[]{:S(2)}, u32[]{:S(2)}) collective-permute-start(f32[2,100,128]{2,1,0:T(8,128)S(1)} %get-tuple-element.58), channel_id=1, source_target_pairs={{0,64},{64,0},{128,192},{192,128},{1,65},{65,1},{129,193},{193,129... | collective-permute-start | bytes 307208 | tf_op jit(solution)/shard_map/ppermute | solution.py:346
  27.2 4.3 %collective-permute-start.6 = (f32[2,100,128]{2,1,0:T(8,128)S(1)}, f32[2,100,128]{2,1,0:T(8,128)S(1)}, u32[]{:S(2)}, u32[]{:S(2)}) collective-permute-start(f32[2,100,128]{2,1,0:T(8,128)S(1)} %get-tuple-element.59), channel_id=1, source_target_pairs={{0,128},{64,192},{128,0},{192,64},{1,129},{65,193},{129,1},{193,65... | collective-permute-start | bytes 307208 | tf_op jit(solution)/shard_map/ppermute | solution.py:346
  28.5 5.7 %collective-permute-start.7 = (f32[2,100,128]{2,1,0:T(8,128)S(1)}, f32[2,100,128]{2,1,0:T(8,128)S(1)}, u32[]{:S(2)}, u32[]{:S(2)}) collective-permute-start(f32[2,100,128]{2,1,0:T(8,128)S(1)} %get-tuple-element.60), channel_id=1, source_target_pairs={{0,192},{64,128},{128,64},{192,0},{1,193},{65,129},{129,65},{193,1... | collective-permute-start | bytes 307208 | tf_op jit(solution)/shard_map/ppermute | solution.py:346
  42.8 1.7 %collective-permute-start.13 = (f32[4,72,256]{2,1,0:T(8,128)S(1)}, f32[4,72,256]{2,1,0:T(8,128)S(1)}, u32[]{:S(2)}, u32[]{:S(2)}) collective-permute-start(f32[4,72,256]{2,1,0:T(8,128)S(1)} %get-tuple-element.71), channel_id=1, source_target_pairs={{0,64},{1,65},{2,66},{3,67},{4,68},{5,69},{6,70},{7,71},{8,72},{9,... | collective-permute-start | bytes 884744 | tf_op jit(solution)/shard_map/ppermute | solution.py:53
  43.0 11.4 %collective-permute-start.11 = (f32[4,72,256]{2,1,0:T(8,128)S(1)}, f32[4,72,256]{2,1,0:T(8,128)S(1)}, u32[]{:S(2)}, u32[]{:S(2)}) collective-permute-start(f32[4,72,256]{2,1,0:T(8,128)S(1)} %get-tuple-element.69), channel_id=1, source_target_pairs={{0,64},{1,65},{2,66},{3,67},{4,68},{5,69},{6,70},{7,71},{8,72},{9,... | collective-permute-start | bytes 884744 | tf_op jit(solution)/shard_map/ppermute | solution.py:53
  43.4 11.4 %collective-permute-start.9 = (f32[4,72,256]{2,1,0:T(8,128)S(1)}, f32[4,72,256]{2,1,0:T(8,128)S(1)}, u32[]{:S(2)}, u32[]{:S(2)}) collective-permute-start(f32[4,72,256]{2,1,0:T(8,128)S(1)} %get-tuple-element.67), channel_id=1, source_target_pairs={{0,64},{1,65},{2,66},{3,67},{4,68},{5,69},{6,70},{7,71},{8,72},{9,... | collective-permute-start | bytes 884744 | tf_op jit(solution)/shard_map/ppermute | solution.py:53
  43.6 19.8 %collective-permute-start.8 = (f32[4,72,256]{2,1,0:T(8,128)S(1)}, f32[4,72,256]{2,1,0:T(8,128)S(1)}, u32[]{:S(2)}, u32[]{:S(2)}) collective-permute-start(f32[4,72,256]{2,1,0:T(8,128)S(1)} %get-tuple-element.65), channel_id=1, source_target_pairs={{0,64},{1,65},{2,66},{3,67},{4,68},{5,69},{6,70},{7,71},{8,72},{9,... | collective-permute-start | bytes 884744 | tf_op jit(solution)/shard_map/ppermute | solution.py:53
  44.4 11.1 %copy-start.5 = (f32[512,512]{1,0:T(8,128)S(1)}, f32[512,512]{1,0:T(8,128)}, u32[]{:S(2)}) copy-start(f32[512,512]{1,0:T(8,128)} %weight.1) | copy-start | bytes 3145732
  44.5 16.8 %collective-permute-start.14 = (f32[4,72,256]{2,1,0:T(8,128)S(1)}, f32[4,72,256]{2,1,0:T(8,128)S(1)}, u32[]{:S(2)}, u32[]{:S(2)}) collective-permute-start(f32[4,72,256]{2,1,0:T(8,128)S(1)} %add.95), channel_id=1, source_target_pairs={{0,3},{1,2},{2,1},{3,0},{4,7},{5,6},{6,5},{7,4},{8,11},{9,10},{10,... | collective-permute-start | bytes 884744 | tf_op jit(solution)/shard_map/ppermute | solution.py:53
  54.5 8.1 %collective-permute-start.12 = (f32[4,72,256]{2,1,0:T(8,128)S(1)}, f32[4,72,256]{2,1,0:T(8,128)S(1)}, u32[]{:S(2)}, u32[]{:S(2)}) collective-permute-start(f32[4,72,256]{2,1,0:T(8,128)S(1)} %add.94), channel_id=1, source_target_pairs={{0,2},{1,3},{2,0},{3,1},{4,6},{5,7},{6,4},{7,5},{8,10},{9,11},{10,... | collective-permute-start | bytes 884744 | tf_op jit(solution)/shard_map/ppermute | solution.py:53
  54.8 8.7 %collective-permute-start.10 = (f32[4,72,256]{2,1,0:T(8,128)S(1)}, f32[4,72,256]{2,1,0:T(8,128)S(1)}, u32[]{:S(2)}, u32[]{:S(2)}) collective-permute-start(f32[4,72,256]{2,1,0:T(8,128)S(1)} %add.93), channel_id=1, source_target_pairs={{0,1},{1,0},{2,3},{3,2},{4,5},{5,4},{6,7},{7,6},{8,9},{9,8},{10,11... | collective-permute-start | bytes 884744 | tf_op jit(solution)/shard_map/ppermute | solution.py:53
  58.7 8.8 %collective-permute-start.18 = (f32[2,32,512]{2,1,0:T(8,128)S(1)}, f32[2,32,512]{2,1,0:T(8,128)S(1)}, u32[]{:S(2)}, u32[]{:S(2)}) collective-permute-start(f32[2,32,512]{2,1,0:T(8,128)S(1)} %get-tuple-element.79), channel_id=1, source_target_pairs={{0,1},{1,2},{2,3},{3,4},{4,5},{5,6},{6,7},{7,8},{8,9},{9,10},{10,1... | collective-permute-start | bytes 393224 | tf_op jit(solution)/shard_map/ppermute | solution.py:395
  61.2 6.3 %collective-permute-start.19 = (f32[2,32,512]{2,1,0:T(8,128)S(1)}, f32[2,32,512]{2,1,0:T(8,128)S(1)}, u32[]{:S(2)}, u32[]{:S(2)}) collective-permute-start(f32[2,32,512]{2,1,0:T(8,128)S(1)} %get-tuple-element.80), channel_id=1, source_target_pairs={{1,0},{2,1},{3,2},{4,3},{5,4},{6,5},{7,6},{8,7},{9,8},{10,9},{11,1... | collective-permute-start | bytes 393224 | tf_op jit(solution)/shard_map/ppermute | solution.py:396
  63.5 12.9 %copy-start.6 = (f32[512,512]{1,0:T(8,128)S(1)}, f32[512,512]{1,0:T(8,128)}, u32[]{:S(2)}) copy-start(f32[512,512]{1,0:T(8,128)} %src_weight.1) | copy-start | bytes 3145732
  63.6 4.1 %collective-permute-start.15 = (f32[1,72,256]{2,1,0:T(8,128)S(1)}, f32[1,72,256]{2,1,0:T(8,128)S(1)}, u32[]{:S(2)}, u32[]{:S(2)}) collective-permute-start(f32[1,72,256]{2,1,0:T(8,128)S(1)} %get-tuple-element.98), channel_id=1, source_target_pairs={{0,128},{1,129},{2,130},{3,131},{4,132},{5,133},{6,134},{7,135},{8... | collective-permute-start | bytes 221192 | tf_op jit(solution)/shard_map/ppermute | solution.py:53
  64.9 5.6 %collective-permute-start.16 = (f32[1,72,256]{2,1,0:T(8,128)S(1)}, f32[1,72,256]{2,1,0:T(8,128)S(1)}, u32[]{:S(2)}, u32[]{:S(2)}) collective-permute-start(f32[1,72,256]{2,1,0:T(8,128)S(1)} %get-tuple-element.97), channel_id=1, source_target_pairs={{0,32},{1,33},{2,34},{3,35},{4,36},{5,37},{6,38},{7,39},{8,40},{9,... | collective-permute-start | bytes 221192 | tf_op jit(solution)/shard_map/ppermute | solution.py:53
  64.9 7.9 %collective-permute-start.17 = (f32[1,72,256]{2,1,0:T(8,128)S(1)}, f32[1,72,256]{2,1,0:T(8,128)S(1)}, u32[]{:S(2)}, u32[]{:S(2)}) collective-permute-start(f32[1,72,256]{2,1,0:T(8,128)S(1)} %get-tuple-element.96), channel_id=1, source_target_pairs={{0,160},{1,161},{2,162},{3,163},{4,164},{5,165},{6,166},{7,167},{8... | collective-permute-start | bytes 221192 | tf_op jit(solution)/shard_map/ppermute | solution.py:53
  72.8 4.9 %collective-permute-start.20 = (f32[1,72,256]{2,1,0:T(8,128)S(1)}, f32[1,72,256]{2,1,0:T(8,128)S(1)}, u32[]{:S(2)}, u32[]{:S(2)}) collective-permute-start(f32[1,72,256]{2,1,0:T(8,128)S(1)} %fusion.6), channel_id=1, source_target_pairs={{0,4},{1,5},{2,6},{3,7},{4,0},{5,1},{6,2},{7,3},{8,12},{9,13},{10,... | collective-permute-start | bytes 221192 | tf_op jit(solution)/shard_map/ppermute | solution.py:53
  72.9 4.8 %collective-permute-start.21 = (f32[1,72,256]{2,1,0:T(8,128)S(1)}, f32[1,72,256]{2,1,0:T(8,128)S(1)}, u32[]{:S(2)}, u32[]{:S(2)}) collective-permute-start(f32[1,72,256]{2,1,0:T(8,128)S(1)} %fusion.6), channel_id=1, source_target_pairs={{0,8},{1,9},{2,10},{3,11},{4,12},{5,13},{6,14},{7,15},{8,0},{9,1},... | collective-permute-start | bytes 221192 | tf_op jit(solution)/shard_map/ppermute | solution.py:53
  75.0 5.0 %collective-permute-start.22 = (f32[1,72,256]{2,1,0:T(8,128)S(1)}, f32[1,72,256]{2,1,0:T(8,128)S(1)}, u32[]{:S(2)}, u32[]{:S(2)}) collective-permute-start(f32[1,72,256]{2,1,0:T(8,128)S(1)} %fusion.6), channel_id=1, source_target_pairs={{0,12},{1,13},{2,14},{3,15},{4,8},{5,9},{6,10},{7,11},{8,4},{9,5},... | collective-permute-start | bytes 221192 | tf_op jit(solution)/shard_map/ppermute | solution.py:53
  80.1 7.3 %collective-permute-start.23 = (f32[1,72,256]{2,1,0:T(8,128)S(1)}, f32[1,72,256]{2,1,0:T(8,128)S(1)}, u32[]{:S(2)}, u32[]{:S(2)}) collective-permute-start(f32[1,72,256]{2,1,0:T(8,128)S(1)} %add_add_fusion.1), channel_id=1, source_target_pairs={{0,16},{1,17},{2,18},{3,19},{4,20},{5,21},{6,22},{7,23},{8,24},{9,... | collective-permute-start | bytes 221192 | tf_op jit(solution)/shard_map/ppermute | solution.py:53
  87.4 5.0 %collective-permute-start.24 = (f32[1,72,256]{2,1,0:T(8,128)S(1)}, f32[1,72,256]{2,1,0:T(8,128)S(1)}, u32[]{:S(2)}, u32[]{:S(2)}) collective-permute-start(f32[1,72,256]{2,1,0:T(8,128)S(1)} %get-tuple-element.93), channel_id=1, source_target_pairs={{0,128},{1,129},{2,130},{3,131},{4,132},{5,133},{6,134},{7,135},{8... | collective-permute-start | bytes 221192 | tf_op jit(solution)/shard_map/ppermute | solution.py:53
  88.4 6.5 %collective-permute-start.25 = (f32[1,72,256]{2,1,0:T(8,128)S(1)}, f32[1,72,256]{2,1,0:T(8,128)S(1)}, u32[]{:S(2)}, u32[]{:S(2)}) collective-permute-start(f32[1,72,256]{2,1,0:T(8,128)S(1)} %get-tuple-element.93), channel_id=1, source_target_pairs={{0,32},{1,33},{2,34},{3,35},{4,36},{5,37},{6,38},{7,39},{8,40},{9,... | collective-permute-start | bytes 221192 | tf_op jit(solution)/shard_map/ppermute | solution.py:53
  92.4 4.7 %collective-permute-start.26 = (f32[1,72,256]{2,1,0:T(8,128)S(1)}, f32[1,72,256]{2,1,0:T(8,128)S(1)}, u32[]{:S(2)}, u32[]{:S(2)}) collective-permute-start(f32[1,72,256]{2,1,0:T(8,128)S(1)} %get-tuple-element.93), channel_id=1, source_target_pairs={{0,160},{1,161},{2,162},{3,163},{4,164},{5,165},{6,166},{7,167},{8... | collective-permute-start | bytes 221192 | tf_op jit(solution)/shard_map/ppermute | solution.py:53
  97.1 16.6 %collective-permute-start.27 = (f32[4,72,256]{2,1,0:T(8,128)S(1)}, f32[4,72,256]{2,1,0:T(8,128)S(1)}, u32[]{:S(2)}, u32[]{:S(2)}) collective-permute-start(f32[4,72,256]{2,1,0:T(8,128)S(1)} %constant_dynamic-update-slice_fusion.8), channel_id=1, source_target_pairs={{0,1},{1,0},{2,3},{3,2},{4,5},{5,4},{6,7},{7,6},{8,9},{9,8},{10,11... | collective-permute-start | bytes 884744 | tf_op jit(solution)/shard_map/ppermute | solution.py:53
  97.2 18.4 %collective-permute-start.28 = (f32[4,72,256]{2,1,0:T(8,128)S(1)}, f32[4,72,256]{2,1,0:T(8,128)S(1)}, u32[]{:S(2)}, u32[]{:S(2)}) collective-permute-start(f32[4,72,256]{2,1,0:T(8,128)S(1)} %constant_dynamic-update-slice_fusion.8), channel_id=1, source_target_pairs={{0,2},{1,3},{2,0},{3,1},{4,6},{5,7},{6,4},{7,5},{8,10},{9,11},{10,... | collective-permute-start | bytes 884744 | tf_op jit(solution)/shard_map/ppermute | solution.py:53
  103.5 14.0 %collective-permute-start.29 = (f32[4,72,256]{2,1,0:T(8,128)S(1)}, f32[4,72,256]{2,1,0:T(8,128)S(1)}, u32[]{:S(2)}, u32[]{:S(2)}) collective-permute-start(f32[4,72,256]{2,1,0:T(8,128)S(1)} %constant_dynamic-update-slice_fusion.8), channel_id=1, source_target_pairs={{0,3},{1,2},{2,1},{3,0},{4,7},{5,6},{6,5},{7,4},{8,11},{9,10},{10,... | collective-permute-start | bytes 884744 | tf_op jit(solution)/shard_map/ppermute | solution.py:53
  103.5 17.5 %collective-permute-start.30 = (f32[4,72,256]{2,1,0:T(8,128)S(1)}, f32[4,72,256]{2,1,0:T(8,128)S(1)}, u32[]{:S(2)}, u32[]{:S(2)}) collective-permute-start(f32[4,72,256]{2,1,0:T(8,128)S(1)} %constant_dynamic-update-slice_fusion.8), channel_id=1, source_target_pairs={{0,64},{1,65},{2,66},{3,67},{4,68},{5,69},{6,70},{7,71},{8,72},{9,... | collective-permute-start | bytes 884744 | tf_op jit(solution)/shard_map/ppermute | solution.py:53
  113.7 7.4 %collective-permute-start.31 = (f32[4,72,256]{2,1,0:T(8,128)S(1)}, f32[4,72,256]{2,1,0:T(8,128)S(1)}, u32[]{:S(2)}, u32[]{:S(2)}) collective-permute-start(f32[4,72,256]{2,1,0:T(8,128)S(1)} %collective-permute-done.27), channel_id=1, source_target_pairs={{0,64},{1,65},{2,66},{3,67},{4,68},{5,69},{6,70},{7,71},{8,72},{9,... | collective-permute-start | bytes 884744 | tf_op jit(solution)/shard_map/ppermute | solution.py:53
  115.6 5.6 %collective-permute-start.32 = (f32[4,72,256]{2,1,0:T(8,128)S(1)}, f32[4,72,256]{2,1,0:T(8,128)S(1)}, u32[]{:S(2)}, u32[]{:S(2)}) collective-permute-start(f32[4,72,256]{2,1,0:T(8,128)S(1)} %collective-permute-done.28), channel_id=1, source_target_pairs={{0,64},{1,65},{2,66},{3,67},{4,68},{5,69},{6,70},{7,71},{8,72},{9,... | collective-permute-start | bytes 884744 | tf_op jit(solution)/shard_map/ppermute | solution.py:53
  117.5 4.6 %collective-permute-start.33 = (f32[4,72,256]{2,1,0:T(8,128)S(1)}, f32[4,72,256]{2,1,0:T(8,128)S(1)}, u32[]{:S(2)}, u32[]{:S(2)}) collective-permute-start(f32[4,72,256]{2,1,0:T(8,128)S(1)} %collective-permute-done.29), channel_id=1, source_target_pairs={{0,64},{1,65},{2,66},{3,67},{4,68},{5,69},{6,70},{7,71},{8,72},{9,... | collective-permute-start | bytes 884744 | tf_op jit(solution)/shard_map/ppermute | solution.py:53

commit v4 on v3

--- a/solution.py
+++ b/solution.py
@@ -46,7 +46,10 @@
 second_axis = [
     exchange(lambda c, k=k: {"y": c["y"] ^ k} if c["core"] == 0 else {"x": c["x"] ^ k}) for k in range(4)
 ]
-along_z = [exchange(lambda c, k=k: {"z": c["z"] ^ k}) for k in range(8)]
+
+
+def shift_z(step):
+    return exchange(lambda c: {"z": (c["z"] + step) % 8})
 
 
 def send(value, pairs):
@@ -388,26 +391,28 @@
     core = place["core"]
     first = jnp.where(straight, place["x"], place["y"])
     second = jnp.where(straight, place["y"], place["x"])
-    halves = [keep[k] + send(away[k], swap_core) for k in (1, 2, 3, 0)]
+    swapped = [send(away[k], swap_core) for k in (1, 2, 3, 0)]
+    halves = [keep[k] + part for k, part in zip((1, 2, 3), swapped)]
     parts = [send(half, first_axis[k]) for k, half in zip((1, 2, 3), halves)]
-    grid_grad = jnp.einsum("npu,wu->npw", grad_query, dst_weight, precision=lax.Precision.HIGH)
-    upper, lower, grid_grad = lax.optimization_barrier((upper, lower, grid_grad))
+    upper, lower, last = lax.optimization_barrier((upper, lower, swapped[3]))
     from_prev = lax.ppermute(upper, "grid", up)
     from_next = lax.ppermute(lower, "grid", down)
-    *parts, grid_grad = lax.optimization_barrier((*parts, grid_grad))
-    total = tree(halves[3], parts)
+    *parts, from_prev, from_next = lax.optimization_barrier((*parts, from_prev, from_next))
+    total = tree(keep[0] + last, parts)
     parts = [send(total[k : k + 1], second_axis[k]) for k in (1, 2, 3)]
-    *parts, from_prev, from_next = lax.optimization_barrier((*parts, from_prev, from_next))
-    total = tree(total[:1], parts)
-    parts = [send(total, along_z[k]) for k in (1, 2, 3)]
     mesh_grad = jnp.einsum(
         "nru,wu->nrw", middle + from_prev + from_next, src_weight, precision=lax.Precision.HIGH
     )
     *parts, mesh_grad = lax.optimization_barrier((*parts, mesh_grad))
-    total = tree(total, parts)
-    total = total + send(total, along_z[4])
+    total = tree(total[:1], parts)
+    above, below = send(total, shift_z(-1)), send(total, shift_z(1))
+    pair = total + above
+    three = pair + below
+    total = three + (send(three, shift_z(-3)) + send(pair, shift_z(3)))
     total = placed_at(second, total, [send(total, second_axis[k]) for k in (1, 2, 3)])
     parts = [total] + [send(total, first_axis[k]) for k in (1, 2, 3)]
+    grid_grad = jnp.einsum("npu,wu->npw", grad_query, dst_weight, precision=lax.Precision.HIGH)
+    parts[3], grid_grad = lax.optimization_barrier((parts[3], grid_grad))
     others = [send(part, swap_core) for part in parts]
     total = placed_at(first, parts[0], parts[1:]).reshape(1152, 256)
     other = placed_at(second, others[0], others[1:]).reshape(1152, 256)

time: 126 us -> 132 us (1.048)
  waiting for transfers between devices: 29.4 us -> 31.3 us
  other arithmetic: 0.64 us -> 2.18 us
    ppermute x1, waiting for transfers between devices: 0.01 us -> 2.64 us  [body(): from_next = lax.ppermute(lower, 'grid', down)]
    ppermute x24, waiting for transfers between devices: 19.1 us -> 16.5 us  [send(): return lax.ppermute(value, axes, pairs)]
    ppermute x1, waiting for transfers between devices: 0.01 us -> 1.77 us  [body(): from_prev = lax.ppermute(upper, 'grid', up)]
    dynamic_update_slice x1, other arithmetic: 0.02 us -> 1.57 us  [placed_at(): lax.dynamic_update_slice(whole_value, part, ((place ^ k) * size, 0, 0))]
  transfers between devices with their start and end apart: 34 -> 34, of which waited for: 15 -> 18; matrix products, arithmetic and copies ran while one was open for 4% -> 4% of each run, Pallas kernels for 4% -> 4%
where the time goes in v4:
time: 132 us; the launch traced here: 130 us
  starting transfers between devices  66.9 us (51%)
  waiting for transfers between devices  31.3 us (24%)
  Pallas kernels  20.3 us (15%)
  matrix products  4.43 us (3%)
  local copies, waits for them, and re-layouts  3.87 us (3%)
  other arithmetic  2.18 us (2%)
    ppermute x24, starting transfers between devices, send(): return lax.ppermute(value, axes, pairs)  53.3 us
    ppermute x24, waiting for transfers between devices, send(): return lax.ppermute(value, axes, pairs)  16.5 us
    pallas_call x1, Pallas kernels, body(): pl.pallas_call(functools.partial(backward_kernel, tile, scale, loss_scale...  8.43 us
    pallas_call x1, Pallas kernels, body(): pl.pallas_call(functools.partial(forward_kernel, tile), grid_spec=pltpu.P...  5.81 us
    ppermute x3, waiting for transfers between devices, body(): lax.ppermute(parts[k], 'member', to_peer[k])  5.26 us
    ppermute x3, waiting for transfers between devices, body(): lax.ppermute(slopes[k], 'member', to_peer[k])  5.05 us
    pallas_call x1, Pallas kernels, body(): pl.pallas_call(query_kernel, in_specs=[me_spec, whole(), in_hbm, in_hbm,...  4.86 us
    ppermute x1, starting transfers between devices, body(): before = lax.ppermute(mesh_features, 'grid', up)  3.95 us
  transfers between devices with their start and end apart: 34, of which 18 were waited for; matrix products, arithmetic and copies ran while one was open for 4% of the time, Pallas kernels for 4%

profile of v4, /device:TPU:1, one launch (start us, length us, event | category | flops | bytes accessed | tf_op | source)
XLA Modules:
  0.0 129.9 jit_solution(2924819900109841218)
XLA Ops:
  0.6 4.0 %collective-permute-start = (f32[2,32,512]{2,1,0:T(8,128)}, f32[2,32,512]{2,1,0:T(8,128)S(1)}, u32[]{:S(2)}, u32[]{:S(2)}) collective-permute-start(f32[2,32,512]{2,1,0:T(8,128)} %own.3), channel_id=1, source_target_pairs={{0,1},{1,2},{2,3},{3,4},{4,5},{5,6},{6,7},{7,8},{8,9},{9,10},{10,1... | collective-permute-start | bytes 393224 | tf_op jit(solution)/shard_map/ppermute | solution.py:272
  4.6 1.3 collective-permute-start.1
  6.0 4.9 %query.1 = (f32[2,512,512]{2,1,0:T(8,128)S(1)}, s32[512,8]{1,0:T(8,128)S(1)}, bf16[512,512]{1,0:T(8,128)(2,1)S(1)}, bf16[512,512]{1,0:T(8,128)(2,1)S(1)}) custom-call(s32[5]{0:T(128)S(1)} %stack.23.me, s32[4,512]{1,0:T(4,128)} %edges.3, f32[2,512,512]{2,1,0:T(8,128)} %features.3, f32[512,512]{1,0:T(8,128)} %weight.1, f32[512,512]{1,0:T(8,128)} %src_weight.1), custom_call_target="tpu_custom_call" | custom-call | tf_op jit(solution)/shard_map/query/pallas_call | solution.py:277
  10.9 5.8 %forward.1 = (f32[2,4,512,512]{3,2,1,0:T(8,128)S(1)}, f32[2,512,512]{2,1,0:T(8,128)S(1)}, f32[2,100,128]{2,1,0:T(8,128)S(1)}, f32[2,100,128]{2,1,0:T(8,128)S(1)}...) custom-call(s32[5]{0:T(128)S(1)} %stack.23.me, f32[2,512,512]{2,1,0:T(8,128)S(1)} %get-tuple-element.47.query, ...), custom_call_target="tpu_custom_call" | custom-call | tf_op jit(solution)/shard_map/forward/pallas_call | solution.py:306
  16.8 1.8 %collective-permute-start.2 = (f32[2,100,128]{2,1,0:T(8,128)S(1)}, f32[2,100,128]{2,1,0:T(8,128)S(1)}, u32[]{:S(2)}, u32[]{:S(2)}) collective-permute-start(f32[2,100,128]{2,1,0:T(8,128)S(1)} %get-tuple-element.52), channel_id=1, source_target_pairs={{0,64},{64,0},{128,192},{192,128},{1,65},{65,1},{129,193},{193,129... | collective-permute-start | bytes 307208 | tf_op jit(solution)/shard_map/ppermute | solution.py:335
  18.6 1.3 %collective-permute-start.3 = (f32[2,100,128]{2,1,0:T(8,128)S(1)}, f32[2,100,128]{2,1,0:T(8,128)S(1)}, u32[]{:S(2)}, u32[]{:S(2)}) collective-permute-start(f32[2,100,128]{2,1,0:T(8,128)S(1)} %get-tuple-element.53), channel_id=1, source_target_pairs={{0,128},{64,192},{128,0},{192,64},{1,129},{65,193},{129,1},{193,65... | collective-permute-start | bytes 307208 | tf_op jit(solution)/shard_map/ppermute | solution.py:335
  19.9 0.4 collective-permute-start.4
  20.3 2.8 %collective-permute-done.3.part2 = f32[2,100,128]{2,1,0:T(8,128)S(1)} collective-permute-done((f32[2,100,128]{2,1,0:T(8,128)S(1)}, f32[2,100,128]{2,1,0:T(8,128)S(1)}, u32[]{:S(2)}, u32[]{:S(2)}) %collective-permute-start.3) | collective-permute-done | bytes 102432 | tf_op jit(solution)/shard_map/ppermute | solution.py:335
  23.1 2.5 %collective-permute-done.4.part3 = f32[2,100,128]{2,1,0:T(8,128)S(1)} collective-permute-done((f32[2,100,128]{2,1,0:T(8,128)S(1)}, f32[2,100,128]{2,1,0:T(8,128)S(1)}, u32[]{:S(2)}, u32[]{:S(2)}) %collective-permute-start.4) | collective-permute-done | bytes 102432 | tf_op jit(solution)/shard_map/ppermute | solution.py:335
  25.6 1.2 score.1
  27.1 1.3 collective-permute-start.6
  28.4 0.6 collective-permute-start.7
  29.0 2.3 %collective-permute-done.6.part2 = f32[2,100,128]{2,1,0:T(8,128)S(1)} collective-permute-done((f32[2,100,128]{2,1,0:T(8,128)S(1)}, f32[2,100,128]{2,1,0:T(8,128)S(1)}, u32[]{:S(2)}, u32[]{:S(2)}) %collective-permute-start.6) | collective-permute-done | bytes 102432 | tf_op jit(solution)/shard_map/ppermute | solution.py:349
  31.3 2.7 %collective-permute-done.7.part3 = f32[2,100,128]{2,1,0:T(8,128)S(1)} collective-permute-done((f32[2,100,128]{2,1,0:T(8,128)S(1)}, f32[2,100,128]{2,1,0:T(8,128)S(1)}, u32[]{:S(2)}, u32[]{:S(2)}) %collective-permute-start.7) | collective-permute-done | bytes 102432 | tf_op jit(solution)/shard_map/ppermute | solution.py:349
  34.0 8.4 %backward.1 = (f32[2,512,512]{2,1,0:T(8,128)S(1)}, f32[2,32,512]{2,1,0:T(8,128)S(1)}, f32[2,32,512]{2,1,0:T(8,128)S(1)}, f32[2,32,512]{2,1,0:T(8,128)S(1)}, f32[...) custom-call(s32[5]{0:T(128)S(1)} %stack.23.me, ...), custom_call_target="tpu_custom_call" | custom-call | tf_op jit(solution)/shard_map/backward/pallas_call | solution.py:357
  43.6 0.6 collective-permute-done.13
  44.2 9.9 %collective-permute-start.14 = (f32[4,72,256]{2,1,0:T(8,128)S(1)}, f32[4,72,256]{2,1,0:T(8,128)S(1)}, u32[]{:S(2)}, u32[]{:S(2)}) collective-permute-start(f32[4,72,256]{2,1,0:T(8,128)S(1)} %add.95), channel_id=1, source_target_pairs={{0,3},{1,2},{2,1},{3,0},{4,7},{5,6},{6,5},{7,4},{8,11},{9,10},{10,... | collective-permute-start | bytes 884744 | tf_op jit(solution)/shard_map/ppermute | solution.py:56
  54.5 0.8 collective-permute-start.10
  55.3 1.3 collective-permute-start.15
  56.6 1.3 collective-permute-start.16
  57.9 1.8 %collective-permute-done.15 = f32[2,32,512]{2,1,0:T(8,128)S(1)} collective-permute-done((f32[2,32,512]{2,1,0:T(8,128)S(1)}, f32[2,32,512]{2,1,0:T(8,128)S(1)}, u32[]{:S(2)}, u32[]{:S(2)}) %collective-permute-start.15) | collective-permute-done | bytes 131104 | tf_op jit(solution)/shard_map/ppermute | solution.py:398
  59.6 2.6 %collective-permute-done.16 = f32[2,32,512]{2,1,0:T(8,128)S(1)} collective-permute-done((f32[2,32,512]{2,1,0:T(8,128)S(1)}, f32[2,32,512]{2,1,0:T(8,128)S(1)}, u32[]{:S(2)}, u32[]{:S(2)}) %collective-permute-start.16) | collective-permute-done | bytes 131104 | tf_op jit(solution)/shard_map/ppermute | solution.py:399
  62.7 3.2 %collective-permute-start.18 = (f32[1,72,256]{2,1,0:T(8,128)S(1)}, f32[1,72,256]{2,1,0:T(8,128)S(1)}, u32[]{:S(2)}, u32[]{:S(2)}) collective-permute-start(f32[1,72,256]{2,1,0:T(8,128)S(1)} %get-tuple-element.95), channel_id=1, source_target_pairs={{0,32},{1,33},{2,34},{3,35},{4,36},{5,37},{6,38},{7,39},{8,40},{9,... | collective-permute-start | bytes 221192 | tf_op jit(solution)/shard_map/ppermute | solution.py:56
  65.8 0.7 collective-permute-start.19
  66.5 1.3 fusion.2
  67.8 0.8 collective-permute-done.18
  68.6 1.6 %collective-permute-done.19 = f32[1,72,256]{2,1,0:T(8,128)S(1)} collective-permute-done((f32[1,72,256]{2,1,0:T(8,128)S(1)}, f32[1,72,256]{2,1,0:T(8,128)S(1)}, u32[]{:S(2)}, u32[]{:S(2)}) %collective-permute-start.19) | collective-permute-done | bytes 73760 | tf_op jit(solution)/shard_map/ppermute | solution.py:56
  70.3 12.1 %collective-permute-start.20 = (f32[1,72,256]{2,1,0:T(8,128)S(1)}, f32[1,72,256]{2,1,0:T(8,128)S(1)}, u32[]{:S(2)}, u32[]{:S(2)}) collective-permute-start(f32[1,72,256]{2,1,0:T(8,128)S(1)} %fusion.6), channel_id=1, source_target_pairs={{0,28},{1,29},{2,30},{3,31},{4,0},{5,1},{6,2},{7,3},{8,4},{9,5},{1... | collective-permute-start | bytes 221192 | tf_op jit(solution)/shard_map/ppermute | solution.py:56
  82.3 1.4 %collective-permute-done.20 = f32[1,72,256]{2,1,0:T(8,128)S(1)} collective-permute-done((f32[1,72,256]{2,1,0:T(8,128)S(1)}, f32[1,72,256]{2,1,0:T(8,128)S(1)}, u32[]{:S(2)}, u32[]{:S(2)}) %collective-permute-start.20) | collective-permute-done | bytes 73760 | tf_op jit(solution)/shard_map/ppermute | solution.py:56
  83.7 3.0 %collective-permute-done.21 = f32[1,72,256]{2,1,0:T(8,128)S(1)} collective-permute-done((f32[1,72,256]{2,1,0:T(8,128)S(1)}, f32[1,72,256]{2,1,0:T(8,128)S(1)}, u32[]{:S(2)}, u32[]{:S(2)}) %collective-permute-start.21) | collective-permute-done | bytes 73760 | tf_op jit(solution)/shard_map/ppermute | solution.py:56
  86.9 3.3 %collective-permute-start.23 = (f32[1,72,256]{2,1,0:T(8,128)S(1)}, f32[1,72,256]{2,1,0:T(8,128)}, u32[]{:S(2)}, u32[]{:S(2)}) collective-permute-start(f32[1,72,256]{2,1,0:T(8,128)S(1)} %get-tuple-element.91), channel_id=1, source_target_pairs={{0,12},{1,13},{2,14},{3,15},{4,16},{5,17},{6,18},{7,19},{8,20},{9,... | collective-permute-start | bytes 221192 | tf_op jit(solution)/shard_map/ppermute | solution.py:56
  90.1 5.0 %collective-permute-done.22 = f32[1,72,256]{2,1,0:T(8,128)S(1)} collective-permute-done((f32[1,72,256]{2,1,0:T(8,128)S(1)}, f32[1,72,256]{2,1,0:T(8,128)S(1)}, u32[]{:S(2)}, u32[]{:S(2)}) %collective-permute-start.22) | collective-permute-done | bytes 73760 | tf_op jit(solution)/shard_map/ppermute | solution.py:56
  95.1 0.6 copy-done.7
  95.7 0.4 collective-permute-done.23
  96.1 1.6 %constant_dynamic-update-slice_fusion.11 = (f32[4,72,256]{2,1,0:T(8,128)S(1)}, f32[1,72,256]{2,1,0:T(8,128)}) fusion(f32[4,72,256]{2,1,0:T(8,128)S(1)} %broadcast_in_dim.3, s32[]{:T(128)S(6)} %select_n.61, f32[1,72,256]{2,1,0:T(8,128)S(1)} %get-tuple-element.90, f32[1,72,256]{2,1,0:T(8,128)} %copy-done.7, f32[1,72,256]{2,1,0:T(8,128)} %collective-permute-done.23), kind=kLoop, calls=%fused_computation.23 | loop fusion | flops 36864 | bytes 368644 | tf_op jit(solution)/shard_map/dynamic_update_slice | solution.py:248
  97.7 3.9 %collective-permute-start.26 = (f32[1,72,256]{2,1,0:T(8,128)}, f32[1,72,256]{2,1,0:T(8,128)S(1)}, u32[]{:S(2)}, u32[]{:S(2)}) collective-permute-start(f32[1,72,256]{2,1,0:T(8,128)} %get-tuple-element.89), channel_id=1, source_target_pairs={{0,160},{1,161},{2,162},{3,163},{4,164},{5,165},{6,166},{7,167},{8... | collective-permute-start | bytes 221192 | tf_op jit(solution)/shard_map/ppermute | solution.py:56
  101.6 1.0 collective-permute-done.25
  102.7 1.2 collective-permute-done.26
  104.1 3.7 %collective-permute-start.29 = (f32[4,72,256]{2,1,0:T(8,128)S(1)}, f32[4,72,256]{2,1,0:T(8,128)S(1)}, u32[]{:S(2)}, u32[]{:S(2)}) collective-permute-start(f32[4,72,256]{2,1,0:T(8,128)S(1)} %constant_dynamic-update-slice_fusion.8), channel_id=1, source_target_pairs={{0,3},{1,2},{2,1},{3,0},{4,7},{5,6},{6,5},{7,4},{8,11},{9,10},{10,... | collective-permute-start | bytes 884744 | tf_op jit(solution)/shard_map/ppermute | solution.py:56
  107.8 3.2 %fusion = f32[2,512,512]{2,1,0:T(8,128)} fusion(f32[2,512,512]{2,1,0:T(8,128)S(1)} %get-tuple-element.84, f32[512,512]{1,0:T(8,128)S(1)} %copy-done.5), kind=kOutput, calls=%fused_computation.1 | convolution fusion | flops 1610612736 | bytes 5242880 | tf_op jit(solution)/shard_map/npu,wu->npw/dot_general | solution.py:414
  111.0 5.9 %collective-permute-start.30 = (f32[4,72,256]{2,1,0:T(8,128)S(1)}, f32[4,72,256]{2,1,0:T(8,128)S(1)}, u32[]{:S(2)}, u32[]{:S(2)}) collective-permute-start(f32[4,72,256]{2,1,0:T(8,128)S(1)} %constant_dynamic-update-slice_fusion.8), channel_id=1, source_target_pairs={{0,64},{1,65},{2,66},{3,67},{4,68},{5,69},{6,70},{7,71},{8,72},{9,... | collective-permute-start | bytes 884744 | tf_op jit(solution)/shard_map/ppermute | solution.py:56
  117.0 7.7 %collective-permute-start.33 = (f32[4,72,256]{2,1,0:T(8,128)S(1)}, f32[4,72,256]{2,1,0:T(8,128)S(1)}, u32[]{:S(2)}, u32[]{:S(2)}) collective-permute-start(f32[4,72,256]{2,1,0:T(8,128)S(1)} %collective-permute-done.29), channel_id=1, source_target_pairs={{0,64},{1,65},{2,66},{3,67},{4,68},{5,69},{6,70},{7,71},{8,72},{9,... | collective-permute-start | bytes 884744 | tf_op jit(solution)/shard_map/ppermute | solution.py:56
  124.8 0.5 collective-permute-start.32
  125.5 0.9 collective-permute-done.31
  126.4 0.4 collective-permute-done.32
  127.2 1.5 %fusion.8 = (f32[512,512]{1,0:T(8,128)}, f32[512,512]{1,0:T(8,128)}) fusion(f32[1152,512]{1,0:T(8,128)S(1)} %maximum_select_fusion), kind=kLoop, calls=%fused_computation.25 | loop fusion | bytes 4194304 | tf_op jit(solution)/shard_map/slice | solution.py:424
  128.7 0.7 slice_bitcast_fusion
  129.4 0.5 slice.36
  (69 shorter events, 3.4 us)
Async XLA Ops:
  0.6 10.2 %collective-permute-start = (f32[2,32,512]{2,1,0:T(8,128)}, f32[2,32,512]{2,1,0:T(8,128)S(1)}, u32[]{:S(2)}, u32[]{:S(2)}) collective-permute-start(f32[2,32,512]{2,1,0:T(8,128)} %own.3), channel_id=1, source_target_pairs={{0,1},{1,2},{2,3},{3,4},{4,5},{5,6},{6,7},{7,8},{8,9},{9,10},{10,1... | collective-permute-start | bytes 393224 | tf_op jit(solution)/shard_map/ppermute | solution.py:272
  4.6 6.3 %collective-permute-start.1 = (f32[2,32,512]{2,1,0:T(8,128)}, f32[2,32,512]{2,1,0:T(8,128)S(1)}, u32[]{:S(2)}, u32[]{:S(2)}) collective-permute-start(f32[2,32,512]{2,1,0:T(8,128)} %own.3), channel_id=1, source_target_pairs={{1,0},{2,1},{3,2},{4,3},{5,4},{6,5},{7,6},{8,7},{9,8},{10,9},{11,1... | collective-permute-start | bytes 393224 | tf_op jit(solution)/shard_map/ppermute | solution.py:273
  6.0 4.9 %copy-start.1 = (f32[512,100]{0,1:T(8,128)S(1)}, f32[512,100]{0,1:T(8,128)}, u32[]{:S(2)}) copy-start(f32[512,100]{0,1:T(8,128)} %param.13) | copy-start | bytes 614404
  6.0 4.9 %copy-start.2 = (f32[2,32,512]{2,1,0:T(8,128)S(1)}, f32[2,32,512]{2,1,0:T(8,128)}, u32[]{:S(2)}) copy-start(f32[2,32,512]{2,1,0:T(8,128)} %own.3) | copy-start | bytes 393220
  10.9 14.6 %copy-start.3 = (f32[100,512]{1,0:T(8,128)S(1)}, f32[100,512]{1,0:T(8,128)}, u32[]{:S(2)}) copy-start(f32[100,512]{1,0:T(8,128)} %targets.1) | copy-start | bytes 614404
  10.9 23.1 %copy-start = (f32[2,512,512]{2,1,0:T(8,128)S(1)}, f32[2,512,512]{2,1,0:T(8,128)}, u32[]{:S(2)}) copy-start(f32[2,512,512]{2,1,0:T(8,128)} %features.3) | copy-start | bytes 6291460
  10.9 23.1 %copy-start.4 = (s32[4,512]{1,0:T(4,128)S(1)}, s32[4,512]{1,0:T(4,128)}, u32[]{:S(2)}) copy-start(s32[4,512]{1,0:T(4,128)} %edges.3) | copy-start | bytes 24580
  16.8 3.5 %collective-permute-start.2 = (f32[2,100,128]{2,1,0:T(8,128)S(1)}, f32[2,100,128]{2,1,0:T(8,128)S(1)}, u32[]{:S(2)}, u32[]{:S(2)}) collective-permute-start(f32[2,100,128]{2,1,0:T(8,128)S(1)} %get-tuple-element.52), channel_id=1, source_target_pairs={{0,64},{64,0},{128,192},{192,128},{1,65},{65,1},{129,193},{193,129... | collective-permute-start | bytes 307208 | tf_op jit(solution)/shard_map/ppermute | solution.py:335
  18.6 4.5 %collective-permute-start.3 = (f32[2,100,128]{2,1,0:T(8,128)S(1)}, f32[2,100,128]{2,1,0:T(8,128)S(1)}, u32[]{:S(2)}, u32[]{:S(2)}) collective-permute-start(f32[2,100,128]{2,1,0:T(8,128)S(1)} %get-tuple-element.53), channel_id=1, source_target_pairs={{0,128},{64,192},{128,0},{192,64},{1,129},{65,193},{129,1},{193,65... | collective-permute-start | bytes 307208 | tf_op jit(solution)/shard_map/ppermute | solution.py:335
  19.9 5.7 %collective-permute-start.4 = (f32[2,100,128]{2,1,0:T(8,128)S(1)}, f32[2,100,128]{2,1,0:T(8,128)S(1)}, u32[]{:S(2)}, u32[]{:S(2)}) collective-permute-start(f32[2,100,128]{2,1,0:T(8,128)S(1)} %get-tuple-element.54), channel_id=1, source_target_pairs={{0,192},{64,128},{128,64},{192,0},{1,193},{65,129},{129,65},{193,1... | collective-permute-start | bytes 307208 | tf_op jit(solution)/shard_map/ppermute | solution.py:335
  26.8 2.2 %collective-permute-start.5 = (f32[2,100,128]{2,1,0:T(8,128)S(1)}, f32[2,100,128]{2,1,0:T(8,128)S(1)}, u32[]{:S(2)}, u32[]{:S(2)}) collective-permute-start(f32[2,100,128]{2,1,0:T(8,128)S(1)} %get-tuple-element.56), channel_id=1, source_target_pairs={{0,64},{64,0},{128,192},{192,128},{1,65},{65,1},{129,193},{193,129... | collective-permute-start | bytes 307208 | tf_op jit(solution)/shard_map/ppermute | solution.py:349
  27.1 4.3 %collective-permute-start.6 = (f32[2,100,128]{2,1,0:T(8,128)S(1)}, f32[2,100,128]{2,1,0:T(8,128)S(1)}, u32[]{:S(2)}, u32[]{:S(2)}) collective-permute-start(f32[2,100,128]{2,1,0:T(8,128)S(1)} %get-tuple-element.57), channel_id=1, source_target_pairs={{0,128},{64,192},{128,0},{192,64},{1,129},{65,193},{129,1},{193,65... | collective-permute-start | bytes 307208 | tf_op jit(solution)/shard_map/ppermute | solution.py:349
  28.4 5.7 %collective-permute-start.7 = (f32[2,100,128]{2,1,0:T(8,128)S(1)}, f32[2,100,128]{2,1,0:T(8,128)S(1)}, u32[]{:S(2)}, u32[]{:S(2)}) collective-permute-start(f32[2,100,128]{2,1,0:T(8,128)S(1)} %get-tuple-element.58), channel_id=1, source_target_pairs={{0,192},{64,128},{128,64},{192,0},{1,193},{65,129},{129,65},{193,1... | collective-permute-start | bytes 307208 | tf_op jit(solution)/shard_map/ppermute | solution.py:349
  42.5 1.7 %collective-permute-start.13 = (f32[4,72,256]{2,1,0:T(8,128)S(1)}, f32[4,72,256]{2,1,0:T(8,128)S(1)}, u32[]{:S(2)}, u32[]{:S(2)}) collective-permute-start(f32[4,72,256]{2,1,0:T(8,128)S(1)} %get-tuple-element.72), channel_id=1, source_target_pairs={{0,64},{1,65},{2,66},{3,67},{4,68},{5,69},{6,70},{7,71},{8,72},{9,... | collective-permute-start | bytes 884744 | tf_op jit(solution)/shard_map/ppermute | solution.py:56
  42.8 11.4 %collective-permute-start.11 = (f32[4,72,256]{2,1,0:T(8,128)S(1)}, f32[4,72,256]{2,1,0:T(8,128)S(1)}, u32[]{:S(2)}, u32[]{:S(2)}) collective-permute-start(f32[4,72,256]{2,1,0:T(8,128)S(1)} %get-tuple-element.70), channel_id=1, source_target_pairs={{0,64},{1,65},{2,66},{3,67},{4,68},{5,69},{6,70},{7,71},{8,72},{9,... | collective-permute-start | bytes 884744 | tf_op jit(solution)/shard_map/ppermute | solution.py:56
  43.1 11.4 %collective-permute-start.9 = (f32[4,72,256]{2,1,0:T(8,128)S(1)}, f32[4,72,256]{2,1,0:T(8,128)S(1)}, u32[]{:S(2)}, u32[]{:S(2)}) collective-permute-start(f32[4,72,256]{2,1,0:T(8,128)S(1)} %get-tuple-element.68), channel_id=1, source_target_pairs={{0,64},{1,65},{2,66},{3,67},{4,68},{5,69},{6,70},{7,71},{8,72},{9,... | collective-permute-start | bytes 884744 | tf_op jit(solution)/shard_map/ppermute | solution.py:56
  43.4 11.9 %collective-permute-start.8 = (f32[4,72,256]{2,1,0:T(8,128)S(1)}, f32[4,72,256]{2,1,0:T(8,128)S(1)}, u32[]{:S(2)}, u32[]{:S(2)}) collective-permute-start(f32[4,72,256]{2,1,0:T(8,128)S(1)} %get-tuple-element.65), channel_id=1, source_target_pairs={{0,64},{1,65},{2,66},{3,67},{4,68},{5,69},{6,70},{7,71},{8,72},{9,... | collective-permute-start | bytes 884744 | tf_op jit(solution)/shard_map/ppermute | solution.py:56
  44.2 18.1 %collective-permute-start.14 = (f32[4,72,256]{2,1,0:T(8,128)S(1)}, f32[4,72,256]{2,1,0:T(8,128)S(1)}, u32[]{:S(2)}, u32[]{:S(2)}) collective-permute-start(f32[4,72,256]{2,1,0:T(8,128)S(1)} %add.95), channel_id=1, source_target_pairs={{0,3},{1,2},{2,1},{3,0},{4,7},{5,6},{6,5},{7,4},{8,11},{9,10},{10,... | collective-permute-start | bytes 884744 | tf_op jit(solution)/shard_map/ppermute | solution.py:56
  54.2 8.1 %collective-permute-start.12 = (f32[4,72,256]{2,1,0:T(8,128)S(1)}, f32[4,72,256]{2,1,0:T(8,128)S(1)}, u32[]{:S(2)}, u32[]{:S(2)}) collective-permute-start(f32[4,72,256]{2,1,0:T(8,128)S(1)} %add.94), channel_id=1, source_target_pairs={{0,2},{1,3},{2,0},{3,1},{4,6},{5,7},{6,4},{7,5},{8,10},{9,11},{10,... | collective-permute-start | bytes 884744 | tf_op jit(solution)/shard_map/ppermute | solution.py:56
  54.5 12.0 %copy-start.6 = (f32[512,512]{1,0:T(8,128)S(1)}, f32[512,512]{1,0:T(8,128)}, u32[]{:S(2)}) copy-start(f32[512,512]{1,0:T(8,128)} %src_weight.1) | copy-start | bytes 3145732
  54.5 7.9 %collective-permute-start.10 = (f32[4,72,256]{2,1,0:T(8,128)S(1)}, f32[4,72,256]{2,1,0:T(8,128)S(1)}, u32[]{:S(2)}, u32[]{:S(2)}) collective-permute-start(f32[4,72,256]{2,1,0:T(8,128)S(1)} %add.93), channel_id=1, source_target_pairs={{0,1},{1,0},{2,3},{3,2},{4,5},{5,4},{6,7},{7,6},{8,9},{9,8},{10,11... | collective-permute-start | bytes 884744 | tf_op jit(solution)/shard_map/ppermute | solution.py:56
  55.3 4.4 %collective-permute-start.15 = (f32[2,32,512]{2,1,0:T(8,128)S(1)}, f32[2,32,512]{2,1,0:T(8,128)S(1)}, u32[]{:S(2)}, u32[]{:S(2)}) collective-permute-start(f32[2,32,512]{2,1,0:T(8,128)S(1)} %get-tuple-element.73), channel_id=1, source_target_pairs={{0,1},{1,2},{2,3},{3,4},{4,5},{5,6},{6,7},{7,8},{8,9},{9,10},{10,1... | collective-permute-start | bytes 393224 | tf_op jit(solution)/shard_map/ppermute | solution.py:398
  56.6 5.7 %collective-permute-start.16 = (f32[2,32,512]{2,1,0:T(8,128)S(1)}, f32[2,32,512]{2,1,0:T(8,128)S(1)}, u32[]{:S(2)}, u32[]{:S(2)}) collective-permute-start(f32[2,32,512]{2,1,0:T(8,128)S(1)} %get-tuple-element.74), channel_id=1, source_target_pairs={{1,0},{2,1},{3,2},{4,3},{5,4},{6,5},{7,6},{8,7},{9,8},{10,9},{11,1... | collective-permute-start | bytes 393224 | tf_op jit(solution)/shard_map/ppermute | solution.py:399
  62.6 5.2 %collective-permute-start.17 = (f32[1,72,256]{2,1,0:T(8,128)S(1)}, f32[1,72,256]{2,1,0:T(8,128)S(1)}, u32[]{:S(2)}, u32[]{:S(2)}) collective-permute-start(f32[1,72,256]{2,1,0:T(8,128)S(1)} %get-tuple-element.96), channel_id=1, source_target_pairs={{0,128},{1,129},{2,130},{3,131},{4,132},{5,133},{6,134},{7,135},{8... | collective-permute-start | bytes 221192 | tf_op jit(solution)/shard_map/ppermute | solution.py:56
  62.7 6.0 %collective-permute-start.18 = (f32[1,72,256]{2,1,0:T(8,128)S(1)}, f32[1,72,256]{2,1,0:T(8,128)S(1)}, u32[]{:S(2)}, u32[]{:S(2)}) collective-permute-start(f32[1,72,256]{2,1,0:T(8,128)S(1)} %get-tuple-element.95), channel_id=1, source_target_pairs={{0,32},{1,33},{2,34},{3,35},{4,36},{5,37},{6,38},{7,39},{8,40},{9,... | collective-permute-start | bytes 221192 | tf_op jit(solution)/shard_map/ppermute | solution.py:56
  65.8 4.4 %collective-permute-start.19 = (f32[1,72,256]{2,1,0:T(8,128)S(1)}, f32[1,72,256]{2,1,0:T(8,128)S(1)}, u32[]{:S(2)}, u32[]{:S(2)}) collective-permute-start(f32[1,72,256]{2,1,0:T(8,128)S(1)} %get-tuple-element.94), channel_id=1, source_target_pairs={{0,160},{1,161},{2,162},{3,163},{4,164},{5,165},{6,166},{7,167},{8... | collective-permute-start | bytes 221192 | tf_op jit(solution)/shard_map/ppermute | solution.py:56
  67.8 40.0 %copy-start.5 = (f32[512,512]{1,0:T(8,128)S(1)}, f32[512,512]{1,0:T(8,128)}, u32[]{:S(2)}) copy-start(f32[512,512]{1,0:T(8,128)} %weight.1) | copy-start | bytes 3145732
  70.3 13.5 %collective-permute-start.20 = (f32[1,72,256]{2,1,0:T(8,128)S(1)}, f32[1,72,256]{2,1,0:T(8,128)S(1)}, u32[]{:S(2)}, u32[]{:S(2)}) collective-permute-start(f32[1,72,256]{2,1,0:T(8,128)S(1)} %fusion.6), channel_id=1, source_target_pairs={{0,28},{1,29},{2,30},{3,31},{4,0},{5,1},{6,2},{7,3},{8,4},{9,5},{1... | collective-permute-start | bytes 221192 | tf_op jit(solution)/shard_map/ppermute | solution.py:56
  82.3 4.4 %collective-permute-start.21 = (f32[1,72,256]{2,1,0:T(8,128)S(1)}, f32[1,72,256]{2,1,0:T(8,128)S(1)}, u32[]{:S(2)}, u32[]{:S(2)}) collective-permute-start(f32[1,72,256]{2,1,0:T(8,128)S(1)} %fusion.6), channel_id=1, source_target_pairs={{0,4},{1,5},{2,6},{3,7},{4,8},{5,9},{6,10},{7,11},{8,12},{9,13},{1... | collective-permute-start | bytes 221192 | tf_op jit(solution)/shard_map/ppermute | solution.py:56
  86.8 8.3 %collective-permute-start.22 = (f32[1,72,256]{2,1,0:T(8,128)S(1)}, f32[1,72,256]{2,1,0:T(8,128)S(1)}, u32[]{:S(2)}, u32[]{:S(2)}) collective-permute-start(f32[1,72,256]{2,1,0:T(8,128)S(1)} %get-tuple-element.90), channel_id=1, source_target_pairs={{0,20},{1,21},{2,22},{3,23},{4,24},{5,25},{6,26},{7,27},{8,28},{9,... | collective-permute-start | bytes 221192 | tf_op jit(solution)/shard_map/ppermute | solution.py:56
  86.9 9.3 %collective-permute-start.23 = (f32[1,72,256]{2,1,0:T(8,128)S(1)}, f32[1,72,256]{2,1,0:T(8,128)}, u32[]{:S(2)}, u32[]{:S(2)}) collective-permute-start(f32[1,72,256]{2,1,0:T(8,128)S(1)} %get-tuple-element.91), channel_id=1, source_target_pairs={{0,12},{1,13},{2,14},{3,15},{4,16},{5,17},{6,18},{7,19},{8,20},{9,... | collective-permute-start | bytes 221192 | tf_op jit(solution)/shard_map/ppermute | solution.py:56
  95.1 0.6 copy-start.7
  97.7 3.9 %collective-permute-start.24 = (f32[1,72,256]{2,1,0:T(8,128)}, f32[1,72,256]{2,1,0:T(8,128)S(1)}, u32[]{:S(2)}, u32[]{:S(2)}) collective-permute-start(f32[1,72,256]{2,1,0:T(8,128)} %get-tuple-element.89), channel_id=1, source_target_pairs={{0,128},{1,129},{2,130},{3,131},{4,132},{5,133},{6,134},{7,135},{8... | collective-permute-start | bytes 221192 | tf_op jit(solution)/shard_map/ppermute | solution.py:56
  97.7 4.9 %collective-permute-start.25 = (f32[1,72,256]{2,1,0:T(8,128)}, f32[1,72,256]{2,1,0:T(8,128)S(1)}, u32[]{:S(2)}, u32[]{:S(2)}) collective-permute-start(f32[1,72,256]{2,1,0:T(8,128)} %get-tuple-element.89), channel_id=1, source_target_pairs={{0,32},{1,33},{2,34},{3,35},{4,36},{5,37},{6,38},{7,39},{8,40},{9,... | collective-permute-start | bytes 221192 | tf_op jit(solution)/shard_map/ppermute | solution.py:56
  97.7 6.1 %collective-permute-start.26 = (f32[1,72,256]{2,1,0:T(8,128)}, f32[1,72,256]{2,1,0:T(8,128)S(1)}, u32[]{:S(2)}, u32[]{:S(2)}) collective-permute-start(f32[1,72,256]{2,1,0:T(8,128)} %get-tuple-element.89), channel_id=1, source_target_pairs={{0,160},{1,161},{2,162},{3,163},{4,164},{5,165},{6,166},{7,167},{8... | collective-permute-start | bytes 221192 | tf_op jit(solution)/shard_map/ppermute | solution.py:56
  103.9 20.9 %collective-permute-start.27 = (f32[4,72,256]{2,1,0:T(8,128)S(1)}, f32[4,72,256]{2,1,0:T(8,128)S(1)}, u32[]{:S(2)}, u32[]{:S(2)}) collective-permute-start(f32[4,72,256]{2,1,0:T(8,128)S(1)} %constant_dynamic-update-slice_fusion.8), channel_id=1, source_target_pairs={{0,1},{1,0},{2,3},{3,2},{4,5},{5,4},{6,7},{7,6},{8,9},{9,8},{10,11... | collective-permute-start | bytes 884744 | tf_op jit(solution)/shard_map/ppermute | solution.py:56
  104.0 20.8 %collective-permute-start.28 = (f32[4,72,256]{2,1,0:T(8,128)S(1)}, f32[4,72,256]{2,1,0:T(8,128)S(1)}, u32[]{:S(2)}, u32[]{:S(2)}) collective-permute-start(f32[4,72,256]{2,1,0:T(8,128)S(1)} %constant_dynamic-update-slice_fusion.8), channel_id=1, source_target_pairs={{0,2},{1,3},{2,0},{3,1},{4,6},{5,7},{6,4},{7,5},{8,10},{9,11},{10,... | collective-permute-start | bytes 884744 | tf_op jit(solution)/shard_map/ppermute | solution.py:56
  104.1 12.9 %collective-permute-start.29 = (f32[4,72,256]{2,1,0:T(8,128)S(1)}, f32[4,72,256]{2,1,0:T(8,128)S(1)}, u32[]{:S(2)}, u32[]{:S(2)}) collective-permute-start(f32[4,72,256]{2,1,0:T(8,128)S(1)} %constant_dynamic-update-slice_fusion.8), channel_id=1, source_target_pairs={{0,3},{1,2},{2,1},{3,0},{4,7},{5,6},{6,5},{7,4},{8,11},{9,10},{10,... | collective-permute-start | bytes 884744 | tf_op jit(solution)/shard_map/ppermute | solution.py:56
  111.0 14.4 %collective-permute-start.30 = (f32[4,72,256]{2,1,0:T(8,128)S(1)}, f32[4,72,256]{2,1,0:T(8,128)S(1)}, u32[]{:S(2)}, u32[]{:S(2)}) collective-permute-start(f32[4,72,256]{2,1,0:T(8,128)S(1)} %constant_dynamic-update-slice_fusion.8), channel_id=1, source_target_pairs={{0,64},{1,65},{2,66},{3,67},{4,68},{5,69},{6,70},{7,71},{8,72},{9,... | collective-permute-start | bytes 884744 | tf_op jit(solution)/shard_map/ppermute | solution.py:56
  117.0 9.8 %collective-permute-start.33 = (f32[4,72,256]{2,1,0:T(8,128)S(1)}, f32[4,72,256]{2,1,0:T(8,128)S(1)}, u32[]{:S(2)}, u32[]{:S(2)}) collective-permute-start(f32[4,72,256]{2,1,0:T(8,128)S(1)} %collective-permute-done.29), channel_id=1, source_target_pairs={{0,64},{1,65},{2,66},{3,67},{4,68},{5,69},{6,70},{7,71},{8,72},{9,... | collective-permute-start | bytes 884744 | tf_op jit(solution)/shard_map/ppermute | solution.py:56
  124.7 1.6 %collective-permute-start.31 = (f32[4,72,256]{2,1,0:T(8,128)S(1)}, f32[4,72,256]{2,1,0:T(8,128)S(1)}, u32[]{:S(2)}, u32[]{:S(2)}) collective-permute-start(f32[4,72,256]{2,1,0:T(8,128)S(1)} %collective-permute-done.27), channel_id=1, source_target_pairs={{0,64},{1,65},{2,66},{3,67},{4,68},{5,69},{6,70},{7,71},{8,72},{9,... | collective-permute-start | bytes 884744 | tf_op jit(solution)/shard_map/ppermute | solution.py:56
  124.8 2.0 %collective-permute-start.32 = (f32[4,72,256]{2,1,0:T(8,128)S(1)}, f32[4,72,256]{2,1,0:T(8,128)S(1)}, u32[]{:S(2)}, u32[]{:S(2)}) collective-permute-start(f32[4,72,256]{2,1,0:T(8,128)S(1)} %collective-permute-done.28), channel_id=1, source_target_pairs={{0,64},{1,65},{2,66},{3,67},{4,68},{5,69},{6,70},{7,71},{8,72},{9,... | collective-permute-start | bytes 884744 | tf_op jit(solution)/shard_map/ppermute | solution.py:56

commit v5 on v3

--- a/solution.py
+++ b/solution.py
@@ -234,6 +234,9 @@
     return pltpu.CompilerParams(dimension_semantics=("arbitrary",) * dims, vmem_limit_bytes=vmem_limit)
 
 
+order = (2, 1, 3)
+
+
 def tree(total, parts):
     return (total + parts[0]) + (parts[1] + parts[2])
 
@@ -241,7 +244,7 @@
 def placed_at(place, total, parts):
     size = total.shape[0]
     whole_value = jnp.zeros((4 * size,) + total.shape[1:], f32)
-    for k, part in enumerate([total] + parts):
+    for k, part in zip((0,) + order, [total] + parts):
         whole_value = lax.dynamic_update_slice(whole_value, part, ((place ^ k) * size, 0, 0))
     return whole_value
 
@@ -388,26 +391,26 @@
     core = place["core"]
     first = jnp.where(straight, place["x"], place["y"])
     second = jnp.where(straight, place["y"], place["x"])
-    halves = [keep[k] + send(away[k], swap_core) for k in (1, 2, 3, 0)]
-    parts = [send(half, first_axis[k]) for k, half in zip((1, 2, 3), halves)]
-    grid_grad = jnp.einsum("npu,wu->npw", grad_query, dst_weight, precision=lax.Precision.HIGH)
-    upper, lower, grid_grad = lax.optimization_barrier((upper, lower, grid_grad))
+    swapped = [send(away[k], swap_core) for k in order + (0,)]
+    halves = [keep[k] + part for k, part in zip(order, swapped)]
+    parts = [send(half, first_axis[k]) for k, half in zip(order, halves)]
+    upper, lower, last = lax.optimization_barrier((upper, lower, swapped[3]))
     from_prev = lax.ppermute(upper, "grid", up)
     from_next = lax.ppermute(lower, "grid", down)
-    *parts, grid_grad = lax.optimization_barrier((*parts, grid_grad))
-    total = tree(halves[3], parts)
-    parts = [send(total[k : k + 1], second_axis[k]) for k in (1, 2, 3)]
+    total = tree(keep[0] + last, parts)
+    parts = [send(total[k : k + 1], second_axis[k]) for k in order]
     *parts, from_prev, from_next = lax.optimization_barrier((*parts, from_prev, from_next))
     total = tree(total[:1], parts)
-    parts = [send(total, along_z[k]) for k in (1, 2, 3)]
+    total = tree(total, [send(total, along_z[k]) for k in order])
+    part = send(total, along_z[4])
+    grid_grad = jnp.einsum("npu,wu->npw", grad_query, dst_weight, precision=lax.Precision.HIGH)
     mesh_grad = jnp.einsum(
         "nru,wu->nrw", middle + from_prev + from_next, src_weight, precision=lax.Precision.HIGH
     )
-    *parts, mesh_grad = lax.optimization_barrier((*parts, mesh_grad))
-    total = tree(total, parts)
-    total = total + send(total, along_z[4])
-    total = placed_at(second, total, [send(total, second_axis[k]) for k in (1, 2, 3)])
-    parts = [total] + [send(total, first_axis[k]) for k in (1, 2, 3)]
+    part, grid_grad, mesh_grad = lax.optimization_barrier((part, grid_grad, mesh_grad))
+    total = total + part
+    total = placed_at(second, total, [send(total, second_axis[k]) for k in order])
+    parts = [total] + [send(total, first_axis[k]) for k in order]
     others = [send(part, swap_core) for part in parts]
     total = placed_at(first, parts[0], parts[1:]).reshape(1152, 256)
     other = placed_at(second, others[0], others[1:]).reshape(1152, 256)

time: 126 us -> 119 us (0.944)
  starting transfers between devices: 65.8 us -> 60.5 us
  waiting for transfers between devices: 29.4 us -> 27.1 us
  matrix products: 4.48 us -> 5.76 us
    ppermute x24, starting transfers between devices: 52.2 us -> 46.9 us  [send(): return lax.ppermute(value, axes, pairs)]
    ppermute x24, waiting for transfers between devices: 19.1 us -> 16.8 us  [send(): return lax.ppermute(value, axes, pairs)]
    dot_general x1, matrix products: 3.19 us -> 4.46 us  [body(): jnp.einsum('npu,wu->npw', grad_query, dst_weight, precision=lax.Precision...]
  transfers between devices with their start and end apart: 34 -> 34, of which waited for: 15 -> 15; matrix products, arithmetic and copies ran while one was open for 4% -> 5% of each run, Pallas kernels for 4% -> 4%
where the time goes in v5:
time: 119 us
  starting transfers between devices  60.5 us (51%)
  waiting for transfers between devices  27.1 us (23%)
  Pallas kernels  20.3 us (17%)
  matrix products  5.76 us (5%)
  local copies, waits for them, and re-layouts  3.23 us (3%)
    ppermute x24, starting transfers between devices, send(): return lax.ppermute(value, axes, pairs)  46.9 us
    ppermute x24, waiting for transfers between devices, send(): return lax.ppermute(value, axes, pairs)  16.8 us
    pallas_call x1, Pallas kernels, body(): pl.pallas_call(functools.partial(backward_kernel, tile, scale, loss_scale...  8.43 us
    pallas_call x1, Pallas kernels, body(): pl.pallas_call(functools.partial(forward_kernel, tile), grid_spec=pltpu.P...  5.81 us
    ppermute x3, waiting for transfers between devices, body(): lax.ppermute(parts[k], 'member', to_peer[k])  5.26 us
    ppermute x3, waiting for transfers between devices, body(): lax.ppermute(slopes[k], 'member', to_peer[k])  5.05 us
    pallas_call x1, Pallas kernels, body(): pl.pallas_call(query_kernel, in_specs=[me_spec, whole(), in_hbm, in_hbm,...  4.86 us
    dot_general x1, matrix products, body(): jnp.einsum('npu,wu->npw', grad_query, dst_weight, precision=lax.Precision...  4.46 us
  transfers between devices with their start and end apart: 34, of which 15 were waited for; matrix products, arithmetic and copies ran while one was open for 5% of the time, Pallas kernels for 4%

profile of v5, /device:TPU:1, one launch (start us, length us, event | category | flops | bytes accessed | tf_op | source)
XLA Modules:
  0.0 118.6 jit_solution(5166570331027042608)
XLA Ops:
  0.6 4.0 %collective-permute-start = (f32[2,32,512]{2,1,0:T(8,128)}, f32[2,32,512]{2,1,0:T(8,128)S(1)}, u32[]{:S(2)}, u32[]{:S(2)}) collective-permute-start(f32[2,32,512]{2,1,0:T(8,128)} %own.3), channel_id=1, source_target_pairs={{0,1},{1,2},{2,3},{3,4},{4,5},{5,6},{6,7},{7,8},{8,9},{9,10},{10,1... | collective-permute-start | bytes 393224 | tf_op jit(solution)/shard_map/ppermute | solution.py:272
  4.6 1.3 %collective-permute-start.1 = (f32[2,32,512]{2,1,0:T(8,128)}, f32[2,32,512]{2,1,0:T(8,128)S(1)}, u32[]{:S(2)}, u32[]{:S(2)}) collective-permute-start(f32[2,32,512]{2,1,0:T(8,128)} %own.3), channel_id=1, source_target_pairs={{1,0},{2,1},{3,2},{4,3},{5,4},{6,5},{7,6},{8,7},{9,8},{10,9},{11,1... | collective-permute-start | bytes 393224 | tf_op jit(solution)/shard_map/ppermute | solution.py:273
  6.0 4.9 %query.1 = (f32[2,512,512]{2,1,0:T(8,128)S(1)}, s32[512,8]{1,0:T(8,128)S(1)}, bf16[512,512]{1,0:T(8,128)(2,1)S(1)}, bf16[512,512]{1,0:T(8,128)(2,1)S(1)}) custom-call(s32[5]{0:T(128)S(1)} %stack.23.me, s32[4,512]{1,0:T(4,128)} %edges.3, f32[2,512,512]{2,1,0:T(8,128)} %features.3, f32[512,512]{1,0:T(8,128)} %weight.1, f32[512,512]{1,0:T(8,128)} %src_weight.1), custom_call_target="tpu_custom_call" | custom-call | tf_op jit(solution)/shard_map/query/pallas_call | solution.py:277
  10.9 5.8 %forward.1 = (f32[2,4,512,512]{3,2,1,0:T(8,128)S(1)}, f32[2,512,512]{2,1,0:T(8,128)S(1)}, f32[2,100,128]{2,1,0:T(8,128)S(1)}, f32[2,100,128]{2,1,0:T(8,128)S(1)}...) custom-call(s32[5]{0:T(128)S(1)} %stack.23.me, f32[2,512,512]{2,1,0:T(8,128)S(1)} %get-tuple-element.44.query, ...), custom_call_target="tpu_custom_call" | custom-call | tf_op jit(solution)/shard_map/forward/pallas_call | solution.py:306
  16.8 1.8 %collective-permute-start.2 = (f32[2,100,128]{2,1,0:T(8,128)S(1)}, f32[2,100,128]{2,1,0:T(8,128)S(1)}, u32[]{:S(2)}, u32[]{:S(2)}) collective-permute-start(f32[2,100,128]{2,1,0:T(8,128)S(1)} %get-tuple-element.49), channel_id=1, source_target_pairs={{0,64},{64,0},{128,192},{192,128},{1,65},{65,1},{129,193},{193,129... | collective-permute-start | bytes 307208 | tf_op jit(solution)/shard_map/ppermute | solution.py:335
  18.6 1.3 %collective-permute-start.3 = (f32[2,100,128]{2,1,0:T(8,128)S(1)}, f32[2,100,128]{2,1,0:T(8,128)S(1)}, u32[]{:S(2)}, u32[]{:S(2)}) collective-permute-start(f32[2,100,128]{2,1,0:T(8,128)S(1)} %get-tuple-element.50), channel_id=1, source_target_pairs={{0,128},{64,192},{128,0},{192,64},{1,129},{65,193},{129,1},{193,65... | collective-permute-start | bytes 307208 | tf_op jit(solution)/shard_map/ppermute | solution.py:335
  19.9 0.4 collective-permute-start.4
  20.3 2.8 %collective-permute-done.3.part2 = f32[2,100,128]{2,1,0:T(8,128)S(1)} collective-permute-done((f32[2,100,128]{2,1,0:T(8,128)S(1)}, f32[2,100,128]{2,1,0:T(8,128)S(1)}, u32[]{:S(2)}, u32[]{:S(2)}) %collective-permute-start.3) | collective-permute-done | bytes 102432 | tf_op jit(solution)/shard_map/ppermute | solution.py:335
  23.1 2.5 %collective-permute-done.4.part3 = f32[2,100,128]{2,1,0:T(8,128)S(1)} collective-permute-done((f32[2,100,128]{2,1,0:T(8,128)S(1)}, f32[2,100,128]{2,1,0:T(8,128)S(1)}, u32[]{:S(2)}, u32[]{:S(2)}) %collective-permute-start.4) | collective-permute-done | bytes 102432 | tf_op jit(solution)/shard_map/ppermute | solution.py:335
  25.6 1.2 %score.1 = (f32[2,100,128]{2,1,0:T(8,128)S(1)}, f32[2,100,128]{2,1,0:T(8,128)S(1)}, f32[2,100,128]{2,1,0:T(8,128)S(1)}, f32[2,100,128]{2,1,0:T(8,128)S(1)}, f32[8,128]{1,0:T(8,128)S(1)}) custom-call(s32[5]{0:T(128)S(1)} %stack.23.me, f32[2,100,128]{2,1,0:T(8,128)S(1)} %get-tuple-element.48.part0, f32[2,100,128]{2,1,0:T(8,128)S(1)} %collective-permute-done.2.part1, ...), custom_call_target="tpu_custom_call" | custom-call | tf_op jit(solution)/shard_map/score/pallas_call | solution.py:336
  27.1 1.3 %collective-permute-start.6 = (f32[2,100,128]{2,1,0:T(8,128)S(1)}, f32[2,100,128]{2,1,0:T(8,128)S(1)}, u32[]{:S(2)}, u32[]{:S(2)}) collective-permute-start(f32[2,100,128]{2,1,0:T(8,128)S(1)} %get-tuple-element.54), channel_id=1, source_target_pairs={{0,128},{64,192},{128,0},{192,64},{1,129},{65,193},{129,1},{193,65... | collective-permute-start | bytes 307208 | tf_op jit(solution)/shard_map/ppermute | solution.py:349
  28.4 0.6 collective-permute-start.7
  29.0 2.3 %collective-permute-done.6.part2 = f32[2,100,128]{2,1,0:T(8,128)S(1)} collective-permute-done((f32[2,100,128]{2,1,0:T(8,128)S(1)}, f32[2,100,128]{2,1,0:T(8,128)S(1)}, u32[]{:S(2)}, u32[]{:S(2)}) %collective-permute-start.6) | collective-permute-done | bytes 102432 | tf_op jit(solution)/shard_map/ppermute | solution.py:349
  31.3 2.7 %collective-permute-done.7.part3 = f32[2,100,128]{2,1,0:T(8,128)S(1)} collective-permute-done((f32[2,100,128]{2,1,0:T(8,128)S(1)}, f32[2,100,128]{2,1,0:T(8,128)S(1)}, u32[]{:S(2)}, u32[]{:S(2)}) %collective-permute-start.7) | collective-permute-done | bytes 102432 | tf_op jit(solution)/shard_map/ppermute | solution.py:349
  34.0 8.4 %backward.1 = (f32[2,512,512]{2,1,0:T(8,128)S(1)}, f32[2,32,512]{2,1,0:T(8,128)S(1)}, f32[2,32,512]{2,1,0:T(8,128)S(1)}, f32[2,32,512]{2,1,0:T(8,128)S(1)}, f32[...) custom-call(s32[5]{0:T(128)S(1)} %stack.23.me, ...), custom_call_target="tpu_custom_call" | custom-call | tf_op jit(solution)/shard_map/backward/pallas_call | solution.py:357
  42.8 0.3 collective-permute-start.13
  43.6 0.6 collective-permute-done.9
  44.2 9.8 %collective-permute-start.10 = (f32[4,72,256]{2,1,0:T(8,128)S(1)}, f32[4,72,256]{2,1,0:T(8,128)S(1)}, u32[]{:S(2)}, u32[]{:S(2)}) collective-permute-start(f32[4,72,256]{2,1,0:T(8,128)S(1)} %add.93), channel_id=1, source_target_pairs={{0,2},{1,3},{2,0},{3,1},{4,6},{5,7},{6,4},{7,5},{8,10},{9,11},{10,... | collective-permute-start | bytes 884744 | tf_op jit(solution)/shard_map/ppermute | solution.py:53
  54.1 0.5 collective-permute-start.14
  54.6 0.4 collective-permute-start.12
  55.0 1.3 %collective-permute-start.18 = (f32[2,32,512]{2,1,0:T(8,128)S(1)}, f32[2,32,512]{2,1,0:T(8,128)S(1)}, u32[]{:S(2)}, u32[]{:S(2)}) collective-permute-start(f32[2,32,512]{2,1,0:T(8,128)S(1)} %get-tuple-element.70), channel_id=1, source_target_pairs={{0,1},{1,2},{2,3},{3,4},{4,5},{5,6},{6,7},{7,8},{8,9},{9,10},{10,1... | collective-permute-start | bytes 393224 | tf_op jit(solution)/shard_map/ppermute | solution.py:398
  56.3 1.3 %collective-permute-start.19 = (f32[2,32,512]{2,1,0:T(8,128)S(1)}, f32[2,32,512]{2,1,0:T(8,128)S(1)}, u32[]{:S(2)}, u32[]{:S(2)}) collective-permute-start(f32[2,32,512]{2,1,0:T(8,128)S(1)} %get-tuple-element.71), channel_id=1, source_target_pairs={{1,0},{2,1},{3,2},{4,3},{5,4},{6,5},{7,6},{8,7},{9,8},{10,9},{11,1... | collective-permute-start | bytes 393224 | tf_op jit(solution)/shard_map/ppermute | solution.py:399
  57.6 0.6 collective-permute-done.10
  58.2 3.1 %collective-permute-done.14 = f32[4,72,256]{2,1,0:T(8,128)S(1)} collective-permute-done((f32[4,72,256]{2,1,0:T(8,128)S(1)}, f32[4,72,256]{2,1,0:T(8,128)S(1)}, u32[]{:S(2)}, u32[]{:S(2)}) %collective-permute-start.14) | collective-permute-done | bytes 294944 | tf_op jit(solution)/shard_map/ppermute | solution.py:53
  61.3 0.7 collective-permute-done.12
  62.3 3.1 %collective-permute-start.17 = (f32[1,72,256]{2,1,0:T(8,128)S(1)}, f32[1,72,256]{2,1,0:T(8,128)S(1)}, u32[]{:S(2)}, u32[]{:S(2)}) collective-permute-start(f32[1,72,256]{2,1,0:T(8,128)S(1)} %get-tuple-element.86), channel_id=1, source_target_pairs={{0,160},{1,161},{2,162},{3,163},{4,164},{5,165},{6,166},{7,167},{8... | collective-permute-start | bytes 221192 | tf_op jit(solution)/shard_map/ppermute | solution.py:53
  65.5 2.3 %collective-permute-done.15 = f32[1,72,256]{2,1,0:T(8,128)S(1)} collective-permute-done((f32[1,72,256]{2,1,0:T(8,128)S(1)}, f32[1,72,256]{2,1,0:T(8,128)S(1)}, u32[]{:S(2)}, u32[]{:S(2)}) %collective-permute-start.15) | collective-permute-done | bytes 73760 | tf_op jit(solution)/shard_map/ppermute | solution.py:53
  67.8 2.1 %collective-permute-done.17 = f32[1,72,256]{2,1,0:T(8,128)S(1)} collective-permute-done((f32[1,72,256]{2,1,0:T(8,128)S(1)}, f32[1,72,256]{2,1,0:T(8,128)S(1)}, u32[]{:S(2)}, u32[]{:S(2)}) %collective-permute-start.17) | collective-permute-done | bytes 73760 | tf_op jit(solution)/shard_map/ppermute | solution.py:53
  70.0 2.7 %collective-permute-start.21 = (f32[1,72,256]{2,1,0:T(8,128)S(1)}, f32[1,72,256]{2,1,0:T(8,128)S(1)}, u32[]{:S(2)}, u32[]{:S(2)}) collective-permute-start(f32[1,72,256]{2,1,0:T(8,128)S(1)} %fusion.6), channel_id=1, source_target_pairs={{0,4},{1,5},{2,6},{3,7},{4,0},{5,1},{6,2},{7,3},{8,12},{9,13},{10,... | collective-permute-start | bytes 221192 | tf_op jit(solution)/shard_map/ppermute | solution.py:53
  72.7 0.8 collective-permute-start.22
  73.5 4.5 %fusion.2 = f32[2,512,512]{2,1,0:T(8,128)} fusion(f32[2,512,512]{2,1,0:T(8,128)S(1)} %get-tuple-element.75, f32[512,512]{1,0:T(8,128)} %weight.1), kind=kOutput, calls=%fused_computation.3 | convolution fusion | flops 1610612736 | bytes 5242880 | tf_op jit(solution)/shard_map/npu,wu->npw/dot_general | solution.py:406
  78.0 3.8 %collective-permute-start.23 = (f32[1,72,256]{2,1,0:T(8,128)S(1)}, f32[1,72,256]{2,1,0:T(8,128)S(1)}, u32[]{:S(2)}, u32[]{:S(2)}) collective-permute-start(f32[1,72,256]{2,1,0:T(8,128)S(1)} %add_add_fusion.1), channel_id=1, source_target_pairs={{0,16},{1,17},{2,18},{3,19},{4,20},{5,21},{6,22},{7,23},{8,24},{9,... | collective-permute-start | bytes 221192 | tf_op jit(solution)/shard_map/ppermute | solution.py:53
  81.8 1.3 %fusion = f32[2,32,512]{2,1,0:T(8,128)} fusion(f32[512,512]{1,0:T(8,128)S(1)} %copy-done.5, f32[2,32,512]{2,1,0:T(8,128)S(1)} %collective-permute-done.19, f32[2,32,512]{2,1,0:T(8,128)S(1)} %get-tuple-element.76, f32[2,32,512]{2,1,0:T(8,128)S(1)} %collective-permute-done.18), kind=kOutput, calls=%fused_computation.1 | convolution fusion | flops 100728832 | bytes 1572864 | tf_op jit(solution)/shard_map/nru,wu->nrw/dot_general | solution.py:407
  83.1 2.1 %collective-permute-done.23 = f32[1,72,256]{2,1,0:T(8,128)S(1)} collective-permute-done((f32[1,72,256]{2,1,0:T(8,128)S(1)}, f32[1,72,256]{2,1,0:T(8,128)S(1)}, u32[]{:S(2)}, u32[]{:S(2)}) %collective-permute-start.23) | collective-permute-done | bytes 73760 | tf_op jit(solution)/shard_map/ppermute | solution.py:53
  85.4 3.7 %collective-permute-start.25 = (f32[1,72,256]{2,1,0:T(8,128)S(1)}, f32[1,72,256]{2,1,0:T(8,128)S(1)}, u32[]{:S(2)}, u32[]{:S(2)}) collective-permute-start(f32[1,72,256]{2,1,0:T(8,128)S(1)} %get-tuple-element.83), channel_id=1, source_target_pairs={{0,128},{1,129},{2,130},{3,131},{4,132},{5,133},{6,134},{7,135},{8... | collective-permute-start | bytes 221192 | tf_op jit(solution)/shard_map/ppermute | solution.py:53
  89.1 0.9 collective-permute-done.24
  90.1 1.9 %collective-permute-done.25 = f32[1,72,256]{2,1,0:T(8,128)S(1)} collective-permute-done((f32[1,72,256]{2,1,0:T(8,128)S(1)}, f32[1,72,256]{2,1,0:T(8,128)S(1)}, u32[]{:S(2)}, u32[]{:S(2)}) %collective-permute-start.25) | collective-permute-done | bytes 73760 | tf_op jit(solution)/shard_map/ppermute | solution.py:53
  92.0 1.6 %collective-permute-done.26 = f32[1,72,256]{2,1,0:T(8,128)S(1)} collective-permute-done((f32[1,72,256]{2,1,0:T(8,128)S(1)}, f32[1,72,256]{2,1,0:T(8,128)S(1)}, u32[]{:S(2)}, u32[]{:S(2)}) %collective-permute-start.26) | collective-permute-done | bytes 73760 | tf_op jit(solution)/shard_map/ppermute | solution.py:53
  93.6 5.0 %collective-permute-start.27 = (f32[4,72,256]{2,1,0:T(8,128)S(1)}, f32[4,72,256]{2,1,0:T(8,128)S(1)}, u32[]{:S(2)}, u32[]{:S(2)}) collective-permute-start(f32[4,72,256]{2,1,0:T(8,128)S(1)} %constant_dynamic-update-slice_fusion.8), channel_id=1, source_target_pairs={{0,2},{1,3},{2,0},{3,1},{4,6},{5,7},{6,4},{7,5},{8,10},{9,11},{10,... | collective-permute-start | bytes 884744 | tf_op jit(solution)/shard_map/ppermute | solution.py:53
  98.6 0.6 collective-permute-start.29
  99.2 7.8 %collective-permute-start.30 = (f32[4,72,256]{2,1,0:T(8,128)S(1)}, f32[4,72,256]{2,1,0:T(8,128)S(1)}, u32[]{:S(2)}, u32[]{:S(2)}) collective-permute-start(f32[4,72,256]{2,1,0:T(8,128)S(1)} %constant_dynamic-update-slice_fusion.8), channel_id=1, source_target_pairs={{0,64},{1,65},{2,66},{3,67},{4,68},{5,69},{6,70},{7,71},{8,72},{9,... | collective-permute-start | bytes 884744 | tf_op jit(solution)/shard_map/ppermute | solution.py:53
  107.1 4.1 %collective-permute-start.31 = (f32[4,72,256]{2,1,0:T(8,128)S(1)}, f32[4,72,256]{2,1,0:T(8,128)S(1)}, u32[]{:S(2)}, u32[]{:S(2)}) collective-permute-start(f32[4,72,256]{2,1,0:T(8,128)S(1)} %collective-permute-done.27), channel_id=1, source_target_pairs={{0,64},{1,65},{2,66},{3,67},{4,68},{5,69},{6,70},{7,71},{8,72},{9,... | collective-permute-start | bytes 884744 | tf_op jit(solution)/shard_map/ppermute | solution.py:53
  111.5 2.8 %collective-permute-start.33 = (f32[4,72,256]{2,1,0:T(8,128)S(1)}, f32[4,72,256]{2,1,0:T(8,128)S(1)}, u32[]{:S(2)}, u32[]{:S(2)}) collective-permute-start(f32[4,72,256]{2,1,0:T(8,128)S(1)} %collective-permute-done.29), channel_id=1, source_target_pairs={{0,64},{1,65},{2,66},{3,67},{4,68},{5,69},{6,70},{7,71},{8,72},{9,... | collective-permute-start | bytes 884744 | tf_op jit(solution)/shard_map/ppermute | solution.py:53
  114.6 0.9 collective-permute-done.33
  115.5 0.4 maximum_select_fusion
  115.9 1.5 %fusion.7 = (f32[512,512]{1,0:T(8,128)}, f32[512,512]{1,0:T(8,128)}) fusion(f32[1152,512]{1,0:T(8,128)S(1)} %maximum_select_fusion), kind=kLoop, calls=%fused_computation.24 | loop fusion | bytes 4194304 | tf_op jit(solution)/shard_map/slice | solution.py:422
  117.4 0.7 slice_bitcast_fusion
  118.1 0.5 slice.36
  (65 shorter events, 2.6 us)
Async XLA Ops:
  0.6 10.2 %collective-permute-start = (f32[2,32,512]{2,1,0:T(8,128)}, f32[2,32,512]{2,1,0:T(8,128)S(1)}, u32[]{:S(2)}, u32[]{:S(2)}) collective-permute-start(f32[2,32,512]{2,1,0:T(8,128)} %own.3), channel_id=1, source_target_pairs={{0,1},{1,2},{2,3},{3,4},{4,5},{5,6},{6,7},{7,8},{8,9},{9,10},{10,1... | collective-permute-start | bytes 393224 | tf_op jit(solution)/shard_map/ppermute | solution.py:272
  4.6 6.3 %collective-permute-start.1 = (f32[2,32,512]{2,1,0:T(8,128)}, f32[2,32,512]{2,1,0:T(8,128)S(1)}, u32[]{:S(2)}, u32[]{:S(2)}) collective-permute-start(f32[2,32,512]{2,1,0:T(8,128)} %own.3), channel_id=1, source_target_pairs={{1,0},{2,1},{3,2},{4,3},{5,4},{6,5},{7,6},{8,7},{9,8},{10,9},{11,1... | collective-permute-start | bytes 393224 | tf_op jit(solution)/shard_map/ppermute | solution.py:273
  6.0 4.9 %copy-start.1 = (f32[512,100]{0,1:T(8,128)S(1)}, f32[512,100]{0,1:T(8,128)}, u32[]{:S(2)}) copy-start(f32[512,100]{0,1:T(8,128)} %param.13) | copy-start | bytes 614404
  6.0 4.9 %copy-start.2 = (f32[2,32,512]{2,1,0:T(8,128)S(1)}, f32[2,32,512]{2,1,0:T(8,128)}, u32[]{:S(2)}) copy-start(f32[2,32,512]{2,1,0:T(8,128)} %own.3) | copy-start | bytes 393220
  10.9 14.6 %copy-start.3 = (f32[100,512]{1,0:T(8,128)S(1)}, f32[100,512]{1,0:T(8,128)}, u32[]{:S(2)}) copy-start(f32[100,512]{1,0:T(8,128)} %targets.1) | copy-start | bytes 614404
  10.9 23.1 %copy-start = (f32[2,512,512]{2,1,0:T(8,128)S(1)}, f32[2,512,512]{2,1,0:T(8,128)}, u32[]{:S(2)}) copy-start(f32[2,512,512]{2,1,0:T(8,128)} %features.3) | copy-start | bytes 6291460
  10.9 23.1 %copy-start.4 = (s32[4,512]{1,0:T(4,128)S(1)}, s32[4,512]{1,0:T(4,128)}, u32[]{:S(2)}) copy-start(s32[4,512]{1,0:T(4,128)} %edges.3) | copy-start | bytes 24580
  16.8 3.5 %collective-permute-start.2 = (f32[2,100,128]{2,1,0:T(8,128)S(1)}, f32[2,100,128]{2,1,0:T(8,128)S(1)}, u32[]{:S(2)}, u32[]{:S(2)}) collective-permute-start(f32[2,100,128]{2,1,0:T(8,128)S(1)} %get-tuple-element.49), channel_id=1, source_target_pairs={{0,64},{64,0},{128,192},{192,128},{1,65},{65,1},{129,193},{193,129... | collective-permute-start | bytes 307208 | tf_op jit(solution)/shard_map/ppermute | solution.py:335
  18.6 4.5 %collective-permute-start.3 = (f32[2,100,128]{2,1,0:T(8,128)S(1)}, f32[2,100,128]{2,1,0:T(8,128)S(1)}, u32[]{:S(2)}, u32[]{:S(2)}) collective-permute-start(f32[2,100,128]{2,1,0:T(8,128)S(1)} %get-tuple-element.50), channel_id=1, source_target_pairs={{0,128},{64,192},{128,0},{192,64},{1,129},{65,193},{129,1},{193,65... | collective-permute-start | bytes 307208 | tf_op jit(solution)/shard_map/ppermute | solution.py:335
  19.9 5.7 %collective-permute-start.4 = (f32[2,100,128]{2,1,0:T(8,128)S(1)}, f32[2,100,128]{2,1,0:T(8,128)S(1)}, u32[]{:S(2)}, u32[]{:S(2)}) collective-permute-start(f32[2,100,128]{2,1,0:T(8,128)S(1)} %get-tuple-element.51), channel_id=1, source_target_pairs={{0,192},{64,128},{128,64},{192,0},{1,193},{65,129},{129,65},{193,1... | collective-permute-start | bytes 307208 | tf_op jit(solution)/shard_map/ppermute | solution.py:335
  26.8 2.2 %collective-permute-start.5 = (f32[2,100,128]{2,1,0:T(8,128)S(1)}, f32[2,100,128]{2,1,0:T(8,128)S(1)}, u32[]{:S(2)}, u32[]{:S(2)}) collective-permute-start(f32[2,100,128]{2,1,0:T(8,128)S(1)} %get-tuple-element.53), channel_id=1, source_target_pairs={{0,64},{64,0},{128,192},{192,128},{1,65},{65,1},{129,193},{193,129... | collective-permute-start | bytes 307208 | tf_op jit(solution)/shard_map/ppermute | solution.py:349
  27.1 4.3 %collective-permute-start.6 = (f32[2,100,128]{2,1,0:T(8,128)S(1)}, f32[2,100,128]{2,1,0:T(8,128)S(1)}, u32[]{:S(2)}, u32[]{:S(2)}) collective-permute-start(f32[2,100,128]{2,1,0:T(8,128)S(1)} %get-tuple-element.54), channel_id=1, source_target_pairs={{0,128},{64,192},{128,0},{192,64},{1,129},{65,193},{129,1},{193,65... | collective-permute-start | bytes 307208 | tf_op jit(solution)/shard_map/ppermute | solution.py:349
  28.4 5.7 %collective-permute-start.7 = (f32[2,100,128]{2,1,0:T(8,128)S(1)}, f32[2,100,128]{2,1,0:T(8,128)S(1)}, u32[]{:S(2)}, u32[]{:S(2)}) collective-permute-start(f32[2,100,128]{2,1,0:T(8,128)S(1)} %get-tuple-element.55), channel_id=1, source_target_pairs={{0,192},{64,128},{128,64},{192,0},{1,193},{65,129},{129,65},{193,1... | collective-permute-start | bytes 307208 | tf_op jit(solution)/shard_map/ppermute | solution.py:349
  42.5 1.7 %collective-permute-start.9 = (f32[4,72,256]{2,1,0:T(8,128)S(1)}, f32[4,72,256]{2,1,0:T(8,128)S(1)}, u32[]{:S(2)}, u32[]{:S(2)}) collective-permute-start(f32[4,72,256]{2,1,0:T(8,128)S(1)} %get-tuple-element.65), channel_id=1, source_target_pairs={{0,64},{1,65},{2,66},{3,67},{4,68},{5,69},{6,70},{7,71},{8,72},{9,... | collective-permute-start | bytes 884744 | tf_op jit(solution)/shard_map/ppermute | solution.py:53
  42.8 11.3 %collective-permute-start.13 = (f32[4,72,256]{2,1,0:T(8,128)S(1)}, f32[4,72,256]{2,1,0:T(8,128)S(1)}, u32[]{:S(2)}, u32[]{:S(2)}) collective-permute-start(f32[4,72,256]{2,1,0:T(8,128)S(1)} %get-tuple-element.69), channel_id=1, source_target_pairs={{0,64},{1,65},{2,66},{3,67},{4,68},{5,69},{6,70},{7,71},{8,72},{9,... | collective-permute-start | bytes 884744 | tf_op jit(solution)/shard_map/ppermute | solution.py:53
  43.1 11.5 %collective-permute-start.11 = (f32[4,72,256]{2,1,0:T(8,128)S(1)}, f32[4,72,256]{2,1,0:T(8,128)S(1)}, u32[]{:S(2)}, u32[]{:S(2)}) collective-permute-start(f32[4,72,256]{2,1,0:T(8,128)S(1)} %get-tuple-element.67), channel_id=1, source_target_pairs={{0,64},{1,65},{2,66},{3,67},{4,68},{5,69},{6,70},{7,71},{8,72},{9,... | collective-permute-start | bytes 884744 | tf_op jit(solution)/shard_map/ppermute | solution.py:53
  43.4 11.6 %collective-permute-start.8 = (f32[4,72,256]{2,1,0:T(8,128)S(1)}, f32[4,72,256]{2,1,0:T(8,128)S(1)}, u32[]{:S(2)}, u32[]{:S(2)}) collective-permute-start(f32[4,72,256]{2,1,0:T(8,128)S(1)} %get-tuple-element.62), channel_id=1, source_target_pairs={{0,64},{1,65},{2,66},{3,67},{4,68},{5,69},{6,70},{7,71},{8,72},{9,... | collective-permute-start | bytes 884744 | tf_op jit(solution)/shard_map/ppermute | solution.py:53
  44.2 14.0 %collective-permute-start.10 = (f32[4,72,256]{2,1,0:T(8,128)S(1)}, f32[4,72,256]{2,1,0:T(8,128)S(1)}, u32[]{:S(2)}, u32[]{:S(2)}) collective-permute-start(f32[4,72,256]{2,1,0:T(8,128)S(1)} %add.93), channel_id=1, source_target_pairs={{0,2},{1,3},{2,0},{3,1},{4,6},{5,7},{6,4},{7,5},{8,10},{9,11},{10,... | collective-permute-start | bytes 884744 | tf_op jit(solution)/shard_map/ppermute | solution.py:53
  54.1 7.2 %collective-permute-start.14 = (f32[4,72,256]{2,1,0:T(8,128)S(1)}, f32[4,72,256]{2,1,0:T(8,128)S(1)}, u32[]{:S(2)}, u32[]{:S(2)}) collective-permute-start(f32[4,72,256]{2,1,0:T(8,128)S(1)} %add.96), channel_id=1, source_target_pairs={{0,3},{1,2},{2,1},{3,0},{4,7},{5,6},{6,5},{7,4},{8,11},{9,10},{10,... | collective-permute-start | bytes 884744 | tf_op jit(solution)/shard_map/ppermute | solution.py:53
  54.6 7.4 %collective-permute-start.12 = (f32[4,72,256]{2,1,0:T(8,128)S(1)}, f32[4,72,256]{2,1,0:T(8,128)S(1)}, u32[]{:S(2)}, u32[]{:S(2)}) collective-permute-start(f32[4,72,256]{2,1,0:T(8,128)S(1)} %add.95), channel_id=1, source_target_pairs={{0,1},{1,0},{2,3},{3,2},{4,5},{5,4},{6,7},{7,6},{8,9},{9,8},{10,11... | collective-permute-start | bytes 884744 | tf_op jit(solution)/shard_map/ppermute | solution.py:53
  55.0 10.5 %collective-permute-start.18 = (f32[2,32,512]{2,1,0:T(8,128)S(1)}, f32[2,32,512]{2,1,0:T(8,128)S(1)}, u32[]{:S(2)}, u32[]{:S(2)}) collective-permute-start(f32[2,32,512]{2,1,0:T(8,128)S(1)} %get-tuple-element.70), channel_id=1, source_target_pairs={{0,1},{1,2},{2,3},{3,4},{4,5},{5,6},{6,7},{7,8},{8,9},{9,10},{10,1... | collective-permute-start | bytes 393224 | tf_op jit(solution)/shard_map/ppermute | solution.py:398
  56.3 9.2 %collective-permute-start.19 = (f32[2,32,512]{2,1,0:T(8,128)S(1)}, f32[2,32,512]{2,1,0:T(8,128)S(1)}, u32[]{:S(2)}, u32[]{:S(2)}) collective-permute-start(f32[2,32,512]{2,1,0:T(8,128)S(1)} %get-tuple-element.71), channel_id=1, source_target_pairs={{1,0},{2,1},{3,2},{4,3},{5,4},{6,5},{7,6},{8,7},{9,8},{10,9},{11,1... | collective-permute-start | bytes 393224 | tf_op jit(solution)/shard_map/ppermute | solution.py:399
  62.1 5.7 %collective-permute-start.15 = (f32[1,72,256]{2,1,0:T(8,128)S(1)}, f32[1,72,256]{2,1,0:T(8,128)S(1)}, u32[]{:S(2)}, u32[]{:S(2)}) collective-permute-start(f32[1,72,256]{2,1,0:T(8,128)S(1)} %get-tuple-element.88), channel_id=1, source_target_pairs={{0,32},{1,33},{2,34},{3,35},{4,36},{5,37},{6,38},{7,39},{8,40},{9,... | collective-permute-start | bytes 221192 | tf_op jit(solution)/shard_map/ppermute | solution.py:53
  62.2 5.6 %collective-permute-start.16 = (f32[1,72,256]{2,1,0:T(8,128)S(1)}, f32[1,72,256]{2,1,0:T(8,128)S(1)}, u32[]{:S(2)}, u32[]{:S(2)}) collective-permute-start(f32[1,72,256]{2,1,0:T(8,128)S(1)} %get-tuple-element.87), channel_id=1, source_target_pairs={{0,128},{1,129},{2,130},{3,131},{4,132},{5,133},{6,134},{7,135},{8... | collective-permute-start | bytes 221192 | tf_op jit(solution)/shard_map/ppermute | solution.py:53
  62.3 7.5 %collective-permute-start.17 = (f32[1,72,256]{2,1,0:T(8,128)S(1)}, f32[1,72,256]{2,1,0:T(8,128)S(1)}, u32[]{:S(2)}, u32[]{:S(2)}) collective-permute-start(f32[1,72,256]{2,1,0:T(8,128)S(1)} %get-tuple-element.86), channel_id=1, source_target_pairs={{0,160},{1,161},{2,162},{3,163},{4,164},{5,165},{6,166},{7,167},{8... | collective-permute-start | bytes 221192 | tf_op jit(solution)/shard_map/ppermute | solution.py:53
  69.9 8.1 %collective-permute-start.20 = (f32[1,72,256]{2,1,0:T(8,128)S(1)}, f32[1,72,256]{2,1,0:T(8,128)S(1)}, u32[]{:S(2)}, u32[]{:S(2)}) collective-permute-start(f32[1,72,256]{2,1,0:T(8,128)S(1)} %fusion.6), channel_id=1, source_target_pairs={{0,8},{1,9},{2,10},{3,11},{4,12},{5,13},{6,14},{7,15},{8,0},{9,1},... | collective-permute-start | bytes 221192 | tf_op jit(solution)/shard_map/ppermute | solution.py:53
  70.0 8.0 %collective-permute-start.21 = (f32[1,72,256]{2,1,0:T(8,128)S(1)}, f32[1,72,256]{2,1,0:T(8,128)S(1)}, u32[]{:S(2)}, u32[]{:S(2)}) collective-permute-start(f32[1,72,256]{2,1,0:T(8,128)S(1)} %fusion.6), channel_id=1, source_target_pairs={{0,4},{1,5},{2,6},{3,7},{4,0},{5,1},{6,2},{7,3},{8,12},{9,13},{10,... | collective-permute-start | bytes 221192 | tf_op jit(solution)/shard_map/ppermute | solution.py:53
  72.7 5.3 %collective-permute-start.22 = (f32[1,72,256]{2,1,0:T(8,128)S(1)}, f32[1,72,256]{2,1,0:T(8,128)S(1)}, u32[]{:S(2)}, u32[]{:S(2)}) collective-permute-start(f32[1,72,256]{2,1,0:T(8,128)S(1)} %fusion.6), channel_id=1, source_target_pairs={{0,12},{1,13},{2,14},{3,15},{4,8},{5,9},{6,10},{7,11},{8,4},{9,5},... | collective-permute-start | bytes 221192 | tf_op jit(solution)/shard_map/ppermute | solution.py:53
  73.5 8.3 %copy-start.5 = (f32[512,512]{1,0:T(8,128)S(1)}, f32[512,512]{1,0:T(8,128)}, u32[]{:S(2)}) copy-start(f32[512,512]{1,0:T(8,128)} %src_weight.1) | copy-start | bytes 3145732
  78.0 7.2 %collective-permute-start.23 = (f32[1,72,256]{2,1,0:T(8,128)S(1)}, f32[1,72,256]{2,1,0:T(8,128)S(1)}, u32[]{:S(2)}, u32[]{:S(2)}) collective-permute-start(f32[1,72,256]{2,1,0:T(8,128)S(1)} %add_add_fusion.1), channel_id=1, source_target_pairs={{0,16},{1,17},{2,18},{3,19},{4,20},{5,21},{6,22},{7,23},{8,24},{9,... | collective-permute-start | bytes 221192 | tf_op jit(solution)/shard_map/ppermute | solution.py:53
  85.3 4.8 %collective-permute-start.24 = (f32[1,72,256]{2,1,0:T(8,128)S(1)}, f32[1,72,256]{2,1,0:T(8,128)S(1)}, u32[]{:S(2)}, u32[]{:S(2)}) collective-permute-start(f32[1,72,256]{2,1,0:T(8,128)S(1)} %get-tuple-element.83), channel_id=1, source_target_pairs={{0,32},{1,33},{2,34},{3,35},{4,36},{5,37},{6,38},{7,39},{8,40},{9,... | collective-permute-start | bytes 221192 | tf_op jit(solution)/shard_map/ppermute | solution.py:53
  85.4 6.6 %collective-permute-start.25 = (f32[1,72,256]{2,1,0:T(8,128)S(1)}, f32[1,72,256]{2,1,0:T(8,128)S(1)}, u32[]{:S(2)}, u32[]{:S(2)}) collective-permute-start(f32[1,72,256]{2,1,0:T(8,128)S(1)} %get-tuple-element.83), channel_id=1, source_target_pairs={{0,128},{1,129},{2,130},{3,131},{4,132},{5,133},{6,134},{7,135},{8... | collective-permute-start | bytes 221192 | tf_op jit(solution)/shard_map/ppermute | solution.py:53
  89.1 4.4 %collective-permute-start.26 = (f32[1,72,256]{2,1,0:T(8,128)S(1)}, f32[1,72,256]{2,1,0:T(8,128)S(1)}, u32[]{:S(2)}, u32[]{:S(2)}) collective-permute-start(f32[1,72,256]{2,1,0:T(8,128)S(1)} %get-tuple-element.83), channel_id=1, source_target_pairs={{0,160},{1,161},{2,162},{3,163},{4,164},{5,165},{6,166},{7,167},{8... | collective-permute-start | bytes 221192 | tf_op jit(solution)/shard_map/ppermute | solution.py:53
  93.6 13.5 %collective-permute-start.27 = (f32[4,72,256]{2,1,0:T(8,128)S(1)}, f32[4,72,256]{2,1,0:T(8,128)S(1)}, u32[]{:S(2)}, u32[]{:S(2)}) collective-permute-start(f32[4,72,256]{2,1,0:T(8,128)S(1)} %constant_dynamic-update-slice_fusion.8), channel_id=1, source_target_pairs={{0,2},{1,3},{2,0},{3,1},{4,6},{5,7},{6,4},{7,5},{8,10},{9,11},{10,... | collective-permute-start | bytes 884744 | tf_op jit(solution)/shard_map/ppermute | solution.py:53
  98.6 12.6 %collective-permute-start.28 = (f32[4,72,256]{2,1,0:T(8,128)S(1)}, f32[4,72,256]{2,1,0:T(8,128)S(1)}, u32[]{:S(2)}, u32[]{:S(2)}) collective-permute-start(f32[4,72,256]{2,1,0:T(8,128)S(1)} %constant_dynamic-update-slice_fusion.8), channel_id=1, source_target_pairs={{0,1},{1,0},{2,3},{3,2},{4,5},{5,4},{6,7},{7,6},{8,9},{9,8},{10,11... | collective-permute-start | bytes 884744 | tf_op jit(solution)/shard_map/ppermute | solution.py:53
  98.6 12.9 %collective-permute-start.29 = (f32[4,72,256]{2,1,0:T(8,128)S(1)}, f32[4,72,256]{2,1,0:T(8,128)S(1)}, u32[]{:S(2)}, u32[]{:S(2)}) collective-permute-start(f32[4,72,256]{2,1,0:T(8,128)S(1)} %constant_dynamic-update-slice_fusion.8), channel_id=1, source_target_pairs={{0,3},{1,2},{2,1},{3,0},{4,7},{5,6},{6,5},{7,4},{8,11},{9,10},{10,... | collective-permute-start | bytes 884744 | tf_op jit(solution)/shard_map/ppermute | solution.py:53
  99.2 15.2 %collective-permute-start.30 = (f32[4,72,256]{2,1,0:T(8,128)S(1)}, f32[4,72,256]{2,1,0:T(8,128)S(1)}, u32[]{:S(2)}, u32[]{:S(2)}) collective-permute-start(f32[4,72,256]{2,1,0:T(8,128)S(1)} %constant_dynamic-update-slice_fusion.8), channel_id=1, source_target_pairs={{0,64},{1,65},{2,66},{3,67},{4,68},{5,69},{6,70},{7,71},{8,72},{9,... | collective-permute-start | bytes 884744 | tf_op jit(solution)/shard_map/ppermute | solution.py:53
  107.1 7.4 %collective-permute-start.31 = (f32[4,72,256]{2,1,0:T(8,128)S(1)}, f32[4,72,256]{2,1,0:T(8,128)S(1)}, u32[]{:S(2)}, u32[]{:S(2)}) collective-permute-start(f32[4,72,256]{2,1,0:T(8,128)S(1)} %collective-permute-done.27), channel_id=1, source_target_pairs={{0,64},{1,65},{2,66},{3,67},{4,68},{5,69},{6,70},{7,71},{8,72},{9,... | collective-permute-start | bytes 884744 | tf_op jit(solution)/shard_map/ppermute | solution.py:53
  111.2 3.3 %collective-permute-start.32 = (f32[4,72,256]{2,1,0:T(8,128)S(1)}, f32[4,72,256]{2,1,0:T(8,128)S(1)}, u32[]{:S(2)}, u32[]{:S(2)}) collective-permute-start(f32[4,72,256]{2,1,0:T(8,128)S(1)} %collective-permute-done.28), channel_id=1, source_target_pairs={{0,64},{1,65},{2,66},{3,67},{4,68},{5,69},{6,70},{7,71},{8,72},{9,... | collective-permute-start | bytes 884744 | tf_op jit(solution)/shard_map/ppermute | solution.py:53
  111.5 4.0 %collective-permute-start.33 = (f32[4,72,256]{2,1,0:T(8,128)S(1)}, f32[4,72,256]{2,1,0:T(8,128)S(1)}, u32[]{:S(2)}, u32[]{:S(2)}) collective-permute-start(f32[4,72,256]{2,1,0:T(8,128)S(1)} %collective-permute-done.29), channel_id=1, source_target_pairs={{0,64},{1,65},{2,66},{3,67},{4,68},{5,69},{6,70},{7,71},{8,72},{9,... | collective-permute-start | bytes 884744 | tf_op jit(solution)/shard_map/ppermute | solution.py:53

commit v6 on v5

--- a/solution.py
+++ b/solution.py
@@ -93,24 +93,10 @@
     src_high[...], src_low[...] = split(0.5 * held_src[...])
 
 
-def forward_kernel(points, me, query, edges, before, own, after, src_high, src_low, out_weight,
-                   slope, summed, part0, part1, part2, part3, nodes, fields):
-    member, tile = pl.program_id(0), pl.program_id(1)
-    tiles = pl.num_programs(1)
-    rows = own.shape[1]
-
-    @pl.when((member == 0) & (tile == 0))
-    def _():
-        nodes[...] = jnp.zeros_like(nodes)
-        ext = jnp.concatenate([side[n] for n in range(2) for side in (before, own, after)], axis=0)
-        high, low = split(dot3(split(ext), (src_high[...], src_low[...]), NN))
-        for n in range(2):
-            at = slice(n * 3 * rows, (n + 1) * 3 * rows)
-            nodes[n, 0 : 3 * rows] = high[at]
-            nodes[n, 128 : 128 + 3 * rows] = low[at]
-
+def forward(me, member, query, edges, nodes, out_weight, slope, summed, same, flipped):
+    points = query.shape[1]
+    columns = lax.broadcasted_iota(jnp.int32, (points, 256), 1) & 127
     local = edges[...]
-    columns = lax.broadcasted_iota(jnp.int32, (points, 256), 1) & 127
     total = None
     for k in range(4):
         hot = jnp.where(local[:, k : k + 1] == columns, 1.0, 0.0).astype(bf16)
@@ -121,13 +107,33 @@
         slope[0, k] = (curve + 0.5) + active * (0.5 - curve)
         total = active if total is None else total + active
     summed[0] = total
-    weight = split(out_weight[...])
-    fields[:, pl.ds(pl.multiple_of(tile * points, 128), points)] = dot3(weight, split(total), NT)
-
-    @pl.when(tile == tiles - 1)
+    fields = dot3(split(out_weight[...]), split(total), NT)
+    left, right = fields[:, 0:128], fields[:, 128:256]
+    even = (me[0] & 1) == 0
+    same[member] = jnp.where(even, left, right)
+    flipped[member] = jnp.where(even, right, left)
+
+
+def far_forward_kernel(me, query, edges, before, own, after, src_high, src_low, out_weight,
+                       slope, summed, same, flipped, nodes):
+    member = pl.program_id(0)
+    rows = own.shape[1]
+
+    @pl.when(member == 0)
     def _():
-        for k, part in enumerate((part0, part1, part2, part3)):
-            part[member] = fields[:, pl.ds(pl.multiple_of((me[0] ^ k) * 128, 128), 128)]
+        nodes[...] = jnp.zeros_like(nodes)
+        ext = jnp.concatenate([side[n] for n in range(2) for side in (before, own, after)], axis=0)
+        high, low = split(dot3(split(ext), (src_high[...], src_low[...]), NN))
+        for n in range(2):
+            at = slice(n * 3 * rows, (n + 1) * 3 * rows)
+            nodes[n, 0 : 3 * rows] = high[at]
+            nodes[n, 128 : 128 + 3 * rows] = low[at]
+
+    forward(me, member, query, edges, nodes, out_weight, slope, summed, same, flipped)
+
+
+def near_forward_kernel(me, query, edges, nodes, out_weight, slope, summed, same, flipped):
+    forward(me, pl.program_id(0), query, edges, nodes, out_weight, slope, summed, same, flipped)
 
 
 def score_kernel(me, part0, part1, part2, part3, targets, out0, out1, out2, out3, loss):
@@ -170,29 +176,17 @@
     loss[...] = jnp.broadcast_to(near * (1.0 / count) - factor * far, loss.shape)
 
 
-def backward_kernel(points, scale, loss_scale, me, part0, part1, part2, part3, loss, slope, summed, features,
-                    edges, before, own, after, out_weight,
-                    grad_query, lower, middle, upper, *rest):
-    keep, away, (grad_ext, slopes, sums) = rest[:4], rest[4:8], rest[8:]
-    member, tile = pl.program_id(0), pl.program_id(1)
-    members, tiles = pl.num_programs(0), pl.num_programs(1)
-    rows = own.shape[1]
-    width = features.shape[2]
-    vars_rows = out_weight.shape[0]
-
-    @pl.when((member == 0) & (tile == 0))
-    def _():
-        sums[...] = jnp.zeros_like(sums)
-        grad_ext[...] = jnp.zeros_like(grad_ext)
-        for k, part in enumerate((part0, part1, part2, part3)):
-            for n in range(2):
-                slopes[n, :, pl.ds(pl.multiple_of((me[0] ^ k) * 128, 128), 128)] = part[n]
-
-    here = split(slopes[member, :, pl.ds(pl.multiple_of(tile * points, 128), points)])
+def backward(me, member, same, flipped, slope, summed, features, edges, out_weight,
+             grad_query, grad_ext, dst_sum, out_sum):
+    points = summed.shape[1]
+    even = (me[0] & 1) == 0
+    one, two = same[member], flipped[member]
+    left, right = jnp.where(even, one, two), jnp.where(even, two, one)
+    here = split(jnp.concatenate([left, right], axis=1))
     back = dot3(here, split(out_weight[...]), TN)
-    sums[2 * width : 2 * width + vars_rows] += dot3(here, split(summed[0]), NN)
-    local = edges[...] - (me[1] - 1) * rows
-    nodes = lax.broadcasted_iota(jnp.int32, (3 * rows, points), 0)
+    out_sum[...] += dot3(here, split(summed[0]), NN)
+    local = edges[...] - (me[1] - 1) * node_rows
+    nodes = lax.broadcasted_iota(jnp.int32, (3 * node_rows, points), 0)
     scattered = None
     slope_sum = None
     for k in range(4):
@@ -207,9 +201,44 @@
     grad_ext[member] += scattered
     into_query = back * slope_sum
     grad_query[0] = into_query
-    sums[width : 2 * width] += dot3(split(features[0]), split(into_query), TN)
-
-    @pl.when((member == members - 1) & (tile == tiles - 1))
+    dst_sum[...] += dot3(split(features[0]), split(into_query), TN)
+
+
+def near_backward_kernel(me, same, flipped, slope, summed, features, edges, out_weight,
+                         grad_query, grad_ext, dst_sum, out_sum):
+    member = pl.program_id(0)
+
+    @pl.when(member == 0)
+    def _():
+        for total in (grad_ext, dst_sum, out_sum):
+            total[...] = jnp.zeros_like(total)
+
+    backward(me, member, same, flipped, slope, summed, features, edges, out_weight,
+             grad_query, grad_ext, dst_sum, out_sum)
+
+
+def far_backward_kernel(scale, loss_scale, me, same, flipped, slope, summed, features, edges, out_weight,
+                        near_ext, near_dst, near_out, loss, before, own, after,
+                        grad_query, lower, middle, upper, *rest):
+    keep, away, (grad_ext, sums) = rest[:4], rest[4:8], rest[8:]
+    member = pl.program_id(0)
+    rows = own.shape[1]
+    width = features.shape[2]
+    count_vars = out_weight.shape[0]
+    dst_sum = sums.at[width : 2 * width]
+    out_sum = sums.at[2 * width : 2 * width + count_vars]
+
+    @pl.when(member == 0)
+    def _():
+        sums[2 * width :] = jnp.zeros((sums.shape[0] - 2 * width, width), f32)
+        grad_ext[...] = near_ext[...]
+        dst_sum[...] = near_dst[...]
+        out_sum[...] = near_out[...]
+
+    backward(me, member, same, flipped, slope, summed, features, edges, out_weight,
+             grad_query, grad_ext, dst_sum, out_sum)
+
+    @pl.when(member == pl.num_programs(0) - 1)
     def _():
         ext = jnp.concatenate([side[n] for n in range(2) for side in (before, own, after)], axis=0)
         grads = jnp.concatenate([grad_ext[0], grad_ext[1]], axis=0)
@@ -301,38 +330,67 @@
         pltpu.with_memory_space_constraint(src_weight, pltpu.HBM),
     )
 
-    tile = 512
+    half = points // 2
+
+    def near(me):
+        return me[0] >> 1
+
+    def far(me):
+        return 1 - (me[0] >> 1)
+
+    def rows_of(side):
+        return pl.BlockSpec((1, half, width), lambda n, me: (n, side(me), 0))
+
+    halves = pl.BlockSpec((1, half, width), lambda n, me: (n, 0, 0))
+    half_slopes = pl.BlockSpec((1, 4, half, width), lambda n, me: (n, 0, 0, 0))
     part_shape = jax.ShapeDtypeStruct((members, count_vars, 128), f32)
-    slope, summed, *parts = pl.pallas_call(
-        functools.partial(forward_kernel, tile),
-        grid_spec=pltpu.PrefetchScalarGridSpec(
-            num_scalar_prefetch=1,
-            grid=(members, points // tile),
-            in_specs=[
-                pl.BlockSpec((1, tile, width), lambda n, t, me: (n, t, 0)),
-                pl.BlockSpec((tile, 8), lambda n, t, me: (t, 0)),
-                whole(), whole(), whole(), whole(), whole(), whole(),
-            ],
-            out_specs=[
-                pl.BlockSpec((1, 4, tile, width), lambda n, t, me: (n, 0, t, 0)),
-                pl.BlockSpec((1, tile, width), lambda n, t, me: (n, t, 0)),
-            ] + [whole()] * 4,
-            scratch_shapes=[
-                pltpu.VMEM((members, 256, width), bf16),
-                pltpu.VMEM((count_vars, points), f32),
-            ],
-        ),
-        out_shape=[
-            jax.ShapeDtypeStruct((members, 4, points, width), f32),
-            jax.ShapeDtypeStruct((members, points, width), f32),
-        ] + [part_shape] * 4,
-        compiler_params=params(2),
-        name="forward",
-        interpret=interpret,
+    half_shape = jax.ShapeDtypeStruct((members, half, width), f32)
+    slopes_shape = jax.ShapeDtypeStruct((members, 4, half, width), f32)
+
+    def call(kernel, name, work, in_specs, out_specs, out_shape, scratch=()):
+        return pl.pallas_call(
+            kernel,
+            grid_spec=pltpu.PrefetchScalarGridSpec(
+                num_scalar_prefetch=1,
+                grid=(members,),
+                in_specs=in_specs,
+                out_specs=out_specs,
+                scratch_shapes=list(scratch),
+            ),
+            out_shape=out_shape,
+            compiler_params=params(1),
+            cost_estimate=pl.CostEstimate(
+                flops=work, bytes_accessed=4 * members * points * width, transcendentals=0
+            ),
+            name=name,
+            interpret=interpret,
+        )
+
+    forward_work = 2 * members * half * width * (4 * 256 + 3 * count_vars + 1024)
+    backward_work = 2 * members * half * width * (8 * 256 + 6 * count_vars + 3 * width)
+    far_slope, far_summed, part2, part3, nodes = call(
+        far_forward_kernel,
+        "far_forward",
+        forward_work,
+        [rows_of(far), pl.BlockSpec((half, 8), lambda n, me: (far(me), 0))] + [whole()] * 6,
+        [half_slopes, halves] + [whole()] * 3,
+        [slopes_shape, half_shape, part_shape, part_shape]
+        + [jax.ShapeDtypeStruct((members, 256, width), bf16)],
     )(me, query, edges_t, before, mesh_features, after, src_high, src_low, out_weight)
-
     to_peer = [[(i, i ^ k) for i in range(4)] for k in range(4)]
-    parts = [parts[0]] + [lax.ppermute(parts[k], "member", to_peer[k]) for k in (1, 2, 3)]
+    part2 = lax.ppermute(part2, "member", to_peer[2])
+    part3 = lax.ppermute(part3, "member", to_peer[3])
+    near_slope, near_summed, part0, part1 = call(
+        near_forward_kernel,
+        "near_forward",
+        forward_work,
+        [rows_of(near), pl.BlockSpec((half, 8), lambda n, me: (near(me), 0))] + [whole()] * 2,
+        [half_slopes, halves] + [whole()] * 2,
+        [slopes_shape, half_shape, part_shape, part_shape],
+    )(me, query, edges_t, nodes, out_weight)
+    part0, part1, part2, part3 = lax.optimization_barrier((part0, part1, part2, part3))
+    part1 = lax.ppermute(part1, "member", to_peer[1])
+
     *slopes, loss = pl.pallas_call(
         score_kernel,
         grid_spec=pltpu.PrefetchScalarGridSpec(
@@ -345,47 +403,52 @@
         compiler_params=params(1),
         name="score",
         interpret=interpret,
-    )(me, *parts, targets)
-    slopes = [slopes[0]] + [lax.ppermute(slopes[k], "member", to_peer[k]) for k in (1, 2, 3)]
+    )(me, part0, part1, part2, part3, targets)
 
     total_members = lax.axis_size("member") * members
     scale = 1.0 / (total_members * points * slabs) ** 0.5
     loss_scale = 1.0 / (points * slabs * count_vars)
+    ext_shape = jax.ShapeDtypeStruct((members, 3 * rows, width), f32)
+    out_sum_shape = jax.ShapeDtypeStruct((count_vars, width), f32)
+    side = jax.ShapeDtypeStruct((members, rows, width), f32)
     chunks = jax.ShapeDtypeStruct((4, 72, 256), f32)
-    side = jax.ShapeDtypeStruct((members, rows, width), f32)
-    tile = 256
-    grad_query, lower, middle, upper, *parts = pl.pallas_call(
-        functools.partial(backward_kernel, tile, scale, loss_scale),
-        grid_spec=pltpu.PrefetchScalarGridSpec(
-            num_scalar_prefetch=1,
-            grid=(members, points // tile),
-            in_specs=[whole()] * 5 + [
-                pl.BlockSpec((1, 4, tile, width), lambda n, t, me: (n, 0, t, 0)),
-                pl.BlockSpec((1, tile, width), lambda n, t, me: (n, t, 0)),
-                pl.BlockSpec((1, tile, width), lambda n, t, me: (n, t, 0)),
-                pl.BlockSpec((4, tile), lambda n, t, me: (0, t)),
-                whole(), whole(), whole(), whole(),
-            ],
-            out_specs=[
-                pl.BlockSpec((1, tile, width), lambda n, t, me: (n, t, 0)),
-                whole(), whole(), whole(),
-            ] + [whole()] * 8,
-            scratch_shapes=[
-                pltpu.VMEM((members, 3 * rows, width), f32),
-                pltpu.VMEM((members, count_vars, points), f32),
-                pltpu.VMEM((1152, width), f32),
-            ],
-        ),
-        out_shape=[
-            jax.ShapeDtypeStruct((members, points, width), f32),
-            side,
-            side,
-            side,
-        ] + [chunks] * 8,
-        compiler_params=params(2),
-        name="backward",
-        interpret=interpret,
-    )(me, *slopes, loss, slope, summed, grid_features, edges, before, mesh_features, after, out_weight)
+
+    def backward_specs(which):
+        return [whole()] * 2 + [
+            half_slopes,
+            halves,
+            rows_of(which),
+            pl.BlockSpec((4, half), lambda n, me: (0, which(me))),
+            whole(),
+        ]
+
+    slope1 = lax.ppermute(slopes[1], "member", to_peer[1])
+    slope2 = lax.ppermute(slopes[2], "member", to_peer[2])
+    slope3 = lax.ppermute(slopes[3], "member", to_peer[3])
+    near_grad, near_ext, near_dst, near_out = call(
+        near_backward_kernel,
+        "near_backward",
+        backward_work,
+        backward_specs(near),
+        [halves] + [whole()] * 3,
+        [half_shape, ext_shape, jax.ShapeDtypeStruct((width, width), f32), out_sum_shape],
+    )(me, slopes[0], slope1, near_slope, near_summed, grid_features, edges, out_weight)
+    slope2, slope3, near_dst = lax.optimization_barrier((slope2, slope3, near_dst))
+    far_grad, lower, middle, upper, *parts = call(
+        functools.partial(far_backward_kernel, scale, loss_scale),
+        "far_backward",
+        backward_work,
+        backward_specs(far) + [whole()] * 7,
+        [halves] + [whole()] * 11,
+        [half_shape] + [side] * 3 + [chunks] * 8,
+        [pltpu.VMEM((members, 3 * rows, width), f32), pltpu.VMEM((1152, width), f32)],
+    )(me, slope2, slope3, far_slope, far_summed, grid_features, edges, out_weight,
+      near_ext, near_dst, near_out, loss, before, mesh_features, after)
+    grad_query = jnp.where(
+        member < 2,
+        jnp.concatenate([near_grad, far_grad], axis=1),
+        jnp.concatenate([far_grad, near_grad], axis=1),
+    )
 
     keep, away = parts[:4], parts[4:]
     core = place["core"]

time: 119 us -> 115 us (0.966)
  waiting for transfers between devices: 27.1 us -> 21.1 us
  Pallas kernels: 20.3 us -> 22 us
    ppermute x6, waiting for transfers between devices: 10.3 us -> 3.51 us  [the longest x1 1.35 us: body(): part3 = lax.ppermute(part3, 'member', to_peer[3])]
    pallas_call x2 -> x4, Pallas kernels: 14.2 us -> 15.9 us  [the longest x1 4.58 us: body(): call(functools.partial(far_backward_kernel, scale, loss_scale), 'far_back...]
  transfers between devices with their start and end apart: 34 -> 34, of which waited for: 15 -> 15; matrix products, arithmetic and copies ran while one was open for 5% -> 6% of each run, Pallas kernels for 4% -> 11%
where the time goes in v6:
time: 115 us
  starting transfers between devices  61.2 us (53%)
  Pallas kernels  22 us (19%)
  waiting for transfers between devices  21.1 us (18%)
  matrix products  5.78 us (5%)
  local copies, waits for them, and re-layouts  3.23 us (3%)
    ppermute x24, starting transfers between devices, send(): return lax.ppermute(value, axes, pairs)  47.3 us
    ppermute x24, waiting for transfers between devices, send(): return lax.ppermute(value, axes, pairs)  17.6 us
    pallas_call x1, Pallas kernels, body(): pl.pallas_call(query_kernel, in_specs=[me_spec, whole(), in_hbm, in_hbm,...  4.86 us
    pallas_call x1, Pallas kernels, body(): call(functools.partial(far_backward_kernel, scale, loss_scale), 'far_back...  4.58 us
    dot_general x1, matrix products, body(): jnp.einsum('npu,wu->npw', grad_query, dst_weight, precision=lax.Precision...  4.48 us
    pallas_call x1, Pallas kernels, body(): call(far_forward_kernel, 'far_forward', forward_work, [rows_of(far), pl.B...  3.96 us
    ppermute x1, starting transfers between devices, body(): before = lax.ppermute(mesh_features, 'grid', up)  3.95 us
    pallas_call x1, Pallas kernels, body(): call(near_backward_kernel, 'near_backward', backward_work, backward_specs...  3.95 us
  transfers between devices with their start and end apart: 34, of which 15 were waited for; matrix products, arithmetic and copies ran while one was open for 6% of the time, Pallas kernels for 11%

profile of v6, /device:TPU:1, one launch (start us, length us, event | category | flops | bytes accessed | tf_op | source)
XLA Modules:
  0.0 115.0 jit_solution(2439109015180098546)
XLA Ops:
  0.6 4.0 %collective-permute-start = (f32[2,32,512]{2,1,0:T(8,128)}, f32[2,32,512]{2,1,0:T(8,128)S(1)}, u32[]{:S(2)}, u32[]{:S(2)}) collective-permute-start(f32[2,32,512]{2,1,0:T(8,128)} %own.3), channel_id=1, source_target_pairs={{0,1},{1,2},{2,3},{3,4},{4,5},{5,6},{6,7},{7,8},{8,9},{9,10},{10,1... | collective-permute-start | bytes 393224 | tf_op jit(solution)/shard_map/ppermute | solution.py:301
  4.6 1.3 %collective-permute-start.1 = (f32[2,32,512]{2,1,0:T(8,128)}, f32[2,32,512]{2,1,0:T(8,128)S(1)}, u32[]{:S(2)}, u32[]{:S(2)}) collective-permute-start(f32[2,32,512]{2,1,0:T(8,128)} %own.3), channel_id=1, source_target_pairs={{1,0},{2,1},{3,2},{4,3},{5,4},{6,5},{7,6},{8,7},{9,8},{10,9},{11,1... | collective-permute-start | bytes 393224 | tf_op jit(solution)/shard_map/ppermute | solution.py:302
  6.0 4.9 %query.1 = (f32[2,512,512]{2,1,0:T(8,128)S(1)}, s32[512,8]{1,0:T(8,128)S(1)}, bf16[512,512]{1,0:T(8,128)(2,1)S(1)}, bf16[512,512]{1,0:T(8,128)(2,1)S(1)}) custom-call(s32[5]{0:T(128)S(1)} %stack.23.me, s32[4,512]{1,0:T(4,128)} %edges.5, f32[2,512,512]{2,1,0:T(8,128)} %features.5, f32[512,512]{1,0:T(8,128)} %weight.1, f32[512,512]{1,0:T(8,128)} %src_weight.1), custom_call_target="tpu_custom_call" | custom-call | tf_op jit(solution)/shard_map/query/pallas_call | solution.py:306
  10.9 4.0 %far_forward.1 = (f32[2,4,256,512]{3,2,1,0:T(8,128)S(1)}, f32[2,256,512]{2,1,0:T(8,128)S(1)}, f32[2,100,128]{2,1,0:T(8,128)S(1)}, f32[2,100,128]{2,1,0:T(8,128)S(1)}, bf16[2,256,512]{2,1,0:T(8,128)(2,1)S(1)}) custom-call(s32[5]{0:T(128)S(1)} %stack.23.me, f32[2,512,512]{2,1,0:T(8,128)S(1)} %get-tuple-element.58.query, s32[512,8]{1,0:T(8,128)S(1)} %get-tuple-element.59.edges, ...), custom_call_target="tpu_custom_call" | custom-call | flops 1231028224 | bytes 2097152 | tf_op jit(solution)/shard_map/far_forward/pallas_call | solution.py:371
  14.9 1.4 %collective-permute-start.2 = (f32[2,100,128]{2,1,0:T(8,128)S(1)}, f32[2,100,128]{2,1,0:T(8,128)S(1)}, u32[]{:S(2)}, u32[]{:S(2)}) collective-permute-start(f32[2,100,128]{2,1,0:T(8,128)S(1)} %get-tuple-element.65), channel_id=1, source_target_pairs={{0,128},{64,192},{128,0},{192,64},{1,129},{65,193},{129,1},{193,65... | collective-permute-start | bytes 307208 | tf_op jit(solution)/shard_map/ppermute | solution.py:381
  16.3 2.1 %collective-permute-start.3 = (f32[2,100,128]{2,1,0:T(8,128)S(1)}, f32[2,100,128]{2,1,0:T(8,128)S(1)}, u32[]{:S(2)}, u32[]{:S(2)}) collective-permute-start(f32[2,100,128]{2,1,0:T(8,128)S(1)} %get-tuple-element.66), channel_id=1, source_target_pairs={{0,192},{64,128},{128,64},{192,0},{1,193},{65,129},{129,65},{193,1... | collective-permute-start | bytes 307208 | tf_op jit(solution)/shard_map/ppermute | solution.py:382
  18.3 3.4 %near_forward.1 = (f32[2,4,256,512]{3,2,1,0:T(8,128)S(1)}, f32[2,256,512]{2,1,0:T(8,128)S(1)}, f32[2,100,128]{2,1,0:T(8,128)S(1)}, f32[2,100,128]{2,1,0:T(8,128)S(1)}) custom-call(s32[5]{0:T(128)S(1)} %stack.23.me, f32[2,512,512]{2,1,0:T(8,128)S(1)} %get-tuple-element.58.query, s32[512,8]{1,0:T(8,128)S(1)} %get-tuple-element.59.edges, ...), custom_call_target="tpu_custom_call" | custom-call | flops 1231028224 | bytes 2097152 | tf_op jit(solution)/shard_map/near_forward/pallas_call | solution.py:383
  21.8 1.3 %collective-permute-done.3.part3 = f32[2,100,128]{2,1,0:T(8,128)S(1)} collective-permute-done((f32[2,100,128]{2,1,0:T(8,128)S(1)}, f32[2,100,128]{2,1,0:T(8,128)S(1)}, u32[]{:S(2)}, u32[]{:S(2)}) %collective-permute-start.3) | collective-permute-done | bytes 102432 | tf_op jit(solution)/shard_map/ppermute | solution.py:382
  23.1 0.4 collective-permute-start.4
  23.5 1.0 collective-permute-done.4.part1
  24.5 1.2 %score.1 = (f32[2,100,128]{2,1,0:T(8,128)S(1)}, f32[2,100,128]{2,1,0:T(8,128)S(1)}, f32[2,100,128]{2,1,0:T(8,128)S(1)}, f32[2,100,128]{2,1,0:T(8,128)S(1)}, f32[8,128]{1,0:T(8,128)S(1)}) custom-call(s32[5]{0:T(128)S(1)} %stack.23.me, f32[2,100,128]{2,1,0:T(8,128)S(1)} %get-tuple-element.67.part0, f32[2,100,128]{2,1,0:T(8,128)S(1)} %collective-permute-done.4.part1, ...), custom_call_target="tpu_custom_call" | custom-call | tf_op jit(solution)/shard_map/score/pallas_call | solution.py:394
  25.7 0.4 collective-permute-start.7
  26.1 0.8 collective-permute-start.5
  26.9 1.0 collective-permute-start.6
  27.9 3.9 %near_backward.1 = (f32[2,256,512]{2,1,0:T(8,128)S(1)}, f32[2,96,512]{2,1,0:T(8,128)S(1)}, f32[512,512]{1,0:T(8,128)S(1)}, f32[100,512]{1,0:T(8,128)S(1)}) custom-call(s32[5]{0:T(128)S(1)} %stack.23.me, f32[2,100,128]{2,1,0:T(8,128)S(1)} %get-tuple-element.73.same, f32[2,100,128]{2,1,0:T(8,128)S(1)} %collective-permute-done.7.flipped, ...), custom_call_target="tpu_custom_call" | custom-call | flops 2193620992 | bytes 2097152 | tf_op jit(solution)/shard_map/near_backward/pallas_call | solution.py:428
  31.9 1.2 %collective-permute-done.6.flipped = f32[2,100,128]{2,1,0:T(8,128)S(1)} collective-permute-done((f32[2,100,128]{2,1,0:T(8,128)S(1)}, f32[2,100,128]{2,1,0:T(8,128)S(1)}, u32[]{:S(2)}, u32[]{:S(2)}) %collective-permute-start.6) | collective-permute-done | bytes 102432 | tf_op jit(solution)/shard_map/ppermute | solution.py:427
  33.1 4.6 %far_backward.1 = (f32[2,256,512]{2,1,0:T(8,128)S(1)}, f32[2,32,512]{2,1,0:T(8,128)S(1)}, f32[2,32,512]{2,1,0:T(8,128)S(1)}, f32[2,32,512]{2,1,0:T(8,128)S(1)}, ...) custom-call(s32[5]{0:T(128)S(1)} %stack.23.me, ...), custom_call_target="tpu_custom_call" | custom-call | flops 2193620992 | bytes 2097152 | tf_op jit(solution)/shard_map/far_backward/pallas_call | solution.py:437
  37.9 0.4 collective-permute-start.13
  38.4 0.4 collective-permute-start.8
  38.8 0.6 collective-permute-done.9
  39.4 9.5 %collective-permute-start.10 = (f32[4,72,256]{2,1,0:T(8,128)S(1)}, f32[4,72,256]{2,1,0:T(8,128)S(1)}, u32[]{:S(2)}, u32[]{:S(2)}) collective-permute-start(f32[4,72,256]{2,1,0:T(8,128)S(1)} %add.93), channel_id=1, source_target_pairs={{0,2},{1,3},{2,0},{3,1},{4,6},{5,7},{6,4},{7,5},{8,10},{9,11},{10,... | collective-permute-start | bytes 884744 | tf_op jit(solution)/shard_map/ppermute | solution.py:53
  49.1 0.4 collective-permute-start.12
  49.5 1.3 %collective-permute-start.18 = (f32[2,32,512]{2,1,0:T(8,128)S(1)}, f32[2,32,512]{2,1,0:T(8,128)S(1)}, u32[]{:S(2)}, u32[]{:S(2)}) collective-permute-start(f32[2,32,512]{2,1,0:T(8,128)S(1)} %get-tuple-element.97), channel_id=1, source_target_pairs={{0,1},{1,2},{2,3},{3,4},{4,5},{5,6},{6,7},{7,8},{8,9},{9,10},{10,1... | collective-permute-start | bytes 393224 | tf_op jit(solution)/shard_map/ppermute | solution.py:461
  50.8 1.3 %collective-permute-start.19 = (f32[2,32,512]{2,1,0:T(8,128)S(1)}, f32[2,32,512]{2,1,0:T(8,128)S(1)}, u32[]{:S(2)}, u32[]{:S(2)}) collective-permute-start(f32[2,32,512]{2,1,0:T(8,128)S(1)} %get-tuple-element.98), channel_id=1, source_target_pairs={{1,0},{2,1},{3,2},{4,3},{5,4},{6,5},{7,6},{8,7},{9,8},{10,9},{11,1... | collective-permute-start | bytes 393224 | tf_op jit(solution)/shard_map/ppermute | solution.py:462
  52.1 0.9 collective-permute-done.10
  53.1 3.1 %collective-permute-done.14 = f32[4,72,256]{2,1,0:T(8,128)S(1)} collective-permute-done((f32[4,72,256]{2,1,0:T(8,128)S(1)}, f32[4,72,256]{2,1,0:T(8,128)S(1)}, u32[]{:S(2)}, u32[]{:S(2)}) %collective-permute-start.14) | collective-permute-done | bytes 294944 | tf_op jit(solution)/shard_map/ppermute | solution.py:53
  56.9 3.1 %collective-permute-start.17 = (f32[1,72,256]{2,1,0:T(8,128)S(1)}, f32[1,72,256]{2,1,0:T(8,128)S(1)}, u32[]{:S(2)}, u32[]{:S(2)}) collective-permute-start(f32[1,72,256]{2,1,0:T(8,128)S(1)} %get-tuple-element.114), channel_id=1, source_target_pairs={{0,160},{1,161},{2,162},{3,163},{4,164},{5,165},{6,166},{7,167},{8... | collective-permute-start | bytes 221192 | tf_op jit(solution)/shard_map/ppermute | solution.py:53
  60.0 2.3 %collective-permute-done.15 = f32[1,72,256]{2,1,0:T(8,128)S(1)} collective-permute-done((f32[1,72,256]{2,1,0:T(8,128)S(1)}, f32[1,72,256]{2,1,0:T(8,128)S(1)}, u32[]{:S(2)}, u32[]{:S(2)}) %collective-permute-start.15) | collective-permute-done | bytes 73760 | tf_op jit(solution)/shard_map/ppermute | solution.py:53
  62.4 2.4 %collective-permute-done.17 = f32[1,72,256]{2,1,0:T(8,128)S(1)} collective-permute-done((f32[1,72,256]{2,1,0:T(8,128)S(1)}, f32[1,72,256]{2,1,0:T(8,128)S(1)}, u32[]{:S(2)}, u32[]{:S(2)}) %collective-permute-start.17) | collective-permute-done | bytes 73760 | tf_op jit(solution)/shard_map/ppermute | solution.py:53
  64.9 2.7 %collective-permute-start.21 = (f32[1,72,256]{2,1,0:T(8,128)S(1)}, f32[1,72,256]{2,1,0:T(8,128)S(1)}, u32[]{:S(2)}, u32[]{:S(2)}) collective-permute-start(f32[1,72,256]{2,1,0:T(8,128)S(1)} %fusion.12), channel_id=1, source_target_pairs={{0,4},{1,5},{2,6},{3,7},{4,0},{5,1},{6,2},{7,3},{8,12},{9,13},{10,... | collective-permute-start | bytes 221192 | tf_op jit(solution)/shard_map/ppermute | solution.py:53
  67.6 0.8 collective-permute-start.22
  68.4 4.5 %fusion = f32[2,512,512]{2,1,0:T(8,128)} fusion(f32[2,256,512]{2,1,0:T(8,128)S(1)} %get-tuple-element.103, f32[2,256,512]{2,1,0:T(8,128)S(1)} %get-tuple-element.102, f32[512,512]{1,0:T(8,128)} %weight.1, pred[]{:T(512)S(6)} %lt.39), kind=kOutput, calls=%fused_computation.2 | convolution fusion | flops 1612185600 | bytes 5242881 | tf_op jit(solution)/shard_map/npu,wu->npw/dot_general | solution.py:469
  73.1 3.5 %collective-permute-start.23 = (f32[1,72,256]{2,1,0:T(8,128)S(1)}, f32[1,72,256]{2,1,0:T(8,128)S(1)}, u32[]{:S(2)}, u32[]{:S(2)}) collective-permute-start(f32[1,72,256]{2,1,0:T(8,128)S(1)} %add_add_fusion.1), channel_id=1, source_target_pairs={{0,16},{1,17},{2,18},{3,19},{4,20},{5,21},{6,22},{7,23},{8,24},{9,... | collective-permute-start | bytes 221192 | tf_op jit(solution)/shard_map/ppermute | solution.py:53
  76.6 1.3 %fusion.6 = f32[2,32,512]{2,1,0:T(8,128)} fusion(f32[512,512]{1,0:T(8,128)S(1)} %copy-done.5, f32[2,32,512]{2,1,0:T(8,128)S(1)} %collective-permute-done.19, f32[2,32,512]{2,1,0:T(8,128)S(1)} %get-tuple-element.104, f32[2,32,512]{2,1,0:T(8,128)S(1)} %collective-permute-done.18), kind=kOutput, calls=%fused_computation.8 | convolution fusion | flops 100728832 | bytes 1572864 | tf_op jit(solution)/shard_map/nru,wu->nrw/dot_general | solution.py:470
  77.9 2.4 %collective-permute-done.23 = f32[1,72,256]{2,1,0:T(8,128)S(1)} collective-permute-done((f32[1,72,256]{2,1,0:T(8,128)S(1)}, f32[1,72,256]{2,1,0:T(8,128)S(1)}, u32[]{:S(2)}, u32[]{:S(2)}) %collective-permute-start.23) | collective-permute-done | bytes 73760 | tf_op jit(solution)/shard_map/ppermute | solution.py:53
  80.4 3.3 %collective-permute-start.25 = (f32[1,72,256]{2,1,0:T(8,128)S(1)}, f32[1,72,256]{2,1,0:T(8,128)S(1)}, u32[]{:S(2)}, u32[]{:S(2)}) collective-permute-start(f32[1,72,256]{2,1,0:T(8,128)S(1)} %get-tuple-element.111), channel_id=1, source_target_pairs={{0,128},{1,129},{2,130},{3,131},{4,132},{5,133},{6,134},{7,135},{8... | collective-permute-start | bytes 221192 | tf_op jit(solution)/shard_map/ppermute | solution.py:53
  83.7 1.4 %collective-permute-done.24 = f32[1,72,256]{2,1,0:T(8,128)S(1)} collective-permute-done((f32[1,72,256]{2,1,0:T(8,128)S(1)}, f32[1,72,256]{2,1,0:T(8,128)S(1)}, u32[]{:S(2)}, u32[]{:S(2)}) %collective-permute-start.24) | collective-permute-done | bytes 73760 | tf_op jit(solution)/shard_map/ppermute | solution.py:53
  85.1 1.4 %collective-permute-done.25 = f32[1,72,256]{2,1,0:T(8,128)S(1)} collective-permute-done((f32[1,72,256]{2,1,0:T(8,128)S(1)}, f32[1,72,256]{2,1,0:T(8,128)S(1)}, u32[]{:S(2)}, u32[]{:S(2)}) %collective-permute-start.25) | collective-permute-done | bytes 73760 | tf_op jit(solution)/shard_map/ppermute | solution.py:53
  86.5 1.7 %collective-permute-done.26 = f32[1,72,256]{2,1,0:T(8,128)S(1)} collective-permute-done((f32[1,72,256]{2,1,0:T(8,128)S(1)}, f32[1,72,256]{2,1,0:T(8,128)S(1)}, u32[]{:S(2)}, u32[]{:S(2)}) %collective-permute-start.26) | collective-permute-done | bytes 73760 | tf_op jit(solution)/shard_map/ppermute | solution.py:53
  88.2 5.4 %collective-permute-start.27 = (f32[4,72,256]{2,1,0:T(8,128)S(1)}, f32[4,72,256]{2,1,0:T(8,128)S(1)}, u32[]{:S(2)}, u32[]{:S(2)}) collective-permute-start(f32[4,72,256]{2,1,0:T(8,128)S(1)} %constant_dynamic-update-slice_fusion.8), channel_id=1, source_target_pairs={{0,2},{1,3},{2,0},{3,1},{4,6},{5,7},{6,4},{7,5},{8,10},{9,11},{10,... | collective-permute-start | bytes 884744 | tf_op jit(solution)/shard_map/ppermute | solution.py:53
  93.6 0.4 collective-permute-start.29
  94.0 9.4 %collective-permute-start.30 = (f32[4,72,256]{2,1,0:T(8,128)S(1)}, f32[4,72,256]{2,1,0:T(8,128)S(1)}, u32[]{:S(2)}, u32[]{:S(2)}) collective-permute-start(f32[4,72,256]{2,1,0:T(8,128)S(1)} %constant_dynamic-update-slice_fusion.8), channel_id=1, source_target_pairs={{0,64},{1,65},{2,66},{3,67},{4,68},{5,69},{6,70},{7,71},{8,72},{9,... | collective-permute-start | bytes 884744 | tf_op jit(solution)/shard_map/ppermute | solution.py:53
  103.5 4.1 %collective-permute-start.31 = (f32[4,72,256]{2,1,0:T(8,128)S(1)}, f32[4,72,256]{2,1,0:T(8,128)S(1)}, u32[]{:S(2)}, u32[]{:S(2)}) collective-permute-start(f32[4,72,256]{2,1,0:T(8,128)S(1)} %collective-permute-done.27), channel_id=1, source_target_pairs={{0,64},{1,65},{2,66},{3,67},{4,68},{5,69},{6,70},{7,71},{8,72},{9,... | collective-permute-start | bytes 884744 | tf_op jit(solution)/shard_map/ppermute | solution.py:53
  107.6 3.0 %collective-permute-start.33 = (f32[4,72,256]{2,1,0:T(8,128)S(1)}, f32[4,72,256]{2,1,0:T(8,128)S(1)}, u32[]{:S(2)}, u32[]{:S(2)}) collective-permute-start(f32[4,72,256]{2,1,0:T(8,128)S(1)} %collective-permute-done.29), channel_id=1, source_target_pairs={{0,64},{1,65},{2,66},{3,67},{4,68},{5,69},{6,70},{7,71},{8,72},{9,... | collective-permute-start | bytes 884744 | tf_op jit(solution)/shard_map/ppermute | solution.py:53
  111.0 0.9 collective-permute-done.33
  112.3 1.5 %fusion.14 = (f32[512,512]{1,0:T(8,128)}, f32[512,512]{1,0:T(8,128)}) fusion(f32[1152,512]{1,0:T(8,128)S(1)} %maximum_select_fusion), kind=kLoop, calls=%fused_computation.32 | loop fusion | bytes 4194304 | tf_op jit(solution)/shard_map/slice | solution.py:485
  113.8 0.7 slice_bitcast_fusion
  114.5 0.5 slice.36
  (67 shorter events, 2.5 us)
Async XLA Ops:
  0.6 10.2 %collective-permute-start = (f32[2,32,512]{2,1,0:T(8,128)}, f32[2,32,512]{2,1,0:T(8,128)S(1)}, u32[]{:S(2)}, u32[]{:S(2)}) collective-permute-start(f32[2,32,512]{2,1,0:T(8,128)} %own.3), channel_id=1, source_target_pairs={{0,1},{1,2},{2,3},{3,4},{4,5},{5,6},{6,7},{7,8},{8,9},{9,10},{10,1... | collective-permute-start | bytes 393224 | tf_op jit(solution)/shard_map/ppermute | solution.py:301
  4.6 6.3 %collective-permute-start.1 = (f32[2,32,512]{2,1,0:T(8,128)}, f32[2,32,512]{2,1,0:T(8,128)S(1)}, u32[]{:S(2)}, u32[]{:S(2)}) collective-permute-start(f32[2,32,512]{2,1,0:T(8,128)} %own.3), channel_id=1, source_target_pairs={{1,0},{2,1},{3,2},{4,3},{5,4},{6,5},{7,6},{8,7},{9,8},{10,9},{11,1... | collective-permute-start | bytes 393224 | tf_op jit(solution)/shard_map/ppermute | solution.py:302
  6.0 4.9 %copy-start.2 = (f32[512,100]{0,1:T(8,128)S(1)}, f32[512,100]{0,1:T(8,128)}, u32[]{:S(2)}) copy-start(f32[512,100]{0,1:T(8,128)} %param.13) | copy-start | bytes 614404
  6.0 4.9 %copy-start.3 = (f32[2,32,512]{2,1,0:T(8,128)S(1)}, f32[2,32,512]{2,1,0:T(8,128)}, u32[]{:S(2)}) copy-start(f32[2,32,512]{2,1,0:T(8,128)} %own.3) | copy-start | bytes 393220
  14.9 6.9 %collective-permute-start.2 = (f32[2,100,128]{2,1,0:T(8,128)S(1)}, f32[2,100,128]{2,1,0:T(8,128)S(1)}, u32[]{:S(2)}, u32[]{:S(2)}) collective-permute-start(f32[2,100,128]{2,1,0:T(8,128)S(1)} %get-tuple-element.65), channel_id=1, source_target_pairs={{0,128},{64,192},{128,0},{192,64},{1,129},{65,193},{129,1},{193,65... | collective-permute-start | bytes 307208 | tf_op jit(solution)/shard_map/ppermute | solution.py:381
  16.3 6.9 %collective-permute-start.3 = (f32[2,100,128]{2,1,0:T(8,128)S(1)}, f32[2,100,128]{2,1,0:T(8,128)S(1)}, u32[]{:S(2)}, u32[]{:S(2)}) collective-permute-start(f32[2,100,128]{2,1,0:T(8,128)S(1)} %get-tuple-element.66), channel_id=1, source_target_pairs={{0,192},{64,128},{128,64},{192,0},{1,193},{65,129},{129,65},{193,1... | collective-permute-start | bytes 307208 | tf_op jit(solution)/shard_map/ppermute | solution.py:382
  18.3 6.2 %copy-start.1 = (f32[100,512]{1,0:T(8,128)S(1)}, f32[100,512]{1,0:T(8,128)}, u32[]{:S(2)}) copy-start(f32[100,512]{1,0:T(8,128)} %targets.1) | copy-start | bytes 614404
  18.3 9.6 %copy-start = (f32[2,512,512]{2,1,0:T(8,128)S(1)}, f32[2,512,512]{2,1,0:T(8,128)}, u32[]{:S(2)}) copy-start(f32[2,512,512]{2,1,0:T(8,128)} %features.5) | copy-start | bytes 6291460
  18.3 9.6 %copy-start.4 = (s32[4,512]{1,0:T(4,128)S(1)}, s32[4,512]{1,0:T(4,128)}, u32[]{:S(2)}) copy-start(s32[4,512]{1,0:T(4,128)} %edges.5) | copy-start | bytes 24580
  23.1 1.4 %collective-permute-start.4 = (f32[2,100,128]{2,1,0:T(8,128)S(1)}, f32[2,100,128]{2,1,0:T(8,128)S(1)}, u32[]{:S(2)}, u32[]{:S(2)}) collective-permute-start(f32[2,100,128]{2,1,0:T(8,128)S(1)} %get-tuple-element.68), channel_id=1, source_target_pairs={{0,64},{64,0},{128,192},{192,128},{1,65},{65,1},{129,193},{193,129... | collective-permute-start | bytes 307208 | tf_op jit(solution)/shard_map/ppermute | solution.py:392
  25.7 2.2 %collective-permute-start.7 = (f32[2,100,128]{2,1,0:T(8,128)S(1)}, f32[2,100,128]{2,1,0:T(8,128)S(1)}, u32[]{:S(2)}, u32[]{:S(2)}) collective-permute-start(f32[2,100,128]{2,1,0:T(8,128)S(1)} %get-tuple-element.74), channel_id=1, source_target_pairs={{0,64},{64,0},{128,192},{192,128},{1,65},{65,1},{129,193},{193,129... | collective-permute-start | bytes 307208 | tf_op jit(solution)/shard_map/ppermute | solution.py:425
  26.1 5.8 %collective-permute-start.5 = (f32[2,100,128]{2,1,0:T(8,128)S(1)}, f32[2,100,128]{2,1,0:T(8,128)S(1)}, u32[]{:S(2)}, u32[]{:S(2)}) collective-permute-start(f32[2,100,128]{2,1,0:T(8,128)S(1)} %get-tuple-element.71), channel_id=1, source_target_pairs={{0,128},{64,192},{128,0},{192,64},{1,129},{65,193},{129,1},{193,65... | collective-permute-start | bytes 307208 | tf_op jit(solution)/shard_map/ppermute | solution.py:426
  26.9 6.2 %collective-permute-start.6 = (f32[2,100,128]{2,1,0:T(8,128)S(1)}, f32[2,100,128]{2,1,0:T(8,128)S(1)}, u32[]{:S(2)}, u32[]{:S(2)}) collective-permute-start(f32[2,100,128]{2,1,0:T(8,128)S(1)} %get-tuple-element.72), channel_id=1, source_target_pairs={{0,192},{64,128},{128,64},{192,0},{1,193},{65,129},{129,65},{193,1... | collective-permute-start | bytes 307208 | tf_op jit(solution)/shard_map/ppermute | solution.py:427
  37.7 1.7 %collective-permute-start.9 = (f32[4,72,256]{2,1,0:T(8,128)S(1)}, f32[4,72,256]{2,1,0:T(8,128)S(1)}, u32[]{:S(2)}, u32[]{:S(2)}) collective-permute-start(f32[4,72,256]{2,1,0:T(8,128)S(1)} %get-tuple-element.92), channel_id=1, source_target_pairs={{0,64},{1,65},{2,66},{3,67},{4,68},{5,69},{6,70},{7,71},{8,72},{9,... | collective-permute-start | bytes 884744 | tf_op jit(solution)/shard_map/ppermute | solution.py:53
  37.9 11.0 %collective-permute-start.13 = (f32[4,72,256]{2,1,0:T(8,128)S(1)}, f32[4,72,256]{2,1,0:T(8,128)S(1)}, u32[]{:S(2)}, u32[]{:S(2)}) collective-permute-start(f32[4,72,256]{2,1,0:T(8,128)S(1)} %get-tuple-element.96), channel_id=1, source_target_pairs={{0,64},{1,65},{2,66},{3,67},{4,68},{5,69},{6,70},{7,71},{8,72},{9,... | collective-permute-start | bytes 884744 | tf_op jit(solution)/shard_map/ppermute | solution.py:53
  38.3 10.8 %collective-permute-start.11 = (f32[4,72,256]{2,1,0:T(8,128)S(1)}, f32[4,72,256]{2,1,0:T(8,128)S(1)}, u32[]{:S(2)}, u32[]{:S(2)}) collective-permute-start(f32[4,72,256]{2,1,0:T(8,128)S(1)} %get-tuple-element.94), channel_id=1, source_target_pairs={{0,64},{1,65},{2,66},{3,67},{4,68},{5,69},{6,70},{7,71},{8,72},{9,... | collective-permute-start | bytes 884744 | tf_op jit(solution)/shard_map/ppermute | solution.py:53
  38.4 11.1 %collective-permute-start.8 = (f32[4,72,256]{2,1,0:T(8,128)S(1)}, f32[4,72,256]{2,1,0:T(8,128)S(1)}, u32[]{:S(2)}, u32[]{:S(2)}) collective-permute-start(f32[4,72,256]{2,1,0:T(8,128)S(1)} %get-tuple-element.89), channel_id=1, source_target_pairs={{0,64},{1,65},{2,66},{3,67},{4,68},{5,69},{6,70},{7,71},{8,72},{9,... | collective-permute-start | bytes 884744 | tf_op jit(solution)/shard_map/ppermute | solution.py:53
  39.4 13.7 %collective-permute-start.10 = (f32[4,72,256]{2,1,0:T(8,128)S(1)}, f32[4,72,256]{2,1,0:T(8,128)S(1)}, u32[]{:S(2)}, u32[]{:S(2)}) collective-permute-start(f32[4,72,256]{2,1,0:T(8,128)S(1)} %add.93), channel_id=1, source_target_pairs={{0,2},{1,3},{2,0},{3,1},{4,6},{5,7},{6,4},{7,5},{8,10},{9,11},{10,... | collective-permute-start | bytes 884744 | tf_op jit(solution)/shard_map/ppermute | solution.py:53
  49.0 7.2 %collective-permute-start.14 = (f32[4,72,256]{2,1,0:T(8,128)S(1)}, f32[4,72,256]{2,1,0:T(8,128)S(1)}, u32[]{:S(2)}, u32[]{:S(2)}) collective-permute-start(f32[4,72,256]{2,1,0:T(8,128)S(1)} %add.96), channel_id=1, source_target_pairs={{0,3},{1,2},{2,1},{3,0},{4,7},{5,6},{6,5},{7,4},{8,11},{9,10},{10,... | collective-permute-start | bytes 884744 | tf_op jit(solution)/shard_map/ppermute | solution.py:53
  49.1 7.4 %collective-permute-start.12 = (f32[4,72,256]{2,1,0:T(8,128)S(1)}, f32[4,72,256]{2,1,0:T(8,128)S(1)}, u32[]{:S(2)}, u32[]{:S(2)}) collective-permute-start(f32[4,72,256]{2,1,0:T(8,128)S(1)} %add.95), channel_id=1, source_target_pairs={{0,1},{1,0},{2,3},{3,2},{4,5},{5,4},{6,7},{7,6},{8,9},{9,8},{10,11... | collective-permute-start | bytes 884744 | tf_op jit(solution)/shard_map/ppermute | solution.py:53
  49.5 10.5 %collective-permute-start.18 = (f32[2,32,512]{2,1,0:T(8,128)S(1)}, f32[2,32,512]{2,1,0:T(8,128)S(1)}, u32[]{:S(2)}, u32[]{:S(2)}) collective-permute-start(f32[2,32,512]{2,1,0:T(8,128)S(1)} %get-tuple-element.97), channel_id=1, source_target_pairs={{0,1},{1,2},{2,3},{3,4},{4,5},{5,6},{6,7},{7,8},{8,9},{9,10},{10,1... | collective-permute-start | bytes 393224 | tf_op jit(solution)/shard_map/ppermute | solution.py:461
  50.8 9.2 %collective-permute-start.19 = (f32[2,32,512]{2,1,0:T(8,128)S(1)}, f32[2,32,512]{2,1,0:T(8,128)S(1)}, u32[]{:S(2)}, u32[]{:S(2)}) collective-permute-start(f32[2,32,512]{2,1,0:T(8,128)S(1)} %get-tuple-element.98), channel_id=1, source_target_pairs={{1,0},{2,1},{3,2},{4,3},{5,4},{6,5},{7,6},{8,7},{9,8},{10,9},{11,1... | collective-permute-start | bytes 393224 | tf_op jit(solution)/shard_map/ppermute | solution.py:462
  56.7 5.7 %collective-permute-start.15 = (f32[1,72,256]{2,1,0:T(8,128)S(1)}, f32[1,72,256]{2,1,0:T(8,128)S(1)}, u32[]{:S(2)}, u32[]{:S(2)}) collective-permute-start(f32[1,72,256]{2,1,0:T(8,128)S(1)} %get-tuple-element.116), channel_id=1, source_target_pairs={{0,32},{1,33},{2,34},{3,35},{4,36},{5,37},{6,38},{7,39},{8,40},{9,... | collective-permute-start | bytes 221192 | tf_op jit(solution)/shard_map/ppermute | solution.py:53
  56.8 5.6 %collective-permute-start.16 = (f32[1,72,256]{2,1,0:T(8,128)S(1)}, f32[1,72,256]{2,1,0:T(8,128)S(1)}, u32[]{:S(2)}, u32[]{:S(2)}) collective-permute-start(f32[1,72,256]{2,1,0:T(8,128)S(1)} %get-tuple-element.115), channel_id=1, source_target_pairs={{0,128},{1,129},{2,130},{3,131},{4,132},{5,133},{6,134},{7,135},{8... | collective-permute-start | bytes 221192 | tf_op jit(solution)/shard_map/ppermute | solution.py:53
  56.9 7.9 %collective-permute-start.17 = (f32[1,72,256]{2,1,0:T(8,128)S(1)}, f32[1,72,256]{2,1,0:T(8,128)S(1)}, u32[]{:S(2)}, u32[]{:S(2)}) collective-permute-start(f32[1,72,256]{2,1,0:T(8,128)S(1)} %get-tuple-element.114), channel_id=1, source_target_pairs={{0,160},{1,161},{2,162},{3,163},{4,164},{5,165},{6,166},{7,167},{8... | collective-permute-start | bytes 221192 | tf_op jit(solution)/shard_map/ppermute | solution.py:53
  64.8 8.1 %collective-permute-start.20 = (f32[1,72,256]{2,1,0:T(8,128)S(1)}, f32[1,72,256]{2,1,0:T(8,128)S(1)}, u32[]{:S(2)}, u32[]{:S(2)}) collective-permute-start(f32[1,72,256]{2,1,0:T(8,128)S(1)} %fusion.12), channel_id=1, source_target_pairs={{0,8},{1,9},{2,10},{3,11},{4,12},{5,13},{6,14},{7,15},{8,0},{9,1},... | collective-permute-start | bytes 221192 | tf_op jit(solution)/shard_map/ppermute | solution.py:53
  64.9 8.0 %collective-permute-start.21 = (f32[1,72,256]{2,1,0:T(8,128)S(1)}, f32[1,72,256]{2,1,0:T(8,128)S(1)}, u32[]{:S(2)}, u32[]{:S(2)}) collective-permute-start(f32[1,72,256]{2,1,0:T(8,128)S(1)} %fusion.12), channel_id=1, source_target_pairs={{0,4},{1,5},{2,6},{3,7},{4,0},{5,1},{6,2},{7,3},{8,12},{9,13},{10,... | collective-permute-start | bytes 221192 | tf_op jit(solution)/shard_map/ppermute | solution.py:53
  67.6 5.4 %collective-permute-start.22 = (f32[1,72,256]{2,1,0:T(8,128)S(1)}, f32[1,72,256]{2,1,0:T(8,128)S(1)}, u32[]{:S(2)}, u32[]{:S(2)}) collective-permute-start(f32[1,72,256]{2,1,0:T(8,128)S(1)} %fusion.12), channel_id=1, source_target_pairs={{0,12},{1,13},{2,14},{3,15},{4,8},{5,9},{6,10},{7,11},{8,4},{9,5},... | collective-permute-start | bytes 221192 | tf_op jit(solution)/shard_map/ppermute | solution.py:53
  68.4 8.2 %copy-start.5 = (f32[512,512]{1,0:T(8,128)S(1)}, f32[512,512]{1,0:T(8,128)}, u32[]{:S(2)}) copy-start(f32[512,512]{1,0:T(8,128)} %src_weight.1) | copy-start | bytes 3145732
  73.1 7.2 %collective-permute-start.23 = (f32[1,72,256]{2,1,0:T(8,128)S(1)}, f32[1,72,256]{2,1,0:T(8,128)S(1)}, u32[]{:S(2)}, u32[]{:S(2)}) collective-permute-start(f32[1,72,256]{2,1,0:T(8,128)S(1)} %add_add_fusion.1), channel_id=1, source_target_pairs={{0,16},{1,17},{2,18},{3,19},{4,20},{5,21},{6,22},{7,23},{8,24},{9,... | collective-permute-start | bytes 221192 | tf_op jit(solution)/shard_map/ppermute | solution.py:53
  80.3 4.8 %collective-permute-start.24 = (f32[1,72,256]{2,1,0:T(8,128)S(1)}, f32[1,72,256]{2,1,0:T(8,128)S(1)}, u32[]{:S(2)}, u32[]{:S(2)}) collective-permute-start(f32[1,72,256]{2,1,0:T(8,128)S(1)} %get-tuple-element.111), channel_id=1, source_target_pairs={{0,32},{1,33},{2,34},{3,35},{4,36},{5,37},{6,38},{7,39},{8,40},{9,... | collective-permute-start | bytes 221192 | tf_op jit(solution)/shard_map/ppermute | solution.py:53
  80.4 6.1 %collective-permute-start.25 = (f32[1,72,256]{2,1,0:T(8,128)S(1)}, f32[1,72,256]{2,1,0:T(8,128)S(1)}, u32[]{:S(2)}, u32[]{:S(2)}) collective-permute-start(f32[1,72,256]{2,1,0:T(8,128)S(1)} %get-tuple-element.111), channel_id=1, source_target_pairs={{0,128},{1,129},{2,130},{3,131},{4,132},{5,133},{6,134},{7,135},{8... | collective-permute-start | bytes 221192 | tf_op jit(solution)/shard_map/ppermute | solution.py:53
  83.7 4.5 %collective-permute-start.26 = (f32[1,72,256]{2,1,0:T(8,128)S(1)}, f32[1,72,256]{2,1,0:T(8,128)S(1)}, u32[]{:S(2)}, u32[]{:S(2)}) collective-permute-start(f32[1,72,256]{2,1,0:T(8,128)S(1)} %get-tuple-element.111), channel_id=1, source_target_pairs={{0,160},{1,161},{2,162},{3,163},{4,164},{5,165},{6,166},{7,167},{8... | collective-permute-start | bytes 221192 | tf_op jit(solution)/shard_map/ppermute | solution.py:53
  88.2 15.3 %collective-permute-start.27 = (f32[4,72,256]{2,1,0:T(8,128)S(1)}, f32[4,72,256]{2,1,0:T(8,128)S(1)}, u32[]{:S(2)}, u32[]{:S(2)}) collective-permute-start(f32[4,72,256]{2,1,0:T(8,128)S(1)} %constant_dynamic-update-slice_fusion.8), channel_id=1, source_target_pairs={{0,2},{1,3},{2,0},{3,1},{4,6},{5,7},{6,4},{7,5},{8,10},{9,11},{10,... | collective-permute-start | bytes 884744 | tf_op jit(solution)/shard_map/ppermute | solution.py:53
  93.6 14.0 %collective-permute-start.28 = (f32[4,72,256]{2,1,0:T(8,128)S(1)}, f32[4,72,256]{2,1,0:T(8,128)S(1)}, u32[]{:S(2)}, u32[]{:S(2)}) collective-permute-start(f32[4,72,256]{2,1,0:T(8,128)S(1)} %constant_dynamic-update-slice_fusion.8), channel_id=1, source_target_pairs={{0,1},{1,0},{2,3},{3,2},{4,5},{5,4},{6,7},{7,6},{8,9},{9,8},{10,11... | collective-permute-start | bytes 884744 | tf_op jit(solution)/shard_map/ppermute | solution.py:53
  93.6 14.0 %collective-permute-start.29 = (f32[4,72,256]{2,1,0:T(8,128)S(1)}, f32[4,72,256]{2,1,0:T(8,128)S(1)}, u32[]{:S(2)}, u32[]{:S(2)}) collective-permute-start(f32[4,72,256]{2,1,0:T(8,128)S(1)} %constant_dynamic-update-slice_fusion.8), channel_id=1, source_target_pairs={{0,3},{1,2},{2,1},{3,0},{4,7},{5,6},{6,5},{7,4},{8,11},{9,10},{10,... | collective-permute-start | bytes 884744 | tf_op jit(solution)/shard_map/ppermute | solution.py:53
  94.0 16.8 %collective-permute-start.30 = (f32[4,72,256]{2,1,0:T(8,128)S(1)}, f32[4,72,256]{2,1,0:T(8,128)S(1)}, u32[]{:S(2)}, u32[]{:S(2)}) collective-permute-start(f32[4,72,256]{2,1,0:T(8,128)S(1)} %constant_dynamic-update-slice_fusion.8), channel_id=1, source_target_pairs={{0,64},{1,65},{2,66},{3,67},{4,68},{5,69},{6,70},{7,71},{8,72},{9,... | collective-permute-start | bytes 884744 | tf_op jit(solution)/shard_map/ppermute | solution.py:53
  103.5 7.4 %collective-permute-start.31 = (f32[4,72,256]{2,1,0:T(8,128)S(1)}, f32[4,72,256]{2,1,0:T(8,128)S(1)}, u32[]{:S(2)}, u32[]{:S(2)}) collective-permute-start(f32[4,72,256]{2,1,0:T(8,128)S(1)} %collective-permute-done.27), channel_id=1, source_target_pairs={{0,64},{1,65},{2,66},{3,67},{4,68},{5,69},{6,70},{7,71},{8,72},{9,... | collective-permute-start | bytes 884744 | tf_op jit(solution)/shard_map/ppermute | solution.py:53
  107.6 3.3 %collective-permute-start.32 = (f32[4,72,256]{2,1,0:T(8,128)S(1)}, f32[4,72,256]{2,1,0:T(8,128)S(1)}, u32[]{:S(2)}, u32[]{:S(2)}) collective-permute-start(f32[4,72,256]{2,1,0:T(8,128)S(1)} %collective-permute-done.28), channel_id=1, source_target_pairs={{0,64},{1,65},{2,66},{3,67},{4,68},{5,69},{6,70},{7,71},{8,72},{9,... | collective-permute-start | bytes 884744 | tf_op jit(solution)/shard_map/ppermute | solution.py:53
  107.6 4.3 %collective-permute-start.33 = (f32[4,72,256]{2,1,0:T(8,128)S(1)}, f32[4,72,256]{2,1,0:T(8,128)S(1)}, u32[]{:S(2)}, u32[]{:S(2)}) collective-permute-start(f32[4,72,256]{2,1,0:T(8,128)S(1)} %collective-permute-done.29), channel_id=1, source_target_pairs={{0,64},{1,65},{2,66},{3,67},{4,68},{5,69},{6,70},{7,71},{8,72},{9,... | collective-permute-start | bytes 884744 | tf_op jit(solution)/shard_map/ppermute | solution.py:53

commit v7 on v6

--- a/solution.py
+++ b/solution.py
@@ -79,11 +79,13 @@
         piece = (i // 2, pl.ds((i % 2) * half, half))
         loads.append(pltpu.make_async_copy(features.at[piece], held.at[piece], sems.at[1 + i]))
     loads.append(pltpu.make_async_copy(src_weight, held_src, sems.at[1 + 2 * members]))
-    for load in loads:
-        load.start()
+    loads[0].start()
+    loads[1].start()
     local = edges[...] - (me[1] - 1) * node_rows
     edges_t[...] = jnp.concatenate([local, local], axis=0).T
     loads[0].wait()
+    for load in loads[2:]:
+        load.start()
     high, low = split(0.5 * held_weight[...])
     for i in range(2 * members):
         loads[1 + i].wait()
@@ -91,6 +93,10 @@
         query[piece] = dot3(split(held[piece]), (high, low), NN)
     loads[-1].wait()
     src_high[...], src_low[...] = split(0.5 * held_src[...])
+
+
+def chunk_rows(width):
+    return ((0, 0, 32), (32, width, 32), (64, 2 * width, 8))
 
 
 def forward(me, member, query, edges, nodes, out_weight, slope, summed, same, flipped):
@@ -250,9 +256,26 @@
         sums[end : end + 8] = jnp.full((8, width), jnp.sum(loss[0:1]) * (loss_scale / scale), f32)
         for j in range(16):
             for out, core, order in ((keep, me[2], me[3]), (away, 1 - me[2], me[4])):
-                at = pl.ds(pl.multiple_of((j ^ order) * 72, 8), 72)
+                chunk = j ^ order
                 lanes = pl.ds(pl.multiple_of(core * 256, 128), 256)
-                out[j // 4][j % 4] = sums[at, lanes] * scale
+                for to, start, height in chunk_rows(width):
+                    at = pl.ds(pl.multiple_of(start + chunk * height, 8), height)
+                    out[j // 4][j % 4, to : to + height] = sums[at, lanes] * scale
+
+
+def finish_kernel(me, *refs):
+    parts, (src_grad, dst_grad, out_grad, loss, rest) = refs[:8], refs[8:]
+    width = src_grad.shape[0]
+    for i, part in enumerate(parts):
+        core, order = (me[2], me[3]) if i < 4 else (1 - me[2], me[4])
+        group = (order >> 2) ^ peer_order[i % 4]
+        lanes = pl.ds(pl.multiple_of(core * 256, 128), 256)
+        for j in range(4):
+            for out, (to, _, height) in zip((src_grad, dst_grad, rest), chunk_rows(width)):
+                at = pl.ds(pl.multiple_of((group * 4 + j) * height, 8), height)
+                out[at, lanes] = part[j, to : to + height]
+    out_grad[...] = rest[0 : out_grad.shape[0]]
+    loss[0, 0] = jnp.max(rest[loss_row : loss_row + 8, 0:128])
 
 
 def whole(shape=None):
@@ -264,6 +287,7 @@
 
 
 order = (2, 1, 3)
+peer_order = (0,) + order
 
 
 def tree(total, parts):
@@ -451,8 +475,6 @@
     )
 
     keep, away = parts[:4], parts[4:]
-    core = place["core"]
-    first = jnp.where(straight, place["x"], place["y"])
     second = jnp.where(straight, place["y"], place["x"])
     swapped = [send(away[k], swap_core) for k in order + (0,)]
     halves = [keep[k] + part for k, part in zip(order, swapped)]
@@ -464,27 +486,35 @@
     parts = [send(total[k : k + 1], second_axis[k]) for k in order]
     *parts, from_prev, from_next = lax.optimization_barrier((*parts, from_prev, from_next))
     total = tree(total[:1], parts)
-    total = tree(total, [send(total, along_z[k]) for k in order])
-    part = send(total, along_z[4])
-    grid_grad = jnp.einsum("npu,wu->npw", grad_query, dst_weight, precision=lax.Precision.HIGH)
+    parts = [send(total, along_z[k]) for k in order]
     mesh_grad = jnp.einsum(
         "nru,wu->nrw", middle + from_prev + from_next, src_weight, precision=lax.Precision.HIGH
     )
-    part, grid_grad, mesh_grad = lax.optimization_barrier((part, grid_grad, mesh_grad))
+    *parts, mesh_grad = lax.optimization_barrier((*parts, mesh_grad))
+    total = tree(total, parts)
+    part = send(total, along_z[4])
+    grid_grad = jnp.einsum("npu,wu->npw", grad_query, dst_weight, precision=lax.Precision.HIGH)
+    part, grid_grad = lax.optimization_barrier((part, grid_grad))
     total = total + part
     total = placed_at(second, total, [send(total, second_axis[k]) for k in order])
     parts = [total] + [send(total, first_axis[k]) for k in order]
     others = [send(part, swap_core) for part in parts]
-    total = placed_at(first, parts[0], parts[1:]).reshape(1152, 256)
-    other = placed_at(second, others[0], others[1:]).reshape(1152, 256)
-    whole_sum = jnp.where(
-        core == 0, jnp.concatenate([total, other], axis=1), jnp.concatenate([other, total], axis=1)
-    )
-    loss = whole_sum[2 * width + loss_row, 0]
-    src_grad = whole_sum[:width]
-    dst_grad = whole_sum[width : 2 * width]
-    out_grad = whole_sum[2 * width : 2 * width + count_vars].T
-    return loss, grid_grad, mesh_grad, src_grad, dst_grad, out_grad
+    square = jax.ShapeDtypeStruct((width, width), f32)
+    src_grad, dst_grad, out_grad, loss = pl.pallas_call(
+        finish_kernel,
+        grid_spec=pltpu.PrefetchScalarGridSpec(
+            num_scalar_prefetch=1,
+            grid=(1,),
+            in_specs=[whole()] * 8,
+            out_specs=[whole()] * 3 + [pl.BlockSpec(memory_space=pltpu.SMEM)],
+            scratch_shapes=[pltpu.VMEM((128, width), f32)],
+        ),
+        out_shape=[square, square, out_sum_shape, jax.ShapeDtypeStruct((1, 1), f32)],
+        compiler_params=params(1),
+        name="finish",
+        interpret=interpret,
+    )(me, *parts, *others)
+    return loss.reshape(()), grid_grad, mesh_grad, src_grad, dst_grad, out_grad.T
 
 
 def solution(mesh):

time: 115 us -> 113 us (0.983)
  local copies, waits for them, and re-layouts: 3.23 us -> 0.17 us
  Pallas kernels: 22 us -> 24.4 us
  starting transfers between devices: 61.2 us -> 59 us
    pallas_call x0 -> x1, Pallas kernels: none -> 2.11 us  [body(): pl.pallas_call(finish_kernel, grid_spec=pltpu.PrefetchScalarGridSpec(num_...]
    slice x2 -> x0, local copies, waits for them, and re-layouts: 2 us -> none  [the longest x1 1.49 us: body(): dst_grad = whole_sum[width:2 * width]]
    ppermute x24, starting transfers between devices: 47.3 us -> 45.3 us  [send(): return lax.ppermute(value, axes, pairs)]
    dot_general x1, matrix products: 4.48 us -> 3.21 us  [body(): jnp.einsum('npu,wu->npw', grad_query, dst_weight, precision=lax.Precision...]
    dot_general x1, matrix products: 1.3 us -> 2.49 us  [body(): jnp.einsum('nru,wu->nrw', middle + from_prev + from_next, src_weight, pre...]
  transfers between devices with their start and end apart: 34 -> 34, of which waited for: 15 -> 15; matrix products, arithmetic and copies ran while one was open for 6% -> 5% of each run, Pallas kernels for 11% -> 11%
where the time goes in v7:
time: 113 us; the launch traced here: 112 us
  starting transfers between devices  59 us (52%)
  Pallas kernels  24.4 us (22%)
  waiting for transfers between devices  21.9 us (19%)
  matrix products  5.7 us (5%)
    ppermute x24, starting transfers between devices, send(): return lax.ppermute(value, axes, pairs)  45.3 us
    ppermute x24, waiting for transfers between devices, send(): return lax.ppermute(value, axes, pairs)  18.2 us
    pallas_call x1, Pallas kernels, body(): pl.pallas_call(query_kernel, in_specs=[me_spec, whole(), in_hbm, in_hbm,...  5.12 us
    pallas_call x1, Pallas kernels, body(): call(functools.partial(far_backward_kernel, scale, loss_scale), 'far_back...  4.83 us
    ppermute x1, starting transfers between devices, body(): before = lax.ppermute(mesh_features, 'grid', up)  3.95 us
    pallas_call x1, Pallas kernels, body(): call(far_forward_kernel, 'far_forward', forward_work, [rows_of(far), pl.B...  3.89 us
    pallas_call x1, Pallas kernels, body(): call(near_backward_kernel, 'near_backward', backward_work, backward_specs...  3.83 us
    pallas_call x1, Pallas kernels, body(): call(near_forward_kernel, 'near_forward', forward_work, [rows_of(near), p...  3.37 us
  transfers between devices with their start and end apart: 34, of which 15 were waited for; matrix products, arithmetic and copies ran while one was open for 5% of the time, Pallas kernels for 11%

profile of v7, /device:TPU:1, one launch (start us, length us, event | category | flops | bytes accessed | tf_op | source)
XLA Modules:
  0.0 112.5 jit_solution(9738241355571331843)
XLA Ops:
  0.6 4.0 %collective-permute-start = (f32[2,32,512]{2,1,0:T(8,128)}, f32[2,32,512]{2,1,0:T(8,128)S(1)}, u32[]{:S(2)}, u32[]{:S(2)}) collective-permute-start(f32[2,32,512]{2,1,0:T(8,128)} %own.3), channel_id=1, source_target_pairs={{0,1},{1,2},{2,3},{3,4},{4,5},{5,6},{6,7},{7,8},{8,9},{9,10},{10,1... | collective-permute-start | bytes 393224 | tf_op jit(solution)/shard_map/ppermute | solution.py:325
  4.6 1.3 %collective-permute-start.1 = (f32[2,32,512]{2,1,0:T(8,128)}, f32[2,32,512]{2,1,0:T(8,128)S(1)}, u32[]{:S(2)}, u32[]{:S(2)}) collective-permute-start(f32[2,32,512]{2,1,0:T(8,128)} %own.3), channel_id=1, source_target_pairs={{1,0},{2,1},{3,2},{4,3},{5,4},{6,5},{7,6},{8,7},{9,8},{10,9},{11,1... | collective-permute-start | bytes 393224 | tf_op jit(solution)/shard_map/ppermute | solution.py:326
  6.0 5.1 %query.1 = (f32[2,512,512]{2,1,0:T(8,128)S(1)}, s32[512,8]{1,0:T(8,128)S(1)}, bf16[512,512]{1,0:T(8,128)(2,1)S(1)}, bf16[512,512]{1,0:T(8,128)(2,1)S(1)}) custom-call(s32[5]{0:T(128)S(1)} %stack.23.me, s32[4,512]{1,0:T(4,128)} %edges.5, f32[2,512,512]{2,1,0:T(8,128)} %features.5, f32[512,512]{1,0:T(8,128)} %weight.1, f32[512,512]{1,0:T(8,128)} %src_weight.1), custom_call_target="tpu_custom_call" | custom-call | tf_op jit(solution)/shard_map/query/pallas_call | solution.py:330
  11.2 3.9 %far_forward.1 = (f32[2,4,256,512]{3,2,1,0:T(8,128)S(1)}, f32[2,256,512]{2,1,0:T(8,128)S(1)}, f32[2,100,128]{2,1,0:T(8,128)S(1)}, f32[2,100,128]{2,1,0:T(8,128)S(1)}, bf16[2,256,512]{2,1,0:T(8,128)(2,1)S(1)}) custom-call(s32[5]{0:T(128)S(1)} %stack.23.me, f32[2,512,512]{2,1,0:T(8,128)S(1)} %get-tuple-element.65.query, s32[512,8]{1,0:T(8,128)S(1)} %get-tuple-element.66.edges, ...), custom_call_target="tpu_custom_call" | custom-call | flops 1231028224 | bytes 2097152 | tf_op jit(solution)/shard_map/far_forward/pallas_call | solution.py:395
  15.1 1.4 %collective-permute-start.2 = (f32[2,100,128]{2,1,0:T(8,128)S(1)}, f32[2,100,128]{2,1,0:T(8,128)S(1)}, u32[]{:S(2)}, u32[]{:S(2)}) collective-permute-start(f32[2,100,128]{2,1,0:T(8,128)S(1)} %get-tuple-element.72), channel_id=1, source_target_pairs={{0,128},{64,192},{128,0},{192,64},{1,129},{65,193},{129,1},{193,65... | collective-permute-start | bytes 307208 | tf_op jit(solution)/shard_map/ppermute | solution.py:405
  16.5 1.8 %collective-permute-start.3 = (f32[2,100,128]{2,1,0:T(8,128)S(1)}, f32[2,100,128]{2,1,0:T(8,128)S(1)}, u32[]{:S(2)}, u32[]{:S(2)}) collective-permute-start(f32[2,100,128]{2,1,0:T(8,128)S(1)} %get-tuple-element.73), channel_id=1, source_target_pairs={{0,192},{64,128},{128,64},{192,0},{1,193},{65,129},{129,65},{193,1... | collective-permute-start | bytes 307208 | tf_op jit(solution)/shard_map/ppermute | solution.py:406
  18.3 3.4 %near_forward.1 = (f32[2,4,256,512]{3,2,1,0:T(8,128)S(1)}, f32[2,256,512]{2,1,0:T(8,128)S(1)}, f32[2,100,128]{2,1,0:T(8,128)S(1)}, f32[2,100,128]{2,1,0:T(8,128)S(1)}) custom-call(s32[5]{0:T(128)S(1)} %stack.23.me, f32[2,512,512]{2,1,0:T(8,128)S(1)} %get-tuple-element.65.query, s32[512,8]{1,0:T(8,128)S(1)} %get-tuple-element.66.edges, ...), custom_call_target="tpu_custom_call" | custom-call | flops 1231028224 | bytes 2097152 | tf_op jit(solution)/shard_map/near_forward/pallas_call | solution.py:407
  21.6 1.4 %collective-permute-done.3.part3 = f32[2,100,128]{2,1,0:T(8,128)S(1)} collective-permute-done((f32[2,100,128]{2,1,0:T(8,128)S(1)}, f32[2,100,128]{2,1,0:T(8,128)S(1)}, u32[]{:S(2)}, u32[]{:S(2)}) %collective-permute-start.3) | collective-permute-done | bytes 102432 | tf_op jit(solution)/shard_map/ppermute | solution.py:406
  23.1 0.4 collective-permute-start.4
  23.4 1.0 collective-permute-done.4.part1
  24.4 1.2 %score.1 = (f32[2,100,128]{2,1,0:T(8,128)S(1)}, f32[2,100,128]{2,1,0:T(8,128)S(1)}, f32[2,100,128]{2,1,0:T(8,128)S(1)}, f32[2,100,128]{2,1,0:T(8,128)S(1)}, f32[8,128]{1,0:T(8,128)S(1)}) custom-call(s32[5]{0:T(128)S(1)} %stack.23.me, f32[2,100,128]{2,1,0:T(8,128)S(1)} %get-tuple-element.74.part0, f32[2,100,128]{2,1,0:T(8,128)S(1)} %collective-permute-done.4.part1, ...), custom_call_target="tpu_custom_call" | custom-call | tf_op jit(solution)/shard_map/score/pallas_call | solution.py:418
  25.6 0.4 collective-permute-start.7
  26.1 0.8 collective-permute-start.5
  26.9 1.0 collective-permute-start.6
  27.9 3.8 %near_backward.1 = (f32[2,256,512]{2,1,0:T(8,128)S(1)}, f32[2,96,512]{2,1,0:T(8,128)S(1)}, f32[512,512]{1,0:T(8,128)S(1)}, f32[100,512]{1,0:T(8,128)S(1)}) custom-call(s32[5]{0:T(128)S(1)} %stack.23.me, f32[2,100,128]{2,1,0:T(8,128)S(1)} %get-tuple-element.80.same, f32[2,100,128]{2,1,0:T(8,128)S(1)} %collective-permute-done.7.flipped, ...), custom_call_target="tpu_custom_call" | custom-call | flops 2193620992 | bytes 2097152 | tf_op jit(solution)/shard_map/near_backward/pallas_call | solution.py:452
  31.7 1.3 %collective-permute-done.6.flipped = f32[2,100,128]{2,1,0:T(8,128)S(1)} collective-permute-done((f32[2,100,128]{2,1,0:T(8,128)S(1)}, f32[2,100,128]{2,1,0:T(8,128)S(1)}, u32[]{:S(2)}, u32[]{:S(2)}) %collective-permute-start.6) | collective-permute-done | bytes 102432 | tf_op jit(solution)/shard_map/ppermute | solution.py:451
  33.0 4.8 %far_backward.1 = (f32[2,256,512]{2,1,0:T(8,128)S(1)}, f32[2,32,512]{2,1,0:T(8,128)S(1)}, f32[2,32,512]{2,1,0:T(8,128)S(1)}, f32[2,32,512]{2,1,0:T(8,128)S(1)}, ...) custom-call(s32[5]{0:T(128)S(1)} %stack.23.me, ...), custom_call_target="tpu_custom_call" | custom-call | flops 2193620992 | bytes 2097152 | tf_op jit(solution)/shard_map/far_backward/pallas_call | solution.py:461
  38.1 0.4 collective-permute-start.13
  38.6 0.4 collective-permute-start.8
  39.0 0.6 collective-permute-done.9
  39.6 9.8 %collective-permute-start.10 = (f32[4,72,256]{2,1,0:T(8,128)S(1)}, f32[4,72,256]{2,1,0:T(8,128)S(1)}, u32[]{:S(2)}, u32[]{:S(2)}) collective-permute-start(f32[4,72,256]{2,1,0:T(8,128)S(1)} %add.69), channel_id=1, source_target_pairs={{0,2},{1,3},{2,0},{3,1},{4,6},{5,7},{6,4},{7,5},{8,10},{9,11},{10,... | collective-permute-start | bytes 884744 | tf_op jit(solution)/shard_map/ppermute | solution.py:53
  49.6 0.4 collective-permute-start.12
  50.0 1.3 %collective-permute-start.18 = (f32[2,32,512]{2,1,0:T(8,128)S(1)}, f32[2,32,512]{2,1,0:T(8,128)S(1)}, u32[]{:S(2)}, u32[]{:S(2)}) collective-permute-start(f32[2,32,512]{2,1,0:T(8,128)S(1)} %get-tuple-element.104), channel_id=1, source_target_pairs={{0,1},{1,2},{2,3},{3,4},{4,5},{5,6},{6,7},{7,8},{8,9},{9,10},{10,1... | collective-permute-start | bytes 393224 | tf_op jit(solution)/shard_map/ppermute | solution.py:483
  51.3 1.3 %collective-permute-start.19 = (f32[2,32,512]{2,1,0:T(8,128)S(1)}, f32[2,32,512]{2,1,0:T(8,128)S(1)}, u32[]{:S(2)}, u32[]{:S(2)}) collective-permute-start(f32[2,32,512]{2,1,0:T(8,128)S(1)} %get-tuple-element.105), channel_id=1, source_target_pairs={{1,0},{2,1},{3,2},{4,3},{5,4},{6,5},{7,6},{8,7},{9,8},{10,9},{11,1... | collective-permute-start | bytes 393224 | tf_op jit(solution)/shard_map/ppermute | solution.py:484
  52.6 0.9 collective-permute-done.10
  53.5 3.1 %collective-permute-done.14 = f32[4,72,256]{2,1,0:T(8,128)S(1)} collective-permute-done((f32[4,72,256]{2,1,0:T(8,128)S(1)}, f32[4,72,256]{2,1,0:T(8,128)S(1)}, u32[]{:S(2)}, u32[]{:S(2)}) %collective-permute-start.14) | collective-permute-done | bytes 294944 | tf_op jit(solution)/shard_map/ppermute | solution.py:53
  57.3 3.1 %collective-permute-start.17 = (f32[1,72,256]{2,1,0:T(8,128)S(1)}, f32[1,72,256]{2,1,0:T(8,128)S(1)}, u32[]{:S(2)}, u32[]{:S(2)}) collective-permute-start(f32[1,72,256]{2,1,0:T(8,128)S(1)} %get-tuple-element.126), channel_id=1, source_target_pairs={{0,160},{1,161},{2,162},{3,163},{4,164},{5,165},{6,166},{7,167},{8... | collective-permute-start | bytes 221192 | tf_op jit(solution)/shard_map/ppermute | solution.py:53
  60.5 2.3 %collective-permute-done.15 = f32[1,72,256]{2,1,0:T(8,128)S(1)} collective-permute-done((f32[1,72,256]{2,1,0:T(8,128)S(1)}, f32[1,72,256]{2,1,0:T(8,128)S(1)}, u32[]{:S(2)}, u32[]{:S(2)}) %collective-permute-start.15) | collective-permute-done | bytes 73760 | tf_op jit(solution)/shard_map/ppermute | solution.py:53
  62.8 2.4 %collective-permute-done.17 = f32[1,72,256]{2,1,0:T(8,128)S(1)} collective-permute-done((f32[1,72,256]{2,1,0:T(8,128)S(1)}, f32[1,72,256]{2,1,0:T(8,128)S(1)}, u32[]{:S(2)}, u32[]{:S(2)}) %collective-permute-start.17) | collective-permute-done | bytes 73760 | tf_op jit(solution)/shard_map/ppermute | solution.py:53
  65.4 2.5 %collective-permute-start.21 = (f32[1,72,256]{2,1,0:T(8,128)S(1)}, f32[1,72,256]{2,1,0:T(8,128)S(1)}, u32[]{:S(2)}, u32[]{:S(2)}) collective-permute-start(f32[1,72,256]{2,1,0:T(8,128)S(1)} %fusion.12), channel_id=1, source_target_pairs={{0,4},{1,5},{2,6},{3,7},{4,0},{5,1},{6,2},{7,3},{8,12},{9,13},{10,... | collective-permute-start | bytes 221192 | tf_op jit(solution)/shard_map/ppermute | solution.py:53
  67.8 1.1 collective-permute-start.22
  68.9 2.5 %fusion.7 = f32[2,32,512]{2,1,0:T(8,128)} fusion(f32[512,512]{1,0:T(8,128)} %src_weight.1, f32[2,32,512]{2,1,0:T(8,128)S(1)} %collective-permute-done.19, f32[2,32,512]{2,1,0:T(8,128)S(1)} %get-tuple-element.109, f32[2,32,512]{2,1,0:T(8,128)S(1)} %collective-permute-done.18), kind=kOutput, calls=%fused_computation.8 | convolution fusion | flops 100728832 | bytes 1572864 | tf_op jit(solution)/shard_map/nru,wu->nrw/dot_general | solution.py:490
  71.4 1.9 %collective-permute-done.22 = f32[1,72,256]{2,1,0:T(8,128)S(1)} collective-permute-done((f32[1,72,256]{2,1,0:T(8,128)S(1)}, f32[1,72,256]{2,1,0:T(8,128)S(1)}, u32[]{:S(2)}, u32[]{:S(2)}) %collective-permute-start.22) | collective-permute-done | bytes 73760 | tf_op jit(solution)/shard_map/ppermute | solution.py:53
  73.3 3.7 %collective-permute-start.23 = (f32[1,72,256]{2,1,0:T(8,128)S(1)}, f32[1,72,256]{2,1,0:T(8,128)S(1)}, u32[]{:S(2)}, u32[]{:S(2)}) collective-permute-start(f32[1,72,256]{2,1,0:T(8,128)S(1)} %add_add_fusion.1), channel_id=1, source_target_pairs={{0,16},{1,17},{2,18},{3,19},{4,20},{5,21},{6,22},{7,23},{8,24},{9,... | collective-permute-start | bytes 221192 | tf_op jit(solution)/shard_map/ppermute | solution.py:53
  77.0 3.2 %fusion = f32[2,512,512]{2,1,0:T(8,128)} fusion(f32[2,256,512]{2,1,0:T(8,128)S(1)} %get-tuple-element.116, f32[2,256,512]{2,1,0:T(8,128)S(1)} %get-tuple-element.115, f32[512,512]{1,0:T(8,128)S(1)} %copy-done.5, pred[]{:T(512)S(6)} %lt.15), kind=kOutput, calls=%fused_computation.1 | convolution fusion | flops 1612185600 | bytes 5242881 | tf_op jit(solution)/shard_map/npu,wu->npw/dot_general | solution.py:496
  80.2 1.0 collective-permute-done.23
  81.6 4.1 %collective-permute-start.25 = (f32[1,72,256]{2,1,0:T(8,128)S(1)}, f32[1,72,256]{2,1,0:T(8,128)S(1)}, u32[]{:S(2)}, u32[]{:S(2)}) collective-permute-start(f32[1,72,256]{2,1,0:T(8,128)S(1)} %get-tuple-element.125), channel_id=1, source_target_pairs={{0,128},{1,129},{2,130},{3,131},{4,132},{5,133},{6,134},{7,135},{8... | collective-permute-start | bytes 221192 | tf_op jit(solution)/shard_map/ppermute | solution.py:53
  85.7 0.4 collective-permute-done.24
  86.1 2.3 %collective-permute-done.25 = f32[1,72,256]{2,1,0:T(8,128)S(1)} collective-permute-done((f32[1,72,256]{2,1,0:T(8,128)S(1)}, f32[1,72,256]{2,1,0:T(8,128)S(1)}, u32[]{:S(2)}, u32[]{:S(2)}) %collective-permute-start.25) | collective-permute-done | bytes 73760 | tf_op jit(solution)/shard_map/ppermute | solution.py:53
  88.4 1.7 %collective-permute-done.26 = f32[1,72,256]{2,1,0:T(8,128)S(1)} collective-permute-done((f32[1,72,256]{2,1,0:T(8,128)S(1)}, f32[1,72,256]{2,1,0:T(8,128)S(1)}, u32[]{:S(2)}, u32[]{:S(2)}) %collective-permute-start.26) | collective-permute-done | bytes 73760 | tf_op jit(solution)/shard_map/ppermute | solution.py:53
  90.1 1.9 %collective-permute-start.27 = (f32[4,72,256]{2,1,0:T(8,128)S(1)}, f32[4,72,256]{2,1,0:T(8,128)S(1)}, u32[]{:S(2)}, u32[]{:S(2)}) collective-permute-start(f32[4,72,256]{2,1,0:T(8,128)S(1)} %constant_dynamic-update-slice_fusion.refs_0_), channel_id=1, source_target_pairs={{0,2},{1,3},{2,0},{3,1},{4,6},{5,7},{6,4},{7,5},{8,10},{9,11},{10,... | collective-permute-start | bytes 884744 | tf_op jit(solution)/shard_map/ppermute | solution.py:53
  92.1 1.3 %collective-permute-start.29 = (f32[4,72,256]{2,1,0:T(8,128)S(1)}, f32[4,72,256]{2,1,0:T(8,128)S(1)}, u32[]{:S(2)}, u32[]{:S(2)}) collective-permute-start(f32[4,72,256]{2,1,0:T(8,128)S(1)} %constant_dynamic-update-slice_fusion.refs_0_), channel_id=1, source_target_pairs={{0,3},{1,2},{2,1},{3,0},{4,7},{5,6},{6,5},{7,4},{8,11},{9,10},{10,... | collective-permute-start | bytes 884744 | tf_op jit(solution)/shard_map/ppermute | solution.py:53
  93.4 8.2 %collective-permute-start.30 = (f32[4,72,256]{2,1,0:T(8,128)S(1)}, f32[4,72,256]{2,1,0:T(8,128)S(1)}, u32[]{:S(2)}, u32[]{:S(2)}) collective-permute-start(f32[4,72,256]{2,1,0:T(8,128)S(1)} %constant_dynamic-update-slice_fusion.refs_0_), channel_id=1, source_target_pairs={{0,64},{1,65},{2,66},{3,67},{4,68},{5,69},{6,70},{7,71},{8,72},{9,... | collective-permute-start | bytes 884744 | tf_op jit(solution)/shard_map/ppermute | solution.py:53
  101.7 4.2 %collective-permute-start.31 = (f32[4,72,256]{2,1,0:T(8,128)S(1)}, f32[4,72,256]{2,1,0:T(8,128)S(1)}, u32[]{:S(2)}, u32[]{:S(2)}) collective-permute-start(f32[4,72,256]{2,1,0:T(8,128)S(1)} %collective-permute-done.27.refs_1_), channel_id=1, source_target_pairs={{0,64},{1,65},{2,66},{3,67},{4,68},{5,69},{6,70},{7,71},{8,72},{9,... | collective-permute-start | bytes 884744 | tf_op jit(solution)/shard_map/ppermute | solution.py:53
  105.9 1.8 %collective-permute-start.32 = (f32[4,72,256]{2,1,0:T(8,128)S(1)}, f32[4,72,256]{2,1,0:T(8,128)S(1)}, u32[]{:S(2)}, u32[]{:S(2)}) collective-permute-start(f32[4,72,256]{2,1,0:T(8,128)S(1)} %collective-permute-done.28.refs_2_), channel_id=1, source_target_pairs={{0,64},{1,65},{2,66},{3,67},{4,68},{5,69},{6,70},{7,71},{8,72},{9,... | collective-permute-start | bytes 884744 | tf_op jit(solution)/shard_map/ppermute | solution.py:53
  107.7 1.2 %collective-permute-start.33 = (f32[4,72,256]{2,1,0:T(8,128)S(1)}, f32[4,72,256]{2,1,0:T(8,128)S(1)}, u32[]{:S(2)}, u32[]{:S(2)}) collective-permute-start(f32[4,72,256]{2,1,0:T(8,128)S(1)} %collective-permute-done.29.refs_3_), channel_id=1, source_target_pairs={{0,64},{1,65},{2,66},{3,67},{4,68},{5,69},{6,70},{7,71},{8,72},{9,... | collective-permute-start | bytes 884744 | tf_op jit(solution)/shard_map/ppermute | solution.py:53
  109.0 1.2 %collective-permute-done.33.refs_7_ = f32[4,72,256]{2,1,0:T(8,128)S(1)} collective-permute-done((f32[4,72,256]{2,1,0:T(8,128)S(1)}, f32[4,72,256]{2,1,0:T(8,128)S(1)}, u32[]{:S(2)}, u32[]{:S(2)}) %collective-permute-start.33) | collective-permute-done | bytes 294944 | tf_op jit(solution)/shard_map/ppermute | solution.py:53
  110.2 2.1 %finish.1 = (f32[512,512]{1,0:T(8,128)}, f32[512,512]{1,0:T(8,128)}, f32[100,512]{1,0:T(8,128)}, f32[1,1]{1,0:T(1,128)}) custom-call(s32[5]{0:T(128)S(1)} %stack.23.me, f32[4,72,256]{2,1,0:T(8,128)S(1)} %constant_dynamic-update-slice_fusion.refs_0_, f32[4,72,256]{2,1,0:T(8,128)S(1)} %collective-permute-done.27.refs_1_, ...), custom_call_target="tpu_custom_call" | custom-call | tf_op jit(solution)/shard_map/finish/pallas_call | solution.py:503
  (54 shorter events, 2.0 us)
Async XLA Ops:
  0.6 10.5 %collective-permute-start = (f32[2,32,512]{2,1,0:T(8,128)}, f32[2,32,512]{2,1,0:T(8,128)S(1)}, u32[]{:S(2)}, u32[]{:S(2)}) collective-permute-start(f32[2,32,512]{2,1,0:T(8,128)} %own.3), channel_id=1, source_target_pairs={{0,1},{1,2},{2,3},{3,4},{4,5},{5,6},{6,7},{7,8},{8,9},{9,10},{10,1... | collective-permute-start | bytes 393224 | tf_op jit(solution)/shard_map/ppermute | solution.py:325
  4.6 6.6 %collective-permute-start.1 = (f32[2,32,512]{2,1,0:T(8,128)}, f32[2,32,512]{2,1,0:T(8,128)S(1)}, u32[]{:S(2)}, u32[]{:S(2)}) collective-permute-start(f32[2,32,512]{2,1,0:T(8,128)} %own.3), channel_id=1, source_target_pairs={{1,0},{2,1},{3,2},{4,3},{5,4},{6,5},{7,6},{8,7},{9,8},{10,9},{11,1... | collective-permute-start | bytes 393224 | tf_op jit(solution)/shard_map/ppermute | solution.py:326
  6.0 5.2 %copy-start.2 = (f32[512,100]{0,1:T(8,128)S(1)}, f32[512,100]{0,1:T(8,128)}, u32[]{:S(2)}) copy-start(f32[512,100]{0,1:T(8,128)} %param.13) | copy-start | bytes 614404
  6.0 5.2 %copy-start.3 = (f32[2,32,512]{2,1,0:T(8,128)S(1)}, f32[2,32,512]{2,1,0:T(8,128)}, u32[]{:S(2)}) copy-start(f32[2,32,512]{2,1,0:T(8,128)} %own.3) | copy-start | bytes 393220
  15.1 6.6 %collective-permute-start.2 = (f32[2,100,128]{2,1,0:T(8,128)S(1)}, f32[2,100,128]{2,1,0:T(8,128)S(1)}, u32[]{:S(2)}, u32[]{:S(2)}) collective-permute-start(f32[2,100,128]{2,1,0:T(8,128)S(1)} %get-tuple-element.72), channel_id=1, source_target_pairs={{0,128},{64,192},{128,0},{192,64},{1,129},{65,193},{129,1},{193,65... | collective-permute-start | bytes 307208 | tf_op jit(solution)/shard_map/ppermute | solution.py:405
  16.5 6.6 %collective-permute-start.3 = (f32[2,100,128]{2,1,0:T(8,128)S(1)}, f32[2,100,128]{2,1,0:T(8,128)S(1)}, u32[]{:S(2)}, u32[]{:S(2)}) collective-permute-start(f32[2,100,128]{2,1,0:T(8,128)S(1)} %get-tuple-element.73), channel_id=1, source_target_pairs={{0,192},{64,128},{128,64},{192,0},{1,193},{65,129},{129,65},{193,1... | collective-permute-start | bytes 307208 | tf_op jit(solution)/shard_map/ppermute | solution.py:406
  18.3 6.2 %copy-start.1 = (f32[100,512]{1,0:T(8,128)S(1)}, f32[100,512]{1,0:T(8,128)}, u32[]{:S(2)}) copy-start(f32[100,512]{1,0:T(8,128)} %targets.1) | copy-start | bytes 614404
  18.3 9.6 %copy-start = (f32[2,512,512]{2,1,0:T(8,128)S(1)}, f32[2,512,512]{2,1,0:T(8,128)}, u32[]{:S(2)}) copy-start(f32[2,512,512]{2,1,0:T(8,128)} %features.5) | copy-start | bytes 6291460
  18.3 9.6 %copy-start.4 = (s32[4,512]{1,0:T(4,128)S(1)}, s32[4,512]{1,0:T(4,128)}, u32[]{:S(2)}) copy-start(s32[4,512]{1,0:T(4,128)} %edges.5) | copy-start | bytes 24580
  23.1 1.4 %collective-permute-start.4 = (f32[2,100,128]{2,1,0:T(8,128)S(1)}, f32[2,100,128]{2,1,0:T(8,128)S(1)}, u32[]{:S(2)}, u32[]{:S(2)}) collective-permute-start(f32[2,100,128]{2,1,0:T(8,128)S(1)} %get-tuple-element.75), channel_id=1, source_target_pairs={{0,64},{64,0},{128,192},{192,128},{1,65},{65,1},{129,193},{193,129... | collective-permute-start | bytes 307208 | tf_op jit(solution)/shard_map/ppermute | solution.py:416
  25.6 2.2 %collective-permute-start.7 = (f32[2,100,128]{2,1,0:T(8,128)S(1)}, f32[2,100,128]{2,1,0:T(8,128)S(1)}, u32[]{:S(2)}, u32[]{:S(2)}) collective-permute-start(f32[2,100,128]{2,1,0:T(8,128)S(1)} %get-tuple-element.81), channel_id=1, source_target_pairs={{0,64},{64,0},{128,192},{192,128},{1,65},{65,1},{129,193},{193,129... | collective-permute-start | bytes 307208 | tf_op jit(solution)/shard_map/ppermute | solution.py:449
  26.1 5.6 %collective-permute-start.5 = (f32[2,100,128]{2,1,0:T(8,128)S(1)}, f32[2,100,128]{2,1,0:T(8,128)S(1)}, u32[]{:S(2)}, u32[]{:S(2)}) collective-permute-start(f32[2,100,128]{2,1,0:T(8,128)S(1)} %get-tuple-element.78), channel_id=1, source_target_pairs={{0,128},{64,192},{128,0},{192,64},{1,129},{65,193},{129,1},{193,65... | collective-permute-start | bytes 307208 | tf_op jit(solution)/shard_map/ppermute | solution.py:450
  26.9 6.2 %collective-permute-start.6 = (f32[2,100,128]{2,1,0:T(8,128)S(1)}, f32[2,100,128]{2,1,0:T(8,128)S(1)}, u32[]{:S(2)}, u32[]{:S(2)}) collective-permute-start(f32[2,100,128]{2,1,0:T(8,128)S(1)} %get-tuple-element.79), channel_id=1, source_target_pairs={{0,192},{64,128},{128,64},{192,0},{1,193},{65,129},{129,65},{193,1... | collective-permute-start | bytes 307208 | tf_op jit(solution)/shard_map/ppermute | solution.py:451
  37.9 1.7 %collective-permute-start.9 = (f32[4,72,256]{2,1,0:T(8,128)S(1)}, f32[4,72,256]{2,1,0:T(8,128)S(1)}, u32[]{:S(2)}, u32[]{:S(2)}) collective-permute-start(f32[4,72,256]{2,1,0:T(8,128)S(1)} %get-tuple-element.99), channel_id=1, source_target_pairs={{0,64},{1,65},{2,66},{3,67},{4,68},{5,69},{6,70},{7,71},{8,72},{9,... | collective-permute-start | bytes 884744 | tf_op jit(solution)/shard_map/ppermute | solution.py:53
  38.1 11.3 %collective-permute-start.13 = (f32[4,72,256]{2,1,0:T(8,128)S(1)}, f32[4,72,256]{2,1,0:T(8,128)S(1)}, u32[]{:S(2)}, u32[]{:S(2)}) collective-permute-start(f32[4,72,256]{2,1,0:T(8,128)S(1)} %get-tuple-element.103), channel_id=1, source_target_pairs={{0,64},{1,65},{2,66},{3,67},{4,68},{5,69},{6,70},{7,71},{8,72},{9,... | collective-permute-start | bytes 884744 | tf_op jit(solution)/shard_map/ppermute | solution.py:53
  38.5 11.1 %collective-permute-start.11 = (f32[4,72,256]{2,1,0:T(8,128)S(1)}, f32[4,72,256]{2,1,0:T(8,128)S(1)}, u32[]{:S(2)}, u32[]{:S(2)}) collective-permute-start(f32[4,72,256]{2,1,0:T(8,128)S(1)} %get-tuple-element.101), channel_id=1, source_target_pairs={{0,64},{1,65},{2,66},{3,67},{4,68},{5,69},{6,70},{7,71},{8,72},{9,... | collective-permute-start | bytes 884744 | tf_op jit(solution)/shard_map/ppermute | solution.py:53
  38.6 11.4 %collective-permute-start.8 = (f32[4,72,256]{2,1,0:T(8,128)S(1)}, f32[4,72,256]{2,1,0:T(8,128)S(1)}, u32[]{:S(2)}, u32[]{:S(2)}) collective-permute-start(f32[4,72,256]{2,1,0:T(8,128)S(1)} %get-tuple-element.96), channel_id=1, source_target_pairs={{0,64},{1,65},{2,66},{3,67},{4,68},{5,69},{6,70},{7,71},{8,72},{9,... | collective-permute-start | bytes 884744 | tf_op jit(solution)/shard_map/ppermute | solution.py:53
  39.6 13.9 %collective-permute-start.10 = (f32[4,72,256]{2,1,0:T(8,128)S(1)}, f32[4,72,256]{2,1,0:T(8,128)S(1)}, u32[]{:S(2)}, u32[]{:S(2)}) collective-permute-start(f32[4,72,256]{2,1,0:T(8,128)S(1)} %add.69), channel_id=1, source_target_pairs={{0,2},{1,3},{2,0},{3,1},{4,6},{5,7},{6,4},{7,5},{8,10},{9,11},{10,... | collective-permute-start | bytes 884744 | tf_op jit(solution)/shard_map/ppermute | solution.py:53
  49.4 7.2 %collective-permute-start.14 = (f32[4,72,256]{2,1,0:T(8,128)S(1)}, f32[4,72,256]{2,1,0:T(8,128)S(1)}, u32[]{:S(2)}, u32[]{:S(2)}) collective-permute-start(f32[4,72,256]{2,1,0:T(8,128)S(1)} %add.72), channel_id=1, source_target_pairs={{0,3},{1,2},{2,1},{3,0},{4,7},{5,6},{6,5},{7,4},{8,11},{9,10},{10,... | collective-permute-start | bytes 884744 | tf_op jit(solution)/shard_map/ppermute | solution.py:53
  49.6 7.4 %collective-permute-start.12 = (f32[4,72,256]{2,1,0:T(8,128)S(1)}, f32[4,72,256]{2,1,0:T(8,128)S(1)}, u32[]{:S(2)}, u32[]{:S(2)}) collective-permute-start(f32[4,72,256]{2,1,0:T(8,128)S(1)} %add.71), channel_id=1, source_target_pairs={{0,1},{1,0},{2,3},{3,2},{4,5},{5,4},{6,7},{7,6},{8,9},{9,8},{10,11... | collective-permute-start | bytes 884744 | tf_op jit(solution)/shard_map/ppermute | solution.py:53
  50.0 10.5 %collective-permute-start.18 = (f32[2,32,512]{2,1,0:T(8,128)S(1)}, f32[2,32,512]{2,1,0:T(8,128)S(1)}, u32[]{:S(2)}, u32[]{:S(2)}) collective-permute-start(f32[2,32,512]{2,1,0:T(8,128)S(1)} %get-tuple-element.104), channel_id=1, source_target_pairs={{0,1},{1,2},{2,3},{3,4},{4,5},{5,6},{6,7},{7,8},{8,9},{9,10},{10,1... | collective-permute-start | bytes 393224 | tf_op jit(solution)/shard_map/ppermute | solution.py:483
  51.3 9.2 %collective-permute-start.19 = (f32[2,32,512]{2,1,0:T(8,128)S(1)}, f32[2,32,512]{2,1,0:T(8,128)S(1)}, u32[]{:S(2)}, u32[]{:S(2)}) collective-permute-start(f32[2,32,512]{2,1,0:T(8,128)S(1)} %get-tuple-element.105), channel_id=1, source_target_pairs={{1,0},{2,1},{3,2},{4,3},{5,4},{6,5},{7,6},{8,7},{9,8},{10,9},{11,1... | collective-permute-start | bytes 393224 | tf_op jit(solution)/shard_map/ppermute | solution.py:484
  57.1 5.7 %collective-permute-start.15 = (f32[1,72,256]{2,1,0:T(8,128)S(1)}, f32[1,72,256]{2,1,0:T(8,128)S(1)}, u32[]{:S(2)}, u32[]{:S(2)}) collective-permute-start(f32[1,72,256]{2,1,0:T(8,128)S(1)} %get-tuple-element.128), channel_id=1, source_target_pairs={{0,32},{1,33},{2,34},{3,35},{4,36},{5,37},{6,38},{7,39},{8,40},{9,... | collective-permute-start | bytes 221192 | tf_op jit(solution)/shard_map/ppermute | solution.py:53
  57.2 5.6 %collective-permute-start.16 = (f32[1,72,256]{2,1,0:T(8,128)S(1)}, f32[1,72,256]{2,1,0:T(8,128)S(1)}, u32[]{:S(2)}, u32[]{:S(2)}) collective-permute-start(f32[1,72,256]{2,1,0:T(8,128)S(1)} %get-tuple-element.127), channel_id=1, source_target_pairs={{0,128},{1,129},{2,130},{3,131},{4,132},{5,133},{6,134},{7,135},{8... | collective-permute-start | bytes 221192 | tf_op jit(solution)/shard_map/ppermute | solution.py:53
  57.3 7.9 %collective-permute-start.17 = (f32[1,72,256]{2,1,0:T(8,128)S(1)}, f32[1,72,256]{2,1,0:T(8,128)S(1)}, u32[]{:S(2)}, u32[]{:S(2)}) collective-permute-start(f32[1,72,256]{2,1,0:T(8,128)S(1)} %get-tuple-element.126), channel_id=1, source_target_pairs={{0,160},{1,161},{2,162},{3,163},{4,164},{5,165},{6,166},{7,167},{8... | collective-permute-start | bytes 221192 | tf_op jit(solution)/shard_map/ppermute | solution.py:53
  60.5 16.5 %copy-start.5 = (f32[512,512]{1,0:T(8,128)S(1)}, f32[512,512]{1,0:T(8,128)}, u32[]{:S(2)}) copy-start(f32[512,512]{1,0:T(8,128)} %weight.1) | copy-start | bytes 3145732
  65.3 6.1 %collective-permute-start.20 = (f32[1,72,256]{2,1,0:T(8,128)S(1)}, f32[1,72,256]{2,1,0:T(8,128)S(1)}, u32[]{:S(2)}, u32[]{:S(2)}) collective-permute-start(f32[1,72,256]{2,1,0:T(8,128)S(1)} %fusion.12), channel_id=1, source_target_pairs={{0,8},{1,9},{2,10},{3,11},{4,12},{5,13},{6,14},{7,15},{8,0},{9,1},... | collective-permute-start | bytes 221192 | tf_op jit(solution)/shard_map/ppermute | solution.py:53
  65.4 6.0 %collective-permute-start.21 = (f32[1,72,256]{2,1,0:T(8,128)S(1)}, f32[1,72,256]{2,1,0:T(8,128)S(1)}, u32[]{:S(2)}, u32[]{:S(2)}) collective-permute-start(f32[1,72,256]{2,1,0:T(8,128)S(1)} %fusion.12), channel_id=1, source_target_pairs={{0,4},{1,5},{2,6},{3,7},{4,0},{5,1},{6,2},{7,3},{8,12},{9,13},{10,... | collective-permute-start | bytes 221192 | tf_op jit(solution)/shard_map/ppermute | solution.py:53
  67.8 5.4 %collective-permute-start.22 = (f32[1,72,256]{2,1,0:T(8,128)S(1)}, f32[1,72,256]{2,1,0:T(8,128)S(1)}, u32[]{:S(2)}, u32[]{:S(2)}) collective-permute-start(f32[1,72,256]{2,1,0:T(8,128)S(1)} %fusion.12), channel_id=1, source_target_pairs={{0,12},{1,13},{2,14},{3,15},{4,8},{5,9},{6,10},{7,11},{8,4},{9,5},... | collective-permute-start | bytes 221192 | tf_op jit(solution)/shard_map/ppermute | solution.py:53
  73.3 8.0 %collective-permute-start.23 = (f32[1,72,256]{2,1,0:T(8,128)S(1)}, f32[1,72,256]{2,1,0:T(8,128)S(1)}, u32[]{:S(2)}, u32[]{:S(2)}) collective-permute-start(f32[1,72,256]{2,1,0:T(8,128)S(1)} %add_add_fusion.1), channel_id=1, source_target_pairs={{0,16},{1,17},{2,18},{3,19},{4,20},{5,21},{6,22},{7,23},{8,24},{9,... | collective-permute-start | bytes 221192 | tf_op jit(solution)/shard_map/ppermute | solution.py:53
  81.3 4.8 %collective-permute-start.24 = (f32[1,72,256]{2,1,0:T(8,128)S(1)}, f32[1,72,256]{2,1,0:T(8,128)S(1)}, u32[]{:S(2)}, u32[]{:S(2)}) collective-permute-start(f32[1,72,256]{2,1,0:T(8,128)S(1)} %get-tuple-element.125), channel_id=1, source_target_pairs={{0,32},{1,33},{2,34},{3,35},{4,36},{5,37},{6,38},{7,39},{8,40},{9,... | collective-permute-start | bytes 221192 | tf_op jit(solution)/shard_map/ppermute | solution.py:53
  81.6 6.8 %collective-permute-start.25 = (f32[1,72,256]{2,1,0:T(8,128)S(1)}, f32[1,72,256]{2,1,0:T(8,128)S(1)}, u32[]{:S(2)}, u32[]{:S(2)}) collective-permute-start(f32[1,72,256]{2,1,0:T(8,128)S(1)} %get-tuple-element.125), channel_id=1, source_target_pairs={{0,128},{1,129},{2,130},{3,131},{4,132},{5,133},{6,134},{7,135},{8... | collective-permute-start | bytes 221192 | tf_op jit(solution)/shard_map/ppermute | solution.py:53
  85.7 4.4 %collective-permute-start.26 = (f32[1,72,256]{2,1,0:T(8,128)S(1)}, f32[1,72,256]{2,1,0:T(8,128)S(1)}, u32[]{:S(2)}, u32[]{:S(2)}) collective-permute-start(f32[1,72,256]{2,1,0:T(8,128)S(1)} %get-tuple-element.125), channel_id=1, source_target_pairs={{0,160},{1,161},{2,162},{3,163},{4,164},{5,165},{6,166},{7,167},{8... | collective-permute-start | bytes 221192 | tf_op jit(solution)/shard_map/ppermute | solution.py:53
  90.1 11.6 %collective-permute-start.27 = (f32[4,72,256]{2,1,0:T(8,128)S(1)}, f32[4,72,256]{2,1,0:T(8,128)S(1)}, u32[]{:S(2)}, u32[]{:S(2)}) collective-permute-start(f32[4,72,256]{2,1,0:T(8,128)S(1)} %constant_dynamic-update-slice_fusion.refs_0_), channel_id=1, source_target_pairs={{0,2},{1,3},{2,0},{3,1},{4,6},{5,7},{6,4},{7,5},{8,10},{9,11},{10,... | collective-permute-start | bytes 884744 | tf_op jit(solution)/shard_map/ppermute | solution.py:53
  92.0 13.9 %collective-permute-start.28 = (f32[4,72,256]{2,1,0:T(8,128)S(1)}, f32[4,72,256]{2,1,0:T(8,128)S(1)}, u32[]{:S(2)}, u32[]{:S(2)}) collective-permute-start(f32[4,72,256]{2,1,0:T(8,128)S(1)} %constant_dynamic-update-slice_fusion.refs_0_), channel_id=1, source_target_pairs={{0,1},{1,0},{2,3},{3,2},{4,5},{5,4},{6,7},{7,6},{8,9},{9,8},{10,11... | collective-permute-start | bytes 884744 | tf_op jit(solution)/shard_map/ppermute | solution.py:53
  92.1 15.6 %collective-permute-start.29 = (f32[4,72,256]{2,1,0:T(8,128)S(1)}, f32[4,72,256]{2,1,0:T(8,128)S(1)}, u32[]{:S(2)}, u32[]{:S(2)}) collective-permute-start(f32[4,72,256]{2,1,0:T(8,128)S(1)} %constant_dynamic-update-slice_fusion.refs_0_), channel_id=1, source_target_pairs={{0,3},{1,2},{2,1},{3,0},{4,7},{5,6},{6,5},{7,4},{8,11},{9,10},{10,... | collective-permute-start | bytes 884744 | tf_op jit(solution)/shard_map/ppermute | solution.py:53
  93.4 15.5 %collective-permute-start.30 = (f32[4,72,256]{2,1,0:T(8,128)S(1)}, f32[4,72,256]{2,1,0:T(8,128)S(1)}, u32[]{:S(2)}, u32[]{:S(2)}) collective-permute-start(f32[4,72,256]{2,1,0:T(8,128)S(1)} %constant_dynamic-update-slice_fusion.refs_0_), channel_id=1, source_target_pairs={{0,64},{1,65},{2,66},{3,67},{4,68},{5,69},{6,70},{7,71},{8,72},{9,... | collective-permute-start | bytes 884744 | tf_op jit(solution)/shard_map/ppermute | solution.py:53
  101.7 7.3 %collective-permute-start.31 = (f32[4,72,256]{2,1,0:T(8,128)S(1)}, f32[4,72,256]{2,1,0:T(8,128)S(1)}, u32[]{:S(2)}, u32[]{:S(2)}) collective-permute-start(f32[4,72,256]{2,1,0:T(8,128)S(1)} %collective-permute-done.27.refs_1_), channel_id=1, source_target_pairs={{0,64},{1,65},{2,66},{3,67},{4,68},{5,69},{6,70},{7,71},{8,72},{9,... | collective-permute-start | bytes 884744 | tf_op jit(solution)/shard_map/ppermute | solution.py:53
  105.9 3.1 %collective-permute-start.32 = (f32[4,72,256]{2,1,0:T(8,128)S(1)}, f32[4,72,256]{2,1,0:T(8,128)S(1)}, u32[]{:S(2)}, u32[]{:S(2)}) collective-permute-start(f32[4,72,256]{2,1,0:T(8,128)S(1)} %collective-permute-done.28.refs_2_), channel_id=1, source_target_pairs={{0,64},{1,65},{2,66},{3,67},{4,68},{5,69},{6,70},{7,71},{8,72},{9,... | collective-permute-start | bytes 884744 | tf_op jit(solution)/shard_map/ppermute | solution.py:53
  107.7 2.5 %collective-permute-start.33 = (f32[4,72,256]{2,1,0:T(8,128)S(1)}, f32[4,72,256]{2,1,0:T(8,128)S(1)}, u32[]{:S(2)}, u32[]{:S(2)}) collective-permute-start(f32[4,72,256]{2,1,0:T(8,128)S(1)} %collective-permute-done.29.refs_3_), channel_id=1, source_target_pairs={{0,64},{1,65},{2,66},{3,67},{4,68},{5,69},{6,70},{7,71},{8,72},{9,... | collective-permute-start | bytes 884744 | tf_op jit(solution)/shard_map/ppermute | solution.py:53

commit v8 on v7

--- a/solution.py
+++ b/solution.py
@@ -27,12 +27,19 @@
     }
 
 
+def role_of(place):
+    return place["core"] ^ ((place["x"] ^ place["y"]) & 1)
+
+
 def exchange(change):
     pairs = []
     for member in range(4):
         for grid in range(64):
             place = place_of(member, grid)
-            place = {**place, **change(place)}
+            role, changed = role_of(place), change(place)
+            place = {**place, **changed}
+            if "core" not in changed:
+                place["core"] = role ^ ((place["x"] ^ place["y"]) & 1)
             member_to = ((place["y"] & 1) << 1) | place["core"]
             grid_to = ((place["y"] >> 1) << 5) | (place["z"] << 2) | place["x"]
             pairs.append((member * 64 + grid, member_to * 64 + grid_to))
@@ -41,10 +48,10 @@
 
 swap_core = exchange(lambda c: {"core": c["core"] ^ 1})
 first_axis = [
-    exchange(lambda c, k=k: {"x": c["x"] ^ k} if c["core"] == 0 else {"y": c["y"] ^ k}) for k in range(4)
+    exchange(lambda c, k=k: {"x": c["x"] ^ k} if role_of(c) == 0 else {"y": c["y"] ^ k}) for k in range(4)
 ]
 second_axis = [
-    exchange(lambda c, k=k: {"y": c["y"] ^ k} if c["core"] == 0 else {"x": c["x"] ^ k}) for k in range(4)
+    exchange(lambda c, k=k: {"y": c["y"] ^ k} if role_of(c) == 0 else {"x": c["x"] ^ k}) for k in range(4)
 ]
 along_z = [exchange(lambda c, k=k: {"z": c["z"] ^ k}) for k in range(8)]
 
@@ -79,13 +86,11 @@
         piece = (i // 2, pl.ds((i % 2) * half, half))
         loads.append(pltpu.make_async_copy(features.at[piece], held.at[piece], sems.at[1 + i]))
     loads.append(pltpu.make_async_copy(src_weight, held_src, sems.at[1 + 2 * members]))
-    loads[0].start()
-    loads[1].start()
+    for load in loads:
+        load.start()
     local = edges[...] - (me[1] - 1) * node_rows
     edges_t[...] = jnp.concatenate([local, local], axis=0).T
     loads[0].wait()
-    for load in loads[2:]:
-        load.start()
     high, low = split(0.5 * held_weight[...])
     for i in range(2 * members):
         loads[1 + i].wait()
@@ -311,11 +316,12 @@
     place = place_of(member, grid)
     x_then_y = place["x"] * 4 + place["y"]
     y_then_x = place["y"] * 4 + place["x"]
-    straight = place["core"] == 0
+    role = role_of(place)
+    straight = role == 0
     me = jnp.stack([
         member,
         grid,
-        place["core"],
+        role,
         jnp.where(straight, x_then_y, y_then_x),
         jnp.where(straight, y_then_x, x_then_y),
     ]).astype(jnp.int32)

time: 113 us -> 108 us (0.956)
  starting transfers between devices: 59 us -> 49.1 us
  waiting for transfers between devices: 21.9 us -> 27.5 us
    ppermute x24, starting transfers between devices: 45.3 us -> 35.2 us  [send(): return lax.ppermute(value, axes, pairs)]
    ppermute x24, waiting for transfers between devices: 18.2 us -> 23.8 us  [send(): return lax.ppermute(value, axes, pairs)]
  transfers between devices with their start and end apart: 34 -> 34, of which waited for: 15 -> 18; matrix products, arithmetic and copies ran while one was open for 5% -> 6% of each run, Pallas kernels for 11% -> 11%
where the time goes in v8:
time: 108 us
  starting transfers between devices  49.1 us (45%)
  waiting for transfers between devices  27.5 us (25%)
  Pallas kernels  24.1 us (22%)
  matrix products  5.7 us (5%)
  between operations  1.08 us (1%)
    ppermute x24, starting transfers between devices, send(): return lax.ppermute(value, axes, pairs)  35.2 us
    ppermute x24, waiting for transfers between devices, send(): return lax.ppermute(value, axes, pairs)  23.8 us
    pallas_call x1, Pallas kernels, body(): pl.pallas_call(query_kernel, in_specs=[me_spec, whole(), in_hbm, in_hbm,...  4.85 us
    pallas_call x1, Pallas kernels, body(): call(functools.partial(far_backward_kernel, scale, loss_scale), 'far_back...  4.83 us
    ppermute x1, starting transfers between devices, body(): before = lax.ppermute(mesh_features, 'grid', up)  3.95 us
    pallas_call x1, Pallas kernels, body(): call(far_forward_kernel, 'far_forward', forward_work, [rows_of(far), pl.B...  3.89 us
    pallas_call x1, Pallas kernels, body(): call(near_backward_kernel, 'near_backward', backward_work, backward_specs...  3.83 us
    pallas_call x1, Pallas kernels, body(): call(near_forward_kernel, 'near_forward', forward_work, [rows_of(near), p...  3.38 us
  transfers between devices with their start and end apart: 34, of which 18 were waited for; matrix products, arithmetic and copies ran while one was open for 6% of the time, Pallas kernels for 11%

profile of v8, /device:TPU:1, one launch (start us, length us, event | category | flops | bytes accessed | tf_op | source)
XLA Modules:
  0.0 107.9 jit_solution(9825533075156636412)
XLA Ops:
  0.6 4.0 %collective-permute-start = (f32[2,32,512]{2,1,0:T(8,128)}, f32[2,32,512]{2,1,0:T(8,128)S(1)}, u32[]{:S(2)}, u32[]{:S(2)}) collective-permute-start(f32[2,32,512]{2,1,0:T(8,128)} %own.3), channel_id=1, source_target_pairs={{0,1},{1,2},{2,3},{3,4},{4,5},{5,6},{6,7},{7,8},{8,9},{9,10},{10,1... | collective-permute-start | bytes 393224 | tf_op jit(solution)/shard_map/ppermute | solution.py:331
  4.6 1.3 %collective-permute-start.1 = (f32[2,32,512]{2,1,0:T(8,128)}, f32[2,32,512]{2,1,0:T(8,128)S(1)}, u32[]{:S(2)}, u32[]{:S(2)}) collective-permute-start(f32[2,32,512]{2,1,0:T(8,128)} %own.3), channel_id=1, source_target_pairs={{1,0},{2,1},{3,2},{4,3},{5,4},{6,5},{7,6},{8,7},{9,8},{10,9},{11,1... | collective-permute-start | bytes 393224 | tf_op jit(solution)/shard_map/ppermute | solution.py:332
  6.0 4.9 %query.1 = (f32[2,512,512]{2,1,0:T(8,128)S(1)}, s32[512,8]{1,0:T(8,128)S(1)}, bf16[512,512]{1,0:T(8,128)(2,1)S(1)}, bf16[512,512]{1,0:T(8,128)(2,1)S(1)}) custom-call(s32[5]{0:T(128)S(1)} %stack.23.me, s32[4,512]{1,0:T(4,128)} %edges.5, f32[2,512,512]{2,1,0:T(8,128)} %features.5, f32[512,512]{1,0:T(8,128)} %weight.1, f32[512,512]{1,0:T(8,128)} %src_weight.1), custom_call_target="tpu_custom_call" | custom-call | tf_op jit(solution)/shard_map/query/pallas_call | solution.py:336
  10.9 3.9 %far_forward.1 = (f32[2,4,256,512]{3,2,1,0:T(8,128)S(1)}, f32[2,256,512]{2,1,0:T(8,128)S(1)}, f32[2,100,128]{2,1,0:T(8,128)S(1)}, f32[2,100,128]{2,1,0:T(8,128)S(1)}, bf16[2,256,512]{2,1,0:T(8,128)(2,1)S(1)}) custom-call(s32[5]{0:T(128)S(1)} %stack.23.me, f32[2,512,512]{2,1,0:T(8,128)S(1)} %get-tuple-element.65.query, s32[512,8]{1,0:T(8,128)S(1)} %get-tuple-element.66.edges, ...), custom_call_target="tpu_custom_call" | custom-call | flops 1231028224 | bytes 2097152 | tf_op jit(solution)/shard_map/far_forward/pallas_call | solution.py:401
  14.8 1.4 %collective-permute-start.2 = (f32[2,100,128]{2,1,0:T(8,128)S(1)}, f32[2,100,128]{2,1,0:T(8,128)S(1)}, u32[]{:S(2)}, u32[]{:S(2)}) collective-permute-start(f32[2,100,128]{2,1,0:T(8,128)S(1)} %get-tuple-element.72), channel_id=1, source_target_pairs={{0,128},{64,192},{128,0},{192,64},{1,129},{65,193},{129,1},{193,65... | collective-permute-start | bytes 307208 | tf_op jit(solution)/shard_map/ppermute | solution.py:411
  16.2 2.0 %collective-permute-start.3 = (f32[2,100,128]{2,1,0:T(8,128)S(1)}, f32[2,100,128]{2,1,0:T(8,128)S(1)}, u32[]{:S(2)}, u32[]{:S(2)}) collective-permute-start(f32[2,100,128]{2,1,0:T(8,128)S(1)} %get-tuple-element.73), channel_id=1, source_target_pairs={{0,192},{64,128},{128,64},{192,0},{1,193},{65,129},{129,65},{193,1... | collective-permute-start | bytes 307208 | tf_op jit(solution)/shard_map/ppermute | solution.py:412
  18.2 3.4 %near_forward.1 = (f32[2,4,256,512]{3,2,1,0:T(8,128)S(1)}, f32[2,256,512]{2,1,0:T(8,128)S(1)}, f32[2,100,128]{2,1,0:T(8,128)S(1)}, f32[2,100,128]{2,1,0:T(8,128)S(1)}) custom-call(s32[5]{0:T(128)S(1)} %stack.23.me, f32[2,512,512]{2,1,0:T(8,128)S(1)} %get-tuple-element.65.query, s32[512,8]{1,0:T(8,128)S(1)} %get-tuple-element.66.edges, ...), custom_call_target="tpu_custom_call" | custom-call | flops 1231028224 | bytes 2097152 | tf_op jit(solution)/shard_map/near_forward/pallas_call | solution.py:413
  21.6 1.4 %collective-permute-done.3.part3 = f32[2,100,128]{2,1,0:T(8,128)S(1)} collective-permute-done((f32[2,100,128]{2,1,0:T(8,128)S(1)}, f32[2,100,128]{2,1,0:T(8,128)S(1)}, u32[]{:S(2)}, u32[]{:S(2)}) %collective-permute-start.3) | collective-permute-done | bytes 102432 | tf_op jit(solution)/shard_map/ppermute | solution.py:412
  23.1 0.4 collective-permute-start.4
  23.5 1.0 collective-permute-done.4.part1
  24.4 1.2 %score.1 = (f32[2,100,128]{2,1,0:T(8,128)S(1)}, f32[2,100,128]{2,1,0:T(8,128)S(1)}, f32[2,100,128]{2,1,0:T(8,128)S(1)}, f32[2,100,128]{2,1,0:T(8,128)S(1)}, f32[8,128]{1,0:T(8,128)S(1)}) custom-call(s32[5]{0:T(128)S(1)} %stack.23.me, f32[2,100,128]{2,1,0:T(8,128)S(1)} %get-tuple-element.74.part0, f32[2,100,128]{2,1,0:T(8,128)S(1)} %collective-permute-done.4.part1, ...), custom_call_target="tpu_custom_call" | custom-call | tf_op jit(solution)/shard_map/score/pallas_call | solution.py:424
  25.6 0.4 collective-permute-start.7
  26.1 0.8 collective-permute-start.5
  26.8 1.0 collective-permute-start.6
  27.9 3.8 %near_backward.1 = (f32[2,256,512]{2,1,0:T(8,128)S(1)}, f32[2,96,512]{2,1,0:T(8,128)S(1)}, f32[512,512]{1,0:T(8,128)S(1)}, f32[100,512]{1,0:T(8,128)S(1)}) custom-call(s32[5]{0:T(128)S(1)} %stack.23.me, f32[2,100,128]{2,1,0:T(8,128)S(1)} %get-tuple-element.80.same, f32[2,100,128]{2,1,0:T(8,128)S(1)} %collective-permute-done.7.flipped, ...), custom_call_target="tpu_custom_call" | custom-call | flops 2193620992 | bytes 2097152 | tf_op jit(solution)/shard_map/near_backward/pallas_call | solution.py:458
  31.7 1.3 %collective-permute-done.6.flipped = f32[2,100,128]{2,1,0:T(8,128)S(1)} collective-permute-done((f32[2,100,128]{2,1,0:T(8,128)S(1)}, f32[2,100,128]{2,1,0:T(8,128)S(1)}, u32[]{:S(2)}, u32[]{:S(2)}) %collective-permute-start.6) | collective-permute-done | bytes 102432 | tf_op jit(solution)/shard_map/ppermute | solution.py:457
  33.0 4.8 %far_backward.1 = (f32[2,256,512]{2,1,0:T(8,128)S(1)}, f32[2,32,512]{2,1,0:T(8,128)S(1)}, f32[2,32,512]{2,1,0:T(8,128)S(1)}, f32[2,32,512]{2,1,0:T(8,128)S(1)}, ...) custom-call(s32[5]{0:T(128)S(1)} %stack.23.me, ...), custom_call_target="tpu_custom_call" | custom-call | flops 2193620992 | bytes 2097152 | tf_op jit(solution)/shard_map/far_backward/pallas_call | solution.py:467
  38.1 0.4 collective-permute-start.13
  38.6 0.4 collective-permute-start.8
  39.0 0.6 collective-permute-done.9
  39.6 9.5 %collective-permute-start.10 = (f32[4,72,256]{2,1,0:T(8,128)S(1)}, f32[4,72,256]{2,1,0:T(8,128)S(1)}, u32[]{:S(2)}, u32[]{:S(2)}) collective-permute-start(f32[4,72,256]{2,1,0:T(8,128)S(1)} %add.69), channel_id=1, source_target_pairs={{0,2},{1,33},{2,0},{3,35},{4,6},{5,37},{6,4},{7,39},{8,10},{9,41},... | collective-permute-start | bytes 884744 | tf_op jit(solution)/shard_map/ppermute | solution.py:60
  49.3 0.7 collective-permute-start.12
  50.0 1.3 %collective-permute-start.18 = (f32[2,32,512]{2,1,0:T(8,128)S(1)}, f32[2,32,512]{2,1,0:T(8,128)S(1)}, u32[]{:S(2)}, u32[]{:S(2)}) collective-permute-start(f32[2,32,512]{2,1,0:T(8,128)S(1)} %get-tuple-element.104), channel_id=1, source_target_pairs={{0,1},{1,2},{2,3},{3,4},{4,5},{5,6},{6,7},{7,8},{8,9},{9,10},{10,1... | collective-permute-start | bytes 393224 | tf_op jit(solution)/shard_map/ppermute | solution.py:489
  51.3 1.3 %collective-permute-start.19 = (f32[2,32,512]{2,1,0:T(8,128)S(1)}, f32[2,32,512]{2,1,0:T(8,128)S(1)}, u32[]{:S(2)}, u32[]{:S(2)}) collective-permute-start(f32[2,32,512]{2,1,0:T(8,128)S(1)} %get-tuple-element.105), channel_id=1, source_target_pairs={{1,0},{2,1},{3,2},{4,3},{5,4},{6,5},{7,6},{8,7},{9,8},{10,9},{11,1... | collective-permute-start | bytes 393224 | tf_op jit(solution)/shard_map/ppermute | solution.py:490
  52.6 0.6 collective-permute-done.10
  53.2 3.4 %collective-permute-done.14 = f32[4,72,256]{2,1,0:T(8,128)S(1)} collective-permute-done((f32[4,72,256]{2,1,0:T(8,128)S(1)}, f32[4,72,256]{2,1,0:T(8,128)S(1)}, u32[]{:S(2)}, u32[]{:S(2)}) %collective-permute-start.14) | collective-permute-done | bytes 294944 | tf_op jit(solution)/shard_map/ppermute | solution.py:60
  56.6 0.7 collective-permute-done.12
  57.7 3.4 %collective-permute-start.17 = (f32[1,72,256]{2,1,0:T(8,128)S(1)}, f32[1,72,256]{2,1,0:T(8,128)S(1)}, u32[]{:S(2)}, u32[]{:S(2)}) collective-permute-start(f32[1,72,256]{2,1,0:T(8,128)S(1)} %get-tuple-element.126), channel_id=1, source_target_pairs={{0,224},{1,66},{2,226},{3,64},{4,228},{5,70},{6,230},{7,68},{8,232... | collective-permute-start | bytes 221192 | tf_op jit(solution)/shard_map/ppermute | solution.py:60
  61.1 2.0 %collective-permute-done.15 = f32[1,72,256]{2,1,0:T(8,128)S(1)} collective-permute-done((f32[1,72,256]{2,1,0:T(8,128)S(1)}, f32[1,72,256]{2,1,0:T(8,128)S(1)}, u32[]{:S(2)}, u32[]{:S(2)}) %collective-permute-start.15) | collective-permute-done | bytes 73760 | tf_op jit(solution)/shard_map/ppermute | solution.py:60
  63.1 1.8 %collective-permute-done.17 = f32[1,72,256]{2,1,0:T(8,128)S(1)} collective-permute-done((f32[1,72,256]{2,1,0:T(8,128)S(1)}, f32[1,72,256]{2,1,0:T(8,128)S(1)}, u32[]{:S(2)}, u32[]{:S(2)}) %collective-permute-start.17) | collective-permute-done | bytes 73760 | tf_op jit(solution)/shard_map/ppermute | solution.py:60
  64.9 0.6 collective-permute-start.20
  65.5 3.9 %collective-permute-start.21 = (f32[1,72,256]{2,1,0:T(8,128)S(1)}, f32[1,72,256]{2,1,0:T(8,128)S(1)}, u32[]{:S(2)}, u32[]{:S(2)}) collective-permute-start(f32[1,72,256]{2,1,0:T(8,128)S(1)} %fusion.12), channel_id=1, source_target_pairs={{0,4},{1,5},{2,6},{3,7},{4,0},{5,1},{6,2},{7,3},{8,12},{9,13},{10,... | collective-permute-start | bytes 221192 | tf_op jit(solution)/shard_map/ppermute | solution.py:60
  69.4 2.5 %fusion.7 = f32[2,32,512]{2,1,0:T(8,128)} fusion(f32[512,512]{1,0:T(8,128)} %src_weight.1, f32[2,32,512]{2,1,0:T(8,128)S(1)} %collective-permute-done.19, f32[2,32,512]{2,1,0:T(8,128)S(1)} %get-tuple-element.109, f32[2,32,512]{2,1,0:T(8,128)S(1)} %collective-permute-done.18), kind=kOutput, calls=%fused_computation.8 | convolution fusion | flops 100728832 | bytes 1572864 | tf_op jit(solution)/shard_map/nru,wu->nrw/dot_general | solution.py:496
  71.9 2.7 %collective-permute-done.22 = f32[1,72,256]{2,1,0:T(8,128)S(1)} collective-permute-done((f32[1,72,256]{2,1,0:T(8,128)S(1)}, f32[1,72,256]{2,1,0:T(8,128)S(1)}, u32[]{:S(2)}, u32[]{:S(2)}) %collective-permute-start.22) | collective-permute-done | bytes 73760 | tf_op jit(solution)/shard_map/ppermute | solution.py:60
  74.6 4.1 %collective-permute-start.23 = (f32[1,72,256]{2,1,0:T(8,128)S(1)}, f32[1,72,256]{2,1,0:T(8,128)S(1)}, u32[]{:S(2)}, u32[]{:S(2)}) collective-permute-start(f32[1,72,256]{2,1,0:T(8,128)S(1)} %add_add_fusion.1), channel_id=1, source_target_pairs={{0,16},{1,17},{2,18},{3,19},{4,20},{5,21},{6,22},{7,23},{8,24},{9,... | collective-permute-start | bytes 221192 | tf_op jit(solution)/shard_map/ppermute | solution.py:60
  78.6 3.2 %fusion = f32[2,512,512]{2,1,0:T(8,128)} fusion(f32[2,256,512]{2,1,0:T(8,128)S(1)} %get-tuple-element.116, f32[2,256,512]{2,1,0:T(8,128)S(1)} %get-tuple-element.115, f32[512,512]{1,0:T(8,128)S(1)} %copy-done.5, pred[]{:T(512)S(6)} %lt.15), kind=kOutput, calls=%fused_computation.1 | convolution fusion | flops 1612185600 | bytes 5242881 | tf_op jit(solution)/shard_map/npu,wu->npw/dot_general | solution.py:502
  82.2 6.6 %collective-permute-start.25 = (f32[1,72,256]{2,1,0:T(8,128)S(1)}, f32[1,72,256]{2,1,0:T(8,128)S(1)}, u32[]{:S(2)}, u32[]{:S(2)}) collective-permute-start(f32[1,72,256]{2,1,0:T(8,128)S(1)} %get-tuple-element.125), channel_id=1, source_target_pairs={{0,192},{1,64},{2,194},{3,66},{4,196},{5,68},{6,198},{7,70},{8,200... | collective-permute-start | bytes 221192 | tf_op jit(solution)/shard_map/ppermute | solution.py:60
  88.7 3.1 %collective-permute-done.25 = f32[1,72,256]{2,1,0:T(8,128)S(1)} collective-permute-done((f32[1,72,256]{2,1,0:T(8,128)S(1)}, f32[1,72,256]{2,1,0:T(8,128)S(1)}, u32[]{:S(2)}, u32[]{:S(2)}) %collective-permute-start.25) | collective-permute-done | bytes 73760 | tf_op jit(solution)/shard_map/ppermute | solution.py:60
  91.9 1.9 %collective-permute-done.26 = f32[1,72,256]{2,1,0:T(8,128)S(1)} collective-permute-done((f32[1,72,256]{2,1,0:T(8,128)S(1)}, f32[1,72,256]{2,1,0:T(8,128)S(1)}, u32[]{:S(2)}, u32[]{:S(2)}) %collective-permute-start.26) | collective-permute-done | bytes 73760 | tf_op jit(solution)/shard_map/ppermute | solution.py:60
  93.7 2.3 %collective-permute-start.27 = (f32[4,72,256]{2,1,0:T(8,128)S(1)}, f32[4,72,256]{2,1,0:T(8,128)S(1)}, u32[]{:S(2)}, u32[]{:S(2)}) collective-permute-start(f32[4,72,256]{2,1,0:T(8,128)S(1)} %constant_dynamic-update-slice_fusion.refs_0_), channel_id=1, source_target_pairs={{0,2},{1,33},{2,0},{3,35},{4,6},{5,37},{6,4},{7,39},{8,10},{9,41},... | collective-permute-start | bytes 884744 | tf_op jit(solution)/shard_map/ppermute | solution.py:60
  96.0 1.4 %collective-permute-start.29 = (f32[4,72,256]{2,1,0:T(8,128)S(1)}, f32[4,72,256]{2,1,0:T(8,128)S(1)}, u32[]{:S(2)}, u32[]{:S(2)}) collective-permute-start(f32[4,72,256]{2,1,0:T(8,128)S(1)} %constant_dynamic-update-slice_fusion.refs_0_), channel_id=1, source_target_pairs={{0,67},{1,225},{2,65},{3,227},{4,71},{5,229},{6,69},{7,231},{8,75}... | collective-permute-start | bytes 884744 | tf_op jit(solution)/shard_map/ppermute | solution.py:60
  97.4 3.6 %collective-permute-done.27.refs_1_ = f32[4,72,256]{2,1,0:T(8,128)S(1)} collective-permute-done((f32[4,72,256]{2,1,0:T(8,128)S(1)}, f32[4,72,256]{2,1,0:T(8,128)S(1)}, u32[]{:S(2)}, u32[]{:S(2)}) %collective-permute-start.27) | collective-permute-done | bytes 294944 | tf_op jit(solution)/shard_map/ppermute | solution.py:60
  101.0 0.4 collective-permute-start.31
  101.3 1.5 %collective-permute-done.28.refs_2_ = f32[4,72,256]{2,1,0:T(8,128)S(1)} collective-permute-done((f32[4,72,256]{2,1,0:T(8,128)S(1)}, f32[4,72,256]{2,1,0:T(8,128)S(1)}, u32[]{:S(2)}, u32[]{:S(2)}) %collective-permute-start.28) | collective-permute-done | bytes 294944 | tf_op jit(solution)/shard_map/ppermute | solution.py:60
  102.9 0.6 collective-permute-start.32
  103.5 0.6 collective-permute-done.29.refs_3_
  104.7 1.0 collective-permute-done.33.refs_7_
  105.6 2.1 %finish.1 = (f32[512,512]{1,0:T(8,128)}, f32[512,512]{1,0:T(8,128)}, f32[100,512]{1,0:T(8,128)}, f32[1,1]{1,0:T(1,128)}) custom-call(s32[5]{0:T(128)S(1)} %stack.23.me, f32[4,72,256]{2,1,0:T(8,128)S(1)} %constant_dynamic-update-slice_fusion.refs_0_, f32[4,72,256]{2,1,0:T(8,128)S(1)} %collective-permute-done.27.refs_1_, ...), custom_call_target="tpu_custom_call" | custom-call | tf_op jit(solution)/shard_map/finish/pallas_call | solution.py:509
  (54 shorter events, 2.0 us)
Async XLA Ops:
  0.6 10.2 %collective-permute-start = (f32[2,32,512]{2,1,0:T(8,128)}, f32[2,32,512]{2,1,0:T(8,128)S(1)}, u32[]{:S(2)}, u32[]{:S(2)}) collective-permute-start(f32[2,32,512]{2,1,0:T(8,128)} %own.3), channel_id=1, source_target_pairs={{0,1},{1,2},{2,3},{3,4},{4,5},{5,6},{6,7},{7,8},{8,9},{9,10},{10,1... | collective-permute-start | bytes 393224 | tf_op jit(solution)/shard_map/ppermute | solution.py:331
  4.6 6.3 %collective-permute-start.1 = (f32[2,32,512]{2,1,0:T(8,128)}, f32[2,32,512]{2,1,0:T(8,128)S(1)}, u32[]{:S(2)}, u32[]{:S(2)}) collective-permute-start(f32[2,32,512]{2,1,0:T(8,128)} %own.3), channel_id=1, source_target_pairs={{1,0},{2,1},{3,2},{4,3},{5,4},{6,5},{7,6},{8,7},{9,8},{10,9},{11,1... | collective-permute-start | bytes 393224 | tf_op jit(solution)/shard_map/ppermute | solution.py:332
  6.0 4.9 %copy-start.2 = (f32[512,100]{0,1:T(8,128)S(1)}, f32[512,100]{0,1:T(8,128)}, u32[]{:S(2)}) copy-start(f32[512,100]{0,1:T(8,128)} %param.13) | copy-start | bytes 614404
  6.0 4.9 %copy-start.3 = (f32[2,32,512]{2,1,0:T(8,128)S(1)}, f32[2,32,512]{2,1,0:T(8,128)}, u32[]{:S(2)}) copy-start(f32[2,32,512]{2,1,0:T(8,128)} %own.3) | copy-start | bytes 393220
  14.8 6.8 %collective-permute-start.2 = (f32[2,100,128]{2,1,0:T(8,128)S(1)}, f32[2,100,128]{2,1,0:T(8,128)S(1)}, u32[]{:S(2)}, u32[]{:S(2)}) collective-permute-start(f32[2,100,128]{2,1,0:T(8,128)S(1)} %get-tuple-element.72), channel_id=1, source_target_pairs={{0,128},{64,192},{128,0},{192,64},{1,129},{65,193},{129,1},{193,65... | collective-permute-start | bytes 307208 | tf_op jit(solution)/shard_map/ppermute | solution.py:411
  16.2 6.9 %collective-permute-start.3 = (f32[2,100,128]{2,1,0:T(8,128)S(1)}, f32[2,100,128]{2,1,0:T(8,128)S(1)}, u32[]{:S(2)}, u32[]{:S(2)}) collective-permute-start(f32[2,100,128]{2,1,0:T(8,128)S(1)} %get-tuple-element.73), channel_id=1, source_target_pairs={{0,192},{64,128},{128,64},{192,0},{1,193},{65,129},{129,65},{193,1... | collective-permute-start | bytes 307208 | tf_op jit(solution)/shard_map/ppermute | solution.py:412
  18.2 6.2 %copy-start.1 = (f32[100,512]{1,0:T(8,128)S(1)}, f32[100,512]{1,0:T(8,128)}, u32[]{:S(2)}) copy-start(f32[100,512]{1,0:T(8,128)} %targets.1) | copy-start | bytes 614404
  18.2 9.6 %copy-start = (f32[2,512,512]{2,1,0:T(8,128)S(1)}, f32[2,512,512]{2,1,0:T(8,128)}, u32[]{:S(2)}) copy-start(f32[2,512,512]{2,1,0:T(8,128)} %features.5) | copy-start | bytes 6291460
  18.2 9.6 %copy-start.4 = (s32[4,512]{1,0:T(4,128)S(1)}, s32[4,512]{1,0:T(4,128)}, u32[]{:S(2)}) copy-start(s32[4,512]{1,0:T(4,128)} %edges.5) | copy-start | bytes 24580
  23.1 1.4 %collective-permute-start.4 = (f32[2,100,128]{2,1,0:T(8,128)S(1)}, f32[2,100,128]{2,1,0:T(8,128)S(1)}, u32[]{:S(2)}, u32[]{:S(2)}) collective-permute-start(f32[2,100,128]{2,1,0:T(8,128)S(1)} %get-tuple-element.75), channel_id=1, source_target_pairs={{0,64},{64,0},{128,192},{192,128},{1,65},{65,1},{129,193},{193,129... | collective-permute-start | bytes 307208 | tf_op jit(solution)/shard_map/ppermute | solution.py:422
  25.6 2.2 %collective-permute-start.7 = (f32[2,100,128]{2,1,0:T(8,128)S(1)}, f32[2,100,128]{2,1,0:T(8,128)S(1)}, u32[]{:S(2)}, u32[]{:S(2)}) collective-permute-start(f32[2,100,128]{2,1,0:T(8,128)S(1)} %get-tuple-element.81), channel_id=1, source_target_pairs={{0,64},{64,0},{128,192},{192,128},{1,65},{65,1},{129,193},{193,129... | collective-permute-start | bytes 307208 | tf_op jit(solution)/shard_map/ppermute | solution.py:455
  26.1 5.7 %collective-permute-start.5 = (f32[2,100,128]{2,1,0:T(8,128)S(1)}, f32[2,100,128]{2,1,0:T(8,128)S(1)}, u32[]{:S(2)}, u32[]{:S(2)}) collective-permute-start(f32[2,100,128]{2,1,0:T(8,128)S(1)} %get-tuple-element.78), channel_id=1, source_target_pairs={{0,128},{64,192},{128,0},{192,64},{1,129},{65,193},{129,1},{193,65... | collective-permute-start | bytes 307208 | tf_op jit(solution)/shard_map/ppermute | solution.py:456
  26.8 6.2 %collective-permute-start.6 = (f32[2,100,128]{2,1,0:T(8,128)S(1)}, f32[2,100,128]{2,1,0:T(8,128)S(1)}, u32[]{:S(2)}, u32[]{:S(2)}) collective-permute-start(f32[2,100,128]{2,1,0:T(8,128)S(1)} %get-tuple-element.79), channel_id=1, source_target_pairs={{0,192},{64,128},{128,64},{192,0},{1,193},{65,129},{129,65},{193,1... | collective-permute-start | bytes 307208 | tf_op jit(solution)/shard_map/ppermute | solution.py:457
  37.9 1.7 %collective-permute-start.9 = (f32[4,72,256]{2,1,0:T(8,128)S(1)}, f32[4,72,256]{2,1,0:T(8,128)S(1)}, u32[]{:S(2)}, u32[]{:S(2)}) collective-permute-start(f32[4,72,256]{2,1,0:T(8,128)S(1)} %get-tuple-element.99), channel_id=1, source_target_pairs={{0,64},{1,65},{2,66},{3,67},{4,68},{5,69},{6,70},{7,71},{8,72},{9,... | collective-permute-start | bytes 884744 | tf_op jit(solution)/shard_map/ppermute | solution.py:60
  38.1 11.0 %collective-permute-start.13 = (f32[4,72,256]{2,1,0:T(8,128)S(1)}, f32[4,72,256]{2,1,0:T(8,128)S(1)}, u32[]{:S(2)}, u32[]{:S(2)}) collective-permute-start(f32[4,72,256]{2,1,0:T(8,128)S(1)} %get-tuple-element.103), channel_id=1, source_target_pairs={{0,64},{1,65},{2,66},{3,67},{4,68},{5,69},{6,70},{7,71},{8,72},{9,... | collective-permute-start | bytes 884744 | tf_op jit(solution)/shard_map/ppermute | solution.py:60
  38.5 10.8 %collective-permute-start.11 = (f32[4,72,256]{2,1,0:T(8,128)S(1)}, f32[4,72,256]{2,1,0:T(8,128)S(1)}, u32[]{:S(2)}, u32[]{:S(2)}) collective-permute-start(f32[4,72,256]{2,1,0:T(8,128)S(1)} %get-tuple-element.101), channel_id=1, source_target_pairs={{0,64},{1,65},{2,66},{3,67},{4,68},{5,69},{6,70},{7,71},{8,72},{9,... | collective-permute-start | bytes 884744 | tf_op jit(solution)/shard_map/ppermute | solution.py:60
  38.6 11.4 %collective-permute-start.8 = (f32[4,72,256]{2,1,0:T(8,128)S(1)}, f32[4,72,256]{2,1,0:T(8,128)S(1)}, u32[]{:S(2)}, u32[]{:S(2)}) collective-permute-start(f32[4,72,256]{2,1,0:T(8,128)S(1)} %get-tuple-element.96), channel_id=1, source_target_pairs={{0,64},{1,65},{2,66},{3,67},{4,68},{5,69},{6,70},{7,71},{8,72},{9,... | collective-permute-start | bytes 884744 | tf_op jit(solution)/shard_map/ppermute | solution.py:60
  39.6 13.6 %collective-permute-start.10 = (f32[4,72,256]{2,1,0:T(8,128)S(1)}, f32[4,72,256]{2,1,0:T(8,128)S(1)}, u32[]{:S(2)}, u32[]{:S(2)}) collective-permute-start(f32[4,72,256]{2,1,0:T(8,128)S(1)} %add.69), channel_id=1, source_target_pairs={{0,2},{1,33},{2,0},{3,35},{4,6},{5,37},{6,4},{7,39},{8,10},{9,41},... | collective-permute-start | bytes 884744 | tf_op jit(solution)/shard_map/ppermute | solution.py:60
  49.2 7.4 %collective-permute-start.14 = (f32[4,72,256]{2,1,0:T(8,128)S(1)}, f32[4,72,256]{2,1,0:T(8,128)S(1)}, u32[]{:S(2)}, u32[]{:S(2)}) collective-permute-start(f32[4,72,256]{2,1,0:T(8,128)S(1)} %add.72), channel_id=1, source_target_pairs={{0,67},{1,225},{2,65},{3,227},{4,71},{5,229},{6,69},{7,231},{8,75}... | collective-permute-start | bytes 884744 | tf_op jit(solution)/shard_map/ppermute | solution.py:60
  49.3 8.0 %collective-permute-start.12 = (f32[4,72,256]{2,1,0:T(8,128)S(1)}, f32[4,72,256]{2,1,0:T(8,128)S(1)}, u32[]{:S(2)}, u32[]{:S(2)}) collective-permute-start(f32[4,72,256]{2,1,0:T(8,128)S(1)} %add.71), channel_id=1, source_target_pairs={{0,65},{1,193},{2,67},{3,195},{4,69},{5,197},{6,71},{7,199},{8,73}... | collective-permute-start | bytes 884744 | tf_op jit(solution)/shard_map/ppermute | solution.py:60
  50.0 11.1 %collective-permute-start.18 = (f32[2,32,512]{2,1,0:T(8,128)S(1)}, f32[2,32,512]{2,1,0:T(8,128)S(1)}, u32[]{:S(2)}, u32[]{:S(2)}) collective-permute-start(f32[2,32,512]{2,1,0:T(8,128)S(1)} %get-tuple-element.104), channel_id=1, source_target_pairs={{0,1},{1,2},{2,3},{3,4},{4,5},{5,6},{6,7},{7,8},{8,9},{9,10},{10,1... | collective-permute-start | bytes 393224 | tf_op jit(solution)/shard_map/ppermute | solution.py:489
  51.3 9.8 %collective-permute-start.19 = (f32[2,32,512]{2,1,0:T(8,128)S(1)}, f32[2,32,512]{2,1,0:T(8,128)S(1)}, u32[]{:S(2)}, u32[]{:S(2)}) collective-permute-start(f32[2,32,512]{2,1,0:T(8,128)S(1)} %get-tuple-element.105), channel_id=1, source_target_pairs={{1,0},{2,1},{3,2},{4,3},{5,4},{6,5},{7,6},{8,7},{9,8},{10,9},{11,1... | collective-permute-start | bytes 393224 | tf_op jit(solution)/shard_map/ppermute | solution.py:490
  57.5 5.7 %collective-permute-start.15 = (f32[1,72,256]{2,1,0:T(8,128)S(1)}, f32[1,72,256]{2,1,0:T(8,128)S(1)}, u32[]{:S(2)}, u32[]{:S(2)}) collective-permute-start(f32[1,72,256]{2,1,0:T(8,128)S(1)} %get-tuple-element.128), channel_id=1, source_target_pairs={{0,32},{1,3},{2,34},{3,1},{4,36},{5,7},{6,38},{7,5},{8,40},{9,11},... | collective-permute-start | bytes 221192 | tf_op jit(solution)/shard_map/ppermute | solution.py:60
  57.6 5.6 %collective-permute-start.16 = (f32[1,72,256]{2,1,0:T(8,128)S(1)}, f32[1,72,256]{2,1,0:T(8,128)S(1)}, u32[]{:S(2)}, u32[]{:S(2)}) collective-permute-start(f32[1,72,256]{2,1,0:T(8,128)S(1)} %get-tuple-element.127), channel_id=1, source_target_pairs={{0,192},{1,64},{2,194},{3,66},{4,196},{5,68},{6,198},{7,70},{8,200... | collective-permute-start | bytes 221192 | tf_op jit(solution)/shard_map/ppermute | solution.py:60
  57.7 7.2 %collective-permute-start.17 = (f32[1,72,256]{2,1,0:T(8,128)S(1)}, f32[1,72,256]{2,1,0:T(8,128)S(1)}, u32[]{:S(2)}, u32[]{:S(2)}) collective-permute-start(f32[1,72,256]{2,1,0:T(8,128)S(1)} %get-tuple-element.126), channel_id=1, source_target_pairs={{0,224},{1,66},{2,226},{3,64},{4,228},{5,70},{6,230},{7,68},{8,232... | collective-permute-start | bytes 221192 | tf_op jit(solution)/shard_map/ppermute | solution.py:60
  61.1 17.6 %copy-start.5 = (f32[512,512]{1,0:T(8,128)S(1)}, f32[512,512]{1,0:T(8,128)}, u32[]{:S(2)}) copy-start(f32[512,512]{1,0:T(8,128)} %weight.1) | copy-start | bytes 3145732
  64.9 7.0 %collective-permute-start.20 = (f32[1,72,256]{2,1,0:T(8,128)S(1)}, f32[1,72,256]{2,1,0:T(8,128)S(1)}, u32[]{:S(2)}, u32[]{:S(2)}) collective-permute-start(f32[1,72,256]{2,1,0:T(8,128)S(1)} %fusion.12), channel_id=1, source_target_pairs={{0,8},{1,9},{2,10},{3,11},{4,12},{5,13},{6,14},{7,15},{8,0},{9,1},... | collective-permute-start | bytes 221192 | tf_op jit(solution)/shard_map/ppermute | solution.py:60
  65.5 6.4 %collective-permute-start.21 = (f32[1,72,256]{2,1,0:T(8,128)S(1)}, f32[1,72,256]{2,1,0:T(8,128)S(1)}, u32[]{:S(2)}, u32[]{:S(2)}) collective-permute-start(f32[1,72,256]{2,1,0:T(8,128)S(1)} %fusion.12), channel_id=1, source_target_pairs={{0,4},{1,5},{2,6},{3,7},{4,0},{5,1},{6,2},{7,3},{8,12},{9,13},{10,... | collective-permute-start | bytes 221192 | tf_op jit(solution)/shard_map/ppermute | solution.py:60
  69.4 5.2 %collective-permute-start.22 = (f32[1,72,256]{2,1,0:T(8,128)S(1)}, f32[1,72,256]{2,1,0:T(8,128)S(1)}, u32[]{:S(2)}, u32[]{:S(2)}) collective-permute-start(f32[1,72,256]{2,1,0:T(8,128)S(1)} %fusion.12), channel_id=1, source_target_pairs={{0,12},{1,13},{2,14},{3,15},{4,8},{5,9},{6,10},{7,11},{8,4},{9,5},... | collective-permute-start | bytes 221192 | tf_op jit(solution)/shard_map/ppermute | solution.py:60
  74.6 7.4 %collective-permute-start.23 = (f32[1,72,256]{2,1,0:T(8,128)S(1)}, f32[1,72,256]{2,1,0:T(8,128)S(1)}, u32[]{:S(2)}, u32[]{:S(2)}) collective-permute-start(f32[1,72,256]{2,1,0:T(8,128)S(1)} %add_add_fusion.1), channel_id=1, source_target_pairs={{0,16},{1,17},{2,18},{3,19},{4,20},{5,21},{6,22},{7,23},{8,24},{9,... | collective-permute-start | bytes 221192 | tf_op jit(solution)/shard_map/ppermute | solution.py:60
  82.0 6.7 %collective-permute-start.24 = (f32[1,72,256]{2,1,0:T(8,128)S(1)}, f32[1,72,256]{2,1,0:T(8,128)S(1)}, u32[]{:S(2)}, u32[]{:S(2)}) collective-permute-start(f32[1,72,256]{2,1,0:T(8,128)S(1)} %get-tuple-element.125), channel_id=1, source_target_pairs={{0,32},{1,3},{2,34},{3,1},{4,36},{5,7},{6,38},{7,5},{8,40},{9,11},... | collective-permute-start | bytes 221192 | tf_op jit(solution)/shard_map/ppermute | solution.py:60
  82.2 9.7 %collective-permute-start.25 = (f32[1,72,256]{2,1,0:T(8,128)S(1)}, f32[1,72,256]{2,1,0:T(8,128)S(1)}, u32[]{:S(2)}, u32[]{:S(2)}) collective-permute-start(f32[1,72,256]{2,1,0:T(8,128)S(1)} %get-tuple-element.125), channel_id=1, source_target_pairs={{0,192},{1,64},{2,194},{3,66},{4,196},{5,68},{6,198},{7,70},{8,200... | collective-permute-start | bytes 221192 | tf_op jit(solution)/shard_map/ppermute | solution.py:60
  88.7 5.0 %collective-permute-start.26 = (f32[1,72,256]{2,1,0:T(8,128)S(1)}, f32[1,72,256]{2,1,0:T(8,128)S(1)}, u32[]{:S(2)}, u32[]{:S(2)}) collective-permute-start(f32[1,72,256]{2,1,0:T(8,128)S(1)} %get-tuple-element.125), channel_id=1, source_target_pairs={{0,224},{1,66},{2,226},{3,64},{4,228},{5,70},{6,230},{7,68},{8,232... | collective-permute-start | bytes 221192 | tf_op jit(solution)/shard_map/ppermute | solution.py:60
  93.7 7.2 %collective-permute-start.27 = (f32[4,72,256]{2,1,0:T(8,128)S(1)}, f32[4,72,256]{2,1,0:T(8,128)S(1)}, u32[]{:S(2)}, u32[]{:S(2)}) collective-permute-start(f32[4,72,256]{2,1,0:T(8,128)S(1)} %constant_dynamic-update-slice_fusion.refs_0_), channel_id=1, source_target_pairs={{0,2},{1,33},{2,0},{3,35},{4,6},{5,37},{6,4},{7,39},{8,10},{9,41},... | collective-permute-start | bytes 884744 | tf_op jit(solution)/shard_map/ppermute | solution.py:60
  96.0 6.9 %collective-permute-start.28 = (f32[4,72,256]{2,1,0:T(8,128)S(1)}, f32[4,72,256]{2,1,0:T(8,128)S(1)}, u32[]{:S(2)}, u32[]{:S(2)}) collective-permute-start(f32[4,72,256]{2,1,0:T(8,128)S(1)} %constant_dynamic-update-slice_fusion.refs_0_), channel_id=1, source_target_pairs={{0,65},{1,193},{2,67},{3,195},{4,69},{5,197},{6,71},{7,199},{8,73}... | collective-permute-start | bytes 884744 | tf_op jit(solution)/shard_map/ppermute | solution.py:60
  96.0 8.1 %collective-permute-start.29 = (f32[4,72,256]{2,1,0:T(8,128)S(1)}, f32[4,72,256]{2,1,0:T(8,128)S(1)}, u32[]{:S(2)}, u32[]{:S(2)}) collective-permute-start(f32[4,72,256]{2,1,0:T(8,128)S(1)} %constant_dynamic-update-slice_fusion.refs_0_), channel_id=1, source_target_pairs={{0,67},{1,225},{2,65},{3,227},{4,71},{5,229},{6,69},{7,231},{8,75}... | collective-permute-start | bytes 884744 | tf_op jit(solution)/shard_map/ppermute | solution.py:60
  97.4 7.0 %collective-permute-start.30 = (f32[4,72,256]{2,1,0:T(8,128)S(1)}, f32[4,72,256]{2,1,0:T(8,128)S(1)}, u32[]{:S(2)}, u32[]{:S(2)}) collective-permute-start(f32[4,72,256]{2,1,0:T(8,128)S(1)} %constant_dynamic-update-slice_fusion.refs_0_), channel_id=1, source_target_pairs={{0,64},{1,65},{2,66},{3,67},{4,68},{5,69},{6,70},{7,71},{8,72},{9,... | collective-permute-start | bytes 884744 | tf_op jit(solution)/shard_map/ppermute | solution.py:60
  101.0 3.4 %collective-permute-start.31 = (f32[4,72,256]{2,1,0:T(8,128)S(1)}, f32[4,72,256]{2,1,0:T(8,128)S(1)}, u32[]{:S(2)}, u32[]{:S(2)}) collective-permute-start(f32[4,72,256]{2,1,0:T(8,128)S(1)} %collective-permute-done.27.refs_1_), channel_id=1, source_target_pairs={{0,64},{1,65},{2,66},{3,67},{4,68},{5,69},{6,70},{7,71},{8,72},{9,... | collective-permute-start | bytes 884744 | tf_op jit(solution)/shard_map/ppermute | solution.py:60
  102.9 1.8 %collective-permute-start.32 = (f32[4,72,256]{2,1,0:T(8,128)S(1)}, f32[4,72,256]{2,1,0:T(8,128)S(1)}, u32[]{:S(2)}, u32[]{:S(2)}) collective-permute-start(f32[4,72,256]{2,1,0:T(8,128)S(1)} %collective-permute-done.28.refs_2_), channel_id=1, source_target_pairs={{0,64},{1,65},{2,66},{3,67},{4,68},{5,69},{6,70},{7,71},{8,72},{9,... | collective-permute-start | bytes 884744 | tf_op jit(solution)/shard_map/ppermute | solution.py:60
  104.1 1.6 %collective-permute-start.33 = (f32[4,72,256]{2,1,0:T(8,128)S(1)}, f32[4,72,256]{2,1,0:T(8,128)S(1)}, u32[]{:S(2)}, u32[]{:S(2)}) collective-permute-start(f32[4,72,256]{2,1,0:T(8,128)S(1)} %collective-permute-done.29.refs_3_), channel_id=1, source_target_pairs={{0,64},{1,65},{2,66},{3,67},{4,68},{5,69},{6,70},{7,71},{8,72},{9,... | collective-permute-start | bytes 884744 | tf_op jit(solution)/shard_map/ppermute | solution.py:60

commit v9 on v8

--- a/solution.py
+++ b/solution.py
@@ -125,7 +125,15 @@
     flipped[member] = jnp.where(even, right, left)
 
 
-def far_forward_kernel(me, query, edges, before, own, after, src_high, src_low, out_weight,
+def extended(me, one, own, two):
+    even = (me[1] & 1) == 0
+    rows = []
+    for n in range(own.shape[0]):
+        rows += [jnp.where(even, two[n], one[n]), own[n], jnp.where(even, one[n], two[n])]
+    return jnp.concatenate(rows, axis=0)
+
+
+def far_forward_kernel(me, query, edges, one, own, two, src_high, src_low, out_weight,
                        slope, summed, same, flipped, nodes):
     member = pl.program_id(0)
     rows = own.shape[1]
@@ -133,7 +141,7 @@
     @pl.when(member == 0)
     def _():
         nodes[...] = jnp.zeros_like(nodes)
-        ext = jnp.concatenate([side[n] for n in range(2) for side in (before, own, after)], axis=0)
+        ext = extended(me, one, own, two)
         high, low = split(dot3(split(ext), (src_high[...], src_low[...]), NN))
         for n in range(2):
             at = slice(n * 3 * rows, (n + 1) * 3 * rows)
@@ -229,8 +237,8 @@
 
 
 def far_backward_kernel(scale, loss_scale, me, same, flipped, slope, summed, features, edges, out_weight,
-                        near_ext, near_dst, near_out, loss, before, own, after,
-                        grad_query, lower, middle, upper, *rest):
+                        near_ext, near_dst, near_out, loss, one, own, two,
+                        grad_query, to_one, middle, to_two, *rest):
     keep, away, (grad_ext, sums) = rest[:4], rest[4:8], rest[8:]
     member = pl.program_id(0)
     rows = own.shape[1]
@@ -251,12 +259,15 @@
 
     @pl.when(member == pl.num_programs(0) - 1)
     def _():
-        ext = jnp.concatenate([side[n] for n in range(2) for side in (before, own, after)], axis=0)
+        ext = extended(me, one, own, two)
         grads = jnp.concatenate([grad_ext[0], grad_ext[1]], axis=0)
         sums[0:width] = dot3(split(ext), split(grads), TN)
+        even = (me[1] & 1) == 0
         for n in range(2):
-            for i, side in enumerate((lower, middle, upper)):
-                side[n] = grad_ext[n, i * rows : (i + 1) * rows]
+            lower, upper = grad_ext[n, 0:rows], grad_ext[n, 2 * rows : 3 * rows]
+            to_one[n] = jnp.where(even, upper, lower)
+            to_two[n] = jnp.where(even, lower, upper)
+            middle[n] = grad_ext[n, rows : 2 * rows]
         end = 2 * width + loss_row
         sums[end : end + 8] = jnp.full((8, width), jnp.sum(loss[0:1]) * (loss_scale / scale), f32)
         for j in range(16):
@@ -326,10 +337,11 @@
         jnp.where(straight, y_then_x, x_then_y),
     ]).astype(jnp.int32)
 
-    up = [(i, i + 1) for i in range(slabs - 1)]
-    down = [(j, i) for i, j in up]
-    before = lax.ppermute(mesh_features, "grid", up)
-    after = lax.ppermute(mesh_features, "grid", down)
+    even_pairs = [(i, i ^ 1) for i in range(slabs)]
+    odd_pairs = [(i, i + 1) for i in range(1, slabs - 1, 2)]
+    odd_pairs += [(j, i) for i, j in odd_pairs]
+    one = lax.ppermute(mesh_features, "grid", even_pairs)
+    two = lax.ppermute(mesh_features, "grid", odd_pairs)
     out_weight = output_weight.T
     me_spec = pl.BlockSpec(memory_space=pltpu.SMEM)
     in_hbm = pl.BlockSpec(memory_space=pltpu.HBM)
@@ -406,7 +418,7 @@
         [half_slopes, halves] + [whole()] * 3,
         [slopes_shape, half_shape, part_shape, part_shape]
         + [jax.ShapeDtypeStruct((members, 256, width), bf16)],
-    )(me, query, edges_t, before, mesh_features, after, src_high, src_low, out_weight)
+    )(me, query, edges_t, one, mesh_features, two, src_high, src_low, out_weight)
     to_peer = [[(i, i ^ k) for i in range(4)] for k in range(4)]
     part2 = lax.ppermute(part2, "member", to_peer[2])
     part3 = lax.ppermute(part3, "member", to_peer[3])
@@ -464,7 +476,7 @@
         [half_shape, ext_shape, jax.ShapeDtypeStruct((width, width), f32), out_sum_shape],
     )(me, slopes[0], slope1, near_slope, near_summed, grid_features, edges, out_weight)
     slope2, slope3, near_dst = lax.optimization_barrier((slope2, slope3, near_dst))
-    far_grad, lower, middle, upper, *parts = call(
+    far_grad, to_one, middle, to_two, *parts = call(
         functools.partial(far_backward_kernel, scale, loss_scale),
         "far_backward",
         backward_work,
@@ -473,7 +485,7 @@
         [half_shape] + [side] * 3 + [chunks] * 8,
         [pltpu.VMEM((members, 3 * rows, width), f32), pltpu.VMEM((1152, width), f32)],
     )(me, slope2, slope3, far_slope, far_summed, grid_features, edges, out_weight,
-      near_ext, near_dst, near_out, loss, before, mesh_features, after)
+      near_ext, near_dst, near_out, loss, one, mesh_features, two)
     grad_query = jnp.where(
         member < 2,
         jnp.concatenate([near_grad, far_grad], axis=1),
@@ -485,16 +497,16 @@
     swapped = [send(away[k], swap_core) for k in order + (0,)]
     halves = [keep[k] + part for k, part in zip(order, swapped)]
     parts = [send(half, first_axis[k]) for k, half in zip(order, halves)]
-    upper, lower, last = lax.optimization_barrier((upper, lower, swapped[3]))
-    from_prev = lax.ppermute(upper, "grid", up)
-    from_next = lax.ppermute(lower, "grid", down)
+    to_one, last = lax.optimization_barrier((to_one, swapped[3]))
+    from_one = lax.ppermute(to_one, "grid", even_pairs)
     total = tree(keep[0] + last, parts)
     parts = [send(total[k : k + 1], second_axis[k]) for k in order]
-    *parts, from_prev, from_next = lax.optimization_barrier((*parts, from_prev, from_next))
+    parts[0], from_one, to_two = lax.optimization_barrier((parts[0], from_one, to_two))
+    from_two = lax.ppermute(to_two, "grid", odd_pairs)
     total = tree(total[:1], parts)
     parts = [send(total, along_z[k]) for k in order]
     mesh_grad = jnp.einsum(
-        "nru,wu->nrw", middle + from_prev + from_next, src_weight, precision=lax.Precision.HIGH
+        "nru,wu->nrw", middle + from_one + from_two, src_weight, precision=lax.Precision.HIGH
     )
     *parts, mesh_grad = lax.optimization_barrier((*parts, mesh_grad))
     total = tree(total, parts)

time: 108 us -> 111 us (1.028)
  starting transfers between devices: 49.1 us -> 54.4 us
  waiting for transfers between devices: 27.5 us -> 24.7 us
    ppermute x24, starting transfers between devices: 35.2 us -> 45.4 us  [send(): return lax.ppermute(value, axes, pairs)]
    ppermute x4, starting transfers between devices: 7.82 us -> 3.44 us  [the longest x1 2.13 us: body(): one = lax.ppermute(mesh_features, 'grid', even_pairs)]
    ppermute x24, waiting for transfers between devices: 23.8 us -> 19.5 us  [send(): return lax.ppermute(value, axes, pairs)]
  transfers between devices with their start and end apart: 34 -> 34, of which waited for: 18 -> 15; matrix products, arithmetic and copies ran while one was open for 6% -> 5% of each run, Pallas kernels for 11% -> 11%
where the time goes in v9:
time: 111 us; the launch traced here: 110 us
  starting transfers between devices  54.4 us (49%)
  waiting for transfers between devices  24.7 us (22%)
  Pallas kernels  24.1 us (22%)
  matrix products  5.7 us (5%)
    ppermute x24, starting transfers between devices, send(): return lax.ppermute(value, axes, pairs)  45.4 us
    ppermute x24, waiting for transfers between devices, send(): return lax.ppermute(value, axes, pairs)  19.5 us
    pallas_call x1, Pallas kernels, body(): pl.pallas_call(query_kernel, in_specs=[me_spec, whole(), in_hbm, in_hbm,...  4.86 us
    pallas_call x1, Pallas kernels, body(): call(functools.partial(far_backward_kernel, scale, loss_scale), 'far_back...  4.84 us
    pallas_call x1, Pallas kernels, body(): call(far_forward_kernel, 'far_forward', forward_work, [rows_of(far), pl.B...  3.88 us
    pallas_call x1, Pallas kernels, body(): call(near_backward_kernel, 'near_backward', backward_work, backward_specs...  3.83 us
    pallas_call x1, Pallas kernels, body(): call(near_forward_kernel, 'near_forward', forward_work, [rows_of(near), p...  3.37 us
    dot_general x1, matrix products, body(): jnp.einsum('npu,wu->npw', grad_query, dst_weight, precision=lax.Precision...  3.21 us
  transfers between devices with their start and end apart: 34, of which 15 were waited for; matrix products, arithmetic and copies ran while one was open for 5% of the time, Pallas kernels for 11%

profile of v9, /device:TPU:1, one launch (start us, length us, event | category | flops | bytes accessed | tf_op | source)
XLA Modules:
  0.0 110.4 jit_solution(2788237324875498645)
XLA Ops:
  0.6 2.1 %collective-permute-start = (f32[2,32,512]{2,1,0:T(8,128)}, f32[2,32,512]{2,1,0:T(8,128)S(1)}, u32[]{:S(2)}, u32[]{:S(2)}) collective-permute-start(f32[2,32,512]{2,1,0:T(8,128)} %own.3), channel_id=1, source_target_pairs={{0,1},{1,0},{2,3},{3,2},{4,5},{5,4},{6,7},{7,6},{8,9},{9,8},{10,11... | collective-permute-start | bytes 393224 | tf_op jit(solution)/shard_map/ppermute | solution.py:343
  2.8 0.7 collective-permute-start.1
  3.5 4.9 %query.1 = (f32[2,512,512]{2,1,0:T(8,128)S(1)}, s32[512,8]{1,0:T(8,128)S(1)}, bf16[512,512]{1,0:T(8,128)(2,1)S(1)}, bf16[512,512]{1,0:T(8,128)(2,1)S(1)}) custom-call(s32[5]{0:T(128)S(1)} %stack.23.me, s32[4,512]{1,0:T(4,128)} %edges.5, f32[2,512,512]{2,1,0:T(8,128)} %features.5, f32[512,512]{1,0:T(8,128)} %weight.1, f32[512,512]{1,0:T(8,128)} %src_weight.1), custom_call_target="tpu_custom_call" | custom-call | tf_op jit(solution)/shard_map/query/pallas_call | solution.py:348
  8.4 3.9 %far_forward.1 = (f32[2,4,256,512]{3,2,1,0:T(8,128)S(1)}, f32[2,256,512]{2,1,0:T(8,128)S(1)}, f32[2,100,128]{2,1,0:T(8,128)S(1)}, f32[2,100,128]{2,1,0:T(8,128)S(1)}, bf16[2,256,512]{2,1,0:T(8,128)(2,1)S(1)}) custom-call(s32[5]{0:T(128)S(1)} %stack.23.me, f32[2,512,512]{2,1,0:T(8,128)S(1)} %get-tuple-element.62.query, s32[512,8]{1,0:T(8,128)S(1)} %get-tuple-element.63.edges, ...), custom_call_target="tpu_custom_call" | custom-call | flops 1231028224 | bytes 2097152 | tf_op jit(solution)/shard_map/far_forward/pallas_call | solution.py:413
  12.3 1.4 %collective-permute-start.2 = (f32[2,100,128]{2,1,0:T(8,128)S(1)}, f32[2,100,128]{2,1,0:T(8,128)S(1)}, u32[]{:S(2)}, u32[]{:S(2)}) collective-permute-start(f32[2,100,128]{2,1,0:T(8,128)S(1)} %get-tuple-element.69), channel_id=1, source_target_pairs={{0,128},{64,192},{128,0},{192,64},{1,129},{65,193},{129,1},{193,65... | collective-permute-start | bytes 307208 | tf_op jit(solution)/shard_map/ppermute | solution.py:423
  13.7 1.6 %collective-permute-start.3 = (f32[2,100,128]{2,1,0:T(8,128)S(1)}, f32[2,100,128]{2,1,0:T(8,128)S(1)}, u32[]{:S(2)}, u32[]{:S(2)}) collective-permute-start(f32[2,100,128]{2,1,0:T(8,128)S(1)} %get-tuple-element.70), channel_id=1, source_target_pairs={{0,192},{64,128},{128,64},{192,0},{1,193},{65,129},{129,65},{193,1... | collective-permute-start | bytes 307208 | tf_op jit(solution)/shard_map/ppermute | solution.py:424
  15.3 3.4 %near_forward.1 = (f32[2,4,256,512]{3,2,1,0:T(8,128)S(1)}, f32[2,256,512]{2,1,0:T(8,128)S(1)}, f32[2,100,128]{2,1,0:T(8,128)S(1)}, f32[2,100,128]{2,1,0:T(8,128)S(1)}) custom-call(s32[5]{0:T(128)S(1)} %stack.23.me, f32[2,512,512]{2,1,0:T(8,128)S(1)} %get-tuple-element.62.query, s32[512,8]{1,0:T(8,128)S(1)} %get-tuple-element.63.edges, ...), custom_call_target="tpu_custom_call" | custom-call | flops 1231028224 | bytes 2097152 | tf_op jit(solution)/shard_map/near_forward/pallas_call | solution.py:425
  18.7 0.6 collective-permute-done.2.part2
  19.2 2.3 %collective-permute-done.3.part3 = f32[2,100,128]{2,1,0:T(8,128)S(1)} collective-permute-done((f32[2,100,128]{2,1,0:T(8,128)S(1)}, f32[2,100,128]{2,1,0:T(8,128)S(1)}, u32[]{:S(2)}, u32[]{:S(2)}) %collective-permute-start.3) | collective-permute-done | bytes 102432 | tf_op jit(solution)/shard_map/ppermute | solution.py:424
  21.5 0.4 collective-permute-start.4
  21.9 1.0 collective-permute-done.4.part1
  22.9 1.2 %score.1 = (f32[2,100,128]{2,1,0:T(8,128)S(1)}, f32[2,100,128]{2,1,0:T(8,128)S(1)}, f32[2,100,128]{2,1,0:T(8,128)S(1)}, f32[2,100,128]{2,1,0:T(8,128)S(1)}, f32[8,128]{1,0:T(8,128)S(1)}) custom-call(s32[5]{0:T(128)S(1)} %stack.23.me, f32[2,100,128]{2,1,0:T(8,128)S(1)} %get-tuple-element.71.part0, f32[2,100,128]{2,1,0:T(8,128)S(1)} %collective-permute-done.4.part1, ...), custom_call_target="tpu_custom_call" | custom-call | tf_op jit(solution)/shard_map/score/pallas_call | solution.py:436
  24.1 0.4 collective-permute-start.7
  24.5 0.2 collective-permute-start.5
  24.8 1.6 %collective-permute-start.6 = (f32[2,100,128]{2,1,0:T(8,128)S(1)}, f32[2,100,128]{2,1,0:T(8,128)S(1)}, u32[]{:S(2)}, u32[]{:S(2)}) collective-permute-start(f32[2,100,128]{2,1,0:T(8,128)S(1)} %get-tuple-element.76), channel_id=1, source_target_pairs={{0,192},{64,128},{128,64},{192,0},{1,193},{65,129},{129,65},{193,1... | collective-permute-start | bytes 307208 | tf_op jit(solution)/shard_map/ppermute | solution.py:469
  26.3 3.8 %near_backward.1 = (f32[2,256,512]{2,1,0:T(8,128)S(1)}, f32[2,96,512]{2,1,0:T(8,128)S(1)}, f32[512,512]{1,0:T(8,128)S(1)}, f32[100,512]{1,0:T(8,128)S(1)}) custom-call(s32[5]{0:T(128)S(1)} %stack.23.me, f32[2,100,128]{2,1,0:T(8,128)S(1)} %get-tuple-element.77.same, f32[2,100,128]{2,1,0:T(8,128)S(1)} %collective-permute-done.7.flipped, ...), custom_call_target="tpu_custom_call" | custom-call | flops 2193620992 | bytes 2097152 | tf_op jit(solution)/shard_map/near_backward/pallas_call | solution.py:470
  30.2 1.3 %collective-permute-done.6.flipped = f32[2,100,128]{2,1,0:T(8,128)S(1)} collective-permute-done((f32[2,100,128]{2,1,0:T(8,128)S(1)}, f32[2,100,128]{2,1,0:T(8,128)S(1)}, u32[]{:S(2)}, u32[]{:S(2)}) %collective-permute-start.6) | collective-permute-done | bytes 102432 | tf_op jit(solution)/shard_map/ppermute | solution.py:469
  31.5 4.8 %far_backward.1 = (f32[2,256,512]{2,1,0:T(8,128)S(1)}, f32[2,32,512]{2,1,0:T(8,128)S(1)}, f32[2,32,512]{2,1,0:T(8,128)S(1)}, f32[2,32,512]{2,1,0:T(8,128)S(1)}, ...) custom-call(s32[5]{0:T(128)S(1)} %stack.23.me, ...), custom_call_target="tpu_custom_call" | custom-call | flops 2193620992 | bytes 2097152 | tf_op jit(solution)/shard_map/far_backward/pallas_call | solution.py:479
  36.5 0.4 collective-permute-start.13
  37.1 0.4 collective-permute-start.8
  37.5 0.6 collective-permute-done.9
  38.1 10.0 %collective-permute-start.10 = (f32[4,72,256]{2,1,0:T(8,128)S(1)}, f32[4,72,256]{2,1,0:T(8,128)S(1)}, u32[]{:S(2)}, u32[]{:S(2)}) collective-permute-start(f32[4,72,256]{2,1,0:T(8,128)S(1)} %add.69), channel_id=1, source_target_pairs={{0,2},{1,33},{2,0},{3,35},{4,6},{5,37},{6,4},{7,39},{8,10},{9,41},... | collective-permute-start | bytes 884744 | tf_op jit(solution)/shard_map/ppermute | solution.py:60
  48.3 0.5 collective-permute-start.12
  48.8 3.4 %collective-permute-done.10 = f32[4,72,256]{2,1,0:T(8,128)S(1)} collective-permute-done((f32[4,72,256]{2,1,0:T(8,128)S(1)}, f32[4,72,256]{2,1,0:T(8,128)S(1)}, u32[]{:S(2)}, u32[]{:S(2)}) %collective-permute-start.10) | collective-permute-done | bytes 294944 | tf_op jit(solution)/shard_map/ppermute | solution.py:60
  52.2 3.4 %collective-permute-done.14 = f32[4,72,256]{2,1,0:T(8,128)S(1)} collective-permute-done((f32[4,72,256]{2,1,0:T(8,128)S(1)}, f32[4,72,256]{2,1,0:T(8,128)S(1)}, u32[]{:S(2)}, u32[]{:S(2)}) %collective-permute-start.14) | collective-permute-done | bytes 294944 | tf_op jit(solution)/shard_map/ppermute | solution.py:60
  55.6 0.5 collective-permute-done.12
  56.4 3.4 %collective-permute-start.18 = (f32[1,72,256]{2,1,0:T(8,128)S(1)}, f32[1,72,256]{2,1,0:T(8,128)S(1)}, u32[]{:S(2)}, u32[]{:S(2)}) collective-permute-start(f32[1,72,256]{2,1,0:T(8,128)S(1)} %get-tuple-element.120), channel_id=1, source_target_pairs={{0,224},{1,66},{2,226},{3,64},{4,228},{5,70},{6,230},{7,68},{8,232... | collective-permute-start | bytes 221192 | tf_op jit(solution)/shard_map/ppermute | solution.py:60
  59.9 1.5 %collective-permute-done.15 = f32[1,72,256]{2,1,0:T(8,128)S(1)} collective-permute-done((f32[1,72,256]{2,1,0:T(8,128)S(1)}, f32[1,72,256]{2,1,0:T(8,128)S(1)}, u32[]{:S(2)}, u32[]{:S(2)}) %collective-permute-start.15) | collective-permute-done | bytes 73760 | tf_op jit(solution)/shard_map/ppermute | solution.py:60
  61.3 0.7 collective-permute-start.22
  62.1 0.8 collective-permute-start.19
  62.9 3.4 %collective-permute-start.20 = (f32[1,72,256]{2,1,0:T(8,128)S(1)}, f32[1,72,256]{2,1,0:T(8,128)S(1)}, u32[]{:S(2)}, u32[]{:S(2)}) collective-permute-start(f32[1,72,256]{2,1,0:T(8,128)S(1)} %fusion.12), channel_id=1, source_target_pairs={{0,4},{1,5},{2,6},{3,7},{4,0},{5,1},{6,2},{7,3},{8,12},{9,13},{10,... | collective-permute-start | bytes 221192 | tf_op jit(solution)/shard_map/ppermute | solution.py:60
  66.2 2.0 %collective-permute-start.21 = (f32[1,72,256]{2,1,0:T(8,128)S(1)}, f32[1,72,256]{2,1,0:T(8,128)S(1)}, u32[]{:S(2)}, u32[]{:S(2)}) collective-permute-start(f32[1,72,256]{2,1,0:T(8,128)S(1)} %fusion.12), channel_id=1, source_target_pairs={{0,12},{1,13},{2,14},{3,15},{4,8},{5,9},{6,10},{7,11},{8,4},{9,5},... | collective-permute-start | bytes 221192 | tf_op jit(solution)/shard_map/ppermute | solution.py:60
  68.2 2.5 %fusion.7 = f32[2,32,512]{2,1,0:T(8,128)} fusion(f32[512,512]{1,0:T(8,128)} %src_weight.1, f32[2,32,512]{2,1,0:T(8,128)S(1)} %collective-permute-done.22, f32[2,32,512]{2,1,0:T(8,128)S(1)} %get-tuple-element.103, f32[2,32,512]{2,1,0:T(8,128)S(1)} %collective-permute-done.16), kind=kOutput, calls=%fused_computation.8 | convolution fusion | flops 100728832 | bytes 1572864 | tf_op jit(solution)/shard_map/nru,wu->nrw/dot_general | solution.py:508
  70.7 2.6 %collective-permute-done.21 = f32[1,72,256]{2,1,0:T(8,128)S(1)} collective-permute-done((f32[1,72,256]{2,1,0:T(8,128)S(1)}, f32[1,72,256]{2,1,0:T(8,128)S(1)}, u32[]{:S(2)}, u32[]{:S(2)}) %collective-permute-start.21) | collective-permute-done | bytes 73760 | tf_op jit(solution)/shard_map/ppermute | solution.py:60
  73.3 4.4 %collective-permute-start.23 = (f32[1,72,256]{2,1,0:T(8,128)S(1)}, f32[1,72,256]{2,1,0:T(8,128)S(1)}, u32[]{:S(2)}, u32[]{:S(2)}) collective-permute-start(f32[1,72,256]{2,1,0:T(8,128)S(1)} %add_add_fusion.1), channel_id=1, source_target_pairs={{0,16},{1,17},{2,18},{3,19},{4,20},{5,21},{6,22},{7,23},{8,24},{9,... | collective-permute-start | bytes 221192 | tf_op jit(solution)/shard_map/ppermute | solution.py:60
  77.7 3.2 %fusion = f32[2,512,512]{2,1,0:T(8,128)} fusion(f32[2,256,512]{2,1,0:T(8,128)S(1)} %get-tuple-element.110, f32[2,256,512]{2,1,0:T(8,128)S(1)} %get-tuple-element.109, f32[512,512]{1,0:T(8,128)S(1)} %copy-done.5, pred[]{:T(512)S(6)} %lt.15), kind=kOutput, calls=%fused_computation.1 | convolution fusion | flops 1612185600 | bytes 5242881 | tf_op jit(solution)/shard_map/npu,wu->npw/dot_general | solution.py:514
  81.1 6.0 %collective-permute-start.25 = (f32[1,72,256]{2,1,0:T(8,128)S(1)}, f32[1,72,256]{2,1,0:T(8,128)S(1)}, u32[]{:S(2)}, u32[]{:S(2)}) collective-permute-start(f32[1,72,256]{2,1,0:T(8,128)S(1)} %get-tuple-element.119), channel_id=1, source_target_pairs={{0,192},{1,64},{2,194},{3,66},{4,196},{5,68},{6,198},{7,70},{8,200... | collective-permute-start | bytes 221192 | tf_op jit(solution)/shard_map/ppermute | solution.py:60
  87.2 2.8 %collective-permute-done.25 = f32[1,72,256]{2,1,0:T(8,128)S(1)} collective-permute-done((f32[1,72,256]{2,1,0:T(8,128)S(1)}, f32[1,72,256]{2,1,0:T(8,128)S(1)}, u32[]{:S(2)}, u32[]{:S(2)}) %collective-permute-start.25) | collective-permute-done | bytes 73760 | tf_op jit(solution)/shard_map/ppermute | solution.py:60
  90.0 2.4 %collective-permute-done.26 = f32[1,72,256]{2,1,0:T(8,128)S(1)} collective-permute-done((f32[1,72,256]{2,1,0:T(8,128)S(1)}, f32[1,72,256]{2,1,0:T(8,128)S(1)}, u32[]{:S(2)}, u32[]{:S(2)}) %collective-permute-start.26) | collective-permute-done | bytes 73760 | tf_op jit(solution)/shard_map/ppermute | solution.py:60
  92.4 2.1 %collective-permute-start.27 = (f32[4,72,256]{2,1,0:T(8,128)S(1)}, f32[4,72,256]{2,1,0:T(8,128)S(1)}, u32[]{:S(2)}, u32[]{:S(2)}) collective-permute-start(f32[4,72,256]{2,1,0:T(8,128)S(1)} %constant_dynamic-update-slice_fusion.refs_0_), channel_id=1, source_target_pairs={{0,2},{1,33},{2,0},{3,35},{4,6},{5,37},{6,4},{7,39},{8,10},{9,41},... | collective-permute-start | bytes 884744 | tf_op jit(solution)/shard_map/ppermute | solution.py:60
  94.5 2.4 %collective-permute-start.28 = (f32[4,72,256]{2,1,0:T(8,128)S(1)}, f32[4,72,256]{2,1,0:T(8,128)S(1)}, u32[]{:S(2)}, u32[]{:S(2)}) collective-permute-start(f32[4,72,256]{2,1,0:T(8,128)S(1)} %constant_dynamic-update-slice_fusion.refs_0_), channel_id=1, source_target_pairs={{0,65},{1,193},{2,67},{3,195},{4,69},{5,197},{6,71},{7,199},{8,73}... | collective-permute-start | bytes 884744 | tf_op jit(solution)/shard_map/ppermute | solution.py:60
  96.9 2.4 %collective-permute-start.30 = (f32[4,72,256]{2,1,0:T(8,128)S(1)}, f32[4,72,256]{2,1,0:T(8,128)S(1)}, u32[]{:S(2)}, u32[]{:S(2)}) collective-permute-start(f32[4,72,256]{2,1,0:T(8,128)S(1)} %constant_dynamic-update-slice_fusion.refs_0_), channel_id=1, source_target_pairs={{0,64},{1,65},{2,66},{3,67},{4,68},{5,69},{6,70},{7,71},{8,72},{9,... | collective-permute-start | bytes 884744 | tf_op jit(solution)/shard_map/ppermute | solution.py:60
  99.4 0.2 collective-permute-done.27.refs_1_
  99.6 4.3 %collective-permute-start.31 = (f32[4,72,256]{2,1,0:T(8,128)S(1)}, f32[4,72,256]{2,1,0:T(8,128)S(1)}, u32[]{:S(2)}, u32[]{:S(2)}) collective-permute-start(f32[4,72,256]{2,1,0:T(8,128)S(1)} %collective-permute-done.27.refs_1_), channel_id=1, source_target_pairs={{0,64},{1,65},{2,66},{3,67},{4,68},{5,69},{6,70},{7,71},{8,72},{9,... | collective-permute-start | bytes 884744 | tf_op jit(solution)/shard_map/ppermute | solution.py:60
  103.9 0.9 collective-permute-done.28.refs_2_
  104.8 2.1 %collective-permute-start.33 = (f32[4,72,256]{2,1,0:T(8,128)S(1)}, f32[4,72,256]{2,1,0:T(8,128)S(1)}, u32[]{:S(2)}, u32[]{:S(2)}) collective-permute-start(f32[4,72,256]{2,1,0:T(8,128)S(1)} %collective-permute-done.29.refs_3_), channel_id=1, source_target_pairs={{0,64},{1,65},{2,66},{3,67},{4,68},{5,69},{6,70},{7,71},{8,72},{9,... | collective-permute-start | bytes 884744 | tf_op jit(solution)/shard_map/ppermute | solution.py:60
  106.9 1.2 %collective-permute-done.33.refs_7_ = f32[4,72,256]{2,1,0:T(8,128)S(1)} collective-permute-done((f32[4,72,256]{2,1,0:T(8,128)S(1)}, f32[4,72,256]{2,1,0:T(8,128)S(1)}, u32[]{:S(2)}, u32[]{:S(2)}) %collective-permute-start.33) | collective-permute-done | bytes 294944 | tf_op jit(solution)/shard_map/ppermute | solution.py:60
  108.1 2.1 %finish.1 = (f32[512,512]{1,0:T(8,128)}, f32[512,512]{1,0:T(8,128)}, f32[100,512]{1,0:T(8,128)}, f32[1,1]{1,0:T(1,128)}) custom-call(s32[5]{0:T(128)S(1)} %stack.23.me, f32[4,72,256]{2,1,0:T(8,128)S(1)} %constant_dynamic-update-slice_fusion.refs_0_, f32[4,72,256]{2,1,0:T(8,128)S(1)} %collective-permute-done.27.refs_1_, ...), custom_call_target="tpu_custom_call" | custom-call | tf_op jit(solution)/shard_map/finish/pallas_call | solution.py:521
  (54 shorter events, 1.2 us)
Async XLA Ops:
  0.6 7.8 %collective-permute-start = (f32[2,32,512]{2,1,0:T(8,128)}, f32[2,32,512]{2,1,0:T(8,128)S(1)}, u32[]{:S(2)}, u32[]{:S(2)}) collective-permute-start(f32[2,32,512]{2,1,0:T(8,128)} %own.3), channel_id=1, source_target_pairs={{0,1},{1,0},{2,3},{3,2},{4,5},{5,4},{6,7},{7,6},{8,9},{9,8},{10,11... | collective-permute-start | bytes 393224 | tf_op jit(solution)/shard_map/ppermute | solution.py:343
  2.8 5.7 %collective-permute-start.1 = (f32[2,32,512]{2,1,0:T(8,128)}, f32[2,32,512]{2,1,0:T(8,128)S(1)}, u32[]{:S(2)}, u32[]{:S(2)}) collective-permute-start(f32[2,32,512]{2,1,0:T(8,128)} %own.3), channel_id=1, source_target_pairs={{1,2},{3,4},{5,6},{7,8},{9,10},{11,12},{13,14},{15,16},{17,18},{19... | collective-permute-start | bytes 393224 | tf_op jit(solution)/shard_map/ppermute | solution.py:344
  3.5 4.9 %copy-start.2 = (f32[512,100]{0,1:T(8,128)S(1)}, f32[512,100]{0,1:T(8,128)}, u32[]{:S(2)}) copy-start(f32[512,100]{0,1:T(8,128)} %param.13) | copy-start | bytes 614404
  3.5 4.9 %copy-start.3 = (f32[2,32,512]{2,1,0:T(8,128)S(1)}, f32[2,32,512]{2,1,0:T(8,128)}, u32[]{:S(2)}) copy-start(f32[2,32,512]{2,1,0:T(8,128)} %own.3) | copy-start | bytes 393220
  12.3 6.9 %collective-permute-start.2 = (f32[2,100,128]{2,1,0:T(8,128)S(1)}, f32[2,100,128]{2,1,0:T(8,128)S(1)}, u32[]{:S(2)}, u32[]{:S(2)}) collective-permute-start(f32[2,100,128]{2,1,0:T(8,128)S(1)} %get-tuple-element.69), channel_id=1, source_target_pairs={{0,128},{64,192},{128,0},{192,64},{1,129},{65,193},{129,1},{193,65... | collective-permute-start | bytes 307208 | tf_op jit(solution)/shard_map/ppermute | solution.py:423
  13.7 7.8 %collective-permute-start.3 = (f32[2,100,128]{2,1,0:T(8,128)S(1)}, f32[2,100,128]{2,1,0:T(8,128)S(1)}, u32[]{:S(2)}, u32[]{:S(2)}) collective-permute-start(f32[2,100,128]{2,1,0:T(8,128)S(1)} %get-tuple-element.70), channel_id=1, source_target_pairs={{0,192},{64,128},{128,64},{192,0},{1,193},{65,129},{129,65},{193,1... | collective-permute-start | bytes 307208 | tf_op jit(solution)/shard_map/ppermute | solution.py:424
  15.3 7.6 %copy-start.1 = (f32[100,512]{1,0:T(8,128)S(1)}, f32[100,512]{1,0:T(8,128)}, u32[]{:S(2)}) copy-start(f32[100,512]{1,0:T(8,128)} %targets.1) | copy-start | bytes 614404
  15.3 11.0 %copy-start = (f32[2,512,512]{2,1,0:T(8,128)S(1)}, f32[2,512,512]{2,1,0:T(8,128)}, u32[]{:S(2)}) copy-start(f32[2,512,512]{2,1,0:T(8,128)} %features.5) | copy-start | bytes 6291460
  15.3 11.0 %copy-start.4 = (s32[4,512]{1,0:T(4,128)S(1)}, s32[4,512]{1,0:T(4,128)}, u32[]{:S(2)}) copy-start(s32[4,512]{1,0:T(4,128)} %edges.5) | copy-start | bytes 24580
  21.5 1.4 %collective-permute-start.4 = (f32[2,100,128]{2,1,0:T(8,128)S(1)}, f32[2,100,128]{2,1,0:T(8,128)S(1)}, u32[]{:S(2)}, u32[]{:S(2)}) collective-permute-start(f32[2,100,128]{2,1,0:T(8,128)S(1)} %get-tuple-element.72), channel_id=1, source_target_pairs={{0,64},{64,0},{128,192},{192,128},{1,65},{65,1},{129,193},{193,129... | collective-permute-start | bytes 307208 | tf_op jit(solution)/shard_map/ppermute | solution.py:434
  24.1 2.2 %collective-permute-start.7 = (f32[2,100,128]{2,1,0:T(8,128)S(1)}, f32[2,100,128]{2,1,0:T(8,128)S(1)}, u32[]{:S(2)}, u32[]{:S(2)}) collective-permute-start(f32[2,100,128]{2,1,0:T(8,128)S(1)} %get-tuple-element.78), channel_id=1, source_target_pairs={{0,64},{64,0},{128,192},{192,128},{1,65},{65,1},{129,193},{193,129... | collective-permute-start | bytes 307208 | tf_op jit(solution)/shard_map/ppermute | solution.py:467
  24.5 5.6 %collective-permute-start.5 = (f32[2,100,128]{2,1,0:T(8,128)S(1)}, f32[2,100,128]{2,1,0:T(8,128)S(1)}, u32[]{:S(2)}, u32[]{:S(2)}) collective-permute-start(f32[2,100,128]{2,1,0:T(8,128)S(1)} %get-tuple-element.75), channel_id=1, source_target_pairs={{0,128},{64,192},{128,0},{192,64},{1,129},{65,193},{129,1},{193,65... | collective-permute-start | bytes 307208 | tf_op jit(solution)/shard_map/ppermute | solution.py:468
  24.8 6.7 %collective-permute-start.6 = (f32[2,100,128]{2,1,0:T(8,128)S(1)}, f32[2,100,128]{2,1,0:T(8,128)S(1)}, u32[]{:S(2)}, u32[]{:S(2)}) collective-permute-start(f32[2,100,128]{2,1,0:T(8,128)S(1)} %get-tuple-element.76), channel_id=1, source_target_pairs={{0,192},{64,128},{128,64},{192,0},{1,193},{65,129},{129,65},{193,1... | collective-permute-start | bytes 307208 | tf_op jit(solution)/shard_map/ppermute | solution.py:469
  36.3 1.7 %collective-permute-start.9 = (f32[4,72,256]{2,1,0:T(8,128)S(1)}, f32[4,72,256]{2,1,0:T(8,128)S(1)}, u32[]{:S(2)}, u32[]{:S(2)}) collective-permute-start(f32[4,72,256]{2,1,0:T(8,128)S(1)} %get-tuple-element.95), channel_id=1, source_target_pairs={{0,64},{1,65},{2,66},{3,67},{4,68},{5,69},{6,70},{7,71},{8,72},{9,... | collective-permute-start | bytes 884744 | tf_op jit(solution)/shard_map/ppermute | solution.py:60
  36.5 11.5 %collective-permute-start.13 = (f32[4,72,256]{2,1,0:T(8,128)S(1)}, f32[4,72,256]{2,1,0:T(8,128)S(1)}, u32[]{:S(2)}, u32[]{:S(2)}) collective-permute-start(f32[4,72,256]{2,1,0:T(8,128)S(1)} %get-tuple-element.99), channel_id=1, source_target_pairs={{0,64},{1,65},{2,66},{3,67},{4,68},{5,69},{6,70},{7,71},{8,72},{9,... | collective-permute-start | bytes 884744 | tf_op jit(solution)/shard_map/ppermute | solution.py:60
  36.9 11.3 %collective-permute-start.11 = (f32[4,72,256]{2,1,0:T(8,128)S(1)}, f32[4,72,256]{2,1,0:T(8,128)S(1)}, u32[]{:S(2)}, u32[]{:S(2)}) collective-permute-start(f32[4,72,256]{2,1,0:T(8,128)S(1)} %get-tuple-element.97), channel_id=1, source_target_pairs={{0,64},{1,65},{2,66},{3,67},{4,68},{5,69},{6,70},{7,71},{8,72},{9,... | collective-permute-start | bytes 884744 | tf_op jit(solution)/shard_map/ppermute | solution.py:60
  37.1 11.7 %collective-permute-start.8 = (f32[4,72,256]{2,1,0:T(8,128)S(1)}, f32[4,72,256]{2,1,0:T(8,128)S(1)}, u32[]{:S(2)}, u32[]{:S(2)}) collective-permute-start(f32[4,72,256]{2,1,0:T(8,128)S(1)} %get-tuple-element.92), channel_id=1, source_target_pairs={{0,64},{1,65},{2,66},{3,67},{4,68},{5,69},{6,70},{7,71},{8,72},{9,... | collective-permute-start | bytes 884744 | tf_op jit(solution)/shard_map/ppermute | solution.py:60
  38.1 14.2 %collective-permute-start.10 = (f32[4,72,256]{2,1,0:T(8,128)S(1)}, f32[4,72,256]{2,1,0:T(8,128)S(1)}, u32[]{:S(2)}, u32[]{:S(2)}) collective-permute-start(f32[4,72,256]{2,1,0:T(8,128)S(1)} %add.69), channel_id=1, source_target_pairs={{0,2},{1,33},{2,0},{3,35},{4,6},{5,37},{6,4},{7,39},{8,10},{9,41},... | collective-permute-start | bytes 884744 | tf_op jit(solution)/shard_map/ppermute | solution.py:60
  48.1 7.4 %collective-permute-start.14 = (f32[4,72,256]{2,1,0:T(8,128)S(1)}, f32[4,72,256]{2,1,0:T(8,128)S(1)}, u32[]{:S(2)}, u32[]{:S(2)}) collective-permute-start(f32[4,72,256]{2,1,0:T(8,128)S(1)} %add.72), channel_id=1, source_target_pairs={{0,67},{1,225},{2,65},{3,227},{4,71},{5,229},{6,69},{7,231},{8,75}... | collective-permute-start | bytes 884744 | tf_op jit(solution)/shard_map/ppermute | solution.py:60
  48.3 7.8 %collective-permute-start.12 = (f32[4,72,256]{2,1,0:T(8,128)S(1)}, f32[4,72,256]{2,1,0:T(8,128)S(1)}, u32[]{:S(2)}, u32[]{:S(2)}) collective-permute-start(f32[4,72,256]{2,1,0:T(8,128)S(1)} %add.71), channel_id=1, source_target_pairs={{0,65},{1,193},{2,67},{3,195},{4,69},{5,197},{6,71},{7,199},{8,73}... | collective-permute-start | bytes 884744 | tf_op jit(solution)/shard_map/ppermute | solution.py:60
  48.8 11.1 %collective-permute-start.16 = (f32[2,32,512]{2,1,0:T(8,128)S(1)}, f32[2,32,512]{2,1,0:T(8,128)S(1)}, u32[]{:S(2)}, u32[]{:S(2)}) collective-permute-start(f32[2,32,512]{2,1,0:T(8,128)S(1)} %get-tuple-element.100), channel_id=1, source_target_pairs={{0,1},{1,0},{2,3},{3,2},{4,5},{5,4},{6,7},{7,6},{8,9},{9,8},{10,11... | collective-permute-start | bytes 393224 | tf_op jit(solution)/shard_map/ppermute | solution.py:501
  56.2 5.1 %collective-permute-start.15 = (f32[1,72,256]{2,1,0:T(8,128)S(1)}, f32[1,72,256]{2,1,0:T(8,128)S(1)}, u32[]{:S(2)}, u32[]{:S(2)}) collective-permute-start(f32[1,72,256]{2,1,0:T(8,128)S(1)} %get-tuple-element.122), channel_id=1, source_target_pairs={{0,32},{1,3},{2,34},{3,1},{4,36},{5,7},{6,38},{7,5},{8,40},{9,11},... | collective-permute-start | bytes 221192 | tf_op jit(solution)/shard_map/ppermute | solution.py:60
  56.3 5.7 %collective-permute-start.17 = (f32[1,72,256]{2,1,0:T(8,128)S(1)}, f32[1,72,256]{2,1,0:T(8,128)S(1)}, u32[]{:S(2)}, u32[]{:S(2)}) collective-permute-start(f32[1,72,256]{2,1,0:T(8,128)S(1)} %get-tuple-element.121), channel_id=1, source_target_pairs={{0,192},{1,64},{2,194},{3,66},{4,196},{5,68},{6,198},{7,70},{8,200... | collective-permute-start | bytes 221192 | tf_op jit(solution)/shard_map/ppermute | solution.py:60
  56.4 5.6 %collective-permute-start.18 = (f32[1,72,256]{2,1,0:T(8,128)S(1)}, f32[1,72,256]{2,1,0:T(8,128)S(1)}, u32[]{:S(2)}, u32[]{:S(2)}) collective-permute-start(f32[1,72,256]{2,1,0:T(8,128)S(1)} %get-tuple-element.120), channel_id=1, source_target_pairs={{0,224},{1,66},{2,226},{3,64},{4,228},{5,70},{6,230},{7,68},{8,232... | collective-permute-start | bytes 221192 | tf_op jit(solution)/shard_map/ppermute | solution.py:60
  59.9 17.9 %copy-start.5 = (f32[512,512]{1,0:T(8,128)S(1)}, f32[512,512]{1,0:T(8,128)}, u32[]{:S(2)}) copy-start(f32[512,512]{1,0:T(8,128)} %weight.1) | copy-start | bytes 3145732
  61.3 6.9 %collective-permute-start.22 = (f32[2,32,512]{2,1,0:T(8,128)S(1)}, f32[2,32,512]{2,1,0:T(8,128)S(1)}, u32[]{:S(2)}, u32[]{:S(2)}) collective-permute-start(f32[2,32,512]{2,1,0:T(8,128)S(1)} %get-tuple-element.105), channel_id=1, source_target_pairs={{1,2},{3,4},{5,6},{7,8},{9,10},{11,12},{13,14},{15,16},{17,18},{19... | collective-permute-start | bytes 393224 | tf_op jit(solution)/shard_map/ppermute | solution.py:505
  62.1 8.7 %collective-permute-start.19 = (f32[1,72,256]{2,1,0:T(8,128)S(1)}, f32[1,72,256]{2,1,0:T(8,128)S(1)}, u32[]{:S(2)}, u32[]{:S(2)}) collective-permute-start(f32[1,72,256]{2,1,0:T(8,128)S(1)} %fusion.12), channel_id=1, source_target_pairs={{0,8},{1,9},{2,10},{3,11},{4,12},{5,13},{6,14},{7,15},{8,0},{9,1},... | collective-permute-start | bytes 221192 | tf_op jit(solution)/shard_map/ppermute | solution.py:60
  62.9 7.8 %collective-permute-start.20 = (f32[1,72,256]{2,1,0:T(8,128)S(1)}, f32[1,72,256]{2,1,0:T(8,128)S(1)}, u32[]{:S(2)}, u32[]{:S(2)}) collective-permute-start(f32[1,72,256]{2,1,0:T(8,128)S(1)} %fusion.12), channel_id=1, source_target_pairs={{0,4},{1,5},{2,6},{3,7},{4,0},{5,1},{6,2},{7,3},{8,12},{9,13},{10,... | collective-permute-start | bytes 221192 | tf_op jit(solution)/shard_map/ppermute | solution.py:60
  66.2 7.1 %collective-permute-start.21 = (f32[1,72,256]{2,1,0:T(8,128)S(1)}, f32[1,72,256]{2,1,0:T(8,128)S(1)}, u32[]{:S(2)}, u32[]{:S(2)}) collective-permute-start(f32[1,72,256]{2,1,0:T(8,128)S(1)} %fusion.12), channel_id=1, source_target_pairs={{0,12},{1,13},{2,14},{3,15},{4,8},{5,9},{6,10},{7,11},{8,4},{9,5},... | collective-permute-start | bytes 221192 | tf_op jit(solution)/shard_map/ppermute | solution.py:60
  73.3 7.6 %collective-permute-start.23 = (f32[1,72,256]{2,1,0:T(8,128)S(1)}, f32[1,72,256]{2,1,0:T(8,128)S(1)}, u32[]{:S(2)}, u32[]{:S(2)}) collective-permute-start(f32[1,72,256]{2,1,0:T(8,128)S(1)} %add_add_fusion.1), channel_id=1, source_target_pairs={{0,16},{1,17},{2,18},{3,19},{4,20},{5,21},{6,22},{7,23},{8,24},{9,... | collective-permute-start | bytes 221192 | tf_op jit(solution)/shard_map/ppermute | solution.py:60
  81.0 6.1 %collective-permute-start.24 = (f32[1,72,256]{2,1,0:T(8,128)S(1)}, f32[1,72,256]{2,1,0:T(8,128)S(1)}, u32[]{:S(2)}, u32[]{:S(2)}) collective-permute-start(f32[1,72,256]{2,1,0:T(8,128)S(1)} %get-tuple-element.119), channel_id=1, source_target_pairs={{0,32},{1,3},{2,34},{3,1},{4,36},{5,7},{6,38},{7,5},{8,40},{9,11},... | collective-permute-start | bytes 221192 | tf_op jit(solution)/shard_map/ppermute | solution.py:60
  81.1 8.8 %collective-permute-start.25 = (f32[1,72,256]{2,1,0:T(8,128)S(1)}, f32[1,72,256]{2,1,0:T(8,128)S(1)}, u32[]{:S(2)}, u32[]{:S(2)}) collective-permute-start(f32[1,72,256]{2,1,0:T(8,128)S(1)} %get-tuple-element.119), channel_id=1, source_target_pairs={{0,192},{1,64},{2,194},{3,66},{4,196},{5,68},{6,198},{7,70},{8,200... | collective-permute-start | bytes 221192 | tf_op jit(solution)/shard_map/ppermute | solution.py:60
  87.1 5.2 %collective-permute-start.26 = (f32[1,72,256]{2,1,0:T(8,128)S(1)}, f32[1,72,256]{2,1,0:T(8,128)S(1)}, u32[]{:S(2)}, u32[]{:S(2)}) collective-permute-start(f32[1,72,256]{2,1,0:T(8,128)S(1)} %get-tuple-element.119), channel_id=1, source_target_pairs={{0,224},{1,66},{2,226},{3,64},{4,228},{5,70},{6,230},{7,68},{8,232... | collective-permute-start | bytes 221192 | tf_op jit(solution)/shard_map/ppermute | solution.py:60
  92.4 7.2 %collective-permute-start.27 = (f32[4,72,256]{2,1,0:T(8,128)S(1)}, f32[4,72,256]{2,1,0:T(8,128)S(1)}, u32[]{:S(2)}, u32[]{:S(2)}) collective-permute-start(f32[4,72,256]{2,1,0:T(8,128)S(1)} %constant_dynamic-update-slice_fusion.refs_0_), channel_id=1, source_target_pairs={{0,2},{1,33},{2,0},{3,35},{4,6},{5,37},{6,4},{7,39},{8,10},{9,41},... | collective-permute-start | bytes 884744 | tf_op jit(solution)/shard_map/ppermute | solution.py:60
  94.5 10.3 %collective-permute-start.28 = (f32[4,72,256]{2,1,0:T(8,128)S(1)}, f32[4,72,256]{2,1,0:T(8,128)S(1)}, u32[]{:S(2)}, u32[]{:S(2)}) collective-permute-start(f32[4,72,256]{2,1,0:T(8,128)S(1)} %constant_dynamic-update-slice_fusion.refs_0_), channel_id=1, source_target_pairs={{0,65},{1,193},{2,67},{3,195},{4,69},{5,197},{6,71},{7,199},{8,73}... | collective-permute-start | bytes 884744 | tf_op jit(solution)/shard_map/ppermute | solution.py:60
  96.9 7.9 %collective-permute-start.29 = (f32[4,72,256]{2,1,0:T(8,128)S(1)}, f32[4,72,256]{2,1,0:T(8,128)S(1)}, u32[]{:S(2)}, u32[]{:S(2)}) collective-permute-start(f32[4,72,256]{2,1,0:T(8,128)S(1)} %constant_dynamic-update-slice_fusion.refs_0_), channel_id=1, source_target_pairs={{0,67},{1,225},{2,65},{3,227},{4,71},{5,229},{6,69},{7,231},{8,75}... | collective-permute-start | bytes 884744 | tf_op jit(solution)/shard_map/ppermute | solution.py:60
  96.9 10.0 %collective-permute-start.30 = (f32[4,72,256]{2,1,0:T(8,128)S(1)}, f32[4,72,256]{2,1,0:T(8,128)S(1)}, u32[]{:S(2)}, u32[]{:S(2)}) collective-permute-start(f32[4,72,256]{2,1,0:T(8,128)S(1)} %constant_dynamic-update-slice_fusion.refs_0_), channel_id=1, source_target_pairs={{0,64},{1,65},{2,66},{3,67},{4,68},{5,69},{6,70},{7,71},{8,72},{9,... | collective-permute-start | bytes 884744 | tf_op jit(solution)/shard_map/ppermute | solution.py:60
  99.6 7.4 %collective-permute-start.31 = (f32[4,72,256]{2,1,0:T(8,128)S(1)}, f32[4,72,256]{2,1,0:T(8,128)S(1)}, u32[]{:S(2)}, u32[]{:S(2)}) collective-permute-start(f32[4,72,256]{2,1,0:T(8,128)S(1)} %collective-permute-done.27.refs_1_), channel_id=1, source_target_pairs={{0,64},{1,65},{2,66},{3,67},{4,68},{5,69},{6,70},{7,71},{8,72},{9,... | collective-permute-start | bytes 884744 | tf_op jit(solution)/shard_map/ppermute | solution.py:60
  104.8 2.1 %collective-permute-start.32 = (f32[4,72,256]{2,1,0:T(8,128)S(1)}, f32[4,72,256]{2,1,0:T(8,128)S(1)}, u32[]{:S(2)}, u32[]{:S(2)}) collective-permute-start(f32[4,72,256]{2,1,0:T(8,128)S(1)} %collective-permute-done.28.refs_2_), channel_id=1, source_target_pairs={{0,64},{1,65},{2,66},{3,67},{4,68},{5,69},{6,70},{7,71},{8,72},{9,... | collective-permute-start | bytes 884744 | tf_op jit(solution)/shard_map/ppermute | solution.py:60
  104.8 3.3 %collective-permute-start.33 = (f32[4,72,256]{2,1,0:T(8,128)S(1)}, f32[4,72,256]{2,1,0:T(8,128)S(1)}, u32[]{:S(2)}, u32[]{:S(2)}) collective-permute-start(f32[4,72,256]{2,1,0:T(8,128)S(1)} %collective-permute-done.29.refs_3_), channel_id=1, source_target_pairs={{0,64},{1,65},{2,66},{3,67},{4,68},{5,69},{6,70},{7,71},{8,72},{9,... | collective-permute-start | bytes 884744 | tf_op jit(solution)/shard_map/ppermute | solution.py:60
